TPU v7x, 256 devices: a whole 4x4x8 slice. The times are simulated.
256 devices in a mesh: lat: 8 (over z_lo, core), lon: 8 (over z_hi, x), dp: 4 (over y).
Axes of the slice: x: 4, y: 4, z: 8 (z_hi: 2, z_lo: 4; z = z_hi * 4 + z_lo), core: 2. Of those that a mesh axis runs over, the one named last changes fastest.
Arguments:
- features: bfloat16 [4, 128, 720, 128], P('dp', 'lat', 'lon'), may hold values from -6 to 6
- cotangent: bfloat16 [4, 128, 720, 128], P('dp', 'lat', 'lon'), may hold values from -6 to 6
- mix_weight: bfloat16 [3, 128, 128], replicated, may hold values from -0.3125 to 0.3125
- amplitude: float32 [3, 128, 5], replicated, may hold values from -4 to 4
- row_spans: int32 [128], replicated, may hold values from 1 to 90, as said below
Outputs:
- convolved: bfloat16 [4, 128, 720, 128], P('dp', 'lat', 'lon')
- grad_features: float32 [4, 128, 720, 128], P('dp', 'lat', 'lon')
- grad_weight: float32 [3, 128, 128], replicated
Inputs may be any that keep to these rules, and one draw needn't show every extreme that they name: For each row i, with base = 2 * 720 // (6 i + 1): row_spans[i] lies between max(1, min(90, base)) and min(90, base + 2), and equals min(90, base + 2) on every even row i. Row 0 reaches 90 cells.
All inputs are finite; a program needn't handle non-finite values.
Results may differ from a plain program's by a relative error of at most 0.0058.
Values may be sent and summed in bfloat16 or wider, within the bound.
No kernel may reach another device: no remote copies, remote signals or barrier semaphores. Data moves between devices by JAX's collectives and lax.ppermute only.
A program may use at most 64 MiB of HBM per device.

v0:
```python
import math

import jax
import jax.numpy as jnp
from jax import lax
from jax.sharding import PartitionSpec as P


def extended(cells, sides, width):
    for axis, dim in sides:
        count = lax.axis_size(axis)
        ends = count - 1
        head = lax.slice_in_dim(cells, 0, width, axis=dim)
        tail = lax.slice_in_dim(cells, cells.shape[dim] - width, cells.shape[dim], axis=dim)
        cells = jnp.concatenate(
            [
                lax.ppermute(tail, axis, [(i, (i + 1) % count) for i in range(ends)]),
                cells,
                lax.ppermute(head, axis, [((i + 1) % count, i) for i in range(ends)]),
            ],
            axis=dim,
        )
    return cells


def basis_values(amplitude_part, extent, offsets):
    divisor = extent.astype(jnp.float32) + 1.0
    scaled = offsets.astype(jnp.float32) / divisor
    shapes = jnp.concatenate([1.0 - jnp.abs(scaled), scaled, jnp.cos(jnp.pi * scaled)], axis=0)
    values = amplitude_part * shapes * (1.0 / jnp.sqrt(divisor))
    return jnp.where(jnp.abs(offsets) <= extent, values, 0.0).astype(jnp.bfloat16)


def body(features, cotangent, mix_weight, amplitude, row_spans):
    samples, row_count, col_count, channels = features.shape
    basis_count = mix_weight.shape[0]
    lon_count = lax.axis_size("lon")
    cycle_rows = row_count // lon_count
    cycle_len = col_count * lon_count
    total_rows = row_count * lax.axis_size("lat")
    reach_cols = cycle_len // 8
    tile_cols = min(128, cycle_len)
    out_tiles = (cycle_len + tile_cols - 1) // tile_cols
    padded_cols = out_tiles * tile_cols
    most_tiles = (2 * reach_cols + 2 * tile_cols - 1) // tile_cols
    ext_width = reach_cols + most_tiles * tile_cols + padded_cols
    first_row = lax.axis_index(("lat", "lon")) * cycle_rows
    column_ids = lax.broadcasted_iota(jnp.int32, (tile_cols, tile_cols), 1)
    row_ids = lax.broadcasted_iota(jnp.int32, (tile_cols, tile_cols), 0)

    def row_setup(global_row):
        extent = row_spans[global_row]
        amplitude_row = lax.dynamic_index_in_dim(amplitude, global_row, 1, keepdims=False)
        tile_count = (2 * extent + 2 * tile_cols - 1) // tile_cols
        return (extent, amplitude_row, tile_count)

    cycle_features, cycle_cotangent = (
        lax.all_to_all(features, "lon", split_axis=1, concat_axis=2, tiled=True),
        lax.all_to_all(cotangent, "lon", split_axis=1, concat_axis=2, tiled=True),
    )
    feature_rows = extended(cycle_features, ((("lat", "lon"), 1),), 2)
    remain = ext_width - reach_cols
    portions = [feature_rows[..., cycle_len - reach_cols :, :]] + [feature_rows] * (
        remain // cycle_len
    )
    portions.append(feature_rows[..., : remain % cycle_len, :])
    feature_wide = jnp.concatenate(portions, axis=-2)

    def forward_row(local_row, basis_buf):
        extent, amplitude_row, tile_count = row_setup(first_row + local_row)
        near_rows = lax.dynamic_slice_in_dim(feature_wide, local_row, 5, 1)

        def forward_add_tile(tile_index, running):
            offsets = column_ids - row_ids + tile_index * tile_cols - extent
            weights = basis_values(
                amplitude_row[:, None, :, None], extent, offsets[None, :, None, :]
            )
            inputs = lax.dynamic_slice_in_dim(
                near_rows, reach_cols + tile_index * tile_cols - extent, padded_cols, 2
            )
            inputs = inputs.reshape(samples, 5, out_tiles, tile_cols, channels)
            return running + jnp.einsum(
                "kveu,bepuc->bkpvc", weights, inputs, preferred_element_type=jnp.float32
            )

        running = lax.fori_loop(
            0,
            tile_count,
            forward_add_tile,
            jnp.zeros((samples, basis_count, out_tiles, tile_cols, channels), jnp.float32),
        )
        basis_row = running.reshape(samples, basis_count, padded_cols, channels)[
            :, :, :cycle_len
        ].astype(jnp.bfloat16)
        return lax.dynamic_update_slice_in_dim(basis_buf, basis_row[:, None], local_row, 1)

    basis = lax.fori_loop(
        0,
        cycle_rows,
        forward_row,
        jnp.zeros((samples, cycle_rows, basis_count, cycle_len, channels), jnp.bfloat16),
    )
    mixed_cycle = jnp.einsum(
        "brkjc,kcd->brjd", basis, mix_weight, preferred_element_type=jnp.float32
    ).astype(jnp.bfloat16)
    convolved = lax.all_to_all(mixed_cycle, "lon", split_axis=2, concat_axis=1, tiled=True)
    local_grad = jnp.einsum(
        "brkjc,brjd->kcd", basis, cycle_cotangent, preferred_element_type=jnp.float32
    )
    cells = samples * lax.axis_size("dp") * total_rows * cycle_len
    grad_weight = lax.psum(local_grad, ("lat", "lon", "dp")) * (1.0 / math.sqrt(cells))
    cograd = jnp.einsum(
        "brjd,kcd->brkjc", cycle_cotangent, mix_weight, preferred_element_type=jnp.float32
    ).astype(jnp.bfloat16)

    def scatter_row(local_row, spread):
        extent, amplitude_row, tile_count = row_setup(first_row + local_row)
        cograd_row = lax.dynamic_index_in_dim(cograd, local_row, 1, keepdims=False)
        cograd_row = jnp.pad(cograd_row, ((0, 0), (0, 0), (0, padded_cols - cycle_len), (0, 0)))
        cograd_row = cograd_row.reshape(samples, basis_count, out_tiles, tile_cols, channels)

        def scatter_add_tile(tile_index, spread):
            offsets = column_ids - row_ids + tile_index * tile_cols - extent
            weights = basis_values(
                amplitude_row[:, None, :, None], extent, offsets[None, :, None, :]
            )
            terms = jnp.einsum(
                "kveu,bkpvc->bepuc", weights, cograd_row, preferred_element_type=jnp.float32
            )
            terms = terms.reshape(samples, 5, padded_cols, channels)
            start_col = reach_cols + tile_index * tile_cols - extent
            current = lax.dynamic_slice(
                spread, (0, local_row, start_col, 0), (samples, 5, padded_cols, channels)
            )
            return lax.dynamic_update_slice(spread, current + terms, (0, local_row, start_col, 0))

        return lax.fori_loop(0, tile_count, scatter_add_tile, spread)

    spread = lax.fori_loop(
        0,
        cycle_rows,
        scatter_row,
        jnp.zeros((samples, cycle_rows + 4, ext_width, channels), jnp.float32),
    )
    folded = jnp.pad(
        spread[:, :, :reach_cols], ((0, 0), (0, 0), (cycle_len - reach_cols, 0), (0, 0))
    )
    segments = (ext_width - reach_cols + cycle_len - 1) // cycle_len
    for segment_index in range(segments):
        begin = reach_cols + segment_index * cycle_len
        segment = spread[:, :, begin : min(begin + cycle_len, ext_width)]
        folded = folded + jnp.pad(
            segment, ((0, 0), (0, 0), (0, cycle_len - segment.shape[2]), (0, 0))
        )
    edges = extended(folded.astype(jnp.bfloat16), ((("lat", "lon"), 1),), 2).astype(folded.dtype)
    upper = edges[:, :2]
    lower = edges[:, -2:]
    grad_cycle = folded[:, 2 : 2 + cycle_rows] + upper + lower
    grad_features = lax.all_to_all(grad_cycle, "lon", split_axis=2, concat_axis=1, tiled=True)
    return (convolved, grad_features, grad_weight)


def solution(mesh):
    placed = (P("dp", "lat", "lon", None), P("dp", "lat", "lon", None), P(), P(), P())
    return jax.shard_map(
        body,
        mesh=mesh,
        in_specs=placed,
        out_specs=(P("dp", "lat", "lon", None), P("dp", "lat", "lon", None), P()),
        check_vma=False,
    )
```

profile of v0, /device:TPU:1, one launch (start us, length us, event | category | flops | bytes accessed | tf_op | source)
XLA Modules:
  0.0 486.7 jit_solution(16572234171155275164)
XLA Ops:
  7.2 1.9 copy.53
  9.1 11.5 %all-to-all-start = ((bf16[1,16,90,128]{3,2,0,1:T(8,128)(2,1)}), bf16[1,16,90,128]{3,2,0,1:T(8,128)(2,1)S(1)}, u32[]{:S(2)}, u32[]{:S(2)}) async-start(bf16[1,16,90,128]{3,2,0,1:T(8,128)(2,1)} %copy.53), calls=%async_computation | async-start | bytes 786432 | tf_op jit(solution)/shard_map/all_to_all | solution.py:58
  20.6 1.8 copy.59
  22.4 8.8 %all-to-all-done = bf16[1,16,90,128]{3,2,0,1:T(8,128)(2,1)S(1)} async-done(((bf16[1,16,90,128]{3,2,0,1:T(8,128)(2,1)}), bf16[1,16,90,128]{3,2,0,1:T(8,128)(2,1)S(1)}, u32[]{:S(2)}, u32[]{:S(2)}) %all-to-all-start) | async-done | bytes 368672 | tf_op jit(solution)/shard_map/all_to_all | solution.py:58
  31.2 4.6 all-to-all-start.2
  35.7 0.9 copy.55
  36.9 12.5 %collective-permute-start.1 = (bf16[1,2,720,128]{3,1,2,0:T(2,128)(2,1)S(1)}, bf16[1,2,720,128]{3,1,2,0:T(2,128)(2,1)S(1)}, u32[]{:S(2)}, u32[]{:S(2)}) collective-permute-start(bf16[1,2,720,128]{3,1,2,0:T(2,128)(2,1)S(1)} %bitcast.150), channel_id=1, source_target_pairs={{4,0},{8,4},{12,8},{16,12},{20,16},{24,20},{28,24},{32,28},{36,32}... | collective-permute-start | bytes 1105928 | tf_op jit(solution)/shard_map/ppermute | solution.py:19
  49.4 1.9 collective-permute-start
  51.7 0.7 copy-done.6
  52.4 1.4 fusion.30
  53.9 2.1 broadcast_in_dim.52
  55.9 55.4 %while.121 = (s32[]{:T(128)}, f32[1,6,1242,128]{3,2,1,0:T(8,128)}, s32[]{:T(128)}, s32[128]{0:T(128)S(1)}, f32[3,128,5]{2,0,1:T(4,128)}, /*index=5*/bf16[1,2,3,7...) while((s32[]{:T(128)}, f32[1,6,1242,128]{3,2,1,0:T(8,128)}, ...), condition=%wide.region_7.8_spmd.clone.clone, body=%wide.region_4.7_spmd.clone.clone.sunk | while | flops 379256864 | bytes 16897140 | solution.py:139
  57.9 0.7 dynamic-slice_bitcast_fusion.7
  58.7 1.1 dynamic-slice_bitcast_fusion.8
  59.9 23.8 %while.123 = (s32[]{:T(128)}, f32[1,6,1242,128]{3,2,1,0:T(8,128)}, s32[]{:T(128)}, s32[]{:T(128)}, s32[]{:T(128)}, /*index=5*/s32[1,128,1,128]{1,3,0,2:T(8,128)S...) while((s32[]{:T(128)}, f32[1,6,1242,128]{3,2,1,0:T(8,128)}, ...), condition=%wide.region_6.6_spmd.clone, body=%wide.region_5.5_spmd.clone.sunk | while | flops 379240448 | bytes 13402419 | solution.py:137
  62.1 0.7 fusion.57
  62.8 1.8 dynamic-slice_add_fusion.2
  64.7 7.1 %dynamic_update_slice.26 = f32[1,6,1242,128]{3,2,1,0:T(8,128)} dynamic-update-slice(f32[1,6,1242,128]{3,2,1,0:T(8,128)} %get-tuple-element.1479, f32[1,5,768,128]{3,2,1,0:T(8,128)S(1)} %dynamic-slice_add_fusion.2, s32[]{:T(128)} %constant.389.clone.1..sunk.3..sunk, s32[]{:T(128)} %get-tuple-element.1497, s32[]{:T(128)S(6)} %select_n.180, s32[]{:T(128)} %constant.389.clone.1..sunk.3..sunk) | dynamic-update-slice | bytes 3932164 | tf_op jit(solution)/shard_map/while/body/eval_jaxpr/while/body/dynamic_update_slice | solution.py:135
  74.0 0.7 fusion.57
  74.7 1.8 dynamic-slice_add_fusion.2
  76.6 7.1 %dynamic_update_slice.26 = f32[1,6,1242,128]{3,2,1,0:T(8,128)} dynamic-update-slice(f32[1,6,1242,128]{3,2,1,0:T(8,128)} %get-tuple-element.1479, f32[1,5,768,128]{3,2,1,0:T(8,128)S(1)} %dynamic-slice_add_fusion.2, s32[]{:T(128)} %constant.389.clone.1..sunk.3..sunk, s32[]{:T(128)} %get-tuple-element.1497, s32[]{:T(128)S(6)} %select_n.180, s32[]{:T(128)} %constant.389.clone.1..sunk.3..sunk) | dynamic-update-slice | bytes 3932164 | tf_op jit(solution)/shard_map/while/body/eval_jaxpr/while/body/dynamic_update_slice | solution.py:135
  85.6 0.7 dynamic-slice_bitcast_fusion.7
  86.4 1.1 dynamic-slice_bitcast_fusion.8
  87.6 23.8 %while.123 = (s32[]{:T(128)}, f32[1,6,1242,128]{3,2,1,0:T(8,128)}, s32[]{:T(128)}, s32[]{:T(128)}, s32[]{:T(128)}, /*index=5*/s32[1,128,1,128]{1,3,0,2:T(8,128)S...) while((s32[]{:T(128)}, f32[1,6,1242,128]{3,2,1,0:T(8,128)}, ...), condition=%wide.region_6.6_spmd.clone, body=%wide.region_5.5_spmd.clone.sunk | while | flops 379240448 | bytes 13402419 | solution.py:137
  89.8 0.7 fusion.57
  90.5 1.8 dynamic-slice_add_fusion.2
  92.4 7.1 %dynamic_update_slice.26 = f32[1,6,1242,128]{3,2,1,0:T(8,128)} dynamic-update-slice(f32[1,6,1242,128]{3,2,1,0:T(8,128)} %get-tuple-element.1479, f32[1,5,768,128]{3,2,1,0:T(8,128)S(1)} %dynamic-slice_add_fusion.2, s32[]{:T(128)} %constant.389.clone.1..sunk.3..sunk, s32[]{:T(128)} %get-tuple-element.1497, s32[]{:T(128)S(6)} %select_n.180, s32[]{:T(128)} %constant.389.clone.1..sunk.3..sunk) | dynamic-update-slice | bytes 3932164 | tf_op jit(solution)/shard_map/while/body/eval_jaxpr/while/body/dynamic_update_slice | solution.py:135
  101.7 0.7 fusion.57
  102.4 1.8 dynamic-slice_add_fusion.2
  104.3 7.1 %dynamic_update_slice.26 = f32[1,6,1242,128]{3,2,1,0:T(8,128)} dynamic-update-slice(f32[1,6,1242,128]{3,2,1,0:T(8,128)} %get-tuple-element.1479, f32[1,5,768,128]{3,2,1,0:T(8,128)S(1)} %dynamic-slice_add_fusion.2, s32[]{:T(128)} %constant.389.clone.1..sunk.3..sunk, s32[]{:T(128)} %get-tuple-element.1497, s32[]{:T(128)S(6)} %select_n.180, s32[]{:T(128)} %constant.389.clone.1..sunk.3..sunk) | dynamic-update-slice | bytes 3932164 | tf_op jit(solution)/shard_map/while/body/eval_jaxpr/while/body/dynamic_update_slice | solution.py:135
  111.4 5.5 %copy.64 = f32[1,6,1242,128]{3,1,0,2:T(8,128)S(1)} copy(f32[1,6,1242,128]{3,2,1,0:T(8,128)} %get-tuple-element.936) | data formatting | bytes 7630848 | tf_op jit(solution)/shard_map/while | solution.py:139
  117.0 2.1 fusion.41
  119.1 1.4 fusion.43
  120.5 1.9 collective-permute-start.2
  122.4 9.8 %collective-permute-start.3 = (bf16[1,2,720,128]{3,1,0,2:T(2,128)(2,1)}, bf16[1,2,720,128]{3,1,0,2:T(2,128)(2,1)}, u32[]{:S(2)}, u32[]{:S(2)}) collective-permute-start(bf16[1,2,720,128]{3,1,0,2:T(2,128)(2,1)} %get-tuple-element.1218), channel_id=1, source_target_pairs={{4,0},{8,4},{12,8},{16,12},{20,16},{24,20},{28,24},{32,28},{36,32}... | collective-permute-start | bytes 1105928 | tf_op jit(solution)/shard_map/ppermute | solution.py:19
  132.3 11.2 %fusion.28 = bf16[1,6,1242,128]{3,1,2,0:T(8,128)(2,1)S(1)} fusion(bf16[1,2,720,128]{3,1,2,0:T(2,128)(2,1)S(1)} %collective-permute-done.1, bf16[1,2,720,128]{3,1,2,0:T(2,128)(2,1)S(1)} %bitcast.152, bf16[1,2,720,128]{3,1,2,0:T(2,128)(2,1)} %collective-permute-done), kind=kLoop, calls=%fused_computation.50 | loop fusion | flops 17169408 | bytes 3013632 | tf_op jit(solution)/shard_map/concatenate | solution.py:67
  143.5 1.5 copy.56
  145.1 27.0 %while.119 = (s32[]{:T(128)}, bf16[1,2,3,720,128]{4,3,2,1,0:T(8,128)(2,1)}, s32[]{:T(128)}, s32[128]{0:T(128)S(1)}, f32[3,128,5]{2,0,1:T(4,128)}, /*index=5*/bf1...) while((s32[]{:T(128)}, ...), condition=%wide.region_3.4_spmd.clone.clone, body=%wide.region_0.3_spmd.clone.clone.sunk | while | flops 379355168 | bytes 23652388 | solution.py:97
  147.0 0.7 dynamic-slice_bitcast_fusion.6
  147.7 1.5 constant_dynamic-slice_fusion.4
  149.4 6.9 %while.122 = (s32[]{:T(128)}, f32[1,3,6,128,128]{3,4,1,2,0:T(8,128)S(1)}, s32[]{:T(128)}, s32[]{:T(128)}, bf16[1,5,1242,128]{3,2,1,0:T(8,128)(2,1)S(1)}, /*index...) while((s32[]{:T(128)}, ...), condition=%wide.region_2.2_spmd.clone, body=%wide.region_1.1_spmd.clone.sunk | while | flops 379043840 | bytes 6324515 | solution.py:86
  150.0 0.7 fusion.60
  151.9 0.9 fusion.61
  155.3 0.9 fusion.61
  156.7 0.8 copy-done.3
  157.6 1.0 copy-done.4
  160.5 0.7 dynamic-slice_bitcast_fusion.6
  161.2 1.5 constant_dynamic-slice_fusion.4
  162.9 6.9 %while.122 = (s32[]{:T(128)}, f32[1,3,6,128,128]{3,4,1,2,0:T(8,128)S(1)}, s32[]{:T(128)}, s32[]{:T(128)}, bf16[1,5,1242,128]{3,2,1,0:T(8,128)(2,1)S(1)}, /*index...) while((s32[]{:T(128)}, ...), condition=%wide.region_2.2_spmd.clone, body=%wide.region_1.1_spmd.clone.sunk | while | flops 379043840 | bytes 6324515 | solution.py:86
  165.4 0.9 fusion.61
  168.8 0.9 fusion.61
  170.2 0.8 copy-done.3
  171.1 1.0 copy-done.4
  172.0 1.8 fusion.32
  173.9 1.0 copy.57
  174.9 10.2 %all-to-all-start.1 = ((bf16[1,2,720,128]{3,1,0,2:T(2,128)(2,1)}), bf16[1,2,720,128]{3,1,0,2:T(2,128)(2,1)S(1)}, u32[]{:S(2)}, u32[]{:S(2)}) async-start(bf16[1,2,720,128]{3,1,0,2:T(2,128)(2,1)} %copy.57), calls=%async_computation.1 | async-start | bytes 737280 | tf_op jit(solution)/shard_map/all_to_all | solution.py:106
  185.2 3.9 fusion.35
  189.1 6.4 %all-to-all-done.1 = bf16[1,2,720,128]{3,1,0,2:T(2,128)(2,1)S(1)} async-done(((bf16[1,2,720,128]{3,1,0,2:T(2,128)(2,1)}), bf16[1,2,720,128]{3,1,0,2:T(2,128)(2,1)S(1)}, u32[]{:S(2)}, u32[]{:S(2)}) %all-to-all-start.1) | async-done | bytes 368672 | tf_op jit(solution)/shard_map/all_to_all | solution.py:106
  195.5 5.7 %all-to-all-start.3 = ((f32[1,2,720,128]{3,1,0,2:T(2,128)}), f32[1,2,720,128]{3,1,0,2:T(2,128)S(1)}, u32[]{:S(2)}, u32[]{:S(2)}) async-start(f32[1,2,720,128]{3,1,0,2:T(2,128)} %fusion.35), calls=%async_computation.3 | async-start | bytes 1474560 | tf_op jit(solution)/shard_map/all_to_all | solution.py:159
  201.3 1.2 convolution_bitcast_fusion.2
  202.5 273.6 %all-reduce.5.cloned.1.call-done = f32[3,128,128]{2,1,0:T(8,128)} async-done(((f32[3,128,128]{2,1,0:T(8,128)}), f32[3,128,128]{2,1,0:T(8,128)}) %all-reduce.5.cloned.1.call-update) | async-done | bytes 196624 | tf_op jit(solution)/shard_map/psum | solution.py:111
  476.1 1.6 broadcast_multiply_fusion
  477.7 1.0 copy.58
  478.7 1.1 copy.67
  (89 shorter events, 17.6 us)
Async XLA Ops:
  7.2 45.2 %copy-start = (bf16[3,128,128]{2,1,0:T(8,128)(2,1)S(1)}, bf16[3,128,128]{2,1,0:T(8,128)(2,1)}, u32[]{:S(2)}) copy-start(bf16[3,128,128]{2,1,0:T(8,128)(2,1)} %param.15) | copy-start | bytes 294916
  7.2 28.6 %copy-start.8 = (f32[3,128,5]{1,0,2:T(4,128)S(1)}, f32[3,128,5]{1,0,2:T(4,128)}, u32[]{:S(2)}) copy-start(f32[3,128,5]{1,0,2:T(4,128)} %param.16) | copy-start | bytes 23044
  9.1 22.1 %all-to-all-start = ((bf16[1,16,90,128]{3,2,0,1:T(8,128)(2,1)}), bf16[1,16,90,128]{3,2,0,1:T(8,128)(2,1)S(1)}, u32[]{:S(2)}, u32[]{:S(2)}) async-start(bf16[1,16,90,128]{3,2,0,1:T(8,128)(2,1)} %copy.53), calls=%async_computation | async-start | bytes 786432 | tf_op jit(solution)/shard_map/all_to_all | solution.py:58
  31.2 20.2 %all-to-all-start.2 = ((bf16[1,16,90,128]{3,2,0,1:T(8,128)(2,1)}), bf16[1,16,90,128]{3,2,0,1:T(8,128)(2,1)S(1)}, u32[]{:S(2)}, u32[]{:S(2)}) async-start(bf16[1,16,90,128]{3,2,0,1:T(8,128)(2,1)} %copy.59), calls=%async_computation.2 | async-start | bytes 786432 | tf_op jit(solution)/shard_map/all_to_all | solution.py:59
  36.9 95.4 %collective-permute-start.1 = (bf16[1,2,720,128]{3,1,2,0:T(2,128)(2,1)S(1)}, bf16[1,2,720,128]{3,1,2,0:T(2,128)(2,1)S(1)}, u32[]{:S(2)}, u32[]{:S(2)}) collective-permute-start(bf16[1,2,720,128]{3,1,2,0:T(2,128)(2,1)S(1)} %bitcast.150), channel_id=1, source_target_pairs={{4,0},{8,4},{12,8},{16,12},{20,16},{24,20},{28,24},{32,28},{36,32}... | collective-permute-start | bytes 1105928 | tf_op jit(solution)/shard_map/ppermute | solution.py:19
  49.4 82.9 %collective-permute-start = (bf16[1,2,720,128]{3,1,2,0:T(2,128)(2,1)S(1)}, bf16[1,2,720,128]{3,1,2,0:T(2,128)(2,1)}, u32[]{:S(2)}, u32[]{:S(2)}) collective-permute-start(bf16[1,2,720,128]{3,1,2,0:T(2,128)(2,1)S(1)} %bitcast.151), channel_id=1, source_target_pairs={{0,4},{4,8},{8,12},{12,16},{16,20},{20,24},{24,28},{28,32},{32,36}... | collective-permute-start | bytes 1105928 | tf_op jit(solution)/shard_map/ppermute | solution.py:17
  51.7 0.8 copy-start.6
  52.4 3.5 copy-start.9
  119.1 24.4 %copy-start.1 = (bf16[1,6,720,128]{3,1,0,2:T(8,128)(2,1)}, bf16[1,6,720,128]{3,1,0,2:T(8,128)(2,1)S(1)}, u32[]{:S(2)}) copy-start(bf16[1,6,720,128]{3,1,0,2:T(8,128)(2,1)S(1)} %get-tuple-element.1215) | copy-start | bytes 3317764
  120.5 64.6 %collective-permute-start.2 = (bf16[1,2,720,128]{3,1,0,2:T(2,128)(2,1)}, bf16[1,2,720,128]{3,1,0,2:T(2,128)(2,1)}, u32[]{:S(2)}, u32[]{:S(2)}) collective-permute-start(bf16[1,2,720,128]{3,1,0,2:T(2,128)(2,1)} %get-tuple-element.1217), channel_id=1, source_target_pairs={{0,4},{4,8},{8,12},{12,16},{16,20},{20,24},{24,28},{28,32},{32,36}... | collective-permute-start | bytes 1105928 | tf_op jit(solution)/shard_map/ppermute | solution.py:17
  122.4 62.7 %collective-permute-start.3 = (bf16[1,2,720,128]{3,1,0,2:T(2,128)(2,1)}, bf16[1,2,720,128]{3,1,0,2:T(2,128)(2,1)}, u32[]{:S(2)}, u32[]{:S(2)}) collective-permute-start(bf16[1,2,720,128]{3,1,0,2:T(2,128)(2,1)} %get-tuple-element.1218), channel_id=1, source_target_pairs={{4,0},{8,4},{12,8},{16,12},{20,16},{24,20},{28,24},{32,28},{36,32}... | collective-permute-start | bytes 1105928 | tf_op jit(solution)/shard_map/ppermute | solution.py:19
  156.3 1.2 copy-start.3
  157.6 1.0 copy-start.4
  169.7 1.2 copy-start.3
  171.1 1.0 copy-start.4
  172.0 13.1 %copy-start.2 = (bf16[1,6,720,128]{3,1,0,2:T(8,128)(2,1)S(1)}, bf16[1,6,720,128]{3,1,0,2:T(8,128)(2,1)}, u32[]{:S(2)}) copy-start(bf16[1,6,720,128]{3,1,0,2:T(8,128)(2,1)} %copy-done.1) | copy-start | bytes 3317764
  174.9 20.7 %all-to-all-start.1 = ((bf16[1,2,720,128]{3,1,0,2:T(2,128)(2,1)}), bf16[1,2,720,128]{3,1,0,2:T(2,128)(2,1)S(1)}, u32[]{:S(2)}, u32[]{:S(2)}) async-start(bf16[1,2,720,128]{3,1,0,2:T(2,128)(2,1)} %copy.57), calls=%async_computation.1 | async-start | bytes 737280 | tf_op jit(solution)/shard_map/all_to_all | solution.py:106
  185.2 16.1 %copy-start.5 = (bf16[1,2,3,720,128]{4,3,2,1,0:T(8,128)(2,1)S(1)}, bf16[1,2,3,720,128]{4,3,2,1,0:T(8,128)(2,1)}, u32[]{:S(2)}) copy-start(bf16[1,2,3,720,128]{4,3,2,1,0:T(8,128)(2,1)} %get-tuple-element.935) | copy-start | bytes 3317764
  185.2 16.1 %copy-start.7 = (bf16[1,8,2,90,128]{4,2,3,1,0:T(2,128)(2,1)S(1)}, bf16[1,8,2,90,128]{4,2,3,1,0:T(2,128)(2,1)}, u32[]{:S(2)}) copy-start(bf16[1,8,2,90,128]{4,2,3,1,0:T(2,128)(2,1)} %copy-done.6) | copy-start | bytes 1105924
  195.5 283.1 %all-to-all-start.3 = ((f32[1,2,720,128]{3,1,0,2:T(2,128)}), f32[1,2,720,128]{3,1,0,2:T(2,128)S(1)}, u32[]{:S(2)}, u32[]{:S(2)}) async-start(f32[1,2,720,128]{3,1,0,2:T(2,128)} %fusion.35), calls=%async_computation.3 | async-start | bytes 1474560 | tf_op jit(solution)/shard_map/all_to_all | solution.py:159
  201.2 274.8 %all-reduce.5.cloned.1.call-start = ((), (), s32[]{:S(2)}) async-start(), calls=%async_computation.4 | async-start | bytes 393216 | tf_op jit(solution)/shard_map/psum | solution.py:111
Sparse Core Ops, SparseCore 0:
  208.1 267.8 all-reduce.4
where the time goes:
time: 489 us; the launch traced here: 487 us
  waiting for transfers between devices  289 us (59%)
  local copies, waits for them, and re-layouts  64.4 us (13%)
  starting transfers between devices  58.2 us (12%)
  other arithmetic  38.8 us (8%)
  between operations  14.2 us (3%)
  loops' own time  11.1 us (2%)
  matrix products  11 us (2%)
    psum x1, waiting for transfers between devices, body(): lax.psum(local_grad, ('lat', 'lon', 'dp')) * (1.0 / math.sqrt(cells))  274 us
    dynamic_update_slice x4, local copies, waits for them, and re-layouts, scatter_add_tile(): lax.dynamic_update_slice(spread, current + terms, (0, local_row, start_co...  28.3 us
    ppermute x2, starting transfers between devices, extended(): lax.ppermute(head, axis, [((i + 1) % count, i) for i in range(ends)])  22.4 us
    all_to_all x1, starting transfers between devices, body(): lax.all_to_all(features, 'lon', split_axis=1, concat_axis=2, tiled=True)  11.5 us
    concatenate x1, other arithmetic, body(): feature_wide = jnp.concatenate(portions, axis=-2)  11.2 us
    all_to_all x1, starting transfers between devices, body(): lax.all_to_all(mixed_cycle, 'lon', split_axis=2, concat_axis=1, tiled=True)  10.2 us
  transfers between devices with their start and end apart: 9, of which 3 were waited for; matrix products, arithmetic and copies ran while one was open for 22% of the time, Pallas kernels for 0%

commit v1 on v0

v1 whole, which is shorter than its diff:
```python
import functools
import math

import jax
import jax.numpy as jnp
from jax import lax
from jax.experimental import pallas as pl
from jax.experimental.pallas import tpu as pltpu
from jax.sharding import PartitionSpec as P

ROWS = 16
COLS = 90
CHAN = 128
PAD = 96
NEAR = 16
HIGH = 7
F32 = jnp.float32
BF16 = jnp.bfloat16
LL = ("lat", "lon")


def offsets_of(group):
    col = lax.broadcasted_iota(jnp.int32, (PAD, 128), 0)
    lane = lax.broadcasted_iota(jnp.int32, (PAD, 128), 1)
    none = jnp.full((PAD, 128), 1000000, jnp.int32)
    if group == 0:
        source = jnp.where(lane < PAD, lane, jnp.where(lane < PAD + NEAR, lane - 112, lane - 22))
        source = jnp.where((lane >= COLS) & (lane < PAD), none, source)
    elif group == 1:
        source = jnp.where(lane < 64, lane - 80, lane + 42)
    else:
        source = jnp.where(lane < 16, lane - 90, lane + 148)
        source = jnp.where((lane >= 10) & (lane < 22), none, source)
        source = jnp.where(lane >= 32, none, source)
    return (source - col).astype(F32)


def fill_shapes(table, offsets, spans, inverse, first, start, count):
    def fill(row, carry):
        ext = first + row
        inside = jnp.abs(offsets) <= spans[ext].astype(F32)
        scaled = jnp.where(inside, offsets * inverse[ext], 0.0)
        square = scaled * scaled
        half = jnp.full(square.shape, 4.7108746e-07, F32)
        for term in (-2.5202042e-05, 9.1926025e-04, -2.0863481e-02, 2.5366950e-01, -1.2337005, 1.0):
            half = half * square + term
        cosine = 2.0 * half * half - 1.0
        shapes = (1.0 - jnp.abs(scaled), scaled, cosine)
        for k in range(3):
            at = pl.multiple_of((row * 3 + k) * PAD, PAD)
            table[pl.ds(at, PAD), :] = jnp.where(inside, shapes[k], 0.0)
        return carry

    lax.fori_loop(start, start + count, fill, 0)


def band_pass(data, total, table, blocks, amps, first, rows, backward, fresh):
    def step(row, carry):
        for slot in range(5):
            for k in range(3):
                if backward:
                    ext, tap, sign = row + slot, 4 - slot, (-1.0 if k == 1 else 1.0)
                else:
                    ext, tap, sign = row + 2, slot, 1.0
                factor = amps[(first + ext) * 15 + k * 5 + tap] * sign
                shape = table[pl.ds(pl.multiple_of((ext * 3 + k) * PAD, PAD), PAD), :]
                blocks[k * PAD : (k + 1) * PAD, slot * 128 : (slot + 1) * 128] = (shape * factor).astype(BF16)
        near = data[pl.ds(pl.multiple_of(row * 128, 128), 640), :]
        term = jnp.dot(blocks[...], near, preferred_element_type=F32)
        at = pl.ds(pl.multiple_of(row * 288, 288), 288)
        if fresh:
            total[at, :] = term
        else:
            total[at, :] += term
        return carry

    lax.fori_loop(0, rows, step, 0)


def convolve(info, spans, inverse, amps, own, halo_a, halo_b, which, data, total, table, blocks, backward):
    lat = info[0]
    first = info[2]
    even = lat % 2 == 0

    def place(group, lo, hi, at_lo):
        for row in range(2):
            a = halo_a[which, row, lo:hi, :]
            b = halo_b[which, row, lo:hi, :] if lo < 128 else jnp.zeros((hi - lo, CHAN), BF16)
            data[row * 128 + at_lo : row * 128 + at_lo + hi - lo, :] = jnp.where(even, b, a)
            data[(18 + row) * 128 + at_lo : (18 + row) * 128 + at_lo + hi - lo, :] = jnp.where(even, a, b)

    data[256 : 256 + 2048, :] = own[0][...].reshape(2048, CHAN)
    place(0, 0, 128, 0)
    ext_start, ext_count = (0, 20) if backward else (2, 16)
    fill_shapes(table, offsets_of(0), spans, inverse, first, ext_start, ext_count)
    band_pass(data, total, table, blocks, amps, first, ROWS, backward, True)

    def wide(rows):
        data[...] = jnp.zeros(data.shape, BF16)
        data[256 : 256 + 2048, :] = own[1][...].reshape(2048, CHAN)
        place(1, 128, 160, 48)
        fill_shapes(table, offsets_of(1), spans, inverse, first, ext_start, ext_count)
        band_pass(data, total, table, blocks, amps, first, rows, backward, False)

    if backward:
        pl.when(lat == 1)(lambda: wide(2))

    @pl.when(lat == 0)
    def _():
        wide(ROWS)
        rows = 5 if backward else 3
        data[...] = jnp.zeros(data.shape, BF16)
        for row in range(5):
            data[(2 + row) * 128 : (2 + row) * 128 + 32, :] = own[2][row]
        if backward:
            fill_shapes(table, offsets_of(2), spans, inverse, first, 0, 9)
        else:
            fill_shapes(table, offsets_of(2), spans, inverse, first, 2, 3)
        band_pass(data, total, table, blocks, amps, first, rows, backward, False)


def forward_kernel(info, spans, inverse, amps, own0, own1, own2, cot, halo_a, halo_b, basis, grad, data, total, table, blocks):
    convolve(info, spans, inverse, amps, (own0, own1, own2), halo_a, halo_b, 0, data, total, table, blocks, False)

    def pack(row, carry):
        for k in range(3):
            at = pl.multiple_of(row * 288 + k * PAD, PAD)
            basis[pl.ds(pl.multiple_of(row * PAD, PAD), PAD), k * 128 : (k + 1) * 128] = total[pl.ds(at, PAD), :].astype(BF16)
        return carry

    lax.fori_loop(0, ROWS, pack, 0)
    cotangent = cot[:, :PAD, :].reshape(ROWS * PAD, CHAN)
    product = lax.dot_general(cotangent, basis[...], (((0,), (0,)), ((), ())), preferred_element_type=F32)
    for k in range(3):
        grad[k * 128 : (k + 1) * 128, :] = product[:, k * 128 : (k + 1) * 128].T


def mix_kernel(basis, weight, out):
    def step(row, carry):
        mixed = jnp.dot(basis[pl.ds(pl.multiple_of(row * PAD, PAD), PAD), :], weight[...], preferred_element_type=F32)
        out[0, row] = mixed.astype(BF16)[:COLS]
        return carry

    lax.fori_loop(0, ROWS, step, 0)


def backward_kernel(info, spans, inverse, amps, own0, own1, own2, halo_a, halo_b, weight, out, data, total, table, blocks):
    convolve(info, spans, inverse, amps, (own0, own1, own2), halo_a, halo_b, 1, data, total, table, blocks, True)

    def step(row, carry):
        mixed = jnp.zeros((PAD, CHAN), F32)
        for k in range(3):
            part = total[pl.ds(pl.multiple_of(row * 288 + k * PAD, PAD), PAD), :].astype(BF16)
            mixed += jnp.dot(part, weight[k], preferred_element_type=F32)
        out[0, row] = mixed[:COLS]
        return carry

    lax.fori_loop(0, ROWS, step, 0)


def assemble_kernel(info, field, cot, small_a, small_b, large_a, large_b, *outs):
    lat, lon = info[0], info[1]
    odd = lon % 2 == 1
    polar = lat < 2
    groups = (outs[0:3], outs[3:6])
    lat_a, lat_b = outs[6], outs[7]
    for which, source in enumerate((field, cot)):
        own0, own1, own2 = groups[which]
        own0[:, :PAD, :] = jnp.zeros((ROWS, PAD, CHAN), BF16)
        own0[:, :COLS, :] = source[0]

        def left_right(at, size, rows, shape):
            a = large_a[which, pl.ds(at, size), :]
            b = large_b[which, pl.ds(at, size), :]
            return jnp.where(odd, b, a).reshape(shape), jnp.where(odd, a, b).reshape(shape)

        left, right = left_right(0, 256, ROWS, (ROWS, NEAR, CHAN))
        own0[:, 96:112, :] = jnp.where(polar, left, jnp.where(odd, small_b[which], small_a[which]))
        own0[:, 112:128, :] = jnp.where(polar, right, jnp.where(odd, small_a[which], small_b[which]))

        @pl.when(polar)
        def _(own1=own1, own2=own2, left_right=left_right):
            own1[...] = jnp.zeros(own1.shape, BF16)
            left, right = left_right(256, HIGH * 64, HIGH, (HIGH, 64, CHAN))
            own1[:HIGH, :64, :] = left
            own1[:HIGH, 64:, :] = right
            rest = ROWS - HIGH
            left, right = left_right(256 + HIGH * 64, rest * 32, rest, (rest, 32, CHAN))
            own1[HIGH:, 32:64, :] = left
            own1[HIGH:, 64:96, :] = right
            left, right = left_right(256 + HIGH * 64 + rest * 32, 80, 5, (5, 16, CHAN))
            own2[:, :16, :] = left
            own2[:, 16:, :] = right

        @pl.when(jnp.logical_not(polar))
        def _(own1=own1, own2=own2):
            own1[...] = jnp.zeros(own1.shape, BF16)
            own2[...] = jnp.zeros(own2.shape, BF16)

        even = lat % 2 == 0
        for row in range(2):
            lat_a[which, row, :128, :] = jnp.where(even, own0[14 + row], own0[row])
            lat_a[which, row, 128:, :] = jnp.where(even, own1[14 + row, 48:80, :], own1[row, 48:80, :])
            lat_b[which, row] = jnp.where(even, own0[row], own0[14 + row])


def edge_of(both, right):
    if right:
        near, far, last = both[:, :, 74:90], both[:, :HIGH, 10:74], both[:, :5, 0:16]
        rest = both[:, HIGH:, 42:74]
    else:
        near, far, last = both[:, :, 0:16], both[:, :HIGH, 16:80], both[:, :5, 74:90]
        rest = both[:, HIGH:, 16:48]
    flat = [part.reshape(2, -1, CHAN) for part in (near, far, rest, last)]
    return near, jnp.concatenate(flat, axis=1)


def pairs_of_lon(parity, lats):
    out = []
    for lat in lats:
        for lon in range(8):
            other = lon ^ 1 if parity == 0 else ((lon + 1) % 8 if lon % 2 else (lon - 1) % 8)
            out.append((lat * 8 + lon, lat * 8 + other))
    return out


def pairs_of_lat(parity):
    out = []
    for lat in range(8):
        other = lat ^ 1 if parity == 0 else (lat + 1 if lat % 2 else lat - 1)
        if 0 <= other < 8:
            out.append((lat, other))
    return out


def z_pairs():
    across = {0: 6, 6: 0, 1: 7, 7: 1, 2: 4, 4: 2, 3: 5, 5: 3}
    out = []
    for lat in range(8):
        for lon in range(8):
            other = across[(lon >> 2) * 4 + (lat >> 1)]
            out.append((lat * 8 + lon, ((other % 4) * 2 + lat % 2) * 8 + (other // 4) * 4 + lon % 4))
    return out


def reduce_all(part):
    flip = lambda x, axis, bit: lax.ppermute(x, axis, [(i, i ^ bit) for i in range(lax.axis_size(axis))])
    core = lax.axis_index("lat") % 2
    half = part.shape[0] // 2
    mine = lax.dynamic_slice_in_dim(part, core * half, half, 0)
    other = lax.dynamic_slice_in_dim(part, (1 - core) * half, half, 0)
    mine = mine + flip(other, "lat", 1)
    for axis in ("dp", "lon"):
        one, two, three = (flip(mine, axis, bit) for bit in (1, 2, 3))
        mine = (mine + one) + (two + three)
    mine = mine + flip(mine, "lat", 2)
    mine = mine + flip(mine, "lat", 4)
    mine = mine + lax.ppermute(mine, LL, z_pairs())
    other = flip(mine, "lat", 1)
    return jnp.where(core == 0, jnp.concatenate([mine, other]), jnp.concatenate([other, mine]))


VMEM = pl.BlockSpec(memory_space=pltpu.VMEM)
SMEM = pl.BlockSpec(memory_space=pltpu.SMEM)
PARAMS = pltpu.CompilerParams(vmem_limit_bytes=48 * 1024 * 1024)


def call(kernel, outs, scratch, flops, scalars, arrays):
    moved = sum(math.prod(x.shape) * x.dtype.itemsize for x in (*arrays, *outs))
    return pl.pallas_call(
        kernel,
        out_shape=outs,
        in_specs=[SMEM] * len(scalars) + [VMEM] * len(arrays),
        out_specs=[VMEM] * len(outs),
        scratch_shapes=scratch,
        compiler_params=PARAMS,
        cost_estimate=pl.CostEstimate(flops=flops, bytes_accessed=moved, transcendentals=0),
    )(*scalars, *arrays)


def shape(dims, dtype=BF16):
    return jax.ShapeDtypeStruct(dims, dtype)


def body(features, cotangent, mix_weight, amplitude, row_spans):
    lat, lon = lax.axis_index("lat"), lax.axis_index("lon")
    info = jnp.stack([lat, lon, lat * ROWS]).astype(jnp.int32)
    divisor = row_spans.astype(F32) + 1.0
    spans = jnp.pad(row_spans, (2, 2))
    inverse = jnp.pad(1.0 / divisor, (2, 2), constant_values=1.0)
    amps = amplitude * (1.0 / jnp.sqrt(divisor))[None, :, None]
    amps = jnp.pad(amps.transpose(1, 0, 2), ((2, 2), (0, 0), (0, 0))).reshape(-1)
    scalars = (info, spans, inverse, amps)

    both = jnp.concatenate([features, cotangent], axis=0)
    right_near, right_all = edge_of(both, True)
    left_near, left_all = edge_of(both, False)
    odd = lon % 2 == 1
    small_a = lax.ppermute(jnp.where(odd, right_near, left_near), LL, pairs_of_lon(1, range(2, 8)))
    large_a = lax.ppermute(jnp.where(odd, right_all, left_all), LL, pairs_of_lon(1, range(2)))
    small_b = lax.ppermute(jnp.where(odd, left_near, right_near), LL, pairs_of_lon(0, range(2, 8)))
    large_b = lax.ppermute(jnp.where(odd, left_all, right_all), LL, pairs_of_lon(0, range(2)))

    groups = [shape((ROWS, 128, CHAN)), shape((ROWS, 128, CHAN)), shape((5, 32, CHAN))]
    outs = groups + groups + [shape((2, 2, 160, CHAN)), shape((2, 2, 128, CHAN))]
    arrays = (features, cotangent, small_a, small_b, large_a, large_b)
    *gathered, lat_a, lat_b = call(assemble_kernel, outs, [], 0, (info,), arrays)
    halo_a = lax.ppermute(lat_a, "lat", pairs_of_lat(0))
    halo_b = lax.ppermute(lat_b, "lat", pairs_of_lat(1))

    scratch = [
        pltpu.VMEM((20 * 128, CHAN), BF16),
        pltpu.VMEM((ROWS * 288, CHAN), F32),
        pltpu.VMEM((20 * 288, 128), F32),
        pltpu.VMEM((288, 640), BF16),
    ]
    band_flops = 2 * ROWS * 288 * 640 * CHAN
    basis, part = call(
        forward_kernel,
        [shape((ROWS * PAD, 384)), shape((384, CHAN), F32)],
        scratch,
        2 * band_flops,
        scalars,
        (*gathered[:3], gathered[3], halo_a, halo_b),
    )
    (convolved,) = call(mix_kernel, [shape(features.shape)], [], 2 * ROWS * PAD * 384 * CHAN, (), (basis, mix_weight.reshape(384, CHAN)))
    (grad_features,) = call(
        backward_kernel,
        [shape(features.shape, F32)],
        scratch,
        2 * band_flops,
        scalars,
        (*gathered[3:], halo_a, halo_b, mix_weight.transpose(0, 2, 1)),
    )
    cells = 4 * 128 * 720
    grad_weight = reduce_all(part).reshape(3, 128, 128) * (1.0 / math.sqrt(cells))
    return convolved, grad_features, grad_weight


def solution(mesh):
    cells = P("dp", "lat", "lon", None)
    return jax.shard_map(
        body,
        mesh=mesh,
        in_specs=(cells, cells, P(), P(), P()),
        out_specs=(cells, cells, P()),
        check_vma=False,
    )
```

time: 489 us -> 112 us (0.23)
  the two profiles are of different devices: /device:TPU:1 before, /device:TPU:6 now
where the time goes in v1:
time: 112 us
  waiting for transfers between devices  39.4 us (35%)
  Pallas kernels  33.2 us (30%)
  starting transfers between devices  27.9 us (25%)
  local copies, waits for them, and re-layouts  8.35 us (7%)
  other arithmetic  1.84 us (2%)
    pallas_call x4, Pallas kernels, call(): pl.pallas_call(kernel, out_shape=outs, in_specs=[SMEM] * len(scalars) + [...  33.2 us
    ppermute x10, waiting for transfers between devices, reduce_all(): lax.ppermute(x, axis, [(i, i ^ bit) for i in range(lax.axis_size(axis))])  23.7 us
    ppermute x10, starting transfers between devices, reduce_all(): lax.ppermute(x, axis, [(i, i ^ bit) for i in range(lax.axis_size(axis))])  11.2 us
    ppermute x1, waiting for transfers between devices, body(): lax.ppermute(jnp.where(odd, right_all, left_all), LL, pairs_of_lon(1, ran...  9.75 us
    ppermute x1, starting transfers between devices, body(): lax.ppermute(jnp.where(odd, right_all, left_all), LL, pairs_of_lon(1, ran...  9.01 us
    unnamed x29, local copies, waits for them, and re-layouts  7.56 us
    ppermute x1, starting transfers between devices, reduce_all(): mine = mine + lax.ppermute(mine, LL, z_pairs())  3.67 us
    ppermute x1, waiting for transfers between devices, reduce_all(): mine = mine + lax.ppermute(mine, LL, z_pairs())  3.32 us
  transfers between devices with their start and end apart: 17, of which 12 were waited for; matrix products, arithmetic and copies ran while one was open for 3% of the time, Pallas kernels for 17%

profile of v1, /device:TPU:6, one launch (start us, length us, event | category | flops | bytes accessed | tf_op | source)
XLA Modules:
  0.0 111.7 jit_solution(6931864682894750193)
XLA Ops:
  0.6 0.0 copy-start.9
  0.6 1.2 %constant_dynamic-update-slice_fusion.1 = (bf16[2,16,90,128]{3,2,1,0:T(8,128)(2,1)S(1)}, bf16[1,16,90,128]{3,2,1,0:T(8,128)(2,1)S(1)}) fusion(bf16[1,16,90,128]{3,1,2,0:T(8,128)(2,1)} %param.5), kind=kLoop, calls=%fused_computation.13 | loop fusion | bytes 1155072
  1.8 0.2 constant_dynamic-update-slice_fusion
  2.0 0.1 fusion.4
  2.1 0.1 fusion.5
  2.2 0.7 fusion.3
  3.0 0.2 broadcast_select_fusion
  3.2 9.0 %collective-permute-start.2 = (bf16[2,1072,128]{2,1,0:T(8,128)(2,1)S(1)}, bf16[2,1072,128]{2,1,0:T(8,128)(2,1)S(1)}, u32[]{:S(2)}, u32[]{:S(2)}) collective-permute-start(bf16[2,1072,128]{2,1,0:T(8,128)(2,1)S(1)} %get-tuple-element.30), channel_id=1, source_target_pairs={{0,28},{4,8},{8,4},{12,16},{16,12},{20,24},{24,20},{28,0},{32,60},... | collective-permute-start | bytes 1646600 | tf_op jit(solution)/shard_map/ppermute | solution.py:300
  12.2 1.9 %collective-permute-start.3 = (bf16[2,1072,128]{2,1,0:T(8,128)(2,1)S(1)}, bf16[2,1072,128]{2,1,0:T(8,128)(2,1)S(1)}, u32[]{:S(2)}, u32[]{:S(2)}) collective-permute-start(bf16[2,1072,128]{2,1,0:T(8,128)(2,1)S(1)} %get-tuple-element.29), channel_id=1, source_target_pairs={{0,4},{4,0},{8,12},{12,8},{16,20},{20,16},{24,28},{28,24},{32,36},... | collective-permute-start | bytes 1646600 | tf_op jit(solution)/shard_map/ppermute | solution.py:302
  14.2 0.0 copy-start.10
  14.2 0.7 collective-permute-start
  14.9 0.7 collective-permute-start.1
  15.6 0.1 pad.12.spans
  15.6 0.1 pad_add_fusion.info
  15.7 0.0 collective-permute-done.small_a
  15.7 0.0 collective-permute-done.1.small_b
  15.7 9.7 %collective-permute-done.2.large_a = bf16[2,1072,128]{2,1,0:T(8,128)(2,1)S(1)} collective-permute-done((bf16[2,1072,128]{2,1,0:T(8,128)(2,1)S(1)}, bf16[2,1072,128]{2,1,0:T(8,128)(2,1)S(1)}, u32[]{:S(2)}, u32[]{:S(2)}) %collective-permute-start.2) | collective-permute-done | bytes 548896 | tf_op jit(solution)/shard_map/ppermute | solution.py:300
  25.5 2.6 %collective-permute-done.3.large_b = bf16[2,1072,128]{2,1,0:T(8,128)(2,1)S(1)} collective-permute-done((bf16[2,1072,128]{2,1,0:T(8,128)(2,1)S(1)}, bf16[2,1072,128]{2,1,0:T(8,128)(2,1)S(1)}, u32[]{:S(2)}, u32[]{:S(2)}) %collective-permute-start.3) | collective-permute-done | bytes 548896 | tf_op jit(solution)/shard_map/ppermute | solution.py:302
  28.0 1.7 %shard_map.76 = (bf16[16,128,128]{2,1,0:T(8,128)(2,1)S(1)}, bf16[16,128,128]{2,1,0:T(8,128)(2,1)S(1)}, bf16[5,32,128]{2,1,0:T(8,128)(2,1)S(1)}, bf16[16,128,128]...) custom-call(s32[3]{0:T(128)S(1)} %pad_add_fusion.info, ...), custom_call_target="tpu_custom_call" | custom-call | bytes 4571136 | tf_op jit(solution)/shard_map/pallas_call | solution.py:270
  29.8 0.8 copy-done.1
  30.6 0.8 copy-done.3
  31.4 0.6 copy-done.5
  32.0 0.6 copy-done.7
  32.6 0.0 collective-permute-start.4
  32.6 0.8 collective-permute-start.5
  33.4 0.0 copy-done.10
  33.4 0.2 copy.23
  33.7 0.2 reshape.44.amps
  33.9 0.1 pad.13.inverse
  34.0 0.0 collective-permute-done.5.halo_b
  34.0 0.0 collective-permute-done.4.halo_a
  34.0 0.0 copy-done.8
  34.0 1.0 copy-done.4
  35.0 12.9 %shard_map.77 = (bf16[1536,384]{1,0:T(8,128)(2,1)S(1)}, f32[384,128]{1,0:T(8,128)S(1)}) custom-call(s32[3]{0:T(128)S(1)} %pad_add_fusion.info, s32[132]{0:T(256)S(1)} %pad.12.spans, f32[132]{0:T(256)S(1)} %pad.13.inverse, f32[1980]{0:T(1024)S(1)} %reshape.44.amps, bf16[16,128,128]{2,1,0:T(8,128)(2,1)S(1)} %copy-done.2, bf16[16,128,128]{2,1,0:T(8,128)(2,1)S(1)} %copy-done.4, ...), custom_call_target="tpu_custom_call" | custom-call | flops 1509949440 | bytes 3284992 | tf_op jit(solution)/shard_map/pallas_call | solution.py:270
  48.0 0.0 copy-start
  48.0 0.1 collective-permute-start.6
  48.1 1.3 %collective-permute-done.6 = f32[192,128]{1,0:T(8,128)S(1)} collective-permute-done((f32[192,128]{1,0:T(8,128)S(1)}, f32[192,128]{1,0:T(8,128)S(1)}, u32[]{:S(2)}, u32[]{:S(2)}) %collective-permute-start.6) | collective-permute-done | bytes 98336 | tf_op jit(solution)/shard_map/ppermute | solution.py:247
  49.4 1.7 %collective-permute-start.7 = (f32[192,128]{1,0:T(8,128)S(1)}, f32[192,128]{1,0:T(8,128)S(1)}, u32[]{:S(2)}, u32[]{:S(2)}) collective-permute-start(f32[192,128]{1,0:T(8,128)S(1)} %dynamic-slice_add_fusion), channel_id=1, source_target_pairs={{0,1},{1,0},{2,3},{3,2},{4,5},{5,4},{6,7},{7,6},{8,9},{9,8},{10,11... | collective-permute-start | bytes 294920 | tf_op jit(solution)/shard_map/ppermute | solution.py:247
  51.1 2.9 %collective-permute-start.8 = (f32[192,128]{1,0:T(8,128)S(1)}, f32[192,128]{1,0:T(8,128)S(1)}, u32[]{:S(2)}, u32[]{:S(2)}) collective-permute-start(f32[192,128]{1,0:T(8,128)S(1)} %dynamic-slice_add_fusion), channel_id=1, source_target_pairs={{0,2},{1,3},{2,0},{3,1},{4,6},{5,7},{6,4},{7,5},{8,10},{9,11},{10,... | collective-permute-start | bytes 294920 | tf_op jit(solution)/shard_map/ppermute | solution.py:247
  54.0 0.2 collective-permute-start.9
  54.2 0.2 collective-permute-done.7
  54.4 4.7 %collective-permute-done.8 = f32[192,128]{1,0:T(8,128)S(1)} collective-permute-done((f32[192,128]{1,0:T(8,128)S(1)}, f32[192,128]{1,0:T(8,128)S(1)}, u32[]{:S(2)}, u32[]{:S(2)}) %collective-permute-start.8) | collective-permute-done | bytes 98336 | tf_op jit(solution)/shard_map/ppermute | solution.py:247
  59.0 1.9 %collective-permute-done.9 = f32[192,128]{1,0:T(8,128)S(1)} collective-permute-done((f32[192,128]{1,0:T(8,128)S(1)}, f32[192,128]{1,0:T(8,128)S(1)}, u32[]{:S(2)}, u32[]{:S(2)}) %collective-permute-start.9) | collective-permute-done | bytes 98336 | tf_op jit(solution)/shard_map/ppermute | solution.py:247
  61.0 0.4 collective-permute-start.10
  61.3 3.9 %collective-permute-start.11 = (f32[192,128]{1,0:T(8,128)S(1)}, f32[192,128]{1,0:T(8,128)S(1)}, u32[]{:S(2)}, u32[]{:S(2)}) collective-permute-start(f32[192,128]{1,0:T(8,128)S(1)} %add_add_fusion.1), channel_id=1, source_target_pairs={{0,8},{4,12},{8,0},{12,4},{16,24},{20,28},{24,16},{28,20},{1,9},{5... | collective-permute-start | bytes 294920 | tf_op jit(solution)/shard_map/ppermute | solution.py:247
  65.3 0.5 collective-permute-start.12
  65.7 0.4 collective-permute-done.10
  66.1 3.9 %collective-permute-done.11 = f32[192,128]{1,0:T(8,128)S(1)} collective-permute-done((f32[192,128]{1,0:T(8,128)S(1)}, f32[192,128]{1,0:T(8,128)S(1)}, u32[]{:S(2)}, u32[]{:S(2)}) %collective-permute-start.11) | collective-permute-done | bytes 98336 | tf_op jit(solution)/shard_map/ppermute | solution.py:247
  70.0 1.8 %collective-permute-done.12 = f32[192,128]{1,0:T(8,128)S(1)} collective-permute-done((f32[192,128]{1,0:T(8,128)S(1)}, f32[192,128]{1,0:T(8,128)S(1)}, u32[]{:S(2)}, u32[]{:S(2)}) %collective-permute-start.12) | collective-permute-done | bytes 98336 | tf_op jit(solution)/shard_map/ppermute | solution.py:247
  71.8 0.1 collective-permute-start.13
  71.9 4.6 %collective-permute-done.13 = f32[192,128]{1,0:T(8,128)S(1)} collective-permute-done((f32[192,128]{1,0:T(8,128)S(1)}, f32[192,128]{1,0:T(8,128)S(1)}, u32[]{:S(2)}, u32[]{:S(2)}) %collective-permute-start.13) | collective-permute-done | bytes 98336 | tf_op jit(solution)/shard_map/ppermute | solution.py:247
  76.5 1.4 %collective-permute-start.14 = (f32[192,128]{1,0:T(8,128)S(1)}, f32[192,128]{1,0:T(8,128)S(1)}, u32[]{:S(2)}, u32[]{:S(2)}) collective-permute-start(f32[192,128]{1,0:T(8,128)S(1)} %add.64), channel_id=1, source_target_pairs={{0,128},{32,160},{64,192},{96,224},{128,0},{160,32},{192,64},{224,... | collective-permute-start | bytes 294920 | tf_op jit(solution)/shard_map/ppermute | solution.py:247
  77.9 5.1 %collective-permute-done.14 = f32[192,128]{1,0:T(8,128)S(1)} collective-permute-done((f32[192,128]{1,0:T(8,128)S(1)}, f32[192,128]{1,0:T(8,128)S(1)}, u32[]{:S(2)}, u32[]{:S(2)}) %collective-permute-start.14) | collective-permute-done | bytes 98336 | tf_op jit(solution)/shard_map/ppermute | solution.py:247
  83.0 3.7 %collective-permute-start.15 = (f32[192,128]{1,0:T(8,128)S(1)}, f32[192,128]{1,0:T(8,128)S(1)}, u32[]{:S(2)}, u32[]{:S(2)}) collective-permute-start(f32[192,128]{1,0:T(8,128)S(1)} %add.65), channel_id=1, source_target_pairs={{0,144},{4,148},{8,152},{12,156},{16,128},{20,132},{24,136},{28,14... | collective-permute-start | bytes 294920 | tf_op jit(solution)/shard_map/ppermute | solution.py:258
  86.6 0.0 copy-done
  86.6 0.1 copy.20
  86.8 3.3 %collective-permute-done.15 = f32[192,128]{1,0:T(8,128)S(1)} collective-permute-done((f32[192,128]{1,0:T(8,128)S(1)}, f32[192,128]{1,0:T(8,128)S(1)}, u32[]{:S(2)}, u32[]{:S(2)}) %collective-permute-start.15) | collective-permute-done | bytes 98336 | tf_op jit(solution)/shard_map/ppermute | solution.py:258
  90.1 0.1 collective-permute-start.16
  90.2 15.9 %shard_map.79 = f32[1,16,90,128]{3,2,1,0:T(8,128)S(1)} custom-call(s32[3]{0:T(128)S(1)} %pad_add_fusion.info, s32[132]{0:T(256)S(1)} %pad.12.spans, f32[132]{0:T(256)S(1)} %pad.13.inverse, f32[1980]{0:T(1024)S(1)} %reshape.44.amps, bf16[16,128,128]{2,1,0:T(8,128)(2,1)S(1)} %get-tuple-element.16.cot.own0, bf16[16,128,128]{2,1,0:T(8,128)(2,1)S(1)} %get-tuple-element.20.own1, ...), custom_call_target="tpu_custom_call" | custom-call | flops 1509949440 | bytes 2220032 | tf_op jit(solution)/shard_map/pallas_call | solution.py:270
  106.2 1.3 %copy.22 = f32[1,16,90,128]{3,1,2,0:T(8,128)} copy(f32[1,16,90,128]{3,2,1,0:T(8,128)S(1)} %shard_map.79) | data formatting | bytes 1474560
  107.5 2.6 %shard_map.78 = bf16[1,16,90,128]{3,2,1,0:T(8,128)(2,1)S(1)} custom-call(bf16[1536,384]{1,0:T(8,128)(2,1)S(1)} %get-tuple-element.19.basis, bf16[384,128]{1,0:T(8,128)(2,1)S(1)} %bitcast.16), custom_call_target="tpu_custom_call" | custom-call | flops 150994944 | bytes 1646592 | tf_op jit(solution)/shard_map/pallas_call | solution.py:270
  110.1 0.9 copy.21
  111.0 0.0 collective-permute-done.16
  111.0 0.7 fusion
  (24 shorter events, 0.2 us)
Async XLA Ops:
  0.6 1.2 %copy-start.9 = (bf16[1,16,90,128]{3,1,2,0:T(8,128)(2,1)S(1)}, bf16[1,16,90,128]{3,1,2,0:T(8,128)(2,1)}, u32[]{:S(2)}) copy-start(bf16[1,16,90,128]{3,1,2,0:T(8,128)(2,1)} %param.6) | copy-start | bytes 1105924
  3.0 12.5 %copy-start.11 = (s32[128]{0:T(128)S(1)}, s32[128]{0:T(128)}, u32[]{:S(2)}) copy-start(s32[128]{0:T(128)} %param.9) | copy-start | bytes 1540
  3.2 22.2 %collective-permute-start.2 = (bf16[2,1072,128]{2,1,0:T(8,128)(2,1)S(1)}, bf16[2,1072,128]{2,1,0:T(8,128)(2,1)S(1)}, u32[]{:S(2)}, u32[]{:S(2)}) collective-permute-start(bf16[2,1072,128]{2,1,0:T(8,128)(2,1)S(1)} %get-tuple-element.30), channel_id=1, source_target_pairs={{0,28},{4,8},{8,4},{12,16},{16,12},{20,24},{24,20},{28,0},{32,60},... | collective-permute-start | bytes 1646600 | tf_op jit(solution)/shard_map/ppermute | solution.py:300
  12.2 15.8 %collective-permute-start.3 = (bf16[2,1072,128]{2,1,0:T(8,128)(2,1)S(1)}, bf16[2,1072,128]{2,1,0:T(8,128)(2,1)S(1)}, u32[]{:S(2)}, u32[]{:S(2)}) collective-permute-start(bf16[2,1072,128]{2,1,0:T(8,128)(2,1)S(1)} %get-tuple-element.29), channel_id=1, source_target_pairs={{0,4},{4,0},{8,12},{12,8},{16,20},{20,16},{24,28},{28,24},{32,36},... | collective-permute-start | bytes 1646600 | tf_op jit(solution)/shard_map/ppermute | solution.py:302
  14.2 19.2 %copy-start.10 = (f32[3,128,5]{1,0,2:T(4,128)S(1)}, f32[3,128,5]{1,0,2:T(4,128)}, u32[]{:S(2)}) copy-start(f32[3,128,5]{1,0,2:T(4,128)} %param.8) | copy-start | bytes 23044
  14.2 1.5 %collective-permute-start = (bf16[2,16,16,128]{3,2,1,0:T(8,128)(2,1)}, bf16[2,16,16,128]{3,2,1,0:T(8,128)(2,1)S(1)}, u32[]{:S(2)}, u32[]{:S(2)}) collective-permute-start(bf16[2,16,16,128]{3,2,1,0:T(8,128)(2,1)} %get-tuple-element.32), channel_id=1, source_target_pairs={{64,92},{68,72},{72,68},{76,80},{80,76},{84,88},{88,84},{92,64},{9... | collective-permute-start | bytes 393224 | tf_op jit(solution)/shard_map/ppermute | solution.py:299
  14.9 0.9 collective-permute-start.1
  29.8 0.8 copy-start.1
  30.6 0.8 copy-start.3
  31.4 0.6 copy-start.5
  32.0 0.6 copy-start.7
  32.6 1.4 %copy-start.2 = (bf16[16,128,128]{2,1,0:T(8,128)(2,1)S(1)}, bf16[16,128,128]{2,1,0:T(8,128)(2,1)}, u32[]{:S(2)}) copy-start(bf16[16,128,128]{2,1,0:T(8,128)(2,1)} %copy-done.1) | copy-start | bytes 1572868
  32.6 1.4 %copy-start.8 = (bf16[5,32,128]{2,1,0:T(8,128)(2,1)S(1)}, bf16[5,32,128]{2,1,0:T(8,128)(2,1)}, u32[]{:S(2)}) copy-start(bf16[5,32,128]{2,1,0:T(8,128)(2,1)} %copy-done.7) | copy-start | bytes 122884
  32.6 1.4 %collective-permute-start.4 = (bf16[2,2,160,128]{3,2,1,0:T(8,128)(2,1)S(1)}, bf16[2,2,160,128]{3,2,1,0:T(8,128)(2,1)S(1)}, u32[]{:S(2)}, u32[]{:S(2)}) collective-permute-start(bf16[2,2,160,128]{3,2,1,0:T(8,128)(2,1)S(1)} %get-tuple-element.17), channel_id=1, source_target_pairs={{0,32},{32,0},{64,96},{96,64},{128,160},{160,128},{192,224},{224,1... | collective-permute-start | bytes 491528 | tf_op jit(solution)/shard_map/ppermute | solution.py:308
  32.6 1.4 %collective-permute-start.5 = (bf16[2,2,128,128]{3,2,1,0:T(8,128)(2,1)}, bf16[2,2,128,128]{3,2,1,0:T(8,128)(2,1)S(1)}, u32[]{:S(2)}, u32[]{:S(2)}) collective-permute-start(bf16[2,2,128,128]{3,2,1,0:T(8,128)(2,1)} %get-tuple-element.18), channel_id=1, source_target_pairs={{32,64},{64,32},{96,128},{128,96},{160,192},{192,160},{33,65},{65,... | collective-permute-start | bytes 393224 | tf_op jit(solution)/shard_map/ppermute | solution.py:309
  34.0 1.0 copy-start.4
  48.0 38.7 %copy-start = (bf16[3,128,128]{2,1,0:T(8,128)(2,1)S(1)}, bf16[3,128,128]{2,1,0:T(8,128)(2,1)}, u32[]{:S(2)}) copy-start(bf16[3,128,128]{2,1,0:T(8,128)(2,1)} %param.7) | copy-start | bytes 294916
  48.0 1.4 %collective-permute-start.6 = (f32[192,128]{1,0:T(8,128)S(1)}, f32[192,128]{1,0:T(8,128)S(1)}, u32[]{:S(2)}, u32[]{:S(2)}) collective-permute-start(f32[192,128]{1,0:T(8,128)S(1)} %constant_dynamic-slice_fusion), channel_id=1, source_target_pairs={{0,32},{32,0},{64,96},{96,64},{128,160},{160,128},{192,224},{224,1... | collective-permute-start | bytes 294920 | tf_op jit(solution)/shard_map/ppermute | solution.py:247
  49.4 40.8 %copy-start.6 = (bf16[5,32,128]{2,1,0:T(8,128)(2,1)S(1)}, bf16[5,32,128]{2,1,0:T(8,128)(2,1)}, u32[]{:S(2)}) copy-start(bf16[5,32,128]{2,1,0:T(8,128)(2,1)} %copy-done.5) | copy-start | bytes 122884
  49.4 4.9 %collective-permute-start.7 = (f32[192,128]{1,0:T(8,128)S(1)}, f32[192,128]{1,0:T(8,128)S(1)}, u32[]{:S(2)}, u32[]{:S(2)}) collective-permute-start(f32[192,128]{1,0:T(8,128)S(1)} %dynamic-slice_add_fusion), channel_id=1, source_target_pairs={{0,1},{1,0},{2,3},{3,2},{4,5},{5,4},{6,7},{7,6},{8,9},{9,8},{10,11... | collective-permute-start | bytes 294920 | tf_op jit(solution)/shard_map/ppermute | solution.py:247
  51.1 8.0 %collective-permute-start.8 = (f32[192,128]{1,0:T(8,128)S(1)}, f32[192,128]{1,0:T(8,128)S(1)}, u32[]{:S(2)}, u32[]{:S(2)}) collective-permute-start(f32[192,128]{1,0:T(8,128)S(1)} %dynamic-slice_add_fusion), channel_id=1, source_target_pairs={{0,2},{1,3},{2,0},{3,1},{4,6},{5,7},{6,4},{7,5},{8,10},{9,11},{10,... | collective-permute-start | bytes 294920 | tf_op jit(solution)/shard_map/ppermute | solution.py:247
  54.0 6.9 %collective-permute-start.9 = (f32[192,128]{1,0:T(8,128)S(1)}, f32[192,128]{1,0:T(8,128)S(1)}, u32[]{:S(2)}, u32[]{:S(2)}) collective-permute-start(f32[192,128]{1,0:T(8,128)S(1)} %dynamic-slice_add_fusion), channel_id=1, source_target_pairs={{0,3},{1,2},{2,1},{3,0},{4,7},{5,6},{6,5},{7,4},{8,11},{9,10},{10,... | collective-permute-start | bytes 294920 | tf_op jit(solution)/shard_map/ppermute | solution.py:247
  61.0 5.2 %collective-permute-start.10 = (f32[192,128]{1,0:T(8,128)S(1)}, f32[192,128]{1,0:T(8,128)S(1)}, u32[]{:S(2)}, u32[]{:S(2)}) collective-permute-start(f32[192,128]{1,0:T(8,128)S(1)} %add_add_fusion.1), channel_id=1, source_target_pairs={{0,4},{4,0},{8,12},{12,8},{16,20},{20,16},{24,28},{28,24},{1,5},{5... | collective-permute-start | bytes 294920 | tf_op jit(solution)/shard_map/ppermute | solution.py:247
  61.3 8.7 %collective-permute-start.11 = (f32[192,128]{1,0:T(8,128)S(1)}, f32[192,128]{1,0:T(8,128)S(1)}, u32[]{:S(2)}, u32[]{:S(2)}) collective-permute-start(f32[192,128]{1,0:T(8,128)S(1)} %add_add_fusion.1), channel_id=1, source_target_pairs={{0,8},{4,12},{8,0},{12,4},{16,24},{20,28},{24,16},{28,20},{1,9},{5... | collective-permute-start | bytes 294920 | tf_op jit(solution)/shard_map/ppermute | solution.py:247
  65.3 6.5 %collective-permute-start.12 = (f32[192,128]{1,0:T(8,128)S(1)}, f32[192,128]{1,0:T(8,128)S(1)}, u32[]{:S(2)}, u32[]{:S(2)}) collective-permute-start(f32[192,128]{1,0:T(8,128)S(1)} %add_add_fusion.1), channel_id=1, source_target_pairs={{0,12},{4,8},{8,4},{12,0},{16,28},{20,24},{24,20},{28,16},{1,13},{... | collective-permute-start | bytes 294920 | tf_op jit(solution)/shard_map/ppermute | solution.py:247
  71.8 4.7 %collective-permute-start.13 = (f32[192,128]{1,0:T(8,128)S(1)}, f32[192,128]{1,0:T(8,128)S(1)}, u32[]{:S(2)}, u32[]{:S(2)}) collective-permute-start(f32[192,128]{1,0:T(8,128)S(1)} %add_add_fusion), channel_id=1, source_target_pairs={{0,64},{32,96},{64,0},{96,32},{128,192},{160,224},{192,128},{224,1... | collective-permute-start | bytes 294920 | tf_op jit(solution)/shard_map/ppermute | solution.py:247
  76.5 6.4 %collective-permute-start.14 = (f32[192,128]{1,0:T(8,128)S(1)}, f32[192,128]{1,0:T(8,128)S(1)}, u32[]{:S(2)}, u32[]{:S(2)}) collective-permute-start(f32[192,128]{1,0:T(8,128)S(1)} %add.64), channel_id=1, source_target_pairs={{0,128},{32,160},{64,192},{96,224},{128,0},{160,32},{192,64},{224,... | collective-permute-start | bytes 294920 | tf_op jit(solution)/shard_map/ppermute | solution.py:247
  83.0 7.1 %collective-permute-start.15 = (f32[192,128]{1,0:T(8,128)S(1)}, f32[192,128]{1,0:T(8,128)S(1)}, u32[]{:S(2)}, u32[]{:S(2)}) collective-permute-start(f32[192,128]{1,0:T(8,128)S(1)} %add.65), channel_id=1, source_target_pairs={{0,144},{4,148},{8,152},{12,156},{16,128},{20,132},{24,136},{28,14... | collective-permute-start | bytes 294920 | tf_op jit(solution)/shard_map/ppermute | solution.py:258
  90.1 20.9 %collective-permute-start.16 = (f32[192,128]{1,0:T(8,128)S(1)}, f32[192,128]{1,0:T(8,128)S(1)}, u32[]{:S(2)}, u32[]{:S(2)}) collective-permute-start(f32[192,128]{1,0:T(8,128)S(1)} %add.66), channel_id=1, source_target_pairs={{0,32},{32,0},{64,96},{96,64},{128,160},{160,128},{192,224},{224,1... | collective-permute-start | bytes 294920 | tf_op jit(solution)/shard_map/ppermute | solution.py:247

commit v2 on v1

v2 whole, which is shorter than its diff:
```python
import functools
import math

import jax
import jax.numpy as jnp
from jax import lax
from jax.experimental import pallas as pl
from jax.experimental.pallas import tpu as pltpu
from jax.sharding import PartitionSpec as P

ROWS = 16
COLS = 90
CHAN = 128
PAD = 96
F32 = jnp.float32
BF16 = jnp.bfloat16
LL = ("lat", "lon")
POLAR_FAR = 40
SECOND = 18
OTHERS = 9


def offsets_of(group):
    col = lax.broadcasted_iota(jnp.int32, (PAD, 128), 0)
    lane = lax.broadcasted_iota(jnp.int32, (PAD, 128), 1)
    none = jnp.full((PAD, 128), 1000000, jnp.int32)
    if group == 0:
        source = jnp.where(lane < PAD, lane, jnp.where(lane < PAD + 16, lane - 112, lane - 22))
        source = jnp.where((lane >= COLS) & (lane < PAD), none, source)
    elif group == 1:
        source = jnp.where(lane < 64, lane - 80, lane + 42)
    else:
        source = jnp.where(lane < 16, lane - 90, lane + 148)
        source = jnp.where((lane >= 10) & (lane < 22), none, source)
        source = jnp.where(lane >= 32, none, source)
    return (source - col).astype(F32)


def fill_shapes(table, offsets, spans, first, low, high):
    def fill(row, carry):
        span = spans[row_of(first, row)].astype(F32)
        divisor = jnp.full((1, 128), span + 1.0, F32)
        norm = lax.rsqrt(divisor)
        inside = jnp.abs(offsets) <= span
        scaled = jnp.where(inside, offsets * (1.0 / divisor), 0.0)
        square = scaled * scaled
        half = jnp.full(square.shape, 4.7108746e-07, F32)
        for term in (-2.5202042e-05, 9.1926025e-04, -2.0863481e-02, 2.5366950e-01, -1.2337005, 1.0):
            half = half * square + term
        cosine = 2.0 * half * half - 1.0
        shapes = (1.0 - jnp.abs(scaled), scaled, cosine)
        for k in range(3):
            at = pl.multiple_of(row * 288 + k * PAD, PAD)
            table[pl.ds(at, PAD), :] = jnp.where(inside, shapes[k] * norm, 0.0).astype(BF16)
        return carry

    lax.fori_loop(low, high, fill, 0)


def row_of(first, ext):
    return jnp.clip(first + ext - 2, 0, 127)


def factor_of(amps, first, ext, k, tap):
    return amps[tap, k, row_of(first, ext)]


def pack_kernel(info, field, cot, near_a, second_a, polar_a, second_b, polar_b, token, whole, sems):
    odd = info[1] % 2 == 1

    def edges(is_odd):
        copies = []
        for which, source in enumerate((field, cot)):
            for out, width, right in ((near_a, OTHERS, is_odd), (second_a, SECOND, is_odd), (second_b, SECOND, not is_odd)):
                begin = COLS - width if right else 0
                copies.append((source.at[0, begin : begin + width], out.at[which]))
        copies = [pltpu.make_async_copy(a, b, sems.at[i]) for i, (a, b) in enumerate(copies)]
        for copy in copies:
            copy.start()

        @pl.when(info[0] == 0)
        def _():
            loads = []
            for which, source in enumerate((field, cot)):
                for part in range(3):
                    at = pl.ds(part * 30, 30)
                    sem = sems.at[6 + which * 3 + part]
                    loads.append(pltpu.make_async_copy(source.at[0, at], whole.at[which, at], sem))
            for load in loads:
                load.start()
            for load in loads:
                load.wait()
            for which in range(2):
                low = whole[which, :, :8]
                left, right = whole[which, :POLAR_FAR, 8:], whole[which, COLS - POLAR_FAR :, 8:]
                polar_a[which, :COLS] = low
                polar_b[which, :COLS] = low
                polar_a[which, COLS:] = right if is_odd else left
                polar_b[which, COLS:] = left if is_odd else right

        for copy in copies:
            copy.wait()

    pl.when(odd)(lambda: edges(True))
    pl.when(jnp.logical_not(odd))(lambda: edges(False))
    token[...] = jnp.zeros((8, 128), F32)


def pre_kernel(info, spans, field, cot, token, own_f, own_c, shape0, shape1, shape2):
    lat, first = info[0], info[2]
    for source, own in ((field, own_f), (cot, own_c)):
        own[:, COLS:, :] = jnp.zeros((ROWS, 128 - COLS, CHAN), BF16)
        own[:, :COLS, :] = jnp.swapaxes(source[0], 0, 1)
    fill_shapes(shape0, offsets_of(0), spans, first, 0, 20)

    @pl.when(lat < 2)
    def _():
        low = jnp.where(lat == 0, 2, 0)
        fill_shapes(shape1, offsets_of(1), spans, first, low, jnp.where(lat == 0, 18, 2))

    @pl.when(lat == 0)
    def _():
        fill_shapes(shape2, offsets_of(2), spans, first, 2, 5)


def assemble_kernel(info, old_f, old_c, near_a, second_a, polar_a, second_b, polar_b, *outs):
    lat, lon = info[0], info[1]
    odd = lon % 2 == 1
    groups = ((outs[0], outs[2], outs[4]), (outs[1], outs[3], outs[5]))
    lat_a, lat_b = outs[6], outs[7]

    def left_right(a_ref, b_ref, which, lo, hi):
        left = jnp.where(odd, b_ref[which, lo:hi], a_ref[which, lo:hi])
        right = jnp.where(odd, a_ref[which, lo:hi], b_ref[which, lo:hi])
        return jnp.swapaxes(left, 0, 1), jnp.swapaxes(right, 0, 1)

    for which in range(2):
        own0, own1, own2 = groups[which]
        own0[...] = (old_f, old_c)[which][...]

        @pl.when(lat >= 2)
        def _(which=which, own0=own0):
            a = near_a[which]
            left = jnp.where(odd, second_b[which, SECOND - OTHERS :], a)
            right = jnp.where(odd, a, second_b[which, :OTHERS])
            own0[:, 112 - OTHERS : 112, :] = jnp.swapaxes(left, 0, 1)
            own0[:, 112 : 112 + OTHERS, :] = jnp.swapaxes(right, 0, 1)

        @pl.when(lat == 1)
        def _(which=which, own0=own0, own1=own1):
            left, right = left_right(second_a, second_b, which, 0, SECOND)
            own0[:, 96:112, :] = left[:, 2:]
            own0[:, 112:128, :] = right[:, :16]
            own1[...] = jnp.zeros(own1.shape, BF16)
            own1[:, 62:64, :] = left[:, :2]
            own1[:, 64:66, :] = right[:, 16:]

        @pl.when(lat == 0)
        def _(which=which, own0=own0, own1=own1, own2=own2):
            left, right = left_right(polar_a, polar_b, which, 0, COLS)
            own0[:8, 96:112, :] = left[:, 74:90]
            own0[:8, 112:128, :] = right[:, 0:16]
            own1[:8, :64, :] = left[:, 10:74]
            own1[:8, 64:, :] = right[:, 16:80]
            own2[:, :16, :] = left[:5, 0:16]
            own2[:, 16:, :] = right[:5, 74:90]
            left, right = left_right(polar_a, polar_b, which, COLS, COLS + POLAR_FAR)
            own0[8:, 96:112, :] = left[:, 24:40]
            own0[8:, 112:128, :] = right[:, 0:16]
            own1[8:] = jnp.zeros((8, 128, CHAN), BF16)
            own1[8:, 40:64, :] = left[:, 0:24]
            own1[8:, 64:88, :] = right[:, 16:40]

        even = lat % 2 == 0
        for row in range(2):
            lat_a[which, row, :128, :] = jnp.where(even, own0[14 + row], own0[row])
            lat_a[which, row, 128:, :] = jnp.where(even, own1[14 + row, 48:80, :], own1[row, 48:80, :])
            lat_b[which, row] = jnp.where(even, own0[row], own0[14 + row])


def filtered(shapes, amps, first, ext, rows):
    total = None
    for taps in ((0, 1), (2, 3), (4,)):
        gathered = jnp.concatenate([rows[tap] for tap in taps], axis=1) if len(taps) > 1 else rows[taps[0]]
        product = jnp.dot(shapes, gathered, preferred_element_type=F32)
        for index, tap in enumerate(taps):
            part = product[:, index * 128 : (index + 1) * 128]
            scaled = [part[k * PAD : (k + 1) * PAD] * factor_of(amps, first, ext, k, tap) for k in range(3)]
            total = scaled if total is None else [x + y for x, y in zip(total, scaled)]
    return total


def rows_at(ref, start, count=288):
    return ref[pl.ds(start if isinstance(start, int) else pl.multiple_of(start, 32), count), :]


def store_basis(basis, row, values):
    at = row * PAD if isinstance(row, int) else pl.multiple_of(row * PAD, PAD)
    for k in range(3):
        basis[pl.ds(at, PAD), k * 128 : (k + 1) * 128] = values[k].astype(BF16)


def times_cotangent(cot, basis):
    return lax.dot_general(cot, basis, (((0,), (0,)), ((), ())), preferred_element_type=F32)


def inner_kernel(info, amps, own0, own1, own2, shape0, shape1, shape2, cot, basis, part):
    lat, first = info[0], info[2]

    def one(row, wide, extra=None):
        shapes = rows_at(shape0, (row + 2) * 288)
        rows = [own0[row - 2 + tap] for tap in range(5)]
        if wide:
            shapes = jnp.concatenate([shapes, rows_at(shape1, (row + 2) * 288)], axis=1)
            rows = [jnp.concatenate([near, own1[row - 2 + tap]], axis=0) for tap, near in enumerate(rows)]
        values = filtered(shapes, amps, first, row + 2, rows)
        if extra is not None:
            values = [x + y for x, y in zip(values, extra)]
        store_basis(basis, row - 2, values)

    def loop(start, wide):
        def step(row, carry):
            one(row, wide)
            return carry

        lax.fori_loop(start, 14, step, 0)

    @pl.when(lat != 0)
    def _():
        loop(2, False)

    @pl.when(lat == 0)
    def _():
        far = filtered(shape2[4 * 288 : 5 * 288, :32], amps, first, 4, [own2[tap] for tap in range(5)])
        one(2, True, far)
        loop(3, True)

    part[...] = times_cotangent(cot[2:14, :PAD, :].reshape(12 * PAD, CHAN), basis[...])


def halo_row(halo_a, halo_b, which, row, even, top):
    a, b = halo_a[which, row, :128], halo_b[which, row]
    return jnp.where(even, b, a) if top else jnp.where(even, a, b)


def far_halo_row(halo_a, which, row):
    zeros = jnp.zeros((48, CHAN), BF16)
    return jnp.concatenate([zeros, halo_a[which, row, 128:], zeros], axis=0)


def outer_kernel(info, amps, own0, own1, own2, shape0, shape1, shape2, cot, halo_a, halo_b, part, basis, mine, other, grad):
    lat, first = info[0], info[2]
    even = lat % 2 == 0

    def run(wide):
        for place, row in enumerate((0, 1, 14, 15)):
            shapes = shape0[(row + 2) * 288 : (row + 3) * 288, :]
            rows = []
            for at in range(row - 2, row + 3):
                if 0 <= at < ROWS:
                    gathered = own0[at]
                else:
                    gathered = halo_row(halo_a, halo_b, 0, at + 2 if at < 0 else at - ROWS, even, at < 0)
                if wide:
                    if 0 <= at < ROWS:
                        far = own1[at]
                    elif at < 0:
                        far = jnp.zeros((128, CHAN), BF16)
                    else:
                        far = far_halo_row(halo_a, 0, at - ROWS)
                    gathered = jnp.concatenate([gathered, far], axis=0)
                rows.append(gathered)
            if wide:
                shapes = jnp.concatenate([shapes, shape1[(row + 2) * 288 : (row + 3) * 288, :]], axis=1)
            values = filtered(shapes, amps, first, row + 2, rows)
            if wide and row < 2:
                zeros = jnp.zeros((32, CHAN), BF16)
                rows = [own2[at] if at >= 0 else zeros for at in range(row - 2, row + 3)]
                far = filtered(shape2[(row + 2) * 288 : (row + 3) * 288, :32], amps, first, row + 2, rows)
                values = [x + y for x, y in zip(values, far)]
            store_basis(basis, place, values)

    pl.when(lat != 0)(lambda: run(False))
    pl.when(lat == 0)(lambda: run(True))
    ends = jnp.concatenate([cot[0:2, :PAD, :], cot[14:16, :PAD, :]], axis=0).reshape(4 * PAD, CHAN)
    product = part[...] + times_cotangent(ends, basis[...])
    for k in range(3):
        grad[k * 128 : (k + 1) * 128, :] = product[:, k * 128 : (k + 1) * 128].T
    core = lat % 2
    mine[...] = grad[pl.ds(pl.multiple_of(core * 192, 192), 192), :]
    other[...] = grad[pl.ds(pl.multiple_of((1 - core) * 192, 192), 192), :]


def mix_kernel(inner, outer, weight, before, out, token):
    w = weight[...]

    def mixed(basis, rows):
        return jnp.dot(basis, w, preferred_element_type=F32).astype(BF16).reshape(rows, PAD, CHAN)[:, :COLS]

    ends = mixed(outer[...], 4)
    whole = jnp.concatenate([ends[:2], mixed(inner[...], 12), ends[2:]], axis=0)
    out[0] = jnp.swapaxes(whole, 0, 1)
    token[...] = before[...]


def back_kernel(piece, info, amps, own0, own1, own2, shape0, shape1, shape2, halo_a, halo_b, weight, before, *refs):
    out, token, spread = refs[-3:]
    lat, first = info[0], info[2]
    even = lat % 2 == 0
    begin = 8 * piece

    def put(index, value, fresh):
        at = index * 288 if isinstance(index, int) else pl.multiple_of(index * 288, 32)
        if fresh:
            spread[pl.ds(at, 288), :] = value
        else:
            spread[pl.ds(at, 288), :] += value

    def own_rows(low, high, wide):
        def step(ext, carry):
            shapes, rows = rows_at(shape0, ext * 288), own0[ext - 2]
            if wide:
                shapes = jnp.concatenate([shapes, rows_at(shape1, ext * 288)], axis=1)
                rows = jnp.concatenate([rows, own1[ext - 2]], axis=0)
            put(ext - begin, jnp.dot(shapes, rows, preferred_element_type=F32), True)
            return carry

        lax.fori_loop(low, high, step, 0)

    low, high = max(begin, 2), min(begin + 12, 18)
    pl.when(lat != 0)(lambda: own_rows(low, high, False))
    pl.when(lat == 0)(lambda: own_rows(low, high, True))
    for row in range(2):
        ext = row if piece == 0 else 18 + row
        gathered = halo_row(halo_a, halo_b, 1, row, even, piece == 0)
        put(ext - begin, jnp.dot(shape0[ext * 288 : (ext + 1) * 288, :], gathered, preferred_element_type=F32), True)
    if piece == 0:

        @pl.when(lat == 1)
        def _():
            for row in range(2):
                far = far_halo_row(halo_a, 1, row)
                put(row, jnp.dot(shape1[row * 288 : (row + 1) * 288, :], far, preferred_element_type=F32), False)

        @pl.when(lat == 0)
        def _():
            for ext in range(2, 5):
                shapes = shape2[ext * 288 : (ext + 1) * 288, :32]
                put(ext, jnp.dot(shapes, own2[ext - 2], preferred_element_type=F32), False)

    if piece:
        out[...] = refs[0][...]
    rows = []
    for row in range(8):
        mixed = None
        for k in range(3):
            total = None
            for slot in range(5):
                factor = factor_of(amps, first, begin + row + slot, k, 4 - slot) * (-1.0 if k == 1 else 1.0)
                at = (row + slot) * 288 + k * PAD
                term = spread[at : at + PAD, :] * factor
                total = term if total is None else total + term
            term = lax.dot_general(total.astype(BF16), weight[k], (((1,), (1,)), ((), ())), preferred_element_type=F32)
            mixed = term if mixed is None else mixed + term
        rows.append(mixed[None, :COLS])
    out[0, :, begin : begin + 8, :] = jnp.swapaxes(jnp.concatenate(rows, axis=0), 0, 1)
    token[...] = before[...]


def sum_kernel(count, *refs):
    parts = [ref[...] for ref in refs[:count]]
    while len(parts) > 1:
        parts = [parts[i] + parts[i + 1] for i in range(0, len(parts), 2)]
    refs[-2][...] = parts[0]
    refs[-1][...] = jnp.zeros((8, 128), F32)


def join_kernel(info, mine, other, out):
    scale = 1.0 / math.sqrt(4 * 128 * 720)
    core = info[0] % 2
    out[pl.ds(pl.multiple_of(core * 192, 192), 192), :] = mine[...] * scale
    out[pl.ds(pl.multiple_of((1 - core) * 192, 192), 192), :] = other[...] * scale


def pairs_of_lon(parity, lats):
    out = []
    for lat in lats:
        for lon in range(8):
            other = lon ^ 1 if parity == 0 else ((lon + 1) % 8 if lon % 2 else (lon - 1) % 8)
            out.append((lat * 8 + lon, lat * 8 + other))
    return out


def pairs_of_lat(parity):
    out = []
    for lat in range(8):
        other = lat ^ 1 if parity == 0 else (lat + 1 if lat % 2 else lat - 1)
        if 0 <= other < 8:
            out.append((lat, other))
    return out


def z_pairs():
    across = {0: 6, 6: 0, 1: 7, 7: 1, 2: 4, 4: 2, 3: 5, 5: 3}
    out = []
    for lat in range(8):
        for lon in range(8):
            other = across[(lon >> 2) * 4 + (lat >> 1)]
            out.append((lat * 8 + lon, ((other % 4) * 2 + lat % 2) * 8 + (other // 4) * 4 + lon % 4))
    return out


def flip(x, axis, bit):
    return lax.ppermute(x, axis, [(i, i ^ bit) for i in range(lax.axis_size(axis))])


VMEM = pl.BlockSpec(memory_space=pltpu.VMEM)
SMEM = pl.BlockSpec(memory_space=pltpu.SMEM)


def call(kernel, outs, scratch, flops, scalars, arrays, limit=12, space=pltpu.VMEM):
    moved = sum(math.prod(x.shape) * x.dtype.itemsize for x in (*arrays, *outs))
    return pl.pallas_call(
        kernel,
        out_shape=outs,
        in_specs=[SMEM] * len(scalars) + [pl.BlockSpec(memory_space=space)] * len(arrays),
        out_specs=[VMEM] * len(outs),
        scratch_shapes=scratch,
        compiler_params=pltpu.CompilerParams(vmem_limit_bytes=limit * 1024 * 1024),
        cost_estimate=pl.CostEstimate(flops=flops, bytes_accessed=moved, transcendentals=0),
    )(*scalars, *arrays)


def shape(dims, dtype=BF16):
    return jax.ShapeDtypeStruct(dims, dtype)


def body(features, cotangent, mix_weight, amplitude, row_spans):
    lat, lon = lax.axis_index("lat"), lax.axis_index("lon")
    info = jnp.stack([lat, lon, lat * ROWS]).astype(jnp.int32)
    amps = amplitude.transpose(2, 0, 1)

    field, cot = features.transpose(0, 2, 1, 3), cotangent.transpose(0, 2, 1, 3)
    token = shape((8, 128), F32)
    near = shape((2, OTHERS, ROWS, CHAN))
    second = shape((2, SECOND, ROWS, CHAN))
    polar = shape((2, COLS + POLAR_FAR, 8, CHAN))
    *messages, before = call(
        pack_kernel,
        [near, second, polar, second, polar, token],
        [pltpu.VMEM((2, COLS, ROWS, CHAN), BF16), pltpu.SemaphoreType.DMA((12,))],
        0,
        (info,),
        (field, cot),
        limit=56,
        space=pl.ANY,
    )
    targets = ((1, range(2, 8)), (1, (1,)), (1, (0,)), (0, range(1, 8)), (0, (0,)))
    got = [None] * 5
    for index in (2, 1, 0, 4, 3):
        got[index] = lax.ppermute(messages[index], LL, pairs_of_lon(*targets[index]))

    gathered = shape((ROWS, 128, CHAN))
    tables = [shape((20 * 288, 128)), shape((20 * 288, 128)), shape((5 * 288, 128))]
    own_f, own_c, *shapes = call(
        pre_kernel, [gathered, gathered, *tables], [], 2 * 10**8, (info, row_spans), (field, cot, before)
    )
    own2 = shape((5, 32, CHAN))
    own0_f, own0_c, own1_f, own1_c, own2_f, own2_c, lat_a, lat_b = call(
        assemble_kernel,
        [gathered] * 4 + [own2] * 2 + [shape((2, 2, 160, CHAN)), shape((2, 2, 128, CHAN))],
        [],
        0,
        (info,),
        (own_f, own_c, *got),
    )
    halo_a = lax.ppermute(lat_a, "lat", pairs_of_lat(0))
    halo_b = lax.ppermute(lat_b, "lat", pairs_of_lat(1))

    row_flops = 2 * 288 * 640 * CHAN
    scalars = (info, amps)
    filters = (own0_f, own1_f, own2_f, *shapes, own0_c)
    inner, part = call(inner_kernel, [shape((12 * PAD, 384)), shape((128, 384), F32)], [], 12 * row_flops, scalars, filters)
    half = shape((192, CHAN), F32)
    outer, mine, other = call(
        outer_kernel,
        [shape((4 * PAD, 384)), half, half],
        [pltpu.VMEM((384, CHAN), F32)],
        4 * row_flops,
        scalars,
        (*filters, halo_a, halo_b, part),
    )

    def add(*parts, after=()):
        return call(functools.partial(sum_kernel, len(parts)), [half, token], [], 0, (), (*parts, *after))

    def back(piece, before, *done):
        return call(
            functools.partial(back_kernel, piece),
            [shape((1, COLS, ROWS, CHAN), F32), token],
            [pltpu.VMEM((12 * 288, CHAN), F32)],
            2 * row_flops,
            scalars,
            (own0_c, own1_c, own2_c, *shapes, halo_a, halo_b, mix_weight, before, *done),
        )

    mine, before = add(mine, flip(other, "lat", 1))
    steps = [flip(mine, "dp", bit) for bit in (1, 2, 3)]
    grad, done = back(0, before)
    mine, before = add(mine, *steps, after=(done,))
    steps = [flip(mine, "lon", bit) for bit in (1, 2, 3)]
    grad, done = back(1, before, grad)
    mine, before = add(mine, *steps, after=(done,))
    step = flip(mine, "lat", 2)
    convolved, done = call(
        mix_kernel,
        [shape((1, COLS, ROWS, CHAN)), token],
        [],
        2 * ROWS * PAD * 384 * CHAN,
        (),
        (inner, outer, mix_weight.reshape(384, CHAN), before),
    )
    mine, _ = add(mine, step, after=(done,))
    mine, _ = add(mine, flip(mine, "lat", 4))
    mine, _ = add(mine, lax.ppermute(mine, LL, z_pairs()))
    other = flip(mine, "lat", 1)
    (whole,) = call(join_kernel, [shape((384, CHAN), F32)], [], 0, (info,), (mine, other))
    return convolved.transpose(0, 2, 1, 3), grad.transpose(0, 2, 1, 3), whole.reshape(3, 128, 128)


def solution(mesh):
    cells = P("dp", "lat", "lon", None)
    return jax.shard_map(
        body,
        mesh=mesh,
        in_specs=(cells, cells, P(), P(), P()),
        out_specs=(cells, cells, P()),
        check_vma=False,
    )
```

time: 112 us -> 81 us (0.72)
  the two profiles are of different devices: /device:TPU:6 before, /device:TPU:1 now
where the time goes in v2:
time: 81 us; the launch traced here: 80.6 us
  starting transfers between devices  37.9 us (47%)
  Pallas kernels  23.5 us (29%)
  waiting for transfers between devices  13.7 us (17%)
  local copies, waits for them, and re-layouts  3.99 us (5%)
  between operations  0.83 us (1%)
    pallas_call x15, Pallas kernels, call(): pl.pallas_call(kernel, out_shape=outs, in_specs=[SMEM] * len(scalars) + [...  23.5 us
    ppermute x5, starting transfers between devices, body(): lax.ppermute(messages[index], LL, pairs_of_lon(*targets[index]))  15.8 us
    ppermute x10, starting transfers between devices, flip(): lax.ppermute(x, axis, [(i, i ^ bit) for i in range(lax.axis_size(axis))])  13.8 us
    ppermute x10, waiting for transfers between devices, flip(): lax.ppermute(x, axis, [(i, i ^ bit) for i in range(lax.axis_size(axis))])  10.3 us
    unnamed x16, local copies, waits for them, and re-layouts  3.99 us
    ppermute x1, starting transfers between devices, body(): halo_a = lax.ppermute(lat_a, 'lat', pairs_of_lat(0))  3.84 us
    ppermute x1, waiting for transfers between devices, body(): mine, _ = add(mine, lax.ppermute(mine, LL, z_pairs()))  3.09 us
    ppermute x1, starting transfers between devices, body(): mine, _ = add(mine, lax.ppermute(mine, LL, z_pairs()))  2.59 us
  transfers between devices with their start and end apart: 18, of which 8 were waited for; matrix products, arithmetic and copies ran while one was open for 0% of the time, Pallas kernels for 18%

profile of v2, /device:TPU:1, one launch (start us, length us, event | category | flops | bytes accessed | tf_op | source)
XLA Modules:
  0.0 80.6 jit_solution(17823436557978051090)
XLA Ops:
  0.6 0.7 pad_add_fusion.info
  1.3 2.9 %shard_map.76 = (bf16[2,9,16,128]{3,2,1,0:T(8,128)(2,1)}, bf16[2,18,16,128]{3,2,1,0:T(8,128)(2,1)}, bf16[2,130,8,128]{3,2,1,0:T(8,128)(2,1)}, bf16[2,18,16,128]{...) custom-call(s32[3]{0:T(128)} %pad_add_fusion.info, bf16[1,90,16,128]{3,2,1,0:T(8,128)(2,1)} %bitcast.10, ...), custom_call_target="tpu_custom_call" | custom-call | bytes 2174976 | tf_op jit(solution)/shard_map/pallas_call | solution.py:423
  4.2 0.7 collective-permute-start.2
  4.9 0.7 collective-permute-start.4
  5.6 11.8 %collective-permute-start.1 = (bf16[2,18,16,128]{3,2,1,0:T(8,128)(2,1)}, bf16[2,18,16,128]{3,2,1,0:T(8,128)(2,1)S(1)}, u32[]{:S(2)}, u32[]{:S(2)}) collective-permute-start(bf16[2,18,16,128]{3,2,1,0:T(8,128)(2,1)} %get-tuple-element.46), channel_id=1, source_target_pairs={{32,60},{36,40},{40,36},{44,48},{48,44},{52,56},{56,52},{60,32},{3... | collective-permute-start | bytes 442376 | tf_op jit(solution)/shard_map/ppermute | solution.py:461
  17.5 1.9 %collective-permute-start.3 = (bf16[2,18,16,128]{3,2,1,0:T(8,128)(2,1)}, bf16[2,18,16,128]{3,2,1,0:T(8,128)(2,1)S(1)}, u32[]{:S(2)}, u32[]{:S(2)}) collective-permute-start(bf16[2,18,16,128]{3,2,1,0:T(8,128)(2,1)} %get-tuple-element.48), channel_id=1, source_target_pairs={{32,36},{36,32},{40,44},{44,40},{48,52},{52,48},{56,60},{60,56},{6... | collective-permute-start | bytes 442376 | tf_op jit(solution)/shard_map/ppermute | solution.py:461
  19.4 0.7 collective-permute-start
  20.1 0.0 copy-start
  20.1 1.0 %copy-done = bf16[1,16,90,128]{3,1,2,0:T(8,128)(2,1)S(1)} copy-done((bf16[1,16,90,128]{3,1,2,0:T(8,128)(2,1)S(1)}, bf16[1,16,90,128]{3,1,2,0:T(8,128)(2,1)}, u32[]{:S(2)}) %copy-start) | copy-done | bytes 368664
  21.1 0.0 copy-start.1
  21.1 1.0 %copy-done.1 = bf16[1,16,90,128]{3,1,2,0:T(8,128)(2,1)S(1)} copy-done((bf16[1,16,90,128]{3,1,2,0:T(8,128)(2,1)S(1)}, bf16[1,16,90,128]{3,1,2,0:T(8,128)(2,1)}, u32[]{:S(2)}) %copy-start.1) | copy-done | bytes 368664
  22.1 0.0 copy-start.4
  22.1 0.7 copy-done.4
  22.7 0.0 copy-start.6
  22.7 0.7 copy-done.6
  23.4 0.0 copy-start.7
  23.4 0.7 copy-done.7
  24.1 0.0 copy-start.3
  24.1 2.3 %shard_map.77 = (bf16[16,128,128]{2,1,0:T(8,128)(2,1)S(1)}, bf16[16,128,128]{2,1,0:T(8,128)(2,1)S(1)}, bf16[5760,128]{1,0:T(8,128)(2,1)S(1)}, bf16[5760,128]{1,0:T(8,128)(2,1)S(1)}, bf16[1440,128]{1,0:T(8,128)(2,1)S(1)}) custom-call(s32[3]{0:T(128)S(1)} %copy-done.4, s32[128]{0:T(128)S(1)} %copy-done.7, bf16[1,90,16,128]{3,2,1,0:T(8,128)(2,1)S(1)} %bitcast.11, ...), custom_call_target="tpu_custom_call" | custom-call | flops 200000000 | bytes 5107712 | tf_op jit(solution)/shard_map/pallas_call | solution.py:423
  26.4 0.0 collective-permute-done.near_a
  26.4 0.0 collective-permute-done.1.second_a
  26.4 0.0 collective-permute-done.3.second_b
  26.5 0.0 collective-permute-done.2.polar_a
  26.5 0.0 collective-permute-done.4.polar_b
  26.5 1.0 %shard_map.78 = (bf16[16,128,128]{2,1,0:T(8,128)(2,1)S(1)}, bf16[16,128,128]{2,1,0:T(8,128)(2,1)S(1)}, bf16[16,128,128]{2,1,0:T(8,128)(2,1)S(1)}, bf16[16,128,12...) custom-call(s32[3]{0:T(128)S(1)} %copy-done.4, ...), custom_call_target="tpu_custom_call" | custom-call | bytes 4956160 | tf_op jit(solution)/shard_map/pallas_call | solution.py:423
  27.5 3.8 %collective-permute-start.5 = (bf16[2,2,160,128]{3,2,1,0:T(8,128)(2,1)S(1)}, bf16[2,2,160,128]{3,2,1,0:T(8,128)(2,1)S(1)}, u32[]{:S(2)}, u32[]{:S(2)}) collective-permute-start(bf16[2,2,160,128]{3,2,1,0:T(8,128)(2,1)S(1)} %get-tuple-element.58), channel_id=1, source_target_pairs={{0,32},{32,0},{64,96},{96,64},{128,160},{160,128},{192,224},{224,1... | collective-permute-start | bytes 491528 | tf_op jit(solution)/shard_map/ppermute | solution.py:477
  31.3 1.9 %collective-permute-start.6 = (bf16[2,2,128,128]{3,2,1,0:T(8,128)(2,1)S(1)}, bf16[2,2,128,128]{3,2,1,0:T(8,128)(2,1)S(1)}, u32[]{:S(2)}, u32[]{:S(2)}) collective-permute-start(bf16[2,2,128,128]{3,2,1,0:T(8,128)(2,1)S(1)} %get-tuple-element.59), channel_id=1, source_target_pairs={{32,64},{64,32},{96,128},{128,96},{160,192},{192,160},{33,65},{65,... | collective-permute-start | bytes 393224 | tf_op jit(solution)/shard_map/ppermute | solution.py:478
  33.2 0.0 copy-done.3
  33.2 4.1 %shard_map.79 = (bf16[1152,384]{1,0:T(8,128)(2,1)S(1)}, f32[128,384]{1,0:T(8,128)S(1)}) custom-call(s32[3]{0:T(128)S(1)} %copy-done.4, f32[5,3,128]{2,1,0:T(4,128)S(1)} %bitcast.15, bf16[16,128,128]{2,1,0:T(8,128)(2,1)S(1)} %get-tuple-element.50.own0, bf16[16,128,128]{2,1,0:T(8,128)(2,1)S(1)} %get-tuple-element.51.own1, ...), custom_call_target="tpu_custom_call" | custom-call | flops 566231040 | bytes 6012928 | tf_op jit(solution)/shard_map/pallas_call | solution.py:423
  37.3 0.3 collective-permute-done.6.halo_b
  37.6 0.0 collective-permute-done.5.halo_a
  37.6 0.0 copy-start.2
  37.6 1.7 %shard_map.80 = (bf16[384,384]{1,0:T(8,128)(2,1)S(1)}, f32[192,128]{1,0:T(8,128)S(1)}, f32[192,128]{1,0:T(8,128)S(1)}) custom-call(s32[3]{0:T(128)S(1)} %copy-done.4, f32[5,3,128]{2,1,0:T(4,128)S(1)} %bitcast.16, bf16[16,128,128]{2,1,0:T(8,128)(2,1)S(1)} %get-tuple-element.50.own0, bf16[16,128,128]{2,1,0:T(8,128)(2,1)S(1)} %get-tuple-element.51.own1, ...), custom_call_target="tpu_custom_call" | custom-call | flops 188743680 | bytes 5914624 | tf_op jit(solution)/shard_map/pallas_call | solution.py:423
  39.3 0.1 collective-permute-start.7
  39.4 1.3 %collective-permute-done.7.refs_1_ = f32[192,128]{1,0:T(8,128)S(1)} collective-permute-done((f32[192,128]{1,0:T(8,128)S(1)}, f32[192,128]{1,0:T(8,128)S(1)}, u32[]{:S(2)}, u32[]{:S(2)}) %collective-permute-start.7) | collective-permute-done | bytes 98336 | tf_op jit(solution)/shard_map/ppermute | solution.py:414
  40.7 2.8 %collective-permute-start.10 = (f32[192,128]{1,0:T(8,128)S(1)}, f32[192,128]{1,0:T(8,128)S(1)}, u32[]{:S(2)}, u32[]{:S(2)}) collective-permute-start(f32[192,128]{1,0:T(8,128)S(1)} %get-tuple-element.64.refs_0_), channel_id=1, source_target_pairs={{0,3},{1,2},{2,1},{3,0},{4,7},{5,6},{6,5},{7,4},{8,11},{9,10},{10,... | collective-permute-start | bytes 294920 | tf_op jit(solution)/shard_map/ppermute | solution.py:414
  43.5 0.3 collective-permute-start.9
  43.8 0.3 collective-permute-start.8
  44.2 0.0 copy-done.2
  44.2 0.0 copy-done.5
  44.2 3.3 %shard_map.82 = (f32[1,90,16,128]{3,2,1,0:T(8,128)S(1)}, f32[8,128]{1,0:T(8,128)S(1)}) custom-call(s32[3]{0:T(128)S(1)} %copy-done.5, f32[5,3,128]{2,1,0:T(4,128)S(1)} %bitcast.17, bf16[16,128,128]{2,1,0:T(8,128)(2,1)S(1)} %get-tuple-element.56.cot.own0, bf16[16,128,128]{2,1,0:T(8,128)(2,1)S(1)} %get-tuple-element.65.own1, ...), custom_call_target="tpu_custom_call" | custom-call | flops 94371840 | bytes 5545984 | tf_op jit(solution)/shard_map/pallas_call | solution.py:423
  47.4 0.2 collective-permute-done.10.refs_3_
  47.6 1.3 %collective-permute-done.9.refs_2_ = f32[192,128]{1,0:T(8,128)S(1)} collective-permute-done((f32[192,128]{1,0:T(8,128)S(1)}, f32[192,128]{1,0:T(8,128)S(1)}, u32[]{:S(2)}, u32[]{:S(2)}) %collective-permute-start.9) | collective-permute-done | bytes 98336 | tf_op jit(solution)/shard_map/ppermute | solution.py:414
  48.9 0.0 collective-permute-done.8.refs_1_
  49.0 0.3 collective-permute-start.13
  49.3 2.3 %collective-permute-start.12 = (f32[192,128]{1,0:T(8,128)S(1)}, f32[192,128]{1,0:T(8,128)S(1)}, u32[]{:S(2)}, u32[]{:S(2)}) collective-permute-start(f32[192,128]{1,0:T(8,128)S(1)} %get-tuple-element.69.refs_0_), channel_id=1, source_target_pairs={{0,8},{4,12},{8,0},{12,4},{16,24},{20,28},{24,16},{28,20},{1,9},{5... | collective-permute-start | bytes 294920 | tf_op jit(solution)/shard_map/ppermute | solution.py:414
  51.5 0.8 collective-permute-start.11
  52.3 3.9 %shard_map.84 = (f32[1,90,16,128]{3,2,1,0:T(8,128)}, f32[8,128]{1,0:T(8,128)S(1)}) custom-call(s32[3]{0:T(128)S(1)} %copy-done.5, f32[5,3,128]{2,1,0:T(4,128)S(1)} %bitcast.18, bf16[16,128,128]{2,1,0:T(8,128)(2,1)S(1)} %get-tuple-element.56.cot.own0, bf16[16,128,128]{2,1,0:T(8,128)(2,1)S(1)} %get-tuple-element.65.own1, ...), custom_call_target="tpu_custom_call" | custom-call | flops 94371840 | bytes 6283264 | tf_op jit(solution)/shard_map/pallas_call | solution.py:423
  56.2 0.0 collective-permute-done.13.refs_3_
  56.2 0.0 collective-permute-done.12.refs_2_
  56.2 0.0 collective-permute-done.11.refs_1_
  56.2 1.1 %collective-permute-start.14 = (f32[192,128]{1,0:T(8,128)S(1)}, f32[192,128]{1,0:T(8,128)S(1)}, u32[]{:S(2)}, u32[]{:S(2)}) collective-permute-start(f32[192,128]{1,0:T(8,128)S(1)} %get-tuple-element.76.refs_0_), channel_id=1, source_target_pairs={{0,64},{32,96},{64,0},{96,32},{128,192},{160,224},{192,128},{224,1... | collective-permute-start | bytes 294920 | tf_op jit(solution)/shard_map/ppermute | solution.py:414
  57.4 1.3 %shard_map.86 = (bf16[1,90,16,128]{3,2,1,0:T(8,128)(2,1)}, f32[8,128]{1,0:T(8,128)S(1)}) custom-call(bf16[1152,384]{1,0:T(8,128)(2,1)S(1)} %get-tuple-element.57.inner, bf16[384,384]{1,0:T(8,128)(2,1)S(1)} %get-tuple-element.61.outer, bf16[384,128]{1,0:T(8,128)(2,1)S(1)} %bitcast.14, f32[8,128]{1,0:T(8,128)S(1)} %get-tuple-element.73.before), custom_call_target="tpu_custom_call" | custom-call | flops 150994944 | bytes 1654784 | tf_op jit(solution)/shard_map/pallas_call | solution.py:423
  58.6 1.1 %collective-permute-done.14.refs_1_ = f32[192,128]{1,0:T(8,128)S(1)} collective-permute-done((f32[192,128]{1,0:T(8,128)S(1)}, f32[192,128]{1,0:T(8,128)S(1)}, u32[]{:S(2)}, u32[]{:S(2)}) %collective-permute-start.14) | collective-permute-done | bytes 98336 | tf_op jit(solution)/shard_map/ppermute | solution.py:414
  59.8 0.6 shard_map.87
  60.4 0.0 collective-permute-start.15
  60.4 5.4 %collective-permute-done.15.refs_1_ = f32[192,128]{1,0:T(8,128)S(1)} collective-permute-done((f32[192,128]{1,0:T(8,128)S(1)}, f32[192,128]{1,0:T(8,128)S(1)}, u32[]{:S(2)}, u32[]{:S(2)}) %collective-permute-start.15) | collective-permute-done | bytes 98336 | tf_op jit(solution)/shard_map/ppermute | solution.py:414
  65.8 0.6 shard_map.88
  66.4 2.6 %collective-permute-start.16 = (f32[192,128]{1,0:T(8,128)S(1)}, f32[192,128]{1,0:T(8,128)S(1)}, u32[]{:S(2)}, u32[]{:S(2)}) collective-permute-start(f32[192,128]{1,0:T(8,128)S(1)} %get-tuple-element.79.refs_0_), channel_id=1, source_target_pairs={{0,144},{4,148},{8,152},{12,156},{16,128},{20,132},{24,136},{28,14... | collective-permute-start | bytes 294920 | tf_op jit(solution)/shard_map/ppermute | solution.py:525
  69.0 3.1 %collective-permute-done.16.refs_1_ = f32[192,128]{1,0:T(8,128)S(1)} collective-permute-done((f32[192,128]{1,0:T(8,128)S(1)}, f32[192,128]{1,0:T(8,128)S(1)}, u32[]{:S(2)}, u32[]{:S(2)}) %collective-permute-start.16) | collective-permute-done | bytes 98336 | tf_op jit(solution)/shard_map/ppermute | solution.py:525
  72.1 0.6 shard_map.89
  72.7 5.7 %collective-permute-start.17 = (f32[192,128]{1,0:T(8,128)S(1)}, f32[192,128]{1,0:T(8,128)S(1)}, u32[]{:S(2)}, u32[]{:S(2)}) collective-permute-start(f32[192,128]{1,0:T(8,128)S(1)} %get-tuple-element.80.mine), channel_id=1, source_target_pairs={{0,32},{32,0},{64,96},{96,64},{128,160},{160,128},{192,224},{224,1... | collective-permute-start | bytes 294920 | tf_op jit(solution)/shard_map/ppermute | solution.py:414
  78.4 0.9 %collective-permute-done.17.other = f32[192,128]{1,0:T(8,128)S(1)} collective-permute-done((f32[192,128]{1,0:T(8,128)S(1)}, f32[192,128]{1,0:T(8,128)S(1)}, u32[]{:S(2)}, u32[]{:S(2)}) %collective-permute-start.17) | collective-permute-done | bytes 98336 | tf_op jit(solution)/shard_map/ppermute | solution.py:414
  79.3 1.2 %shard_map.90 = f32[384,128]{1,0:T(8,128)} custom-call(s32[3]{0:T(128)S(1)} %copy-done.5, f32[192,128]{1,0:T(8,128)S(1)} %get-tuple-element.80.mine, f32[192,128]{1,0:T(8,128)S(1)} %collective-permute-done.17.other), custom_call_target="tpu_custom_call" | custom-call | bytes 393216 | tf_op jit(solution)/shard_map/pallas_call | solution.py:423
  (4 shorter events, 0.1 us)
Async XLA Ops:
  4.2 22.2 %collective-permute-start.2 = (bf16[2,130,8,128]{3,2,1,0:T(8,128)(2,1)}, bf16[2,130,8,128]{3,2,1,0:T(8,128)(2,1)S(1)}, u32[]{:S(2)}, u32[]{:S(2)}) collective-permute-start(bf16[2,130,8,128]{3,2,1,0:T(8,128)(2,1)} %get-tuple-element.47), channel_id=1, source_target_pairs={{0,28},{4,8},{8,4},{12,16},{16,12},{20,24},{24,20},{28,0},{1,29},{... | collective-permute-start | bytes 1597448 | tf_op jit(solution)/shard_map/ppermute | solution.py:461
  4.9 21.5 %collective-permute-start.4 = (bf16[2,130,8,128]{3,2,1,0:T(8,128)(2,1)}, bf16[2,130,8,128]{3,2,1,0:T(8,128)(2,1)S(1)}, u32[]{:S(2)}, u32[]{:S(2)}) collective-permute-start(bf16[2,130,8,128]{3,2,1,0:T(8,128)(2,1)} %get-tuple-element.49), channel_id=1, source_target_pairs={{0,4},{4,0},{8,12},{12,8},{16,20},{20,16},{24,28},{28,24},{1,5},{5... | collective-permute-start | bytes 1597448 | tf_op jit(solution)/shard_map/ppermute | solution.py:461
  5.6 20.8 %collective-permute-start.1 = (bf16[2,18,16,128]{3,2,1,0:T(8,128)(2,1)}, bf16[2,18,16,128]{3,2,1,0:T(8,128)(2,1)S(1)}, u32[]{:S(2)}, u32[]{:S(2)}) collective-permute-start(bf16[2,18,16,128]{3,2,1,0:T(8,128)(2,1)} %get-tuple-element.46), channel_id=1, source_target_pairs={{32,60},{36,40},{40,36},{44,48},{48,44},{52,56},{56,52},{60,32},{3... | collective-permute-start | bytes 442376 | tf_op jit(solution)/shard_map/ppermute | solution.py:461
  17.5 9.0 %collective-permute-start.3 = (bf16[2,18,16,128]{3,2,1,0:T(8,128)(2,1)}, bf16[2,18,16,128]{3,2,1,0:T(8,128)(2,1)S(1)}, u32[]{:S(2)}, u32[]{:S(2)}) collective-permute-start(bf16[2,18,16,128]{3,2,1,0:T(8,128)(2,1)} %get-tuple-element.48), channel_id=1, source_target_pairs={{32,36},{36,32},{40,44},{44,40},{48,52},{52,48},{56,60},{60,56},{6... | collective-permute-start | bytes 442376 | tf_op jit(solution)/shard_map/ppermute | solution.py:461
  19.4 7.0 %collective-permute-start = (bf16[2,9,16,128]{3,2,1,0:T(8,128)(2,1)}, bf16[2,9,16,128]{3,2,1,0:T(8,128)(2,1)S(1)}, u32[]{:S(2)}, u32[]{:S(2)}) collective-permute-start(bf16[2,9,16,128]{3,2,1,0:T(8,128)(2,1)} %get-tuple-element.45), channel_id=1, source_target_pairs={{64,92},{68,72},{72,68},{76,80},{80,76},{84,88},{88,84},{92,64},{9... | collective-permute-start | bytes 221192 | tf_op jit(solution)/shard_map/ppermute | solution.py:461
  20.1 1.0 %copy-start = (bf16[1,16,90,128]{3,1,2,0:T(8,128)(2,1)S(1)}, bf16[1,16,90,128]{3,1,2,0:T(8,128)(2,1)}, u32[]{:S(2)}) copy-start(bf16[1,16,90,128]{3,1,2,0:T(8,128)(2,1)} %param.5) | copy-start | bytes 1105924
  21.1 1.0 %copy-start.1 = (bf16[1,16,90,128]{3,1,2,0:T(8,128)(2,1)S(1)}, bf16[1,16,90,128]{3,1,2,0:T(8,128)(2,1)}, u32[]{:S(2)}) copy-start(bf16[1,16,90,128]{3,1,2,0:T(8,128)(2,1)} %param.6) | copy-start | bytes 1105924
  22.1 0.7 copy-start.4
  22.7 0.7 copy-start.6
  23.4 0.7 copy-start.7
  24.1 9.2 %copy-start.3 = (f32[3,128,5]{1,0,2:T(4,128)S(1)}, f32[3,128,5]{1,0,2:T(4,128)}, u32[]{:S(2)}) copy-start(f32[3,128,5]{1,0,2:T(4,128)} %param.8) | copy-start | bytes 23044
  27.5 10.1 %collective-permute-start.5 = (bf16[2,2,160,128]{3,2,1,0:T(8,128)(2,1)S(1)}, bf16[2,2,160,128]{3,2,1,0:T(8,128)(2,1)S(1)}, u32[]{:S(2)}, u32[]{:S(2)}) collective-permute-start(bf16[2,2,160,128]{3,2,1,0:T(8,128)(2,1)S(1)} %get-tuple-element.58), channel_id=1, source_target_pairs={{0,32},{32,0},{64,96},{96,64},{128,160},{160,128},{192,224},{224,1... | collective-permute-start | bytes 491528 | tf_op jit(solution)/shard_map/ppermute | solution.py:477
  31.3 6.3 %collective-permute-start.6 = (bf16[2,2,128,128]{3,2,1,0:T(8,128)(2,1)S(1)}, bf16[2,2,128,128]{3,2,1,0:T(8,128)(2,1)S(1)}, u32[]{:S(2)}, u32[]{:S(2)}) collective-permute-start(bf16[2,2,128,128]{3,2,1,0:T(8,128)(2,1)S(1)} %get-tuple-element.59), channel_id=1, source_target_pairs={{32,64},{64,32},{96,128},{128,96},{160,192},{192,160},{33,65},{65,... | collective-permute-start | bytes 393224 | tf_op jit(solution)/shard_map/ppermute | solution.py:478
  37.6 6.6 %copy-start.2 = (bf16[3,128,128]{2,1,0:T(8,128)(2,1)S(1)}, bf16[3,128,128]{2,1,0:T(8,128)(2,1)}, u32[]{:S(2)}) copy-start(bf16[3,128,128]{2,1,0:T(8,128)(2,1)} %weight.3) | copy-start | bytes 294916
  37.6 6.6 %copy-start.5 = (s32[3]{0:T(128)S(1)}, s32[3]{0:T(128)}, u32[]{:S(2)}) copy-start(s32[3]{0:T(128)} %pad_add_fusion.info) | copy-start | bytes 40
  39.3 1.4 %collective-permute-start.7 = (f32[192,128]{1,0:T(8,128)S(1)}, f32[192,128]{1,0:T(8,128)S(1)}, u32[]{:S(2)}, u32[]{:S(2)}) collective-permute-start(f32[192,128]{1,0:T(8,128)S(1)} %get-tuple-element.63), channel_id=1, source_target_pairs={{0,32},{32,0},{64,96},{96,64},{128,160},{160,128},{192,224},{224,1... | collective-permute-start | bytes 294920 | tf_op jit(solution)/shard_map/ppermute | solution.py:414
  40.7 7.0 %collective-permute-start.10 = (f32[192,128]{1,0:T(8,128)S(1)}, f32[192,128]{1,0:T(8,128)S(1)}, u32[]{:S(2)}, u32[]{:S(2)}) collective-permute-start(f32[192,128]{1,0:T(8,128)S(1)} %get-tuple-element.64.refs_0_), channel_id=1, source_target_pairs={{0,3},{1,2},{2,1},{3,0},{4,7},{5,6},{6,5},{7,4},{8,11},{9,10},{10,... | collective-permute-start | bytes 294920 | tf_op jit(solution)/shard_map/ppermute | solution.py:414
  43.5 5.4 %collective-permute-start.9 = (f32[192,128]{1,0:T(8,128)S(1)}, f32[192,128]{1,0:T(8,128)S(1)}, u32[]{:S(2)}, u32[]{:S(2)}) collective-permute-start(f32[192,128]{1,0:T(8,128)S(1)} %get-tuple-element.64.refs_0_), channel_id=1, source_target_pairs={{0,2},{1,3},{2,0},{3,1},{4,6},{5,7},{6,4},{7,5},{8,10},{9,11},{10,... | collective-permute-start | bytes 294920 | tf_op jit(solution)/shard_map/ppermute | solution.py:414
  43.8 5.1 %collective-permute-start.8 = (f32[192,128]{1,0:T(8,128)S(1)}, f32[192,128]{1,0:T(8,128)S(1)}, u32[]{:S(2)}, u32[]{:S(2)}) collective-permute-start(f32[192,128]{1,0:T(8,128)S(1)} %get-tuple-element.64.refs_0_), channel_id=1, source_target_pairs={{0,1},{1,0},{2,3},{3,2},{4,5},{5,4},{6,7},{7,6},{8,9},{9,8},{10,11... | collective-permute-start | bytes 294920 | tf_op jit(solution)/shard_map/ppermute | solution.py:414
  49.0 7.2 %collective-permute-start.13 = (f32[192,128]{1,0:T(8,128)S(1)}, f32[192,128]{1,0:T(8,128)S(1)}, u32[]{:S(2)}, u32[]{:S(2)}) collective-permute-start(f32[192,128]{1,0:T(8,128)S(1)} %get-tuple-element.69.refs_0_), channel_id=1, source_target_pairs={{0,12},{4,8},{8,4},{12,0},{16,28},{20,24},{24,20},{28,16},{1,13},{... | collective-permute-start | bytes 294920 | tf_op jit(solution)/shard_map/ppermute | solution.py:414
  49.3 6.9 %collective-permute-start.12 = (f32[192,128]{1,0:T(8,128)S(1)}, f32[192,128]{1,0:T(8,128)S(1)}, u32[]{:S(2)}, u32[]{:S(2)}) collective-permute-start(f32[192,128]{1,0:T(8,128)S(1)} %get-tuple-element.69.refs_0_), channel_id=1, source_target_pairs={{0,8},{4,12},{8,0},{12,4},{16,24},{20,28},{24,16},{28,20},{1,9},{5... | collective-permute-start | bytes 294920 | tf_op jit(solution)/shard_map/ppermute | solution.py:414
  51.5 4.7 %collective-permute-start.11 = (f32[192,128]{1,0:T(8,128)S(1)}, f32[192,128]{1,0:T(8,128)S(1)}, u32[]{:S(2)}, u32[]{:S(2)}) collective-permute-start(f32[192,128]{1,0:T(8,128)S(1)} %get-tuple-element.69.refs_0_), channel_id=1, source_target_pairs={{0,4},{4,0},{8,12},{12,8},{16,20},{20,16},{24,28},{28,24},{1,5},{5... | collective-permute-start | bytes 294920 | tf_op jit(solution)/shard_map/ppermute | solution.py:414
  56.2 3.6 %collective-permute-start.14 = (f32[192,128]{1,0:T(8,128)S(1)}, f32[192,128]{1,0:T(8,128)S(1)}, u32[]{:S(2)}, u32[]{:S(2)}) collective-permute-start(f32[192,128]{1,0:T(8,128)S(1)} %get-tuple-element.76.refs_0_), channel_id=1, source_target_pairs={{0,64},{32,96},{64,0},{96,32},{128,192},{160,224},{192,128},{224,1... | collective-permute-start | bytes 294920 | tf_op jit(solution)/shard_map/ppermute | solution.py:414
  60.4 5.4 %collective-permute-start.15 = (f32[192,128]{1,0:T(8,128)S(1)}, f32[192,128]{1,0:T(8,128)S(1)}, u32[]{:S(2)}, u32[]{:S(2)}) collective-permute-start(f32[192,128]{1,0:T(8,128)S(1)} %get-tuple-element.78.refs_0_), channel_id=1, source_target_pairs={{0,128},{32,160},{64,192},{96,224},{128,0},{160,32},{192,64},{224,... | collective-permute-start | bytes 294920 | tf_op jit(solution)/shard_map/ppermute | solution.py:414
  66.4 5.7 %collective-permute-start.16 = (f32[192,128]{1,0:T(8,128)S(1)}, f32[192,128]{1,0:T(8,128)S(1)}, u32[]{:S(2)}, u32[]{:S(2)}) collective-permute-start(f32[192,128]{1,0:T(8,128)S(1)} %get-tuple-element.79.refs_0_), channel_id=1, source_target_pairs={{0,144},{4,148},{8,152},{12,156},{16,128},{20,132},{24,136},{28,14... | collective-permute-start | bytes 294920 | tf_op jit(solution)/shard_map/ppermute | solution.py:525
  72.7 6.6 %collective-permute-start.17 = (f32[192,128]{1,0:T(8,128)S(1)}, f32[192,128]{1,0:T(8,128)S(1)}, u32[]{:S(2)}, u32[]{:S(2)}) collective-permute-start(f32[192,128]{1,0:T(8,128)S(1)} %get-tuple-element.80.mine), channel_id=1, source_target_pairs={{0,32},{32,0},{64,96},{96,64},{128,160},{160,128},{192,224},{224,1... | collective-permute-start | bytes 294920 | tf_op jit(solution)/shard_map/ppermute | solution.py:414

commit v3 on v2

v3 whole, which is shorter than its diff:
```python
import functools
import math

import jax
import jax.numpy as jnp
from jax import lax
from jax.experimental import pallas as pl
from jax.experimental.pallas import tpu as pltpu
from jax.sharding import PartitionSpec as P

ROWS = 16
COLS = 90
CHAN = 128
PAD = 96
F32 = jnp.float32
BF16 = jnp.bfloat16
LL = ("lat", "lon")
POLAR_FAR = 40
SECOND = 18
OTHERS = 9


def offsets_of(group):
    col = lax.broadcasted_iota(jnp.int32, (PAD, 128), 0)
    lane = lax.broadcasted_iota(jnp.int32, (PAD, 128), 1)
    none = jnp.full((PAD, 128), 1000000, jnp.int32)
    if group == 0:
        source = jnp.where(lane < PAD, lane, jnp.where(lane < PAD + 16, lane - 112, lane - 22))
        source = jnp.where((lane >= COLS) & (lane < PAD), none, source)
    elif group == 1:
        source = jnp.where(lane < 64, lane - 80, lane + 42)
    else:
        source = jnp.where(lane < 16, lane - 90, lane + 148)
        source = jnp.where((lane >= 10) & (lane < 22), none, source)
        source = jnp.where(lane >= 32, none, source)
    return (source - col).astype(F32)


def fill_shapes(table, offsets, spans, first, low, high):
    def fill(row, carry):
        span = spans[row_of(first, row)].astype(F32)
        divisor = jnp.full((1, 128), span + 1.0, F32)
        norm = lax.rsqrt(divisor)
        inside = jnp.abs(offsets) <= span
        scaled = jnp.where(inside, offsets * (1.0 / divisor), 0.0)
        square = scaled * scaled
        half = jnp.full(square.shape, 4.7108746e-07, F32)
        for term in (-2.5202042e-05, 9.1926025e-04, -2.0863481e-02, 2.5366950e-01, -1.2337005, 1.0):
            half = half * square + term
        cosine = 2.0 * half * half - 1.0
        shapes = (1.0 - jnp.abs(scaled), scaled, cosine)
        for k in range(3):
            at = pl.multiple_of(row * 288 + k * PAD, PAD)
            value = jnp.where(inside, shapes[k] * norm, 0.0)
            high = value.astype(BF16)
            table[pl.ds(at, PAD), :128] = high
            table[pl.ds(at, PAD), 128:] = (value - high.astype(F32)).astype(BF16)
        return carry

    def four(index, carry):
        for part in range(4):
            fill(low + index * 4 + part, carry)
        return carry

    lax.fori_loop(0, (high - low) // 4, four, 0)
    lax.fori_loop(low + (high - low) // 4 * 4, high, fill, 0)


def position():
    lat = lax.axis_index("lat")
    return lat, lat * ROWS


def row_of(first, ext):
    if isinstance(ext, int) and 2 <= ext < 18:
        return first + ext - 2
    return jnp.clip(first + ext - 2, 0, 127)


def factor_of(amps, first, ext, k, tap):
    return amps[tap, k, row_of(first, ext)]


def pack_kernel(field, cot, near_a, second_a, polar_a, second_b, polar_b, whole, sems):
    odd = lax.axis_index("lon") % 2 == 1

    def edges(is_odd):
        copies = []
        for which, source in enumerate((field, cot)):
            for out, width, right in ((near_a, OTHERS, is_odd), (second_a, SECOND, is_odd), (second_b, SECOND, not is_odd)):
                begin = COLS - width if right else 0
                copies.append((source.at[0, begin : begin + width], out.at[which]))
        copies = [pltpu.make_async_copy(a, b, sems.at[i]) for i, (a, b) in enumerate(copies)]
        for copy in copies:
            copy.start()

        @pl.when(lax.axis_index("lat") == 0)
        def _():
            loads = []
            for which, source in enumerate((field, cot)):
                for part in range(3):
                    at = pl.ds(part * 30, 30)
                    sem = sems.at[6 + which * 3 + part]
                    loads.append(pltpu.make_async_copy(source.at[0, at], whole.at[which, at], sem))
            for load in loads:
                load.start()
            for load in loads:
                load.wait()
            for which in range(2):
                low = jnp.concatenate([whole[which, :45, :8], whole[which, 45:, :8]], axis=1)
                left = jnp.concatenate([whole[which, :20, 8:], whole[which, 20:40, 8:]], axis=1)
                right = jnp.concatenate([whole[which, 50:70, 8:], whole[which, 70:, 8:]], axis=1)
                polar_a[which, :45] = low
                polar_b[which, :45] = low
                polar_a[which, 45:] = right if is_odd else left
                polar_b[which, 45:] = left if is_odd else right

        for copy in copies:
            copy.wait()

    pl.when(odd)(lambda: edges(True))
    pl.when(jnp.logical_not(odd))(lambda: edges(False))


def pre_kernel(spans, field, cot, own_f, own_c, shape0, shape1, shape2, whole, sems):
    lat, first = position()
    loads = []
    for which, source in enumerate((field, cot)):
        for part in range(3):
            at = pl.ds(part * 30, 30)
            loads.append(pltpu.make_async_copy(source.at[0, at], whole.at[which, at], sems.at[which * 3 + part]))
    for load in loads:
        load.start()
    fill_shapes(shape0, offsets_of(0), spans, first, 0, 20)

    @pl.when(lat < 2)
    def _():
        low = jnp.where(lat == 0, 2, 0)
        fill_shapes(shape1, offsets_of(1), spans, first, low, jnp.where(lat == 0, 18, 2))

    @pl.when(lat == 0)
    def _():
        fill_shapes(shape2, offsets_of(2), spans, first, 2, 5)

    for load in loads:
        load.wait()
    for which, own in enumerate((own_f, own_c)):
        own[:, COLS:, :] = jnp.zeros((ROWS, 128 - COLS, CHAN), BF16)
        own[:, :COLS, :] = jnp.swapaxes(whole[which], 0, 1)


def assemble_kernel(old_f, old_c, near_a, second_a, polar_a, second_b, polar_b, *outs):
    lat = lax.axis_index("lat")
    odd = lax.axis_index("lon") % 2 == 1
    groups = ((outs[0], outs[2], outs[4]), (outs[1], outs[3], outs[5]))
    lat_a, lat_b = outs[6], outs[7]

    def left_right(a_ref, b_ref, which, lo, hi):
        left = jnp.where(odd, b_ref[which, lo:hi], a_ref[which, lo:hi])
        right = jnp.where(odd, a_ref[which, lo:hi], b_ref[which, lo:hi])
        return jnp.swapaxes(left, 0, 1), jnp.swapaxes(right, 0, 1)

    for which in range(2):
        own0, own1, own2 = groups[which]
        own0[...] = (old_f, old_c)[which][...]

        @pl.when(lat >= 2)
        def _(which=which, own0=own0):
            a = near_a[which]
            left = jnp.where(odd, second_b[which, SECOND - OTHERS :], a)
            right = jnp.where(odd, a, second_b[which, :OTHERS])
            own0[:, 112 - OTHERS : 112, :] = jnp.swapaxes(left, 0, 1)
            own0[:, 112 : 112 + OTHERS, :] = jnp.swapaxes(right, 0, 1)

        @pl.when(lat == 1)
        def _(which=which, own0=own0, own1=own1):
            left, right = left_right(second_a, second_b, which, 0, SECOND)
            own0[:, 96:112, :] = left[:, 2:]
            own0[:, 112:128, :] = right[:, :16]
            own1[...] = jnp.zeros(own1.shape, BF16)
            own1[:, 62:64, :] = left[:, :2]
            own1[:, 64:66, :] = right[:, 16:]

        @pl.when(lat == 0)
        def _(which=which, own0=own0, own1=own1, own2=own2):
            a, b = polar_a[which], polar_b[which]
            left, right = jnp.where(odd, b, a), jnp.where(odd, a, b)

            def opened(lo, hi):
                return [jnp.swapaxes(jnp.concatenate([x[lo:hi, :8], x[lo:hi, 8:]], axis=0), 0, 1) for x in (left, right)]

            high_left, high_right = opened(45, 65)
            left, right = opened(0, 45)
            own0[:8, 96:112, :] = left[:, 74:90]
            own0[:8, 112:128, :] = right[:, 0:16]
            own1[:8, :64, :] = left[:, 10:74]
            own1[:8, 64:, :] = right[:, 16:80]
            own2[:, :16, :] = left[:5, 0:16]
            own2[:, 16:, :] = right[:5, 74:90]
            left, right = high_left, high_right
            own0[8:, 96:112, :] = left[:, 24:40]
            own0[8:, 112:128, :] = right[:, 0:16]
            own1[8:] = jnp.zeros((8, 128, CHAN), BF16)
            own1[8:, 40:64, :] = left[:, 0:24]
            own1[8:, 64:88, :] = right[:, 16:40]

        even = lat % 2 == 0
        for row in range(2):
            lat_a[which, row, :128, :] = jnp.where(even, own0[14 + row], own0[row])
            lat_a[which, row, 128:, :] = jnp.where(even, own1[14 + row, 48:80, :], own1[row, 48:80, :])
            lat_b[which, row, :128, :] = jnp.where(even, own0[row], own0[14 + row])


def tapped(amps, first, ext, rows):
    factors = [[factor_of(amps, first, ext, k, tap) for tap in range(5)] for k in range(3)]
    height = rows[0].shape[0]
    parts = [[] for _ in range(3)]
    for at in range(0, height, 32):
        wide = [row[at : at + 32].astype(F32) for row in rows]
        for k in range(3):
            total = wide[0] * factors[k][0]
            for tap in range(1, 5):
                total += wide[tap] * factors[k][tap]
            parts[k].append(total.astype(BF16))
    return [jnp.concatenate(part, axis=0) if len(part) > 1 else part[0] for part in parts]


def filtered(table, at, amps, first, ext, rows):
    out = []
    for k, taps in enumerate(tapped(amps, first, ext, rows)):
        shapes = rows_at(table, at + k * PAD, PAD)
        if taps.shape[0] < 128:
            shapes = jnp.concatenate([shapes[:, : taps.shape[0]], shapes[:, 128 : 128 + taps.shape[0]]], axis=1)
        out.append(jnp.dot(shapes, jnp.concatenate([taps, taps], axis=0), preferred_element_type=F32))
    return out


def plus(values, more):
    return [x + y for x, y in zip(values, more)]


def rows_at(ref, start, count=288):
    return ref[pl.ds(start if isinstance(start, int) else pl.multiple_of(start, 32), count), :]


def store_basis(basis, row, values):
    at = row * PAD if isinstance(row, int) else pl.multiple_of(row * PAD, PAD)
    for k in range(3):
        basis[pl.ds(at, PAD), k * 128 : (k + 1) * 128] = values[k].astype(BF16)


def times_cotangent(cot, basis):
    return lax.dot_general(cot, basis, (((0,), (0,)), ((), ())), preferred_element_type=F32)


def inner_kernel(amps, own0, own1, own2, shape0, shape1, shape2, cot, basis, part):
    lat, first = position()

    def one(row, wide, extra=None):
        at = (row + 2) * 288
        values = filtered(shape0, at, amps, first, row + 2, [own0[row - 2 + tap] for tap in range(5)])
        if wide:
            values = plus(values, filtered(shape1, at, amps, first, row + 2, [own1[row - 2 + tap] for tap in range(5)]))
        store_basis(basis, row - 2, values if extra is None else plus(values, extra))

    def loop(start, wide):
        for row in range(start, 14):
            one(row, wide)

    @pl.when(lat != 0)
    def _():
        loop(2, False)

    @pl.when(lat == 0)
    def _():
        far = filtered(shape2, 4 * 288, amps, first, 4, [own2[tap] for tap in range(5)])
        one(2, True, far)
        loop(3, True)

    part[...] = times_cotangent(cot[2:14, :PAD, :].reshape(12 * PAD, CHAN), basis[...])


def halo_row(halo_a, halo_b, which, row, even, top):
    a, b = halo_a[which, row, :128], halo_b[which, row, :128]
    return jnp.where(even, b, a) if top else jnp.where(even, a, b)


def far_halo_row(halo_a, which, row):
    zeros = jnp.zeros((48, CHAN), BF16)
    return jnp.concatenate([zeros, halo_a[which, row, 128:], zeros], axis=0)


def outer_kernel(amps, own0, own1, own2, shape0, shape1, shape2, cot, halo_a, halo_b, part, basis, mine, other, grad):
    lat, first = position()
    even = lat % 2 == 0

    def run(wide):
        for place, row in enumerate((0, 1, 14, 15)):
            near, far, last = [], [], []
            for at in range(row - 2, row + 3):
                inside = 0 <= at < ROWS
                if inside:
                    near.append(own0[at])
                else:
                    near.append(halo_row(halo_a, halo_b, 0, at + 2 if at < 0 else at - ROWS, even, at < 0))
                if wide:
                    zeros = jnp.zeros((128, CHAN), BF16)
                    far.append(own1[at] if inside else zeros if at < 0 else far_halo_row(halo_a, 0, at - ROWS))
                    last.append(own2[at] if 0 <= at < 5 else zeros[:32])
            at = (row + 2) * 288
            values = filtered(shape0, at, amps, first, row + 2, near)
            if wide:
                values = plus(values, filtered(shape1, at, amps, first, row + 2, far))
            if wide and row < 2:
                values = plus(values, filtered(shape2, at, amps, first, row + 2, last))
            store_basis(basis, place, values)

    pl.when(lat != 0)(lambda: run(False))
    pl.when(lat == 0)(lambda: run(True))
    ends = jnp.concatenate([cot[0:2, :PAD, :], cot[14:16, :PAD, :]], axis=0).reshape(4 * PAD, CHAN)
    product = part[...] + times_cotangent(ends, basis[...])
    for k in range(3):
        grad[k * 128 : (k + 1) * 128, :] = product[:, k * 128 : (k + 1) * 128].T
    core = lat % 2
    mine[...] = grad[pl.ds(pl.multiple_of(core * 192, 192), 192), :]
    other[...] = grad[pl.ds(pl.multiple_of((1 - core) * 192, 192), 192), :]


def mix_kernel(inner, outer, weight, before, out, token):
    w = weight[...]

    def mixed(basis, rows):
        return jnp.dot(basis, w, preferred_element_type=F32).astype(BF16).reshape(rows, PAD, CHAN)[:, :COLS]

    ends = mixed(outer[...], 4)
    whole = jnp.concatenate([ends[:2], mixed(inner[...], 12), ends[2:]], axis=0)
    out[0] = jnp.swapaxes(whole, 0, 1)
    token[...] = before[...]


def back_kernel(piece, amps, own0, own1, own2, shape0, shape1, shape2, halo_a, halo_b, weight, before, *refs):
    out, token, spread, joined = refs[-4:]
    lat, first = position()
    even = lat % 2 == 0
    begin = 8 * piece

    def put(index, value, fresh):
        at = index * 288 if isinstance(index, int) else pl.multiple_of(index * 288, 32)
        if fresh:
            spread[pl.ds(at, 288), :] = value
        else:
            spread[pl.ds(at, 288), :] += value

    def twice(shapes, rows):
        return jnp.dot(shapes, jnp.concatenate([rows, rows], axis=0), preferred_element_type=F32)

    def own_rows(low, high, wide):
        for ext in range(low, high):
            value = twice(rows_at(shape0, ext * 288), own0[ext - 2])
            if wide:
                value += twice(rows_at(shape1, ext * 288), own1[ext - 2])
            put(ext - begin, value, True)

    low, high = max(begin, 2), min(begin + 12, 18)
    pl.when(lat != 0)(lambda: own_rows(low, high, False))
    pl.when(lat == 0)(lambda: own_rows(low, high, True))
    for row in range(2):
        ext = row if piece == 0 else 18 + row
        gathered = halo_row(halo_a, halo_b, 1, row, even, piece == 0)
        put(ext - begin, twice(shape0[ext * 288 : (ext + 1) * 288, :], gathered), True)
    if piece == 0:

        @pl.when(lat == 1)
        def _():
            for row in range(2):
                far = far_halo_row(halo_a, 1, row)
                put(row, twice(shape1[row * 288 : (row + 1) * 288, :], far), False)

        @pl.when(lat == 0)
        def _():
            for ext in range(2, 5):
                at = slice(ext * 288, (ext + 1) * 288)
                shapes = jnp.concatenate([shape2[at, :32], shape2[at, 128:160]], axis=1)
                put(ext, twice(shapes, own2[ext - 2]), False)

    if piece:
        out[...] = refs[0][...]
    for row in range(8):
        for k in range(3):
            total = None
            for slot in range(5):
                factor = factor_of(amps, first, begin + row + slot, k, 4 - slot) * (-1.0 if k == 1 else 1.0)
                at = (row + slot) * 288 + k * PAD
                term = spread[at : at + PAD, :] * factor
                total = term if total is None else total + term
            joined[row * PAD : (row + 1) * PAD, k * 128 : (k + 1) * 128] = total.astype(BF16)
    weights = jnp.concatenate([weight[k] for k in range(3)], axis=1)
    mixed = lax.dot_general(joined[...], weights, (((1,), (1,)), ((), ())), preferred_element_type=F32)
    out[0, :, begin : begin + 8, :] = jnp.swapaxes(mixed.reshape(8, PAD, CHAN)[:, :COLS], 0, 1)
    token[...] = before[...]


def sum_kernel(count, *refs):
    parts = [ref[...] for ref in refs[:count]]
    while len(parts) > 1:
        parts = [parts[i] + parts[i + 1] for i in range(0, len(parts), 2)]
    out, *token = refs[-2:] if refs[-1].shape[0] == 8 else refs[-1:]
    out[...] = parts[0]
    if token:
        token[0][...] = jnp.zeros((8, 128), F32)


def pairs_of_lon(parity, lats):
    out = []
    for lat in lats:
        for lon in range(8):
            other = lon ^ 1 if parity == 0 else ((lon + 1) % 8 if lon % 2 else (lon - 1) % 8)
            out.append((lat * 8 + lon, lat * 8 + other))
    return out


def pairs_of_lat(parity):
    out = []
    for lat in range(8):
        other = lat ^ 1 if parity == 0 else (lat + 1 if lat % 2 else lat - 1)
        if 0 <= other < 8:
            out.append((lat, other))
    return out


def z_pairs():
    across = {0: 6, 6: 0, 1: 7, 7: 1, 2: 4, 4: 2, 3: 5, 5: 3}
    out = []
    for lat in range(8):
        for lon in range(8):
            other = across[(lon >> 2) * 4 + (lat >> 1)]
            out.append((lat * 8 + lon, ((other % 4) * 2 + lat % 2) * 8 + (other // 4) * 4 + lon % 4))
    return out


def flip(x, axis, bit):
    return lax.ppermute(x, axis, [(i, i ^ bit) for i in range(lax.axis_size(axis))])


VMEM = pl.BlockSpec(memory_space=pltpu.VMEM)
SMEM = pl.BlockSpec(memory_space=pltpu.SMEM)


def call(kernel, outs, scratch, flops, scalars, arrays, limit=12, space=pltpu.VMEM):
    moved = sum(math.prod(x.shape) * x.dtype.itemsize for x in (*arrays, *outs))
    return pl.pallas_call(
        kernel,
        out_shape=outs,
        in_specs=[SMEM] * len(scalars) + [pl.BlockSpec(memory_space=space)] * len(arrays),
        out_specs=[VMEM] * len(outs),
        scratch_shapes=scratch,
        compiler_params=pltpu.CompilerParams(vmem_limit_bytes=limit * 1024 * 1024),
        cost_estimate=pl.CostEstimate(flops=flops, bytes_accessed=moved, transcendentals=0),
    )(*scalars, *arrays)


def shape(dims, dtype=BF16):
    return jax.ShapeDtypeStruct(dims, dtype)


def body(features, cotangent, mix_weight, amplitude, row_spans):
    amps = amplitude.transpose(2, 0, 1)

    field, cot = features.transpose(0, 2, 1, 3), cotangent.transpose(0, 2, 1, 3)
    field, cot = (pltpu.with_memory_space_constraint(x, pltpu.HBM) for x in (field, cot))
    token = shape((8, 128), F32)
    near = shape((2, OTHERS, ROWS, CHAN))
    second = shape((2, SECOND, ROWS, CHAN))
    polar = shape((2, 65, ROWS, CHAN))
    scratch = [
        pltpu.VMEM((2, COLS, ROWS, CHAN), BF16),
        pltpu.SemaphoreType.DMA((12,)),
    ]
    messages = call(
        pack_kernel,
        [near, second, polar, second, polar],
        scratch,
        0,
        (),
        (field, cot),
        space=pltpu.HBM,
    )
    targets = ((1, range(2, 8)), (1, (1,)), (1, (0,)), (0, range(1, 8)), (0, (0,)))
    got = [None] * 5
    for index in (2, 1, 0, 4, 3):
        got[index] = lax.ppermute(messages[index], LL, pairs_of_lon(*targets[index]))

    gathered = shape((ROWS, 128, CHAN))
    tables = [shape((20 * 288, 256)), shape((20 * 288, 256)), shape((5 * 288, 256))]
    own_f, own_c, *shapes = call(
        pre_kernel,
        [gathered, gathered, *tables],
        [pltpu.VMEM((2, COLS, ROWS, CHAN), BF16), pltpu.SemaphoreType.DMA((6,))],
        2 * 10**8,
        (row_spans,),
        (field, cot),
        space=pltpu.HBM,
    )
    own2 = shape((5, 32, CHAN))
    own0_f, own0_c, own1_f, own1_c, own2_f, own2_c, lat_a, lat_b = call(
        assemble_kernel,
        [gathered] * 4 + [own2] * 2 + [shape((2, 2, 160, CHAN)), shape((2, 2, 176, CHAN))],
        [],
        0,
        (),
        (own_f, own_c, *got),
    )
    halo_a = lax.ppermute(lat_a, "lat", pairs_of_lat(0))
    halo_b = lax.ppermute(lat_b, "lat", pairs_of_lat(1))

    row_flops = 2 * 288 * 640 * CHAN
    scalars = (amps,)
    filters = (own0_f, own1_f, own2_f, *shapes, own0_c)
    inner, part = call(inner_kernel, [shape((12 * PAD, 384)), shape((128, 384), F32)], [], 12 * row_flops, scalars, filters)
    half = shape((192, CHAN), F32)
    outer, mine, other = call(
        outer_kernel,
        [shape((4 * PAD, 384)), half, half],
        [pltpu.VMEM((384, CHAN), F32)],
        4 * row_flops,
        scalars,
        (*filters, halo_a, halo_b, part),
    )

    def add(*parts, after=(), more=True):
        outs = [half, token] if more else [half]
        return call(functools.partial(sum_kernel, len(parts)), outs, [], 0, (), (*parts, *after))

    def back(piece, before, *done):
        return call(
            functools.partial(back_kernel, piece),
            [shape((1, COLS, ROWS, CHAN), F32), token],
            [pltpu.VMEM((12 * 288, CHAN), F32), pltpu.VMEM((8 * PAD, 384), BF16)],
            2 * row_flops,
            scalars,
            (own0_c, own1_c, own2_c, *shapes, halo_a, halo_b, mix_weight, before, *done),
        )

    mine, before = add(mine, flip(other, "lat", 1))
    steps = [flip(mine, "dp", bit) for bit in (1, 2, 3)]
    convolved, done = call(
        mix_kernel,
        [shape((1, COLS, ROWS, CHAN)), token],
        [],
        2 * ROWS * PAD * 384 * CHAN,
        (),
        (inner, outer, mix_weight.reshape(384, CHAN), before),
    )
    (mine,) = add(mine, *steps, after=(done,), more=False)
    steps = [flip(mine, "lon", bit) for bit in (1, 2, 3)]
    mine, before = add(mine, *steps)
    steps = [flip(mine, "lat", bit) for bit in (2, 4, 6)]
    grad, done = back(0, before)
    mine, before = add(mine, *steps, after=(done,))
    step = lax.ppermute(mine, LL, z_pairs())
    grad, done = back(1, before, grad)
    (mine,) = add(mine, step, after=(done,), more=False)
    other = flip(mine, "lat", 1)
    first_half = lax.axis_index("lat") % 2 == 0
    whole = jnp.concatenate([jnp.where(first_half, mine, other), jnp.where(first_half, other, mine)])
    whole = whole * (1.0 / math.sqrt(4 * 128 * 720))
    return convolved.transpose(0, 2, 1, 3), grad.transpose(0, 2, 1, 3), whole.reshape(3, 128, 128)


def solution(mesh):
    cells = P("dp", "lat", "lon", None)
    return jax.shard_map(
        body,
        mesh=mesh,
        in_specs=(cells, cells, P(), P(), P()),
        out_specs=(cells, cells, P()),
        check_vma=False,
    )
```

time: 81 us -> 75.5 us (0.932)
  Pallas kernels: 23.5 us -> 15.3 us
  starting transfers between devices: 37.9 us -> 45.3 us
  local copies, waits for them, and re-layouts: 3.99 us -> 0.66 us
  waiting for transfers between devices: 13.7 us -> 12.5 us
    pallas_call x15 -> x13, Pallas kernels: 23.5 us -> 15.3 us  [call(): pl.pallas_call(kernel, out_shape=outs, in_specs=[SMEM] * len(scalars) + [...]
    ppermute x1, starting transfers between devices: 2.59 us -> 7.26 us  [body(): step = lax.ppermute(mine, LL, z_pairs())]
    unnamed x16 -> x6, local copies, waits for them, and re-layouts: 3.99 us -> 0.66 us
    ppermute x1, waiting for transfers between devices: 3.09 us -> 0.01 us  [body(): step = lax.ppermute(mine, LL, z_pairs())]
    ppermute x10 -> x11, starting transfers between devices: 13.8 us -> 16.3 us  [flip(): lax.ppermute(x, axis, [(i, i ^ bit) for i in range(lax.axis_size(axis))])]
    ppermute x5, waiting for transfers between devices: 0.01 us -> 1.32 us  [body(): lax.ppermute(messages[index], LL, pairs_of_lon(*targets[index]))]
    ppermute x10 -> x11, waiting for transfers between devices: 10.3 us -> 11.2 us  [flip(): lax.ppermute(x, axis, [(i, i ^ bit) for i in range(lax.axis_size(axis))])]
    ppermute x1, starting transfers between devices: 1.91 us -> 2.72 us  [body(): halo_b = lax.ppermute(lat_b, 'lat', pairs_of_lat(1))]
  transfers between devices with their start and end apart: 18 -> 19, of which waited for: 8 -> 9; matrix products, arithmetic and copies ran while one was open for 0% -> 0% of each run, Pallas kernels for 18% -> 16%
where the time goes in v3:
time: 75.5 us; the launch traced here: 75.3 us
  starting transfers between devices  45.3 us (60%)
  Pallas kernels  15.3 us (20%)
  waiting for transfers between devices  12.5 us (17%)
  between operations  0.82 us (1%)
    ppermute x11, starting transfers between devices, flip(): lax.ppermute(x, axis, [(i, i ^ bit) for i in range(lax.axis_size(axis))])  16.3 us
    ppermute x5, starting transfers between devices, body(): lax.ppermute(messages[index], LL, pairs_of_lon(*targets[index]))  15.8 us
    pallas_call x13, Pallas kernels, call(): pl.pallas_call(kernel, out_shape=outs, in_specs=[SMEM] * len(scalars) + [...  15.3 us
    ppermute x11, waiting for transfers between devices, flip(): lax.ppermute(x, axis, [(i, i ^ bit) for i in range(lax.axis_size(axis))])  11.2 us
    ppermute x1, starting transfers between devices, body(): step = lax.ppermute(mine, LL, z_pairs())  7.26 us
    ppermute x1, starting transfers between devices, body(): halo_a = lax.ppermute(lat_a, 'lat', pairs_of_lat(0))  3.19 us
    ppermute x1, starting transfers between devices, body(): halo_b = lax.ppermute(lat_b, 'lat', pairs_of_lat(1))  2.72 us
  transfers between devices with their start and end apart: 19, of which 9 were waited for; matrix products, arithmetic and copies ran while one was open for 0% of the time, Pallas kernels for 16%

profile of v3, /device:TPU:1, one launch (start us, length us, event | category | flops | bytes accessed | tf_op | source)
XLA Modules:
  0.0 75.3 jit_solution(8174421714075243828)
XLA Ops:
  0.6 0.0 copy-start.1
  0.6 1.2 %shard_map.77 = (bf16[2,9,16,128]{3,2,1,0:T(8,128)(2,1)S(1)}, bf16[2,18,16,128]{3,2,1,0:T(8,128)(2,1)S(1)}, bf16[2,65,16,128]{3,2,1,0:T(8,128)(2,1)S(1)}, bf16[2...) custom-call(bf16[1,90,16,128]{3,2,1,0:T(8,128)(2,1)} %bitcast.12, bf16[1,90,16,128]{3,2,1,0:T(8,128)(2,1)} %bitcast.14), custom_call_target="tpu_custom_call" | custom-call | bytes 2170880 | tf_op jit(solution)/shard_map/pallas_call | solution.py:451
  1.8 0.7 collective-permute-start.2
  2.5 0.7 collective-permute-start.4
  3.2 11.8 %collective-permute-start.1 = (bf16[2,18,16,128]{3,2,1,0:T(8,128)(2,1)S(1)}, bf16[2,18,16,128]{3,2,1,0:T(8,128)(2,1)S(1)}, u32[]{:S(2)}, u32[]{:S(2)}) collective-permute-start(bf16[2,18,16,128]{3,2,1,0:T(8,128)(2,1)S(1)} %get-tuple-element.41), channel_id=1, source_target_pairs={{32,60},{36,40},{40,36},{44,48},{48,44},{52,56},{56,52},{60,32},{3... | collective-permute-start | bytes 442376 | tf_op jit(solution)/shard_map/ppermute | solution.py:491
  15.1 1.9 %collective-permute-start.3 = (bf16[2,18,16,128]{3,2,1,0:T(8,128)(2,1)S(1)}, bf16[2,18,16,128]{3,2,1,0:T(8,128)(2,1)S(1)}, u32[]{:S(2)}, u32[]{:S(2)}) collective-permute-start(bf16[2,18,16,128]{3,2,1,0:T(8,128)(2,1)S(1)} %get-tuple-element.43), channel_id=1, source_target_pairs={{32,36},{36,32},{40,44},{44,40},{48,52},{52,48},{56,60},{60,56},{6... | collective-permute-start | bytes 442376 | tf_op jit(solution)/shard_map/ppermute | solution.py:491
  17.0 0.7 collective-permute-start
  17.7 0.0 copy-start.2
  17.7 0.6 copy-done.2
  18.3 2.8 %shard_map.76 = (bf16[16,128,128]{2,1,0:T(8,128)(2,1)S(1)}, bf16[16,128,128]{2,1,0:T(8,128)(2,1)S(1)}, bf16[5760,256]{1,0:T(8,128)(2,1)S(1)}, bf16[5760,256]{1,0:T(8,128)(2,1)S(1)}, bf16[1440,256]{1,0:T(8,128)(2,1)S(1)}) custom-call(s32[128]{0:T(128)S(1)} %copy-done.2, bf16[1,90,16,128]{3,2,1,0:T(8,128)(2,1)} %bitcast.13, bf16[1,90,16,128]{3,2,1,0:T(8,128)(2,1)} %bitcast.15), custom_call_target="tpu_custom_call" | custom-call | flops 200000000 | bytes 8421376 | tf_op jit(solution)/shard_map/pallas_call | solution.py:451
  21.1 0.0 collective-permute-done.near_a
  21.1 0.0 collective-permute-done.1.second_a
  21.1 1.3 %collective-permute-done.3.second_b = bf16[2,18,16,128]{3,2,1,0:T(8,128)(2,1)S(1)} collective-permute-done((bf16[2,18,16,128]{3,2,1,0:T(8,128)(2,1)S(1)}, bf16[2,18,16,128]{3,2,1,0:T(8,128)(2,1)S(1)}, u32[]{:S(2)}, u32[]{:S(2)}) %collective-permute-start.3) | collective-permute-done | bytes 147488 | tf_op jit(solution)/shard_map/ppermute | solution.py:491
  22.4 0.0 collective-permute-done.2.polar_a
  22.4 0.0 collective-permute-done.4.polar_b
  22.4 0.4 shard_map.78
  22.9 2.7 %collective-permute-start.6 = (bf16[2,2,176,128]{3,2,1,0:T(8,128)(2,1)S(1)}, bf16[2,2,176,128]{3,2,1,0:T(8,128)(2,1)S(1)}, u32[]{:S(2)}, u32[]{:S(2)}) collective-permute-start(bf16[2,2,176,128]{3,2,1,0:T(8,128)(2,1)S(1)} %get-tuple-element.54), channel_id=1, source_target_pairs={{32,64},{64,32},{96,128},{128,96},{160,192},{192,160},{33,65},{65,... | collective-permute-start | bytes 540680 | tf_op jit(solution)/shard_map/ppermute | solution.py:514
  25.6 3.2 %collective-permute-start.5 = (bf16[2,2,160,128]{3,2,1,0:T(8,128)(2,1)S(1)}, bf16[2,2,160,128]{3,2,1,0:T(8,128)(2,1)S(1)}, u32[]{:S(2)}, u32[]{:S(2)}) collective-permute-start(bf16[2,2,160,128]{3,2,1,0:T(8,128)(2,1)S(1)} %get-tuple-element.53), channel_id=1, source_target_pairs={{0,32},{32,0},{64,96},{96,64},{128,160},{160,128},{192,224},{224,1... | collective-permute-start | bytes 491528 | tf_op jit(solution)/shard_map/ppermute | solution.py:513
  28.8 0.0 copy-done.1
  28.8 2.5 %shard_map.79 = (bf16[1152,384]{1,0:T(8,128)(2,1)S(1)}, f32[128,384]{1,0:T(8,128)S(1)}) custom-call(f32[5,3,128]{2,1,0:T(4,128)S(1)} %bitcast.8, bf16[16,128,128]{2,1,0:T(8,128)(2,1)S(1)} %get-tuple-element.45.own0, bf16[16,128,128]{2,1,0:T(8,128)(2,1)S(1)} %get-tuple-element.46.own1, bf16[5,32,128]{2,1,0:T(8,128)(2,1)S(1)} %get-tuple-element.47.own2, ...), custom_call_target="tpu_custom_call" | custom-call | flops 566231040 | bytes 9330688 | tf_op jit(solution)/shard_map/pallas_call | solution.py:451
  31.3 0.0 collective-permute-done.5.halo_a
  31.4 0.0 collective-permute-done.6.halo_b
  31.4 0.0 copy-start
  31.4 1.7 %shard_map.80 = (bf16[384,384]{1,0:T(8,128)(2,1)S(1)}, f32[192,128]{1,0:T(8,128)S(1)}, f32[192,128]{1,0:T(8,128)S(1)}) custom-call(f32[5,3,128]{2,1,0:T(4,128)S(1)} %bitcast.9, bf16[16,128,128]{2,1,0:T(8,128)(2,1)S(1)} %get-tuple-element.45.own0, bf16[16,128,128]{2,1,0:T(8,128)(2,1)S(1)} %get-tuple-element.46.own1, ...), custom_call_target="tpu_custom_call" | custom-call | flops 188743680 | bytes 9281536 | tf_op jit(solution)/shard_map/pallas_call | solution.py:451
  33.1 1.9 %collective-permute-start.7 = (f32[192,128]{1,0:T(8,128)S(1)}, f32[192,128]{1,0:T(8,128)S(1)}, u32[]{:S(2)}, u32[]{:S(2)}) collective-permute-start(f32[192,128]{1,0:T(8,128)S(1)} %get-tuple-element.58), channel_id=1, source_target_pairs={{0,32},{32,0},{64,96},{96,64},{128,160},{160,128},{192,224},{224,1... | collective-permute-start | bytes 294920 | tf_op jit(solution)/shard_map/ppermute | solution.py:442
  35.0 0.9 %collective-permute-done.7.refs_1_ = f32[192,128]{1,0:T(8,128)S(1)} collective-permute-done((f32[192,128]{1,0:T(8,128)S(1)}, f32[192,128]{1,0:T(8,128)S(1)}, u32[]{:S(2)}, u32[]{:S(2)}) %collective-permute-start.7) | collective-permute-done | bytes 98336 | tf_op jit(solution)/shard_map/ppermute | solution.py:442
  36.0 2.8 %collective-permute-start.10 = (f32[192,128]{1,0:T(8,128)S(1)}, f32[192,128]{1,0:T(8,128)S(1)}, u32[]{:S(2)}, u32[]{:S(2)}) collective-permute-start(f32[192,128]{1,0:T(8,128)S(1)} %get-tuple-element.63.refs_0_), channel_id=1, source_target_pairs={{0,3},{1,2},{2,1},{3,0},{4,7},{5,6},{6,5},{7,4},{8,11},{9,10},{10,... | collective-permute-start | bytes 294920 | tf_op jit(solution)/shard_map/ppermute | solution.py:442
  38.8 0.0 collective-permute-start.8
  38.8 1.3 %collective-permute-start.9 = (f32[192,128]{1,0:T(8,128)S(1)}, f32[192,128]{1,0:T(8,128)S(1)}, u32[]{:S(2)}, u32[]{:S(2)}) collective-permute-start(f32[192,128]{1,0:T(8,128)S(1)} %get-tuple-element.63.refs_0_), channel_id=1, source_target_pairs={{0,2},{1,3},{2,0},{3,1},{4,6},{5,7},{6,4},{7,5},{8,10},{9,11},{10,... | collective-permute-start | bytes 294920 | tf_op jit(solution)/shard_map/ppermute | solution.py:442
  40.1 0.0 copy-done
  40.1 1.3 %shard_map.82 = (bf16[1,90,16,128]{3,2,1,0:T(8,128)(2,1)}, f32[8,128]{1,0:T(8,128)S(1)}) custom-call(bf16[1152,384]{1,0:T(8,128)(2,1)S(1)} %get-tuple-element.52.inner, bf16[384,384]{1,0:T(8,128)(2,1)S(1)} %get-tuple-element.56.outer, bf16[384,128]{1,0:T(8,128)(2,1)S(1)} %bitcast.7, f32[8,128]{1,0:T(8,128)S(1)} %get-tuple-element.59.before), custom_call_target="tpu_custom_call" | custom-call | flops 150994944 | bytes 1654784 | tf_op jit(solution)/shard_map/pallas_call | solution.py:451
  41.3 0.1 collective-permute-done.10.refs_3_
  41.4 0.8 %collective-permute-done.8.refs_1_ = f32[192,128]{1,0:T(8,128)S(1)} collective-permute-done((f32[192,128]{1,0:T(8,128)S(1)}, f32[192,128]{1,0:T(8,128)S(1)}, u32[]{:S(2)}, u32[]{:S(2)}) %collective-permute-start.8) | collective-permute-done | bytes 98336 | tf_op jit(solution)/shard_map/ppermute | solution.py:442
  42.2 2.4 %collective-permute-done.9.refs_2_ = f32[192,128]{1,0:T(8,128)S(1)} collective-permute-done((f32[192,128]{1,0:T(8,128)S(1)}, f32[192,128]{1,0:T(8,128)S(1)}, u32[]{:S(2)}, u32[]{:S(2)}) %collective-permute-start.9) | collective-permute-done | bytes 98336 | tf_op jit(solution)/shard_map/ppermute | solution.py:442
  44.7 0.1 collective-permute-start.11
  44.8 1.4 %collective-permute-start.12 = (f32[192,128]{1,0:T(8,128)S(1)}, f32[192,128]{1,0:T(8,128)S(1)}, u32[]{:S(2)}, u32[]{:S(2)}) collective-permute-start(f32[192,128]{1,0:T(8,128)S(1)} %shard_map.83.refs_0_), channel_id=1, source_target_pairs={{0,8},{4,12},{8,0},{12,4},{16,24},{20,28},{24,16},{28,20},{1,9},{5... | collective-permute-start | bytes 294920 | tf_op jit(solution)/shard_map/ppermute | solution.py:442
  46.2 2.5 %collective-permute-start.13 = (f32[192,128]{1,0:T(8,128)S(1)}, f32[192,128]{1,0:T(8,128)S(1)}, u32[]{:S(2)}, u32[]{:S(2)}) collective-permute-start(f32[192,128]{1,0:T(8,128)S(1)} %shard_map.83.refs_0_), channel_id=1, source_target_pairs={{0,12},{4,8},{8,4},{12,0},{16,28},{20,24},{24,20},{28,16},{1,13},{... | collective-permute-start | bytes 294920 | tf_op jit(solution)/shard_map/ppermute | solution.py:442
  48.6 0.0 collective-permute-done.11.refs_1_
  48.6 2.2 %collective-permute-done.12.refs_2_ = f32[192,128]{1,0:T(8,128)S(1)} collective-permute-done((f32[192,128]{1,0:T(8,128)S(1)}, f32[192,128]{1,0:T(8,128)S(1)}, u32[]{:S(2)}, u32[]{:S(2)}) %collective-permute-start.12) | collective-permute-done | bytes 98336 | tf_op jit(solution)/shard_map/ppermute | solution.py:442
  50.9 2.2 %collective-permute-done.13.refs_3_ = f32[192,128]{1,0:T(8,128)S(1)} collective-permute-done((f32[192,128]{1,0:T(8,128)S(1)}, f32[192,128]{1,0:T(8,128)S(1)}, u32[]{:S(2)}, u32[]{:S(2)}) %collective-permute-start.13) | collective-permute-done | bytes 98336 | tf_op jit(solution)/shard_map/ppermute | solution.py:442
  53.1 0.2 collective-permute-start.14
  53.3 1.1 %collective-permute-start.15 = (f32[192,128]{1,0:T(8,128)S(1)}, f32[192,128]{1,0:T(8,128)S(1)}, u32[]{:S(2)}, u32[]{:S(2)}) collective-permute-start(f32[192,128]{1,0:T(8,128)S(1)} %get-tuple-element.65.refs_0_), channel_id=1, source_target_pairs={{0,128},{32,160},{64,192},{96,224},{128,0},{160,32},{192,64},{224,... | collective-permute-start | bytes 294920 | tf_op jit(solution)/shard_map/ppermute | solution.py:442
  54.4 2.3 %collective-permute-start.16 = (f32[192,128]{1,0:T(8,128)S(1)}, f32[192,128]{1,0:T(8,128)S(1)}, u32[]{:S(2)}, u32[]{:S(2)}) collective-permute-start(f32[192,128]{1,0:T(8,128)S(1)} %get-tuple-element.65.refs_0_), channel_id=1, source_target_pairs={{0,192},{32,224},{64,128},{96,160},{128,64},{160,96},{192,0},{224,... | collective-permute-start | bytes 294920 | tf_op jit(solution)/shard_map/ppermute | solution.py:442
  56.7 2.4 %shard_map.85 = (f32[1,90,16,128]{3,2,1,0:T(8,128)S(1)}, f32[8,128]{1,0:T(8,128)S(1)}) custom-call(f32[5,3,128]{2,1,0:T(4,128)S(1)} %bitcast.10, bf16[16,128,128]{2,1,0:T(8,128)(2,1)S(1)} %get-tuple-element.51.cot.own0, bf16[16,128,128]{2,1,0:T(8,128)(2,1)S(1)} %get-tuple-element.61.own1, bf16[5,32,128]{2,1,0:T(8,128)(2,1)S(1)} %get-tuple-element.62.own2, ...), custom_call_target="tpu_custom_call" | custom-call | flops 94371840 | bytes 8912896 | tf_op jit(solution)/shard_map/pallas_call | solution.py:451
  59.1 0.0 collective-permute-done.14.refs_1_
  59.1 0.0 collective-permute-done.15.refs_2_
  59.1 1.6 %collective-permute-done.16.refs_3_ = f32[192,128]{1,0:T(8,128)S(1)} collective-permute-done((f32[192,128]{1,0:T(8,128)S(1)}, f32[192,128]{1,0:T(8,128)S(1)}, u32[]{:S(2)}, u32[]{:S(2)}) %collective-permute-start.16) | collective-permute-done | bytes 98336 | tf_op jit(solution)/shard_map/ppermute | solution.py:442
  60.7 7.3 %collective-permute-start.17 = (f32[192,128]{1,0:T(8,128)S(1)}, f32[192,128]{1,0:T(8,128)S(1)}, u32[]{:S(2)}, u32[]{:S(2)}) collective-permute-start(f32[192,128]{1,0:T(8,128)S(1)} %get-tuple-element.71.refs_0_), channel_id=1, source_target_pairs={{0,144},{4,148},{8,152},{12,156},{16,128},{20,132},{24,136},{28,14... | collective-permute-start | bytes 294920 | tf_op jit(solution)/shard_map/ppermute | solution.py:560
  68.0 2.9 %shard_map.87 = (f32[1,90,16,128]{3,2,1,0:T(8,128)}, f32[8,128]{1,0:T(8,128)S(1)}) custom-call(f32[5,3,128]{2,1,0:T(4,128)S(1)} %bitcast.11, bf16[16,128,128]{2,1,0:T(8,128)(2,1)S(1)} %get-tuple-element.51.cot.own0, bf16[16,128,128]{2,1,0:T(8,128)(2,1)S(1)} %get-tuple-element.61.own1, bf16[5,32,128]{2,1,0:T(8,128)(2,1)S(1)} %get-tuple-element.62.own2, ...), custom_call_target="tpu_custom_call" | custom-call | flops 94371840 | bytes 9650176 | tf_op jit(solution)/shard_map/pallas_call | solution.py:451
  70.9 0.0 collective-permute-done.17.refs_1_
  71.0 2.7 %collective-permute-start.18 = (f32[192,128]{1,0:T(8,128)S(1)}, f32[192,128]{1,0:T(8,128)S(1)}, u32[]{:S(2)}, u32[]{:S(2)}) collective-permute-start(f32[192,128]{1,0:T(8,128)S(1)} %shard_map.88), channel_id=1, source_target_pairs={{0,32},{32,0},{64,96},{96,64},{128,160},{160,128},{192,224},{224,1... | collective-permute-start | bytes 294920 | tf_op jit(solution)/shard_map/ppermute | solution.py:442
  73.6 0.9 %collective-permute-done.18 = f32[192,128]{1,0:T(8,128)S(1)} collective-permute-done((f32[192,128]{1,0:T(8,128)S(1)}, f32[192,128]{1,0:T(8,128)S(1)}, u32[]{:S(2)}, u32[]{:S(2)}) %collective-permute-start.18) | collective-permute-done | bytes 98336 | tf_op jit(solution)/shard_map/ppermute | solution.py:442
  74.6 0.7 maximum_multiply_fusion
  (6 shorter events, 0.1 us)
Async XLA Ops:
  0.6 28.2 %copy-start.1 = (f32[3,128,5]{1,0,2:T(4,128)S(1)}, f32[3,128,5]{1,0,2:T(4,128)}, u32[]{:S(2)}) copy-start(f32[3,128,5]{1,0,2:T(4,128)} %param.8) | copy-start | bytes 23044
  1.8 20.6 %collective-permute-start.2 = (bf16[2,65,16,128]{3,2,1,0:T(8,128)(2,1)S(1)}, bf16[2,65,16,128]{3,2,1,0:T(8,128)(2,1)S(1)}, u32[]{:S(2)}, u32[]{:S(2)}) collective-permute-start(bf16[2,65,16,128]{3,2,1,0:T(8,128)(2,1)S(1)} %get-tuple-element.42), channel_id=1, source_target_pairs={{0,28},{4,8},{8,4},{12,16},{16,12},{20,24},{24,20},{28,0},{1,29},{... | collective-permute-start | bytes 1597448 | tf_op jit(solution)/shard_map/ppermute | solution.py:491
  2.5 19.9 %collective-permute-start.4 = (bf16[2,65,16,128]{3,2,1,0:T(8,128)(2,1)S(1)}, bf16[2,65,16,128]{3,2,1,0:T(8,128)(2,1)S(1)}, u32[]{:S(2)}, u32[]{:S(2)}) collective-permute-start(bf16[2,65,16,128]{3,2,1,0:T(8,128)(2,1)S(1)} %get-tuple-element.44), channel_id=1, source_target_pairs={{0,4},{4,0},{8,12},{12,8},{16,20},{20,16},{24,28},{28,24},{1,5},{5... | collective-permute-start | bytes 1597448 | tf_op jit(solution)/shard_map/ppermute | solution.py:491
  3.2 17.9 %collective-permute-start.1 = (bf16[2,18,16,128]{3,2,1,0:T(8,128)(2,1)S(1)}, bf16[2,18,16,128]{3,2,1,0:T(8,128)(2,1)S(1)}, u32[]{:S(2)}, u32[]{:S(2)}) collective-permute-start(bf16[2,18,16,128]{3,2,1,0:T(8,128)(2,1)S(1)} %get-tuple-element.41), channel_id=1, source_target_pairs={{32,60},{36,40},{40,36},{44,48},{48,44},{52,56},{56,52},{60,32},{3... | collective-permute-start | bytes 442376 | tf_op jit(solution)/shard_map/ppermute | solution.py:491
  15.1 7.4 %collective-permute-start.3 = (bf16[2,18,16,128]{3,2,1,0:T(8,128)(2,1)S(1)}, bf16[2,18,16,128]{3,2,1,0:T(8,128)(2,1)S(1)}, u32[]{:S(2)}, u32[]{:S(2)}) collective-permute-start(bf16[2,18,16,128]{3,2,1,0:T(8,128)(2,1)S(1)} %get-tuple-element.43), channel_id=1, source_target_pairs={{32,36},{36,32},{40,44},{44,40},{48,52},{52,48},{56,60},{60,56},{6... | collective-permute-start | bytes 442376 | tf_op jit(solution)/shard_map/ppermute | solution.py:491
  17.0 4.1 %collective-permute-start = (bf16[2,9,16,128]{3,2,1,0:T(8,128)(2,1)S(1)}, bf16[2,9,16,128]{3,2,1,0:T(8,128)(2,1)S(1)}, u32[]{:S(2)}, u32[]{:S(2)}) collective-permute-start(bf16[2,9,16,128]{3,2,1,0:T(8,128)(2,1)S(1)} %get-tuple-element.40), channel_id=1, source_target_pairs={{64,92},{68,72},{72,68},{76,80},{80,76},{84,88},{88,84},{92,64},{9... | collective-permute-start | bytes 221192 | tf_op jit(solution)/shard_map/ppermute | solution.py:491
  17.7 0.7 copy-start.2
  22.9 8.5 %collective-permute-start.6 = (bf16[2,2,176,128]{3,2,1,0:T(8,128)(2,1)S(1)}, bf16[2,2,176,128]{3,2,1,0:T(8,128)(2,1)S(1)}, u32[]{:S(2)}, u32[]{:S(2)}) collective-permute-start(bf16[2,2,176,128]{3,2,1,0:T(8,128)(2,1)S(1)} %get-tuple-element.54), channel_id=1, source_target_pairs={{32,64},{64,32},{96,128},{128,96},{160,192},{192,160},{33,65},{65,... | collective-permute-start | bytes 540680 | tf_op jit(solution)/shard_map/ppermute | solution.py:514
  25.6 5.7 %collective-permute-start.5 = (bf16[2,2,160,128]{3,2,1,0:T(8,128)(2,1)S(1)}, bf16[2,2,160,128]{3,2,1,0:T(8,128)(2,1)S(1)}, u32[]{:S(2)}, u32[]{:S(2)}) collective-permute-start(bf16[2,2,160,128]{3,2,1,0:T(8,128)(2,1)S(1)} %get-tuple-element.53), channel_id=1, source_target_pairs={{0,32},{32,0},{64,96},{96,64},{128,160},{160,128},{192,224},{224,1... | collective-permute-start | bytes 491528 | tf_op jit(solution)/shard_map/ppermute | solution.py:513
  31.4 8.7 %copy-start = (bf16[3,128,128]{2,1,0:T(8,128)(2,1)S(1)}, bf16[3,128,128]{2,1,0:T(8,128)(2,1)}, u32[]{:S(2)}) copy-start(bf16[3,128,128]{2,1,0:T(8,128)(2,1)} %weight.3) | copy-start | bytes 294916
  33.1 2.9 %collective-permute-start.7 = (f32[192,128]{1,0:T(8,128)S(1)}, f32[192,128]{1,0:T(8,128)S(1)}, u32[]{:S(2)}, u32[]{:S(2)}) collective-permute-start(f32[192,128]{1,0:T(8,128)S(1)} %get-tuple-element.58), channel_id=1, source_target_pairs={{0,32},{32,0},{64,96},{96,64},{128,160},{160,128},{192,224},{224,1... | collective-permute-start | bytes 294920 | tf_op jit(solution)/shard_map/ppermute | solution.py:442
  36.0 5.5 %collective-permute-start.10 = (f32[192,128]{1,0:T(8,128)S(1)}, f32[192,128]{1,0:T(8,128)S(1)}, u32[]{:S(2)}, u32[]{:S(2)}) collective-permute-start(f32[192,128]{1,0:T(8,128)S(1)} %get-tuple-element.63.refs_0_), channel_id=1, source_target_pairs={{0,3},{1,2},{2,1},{3,0},{4,7},{5,6},{6,5},{7,4},{8,11},{9,10},{10,... | collective-permute-start | bytes 294920 | tf_op jit(solution)/shard_map/ppermute | solution.py:442
  38.8 3.5 %collective-permute-start.8 = (f32[192,128]{1,0:T(8,128)S(1)}, f32[192,128]{1,0:T(8,128)S(1)}, u32[]{:S(2)}, u32[]{:S(2)}) collective-permute-start(f32[192,128]{1,0:T(8,128)S(1)} %get-tuple-element.63.refs_0_), channel_id=1, source_target_pairs={{0,1},{1,0},{2,3},{3,2},{4,5},{5,4},{6,7},{7,6},{8,9},{9,8},{10,11... | collective-permute-start | bytes 294920 | tf_op jit(solution)/shard_map/ppermute | solution.py:442
  38.8 5.9 %collective-permute-start.9 = (f32[192,128]{1,0:T(8,128)S(1)}, f32[192,128]{1,0:T(8,128)S(1)}, u32[]{:S(2)}, u32[]{:S(2)}) collective-permute-start(f32[192,128]{1,0:T(8,128)S(1)} %get-tuple-element.63.refs_0_), channel_id=1, source_target_pairs={{0,2},{1,3},{2,0},{3,1},{4,6},{5,7},{6,4},{7,5},{8,10},{9,11},{10,... | collective-permute-start | bytes 294920 | tf_op jit(solution)/shard_map/ppermute | solution.py:442
  44.7 3.9 %collective-permute-start.11 = (f32[192,128]{1,0:T(8,128)S(1)}, f32[192,128]{1,0:T(8,128)S(1)}, u32[]{:S(2)}, u32[]{:S(2)}) collective-permute-start(f32[192,128]{1,0:T(8,128)S(1)} %shard_map.83.refs_0_), channel_id=1, source_target_pairs={{0,4},{4,0},{8,12},{12,8},{16,20},{20,16},{24,28},{28,24},{1,5},{5... | collective-permute-start | bytes 294920 | tf_op jit(solution)/shard_map/ppermute | solution.py:442
  44.8 6.1 %collective-permute-start.12 = (f32[192,128]{1,0:T(8,128)S(1)}, f32[192,128]{1,0:T(8,128)S(1)}, u32[]{:S(2)}, u32[]{:S(2)}) collective-permute-start(f32[192,128]{1,0:T(8,128)S(1)} %shard_map.83.refs_0_), channel_id=1, source_target_pairs={{0,8},{4,12},{8,0},{12,4},{16,24},{20,28},{24,16},{28,20},{1,9},{5... | collective-permute-start | bytes 294920 | tf_op jit(solution)/shard_map/ppermute | solution.py:442
  46.2 6.9 %collective-permute-start.13 = (f32[192,128]{1,0:T(8,128)S(1)}, f32[192,128]{1,0:T(8,128)S(1)}, u32[]{:S(2)}, u32[]{:S(2)}) collective-permute-start(f32[192,128]{1,0:T(8,128)S(1)} %shard_map.83.refs_0_), channel_id=1, source_target_pairs={{0,12},{4,8},{8,4},{12,0},{16,28},{20,24},{24,20},{28,16},{1,13},{... | collective-permute-start | bytes 294920 | tf_op jit(solution)/shard_map/ppermute | solution.py:442
  53.1 6.0 %collective-permute-start.14 = (f32[192,128]{1,0:T(8,128)S(1)}, f32[192,128]{1,0:T(8,128)S(1)}, u32[]{:S(2)}, u32[]{:S(2)}) collective-permute-start(f32[192,128]{1,0:T(8,128)S(1)} %get-tuple-element.65.refs_0_), channel_id=1, source_target_pairs={{0,64},{32,96},{64,0},{96,32},{128,192},{160,224},{192,128},{224,1... | collective-permute-start | bytes 294920 | tf_op jit(solution)/shard_map/ppermute | solution.py:442
  53.3 5.8 %collective-permute-start.15 = (f32[192,128]{1,0:T(8,128)S(1)}, f32[192,128]{1,0:T(8,128)S(1)}, u32[]{:S(2)}, u32[]{:S(2)}) collective-permute-start(f32[192,128]{1,0:T(8,128)S(1)} %get-tuple-element.65.refs_0_), channel_id=1, source_target_pairs={{0,128},{32,160},{64,192},{96,224},{128,0},{160,32},{192,64},{224,... | collective-permute-start | bytes 294920 | tf_op jit(solution)/shard_map/ppermute | solution.py:442
  54.4 6.4 %collective-permute-start.16 = (f32[192,128]{1,0:T(8,128)S(1)}, f32[192,128]{1,0:T(8,128)S(1)}, u32[]{:S(2)}, u32[]{:S(2)}) collective-permute-start(f32[192,128]{1,0:T(8,128)S(1)} %get-tuple-element.65.refs_0_), channel_id=1, source_target_pairs={{0,192},{32,224},{64,128},{96,160},{128,64},{160,96},{192,0},{224,... | collective-permute-start | bytes 294920 | tf_op jit(solution)/shard_map/ppermute | solution.py:442
  60.7 10.2 %collective-permute-start.17 = (f32[192,128]{1,0:T(8,128)S(1)}, f32[192,128]{1,0:T(8,128)S(1)}, u32[]{:S(2)}, u32[]{:S(2)}) collective-permute-start(f32[192,128]{1,0:T(8,128)S(1)} %get-tuple-element.71.refs_0_), channel_id=1, source_target_pairs={{0,144},{4,148},{8,152},{12,156},{16,128},{20,132},{24,136},{28,14... | collective-permute-start | bytes 294920 | tf_op jit(solution)/shard_map/ppermute | solution.py:560
  71.0 3.6 %collective-permute-start.18 = (f32[192,128]{1,0:T(8,128)S(1)}, f32[192,128]{1,0:T(8,128)S(1)}, u32[]{:S(2)}, u32[]{:S(2)}) collective-permute-start(f32[192,128]{1,0:T(8,128)S(1)} %shard_map.88), channel_id=1, source_target_pairs={{0,32},{32,0},{64,96},{96,64},{128,160},{160,128},{192,224},{224,1... | collective-permute-start | bytes 294920 | tf_op jit(solution)/shard_map/ppermute | solution.py:442

commit v4 on v3

--- a/solution.py
+++ b/solution.py
@@ -81,20 +81,26 @@
     return amps[tap, k, row_of(first, ext)]
 
 
-def pack_kernel(field, cot, near_a, second_a, polar_a, second_b, polar_b, whole, sems):
-    odd = lax.axis_index("lon") % 2 == 1
+def pack_kernel(field, cot, near_a, second_a, polar_a, near_b, polar_b, whole, sems):
+    lat, odd = lax.axis_index("lat"), lax.axis_index("lon") % 2 == 1
 
     def edges(is_odd):
-        copies = []
-        for which, source in enumerate((field, cot)):
-            for out, width, right in ((near_a, OTHERS, is_odd), (second_a, SECOND, is_odd), (second_b, SECOND, not is_odd)):
-                begin = COLS - width if right else 0
-                copies.append((source.at[0, begin : begin + width], out.at[which]))
-        copies = [pltpu.make_async_copy(a, b, sems.at[i]) for i, (a, b) in enumerate(copies)]
-        for copy in copies:
-            copy.start()
-
-        @pl.when(lax.axis_index("lat") == 0)
+        def part(out, width, right, sem):
+            source, target = pl.ds(COLS - width if right else 0, width), pl.ds(0, width)
+            return [
+                pltpu.make_async_copy(x.at[0, source], out.at[i, target], sems.at[sem + i]) for i, x in enumerate((field, cot))
+            ]
+
+        def run(copies):
+            for copy in copies:
+                copy.start()
+            for copy in copies:
+                copy.wait()
+
+        pl.when(lat >= 2)(lambda: run(part(near_a, OTHERS + 1, is_odd, 0) + part(near_b, OTHERS, not is_odd, 2)))
+        pl.when(lat == 1)(lambda: run(part(second_a, SECOND, is_odd, 0) + part(polar_b, SECOND, not is_odd, 2)))
+
+        @pl.when(lat == 0)
         def _():
             loads = []
             for which, source in enumerate((field, cot)):
@@ -115,9 +121,6 @@
                 polar_a[which, 45:] = right if is_odd else left
                 polar_b[which, 45:] = left if is_odd else right
 
-        for copy in copies:
-            copy.wait()
-
     pl.when(odd)(lambda: edges(True))
     pl.when(jnp.logical_not(odd))(lambda: edges(False))
 
@@ -149,7 +152,7 @@
         own[:, :COLS, :] = jnp.swapaxes(whole[which], 0, 1)
 
 
-def assemble_kernel(old_f, old_c, near_a, second_a, polar_a, second_b, polar_b, *outs):
+def assemble_kernel(old_f, old_c, near_a, second_a, polar_a, near_b, polar_b, tie, *outs):
     lat = lax.axis_index("lat")
     odd = lax.axis_index("lon") % 2 == 1
     groups = ((outs[0], outs[2], outs[4]), (outs[1], outs[3], outs[5]))
@@ -166,15 +169,14 @@
 
         @pl.when(lat >= 2)
         def _(which=which, own0=own0):
-            a = near_a[which]
-            left = jnp.where(odd, second_b[which, SECOND - OTHERS :], a)
-            right = jnp.where(odd, a, second_b[which, :OTHERS])
+            left = jnp.where(odd, near_b[which], near_a[which, 1:])
+            right = jnp.where(odd, near_a[which, :OTHERS], near_b[which])
             own0[:, 112 - OTHERS : 112, :] = jnp.swapaxes(left, 0, 1)
             own0[:, 112 : 112 + OTHERS, :] = jnp.swapaxes(right, 0, 1)
 
         @pl.when(lat == 1)
         def _(which=which, own0=own0, own1=own1):
-            left, right = left_right(second_a, second_b, which, 0, SECOND)
+            left, right = left_right(second_a, polar_b, which, 0, SECOND)
             own0[:, 96:112, :] = left[:, 2:]
             own0[:, 112:128, :] = right[:, :16]
             own1[...] = jnp.zeros(own1.shape, BF16)
@@ -225,12 +227,13 @@
     return [jnp.concatenate(part, axis=0) if len(part) > 1 else part[0] for part in parts]
 
 
-def filtered(table, at, amps, first, ext, rows):
+def filtered(table, at, amps, first, ext, rows, lane=0):
     out = []
     for k, taps in enumerate(tapped(amps, first, ext, rows)):
         shapes = rows_at(table, at + k * PAD, PAD)
         if taps.shape[0] < 128:
-            shapes = jnp.concatenate([shapes[:, : taps.shape[0]], shapes[:, 128 : 128 + taps.shape[0]]], axis=1)
+            end = lane + taps.shape[0]
+            shapes = jnp.concatenate([shapes[:, lane:end], shapes[:, 128 + lane : 128 + end]], axis=1)
         out.append(jnp.dot(shapes, jnp.concatenate([taps, taps], axis=0), preferred_element_type=F32))
     return out
 
@@ -253,12 +256,22 @@
     return lax.dot_general(cot, basis, (((0,), (0,)), ((), ())), preferred_element_type=F32)
 
 
-def inner_kernel(amps, own0, own1, own2, shape0, shape1, shape2, cot, basis, part):
+def center_kernel(amps, own, shape0, center):
+    _, first = position()
+    for row in range(2, 14):
+        values = filtered(shape0, (row + 2) * 288, amps, first, row + 2, [own[row - 2 + tap, :PAD] for tap in range(5)])
+        for k in range(3):
+            at = (row - 2) * 288 + k * PAD
+            center[at : at + PAD, :] = values[k]
+
+
+def inner_kernel(amps, center, own0, own1, own2, shape0, shape1, shape2, cot, basis, part):
     lat, first = position()
 
     def one(row, wide, extra=None):
         at = (row + 2) * 288
-        values = filtered(shape0, at, amps, first, row + 2, [own0[row - 2 + tap] for tap in range(5)])
+        values = filtered(shape0, at, amps, first, row + 2, [own0[row - 2 + tap, PAD:] for tap in range(5)], PAD)
+        values = plus(values, [center[(row - 2) * 288 + k * PAD : (row - 2) * 288 + (k + 1) * PAD, :] for k in range(3)])
         if wide:
             values = plus(values, filtered(shape1, at, amps, first, row + 2, [own1[row - 2 + tap] for tap in range(5)]))
         store_basis(basis, row - 2, values if extra is None else plus(values, extra))
@@ -401,11 +414,11 @@
 
 
 def sum_kernel(count, *refs):
-    parts = [ref[...] for ref in refs[:count]]
+    parts = [ref[...].astype(F32) for ref in refs[:count]]
     while len(parts) > 1:
         parts = [parts[i] + parts[i + 1] for i in range(0, len(parts), 2)]
     out, *token = refs[-2:] if refs[-1].shape[0] == 8 else refs[-1:]
-    out[...] = parts[0]
+    out[...] = parts[0].astype(out.dtype)
     if token:
         token[0][...] = jnp.zeros((8, 128), F32)
 
@@ -469,7 +482,7 @@
     field, cot = features.transpose(0, 2, 1, 3), cotangent.transpose(0, 2, 1, 3)
     field, cot = (pltpu.with_memory_space_constraint(x, pltpu.HBM) for x in (field, cot))
     token = shape((8, 128), F32)
-    near = shape((2, OTHERS, ROWS, CHAN))
+    near_a, near_b = shape((2, OTHERS + 1, ROWS, CHAN)), shape((2, OTHERS, ROWS, CHAN))
     second = shape((2, SECOND, ROWS, CHAN))
     polar = shape((2, 65, ROWS, CHAN))
     scratch = [
@@ -478,14 +491,14 @@
     ]
     messages = call(
         pack_kernel,
-        [near, second, polar, second, polar],
+        [near_a, second, polar, near_b, polar],
         scratch,
         0,
         (),
         (field, cot),
         space=pltpu.HBM,
     )
-    targets = ((1, range(2, 8)), (1, (1,)), (1, (0,)), (0, range(1, 8)), (0, (0,)))
+    targets = ((1, range(2, 8)), (1, (1,)), (1, (0,)), (0, range(2, 8)), (0, (0, 1)))
     got = [None] * 5
     for index in (2, 1, 0, 4, 3):
         got[index] = lax.ppermute(messages[index], LL, pairs_of_lon(*targets[index]))
@@ -501,6 +514,9 @@
         (field, cot),
         space=pltpu.HBM,
     )
+    row_flops = 2 * 288 * 640 * CHAN
+    scalars = (amps,)
+    (center,) = call(center_kernel, [shape((12 * 288, CHAN), F32)], [], 10**8, scalars, (own_f, shapes[0]))
     own2 = shape((5, 32, CHAN))
     own0_f, own0_c, own1_f, own1_c, own2_f, own2_c, lat_a, lat_b = call(
         assemble_kernel,
@@ -508,15 +524,14 @@
         [],
         0,
         (),
-        (own_f, own_c, *got),
+        (own_f, own_c, *got, center),
     )
     halo_a = lax.ppermute(lat_a, "lat", pairs_of_lat(0))
     halo_b = lax.ppermute(lat_b, "lat", pairs_of_lat(1))
 
-    row_flops = 2 * 288 * 640 * CHAN
-    scalars = (amps,)
     filters = (own0_f, own1_f, own2_f, *shapes, own0_c)
-    inner, part = call(inner_kernel, [shape((12 * PAD, 384)), shape((128, 384), F32)], [], 12 * row_flops, scalars, filters)
+    outs = [shape((12 * PAD, 384)), shape((128, 384), F32)]
+    inner, part = call(inner_kernel, outs, [], 12 * row_flops, scalars, (center, *filters))
     half = shape((192, CHAN), F32)
     outer, mine, other = call(
         outer_kernel,
@@ -527,8 +542,9 @@
         (*filters, halo_a, halo_b, part),
     )
 
-    def add(*parts, after=(), more=True):
-        outs = [half, token] if more else [half]
+    def add(*parts, after=(), more=True, dtype=BF16):
+        total = shape((192, CHAN), dtype)
+        outs = [total, token] if more else [total]
         return call(functools.partial(sum_kernel, len(parts)), outs, [], 0, (), (*parts, *after))
 
     def back(piece, before, *done):
@@ -551,15 +567,14 @@
         (),
         (inner, outer, mix_weight.reshape(384, CHAN), before),
     )
-    (mine,) = add(mine, *steps, after=(done,), more=False)
+    mine, before = add(mine, *steps, after=(done,))
     steps = [flip(mine, "lon", bit) for bit in (1, 2, 3)]
-    mine, before = add(mine, *steps)
-    steps = [flip(mine, "lat", bit) for bit in (2, 4, 6)]
     grad, done = back(0, before)
     mine, before = add(mine, *steps, after=(done,))
-    step = lax.ppermute(mine, LL, z_pairs())
+    steps = [flip(mine, "lat", bit) for bit in (2, 4, 6)]
     grad, done = back(1, before, grad)
-    (mine,) = add(mine, step, after=(done,), more=False)
+    (mine,) = add(mine, *steps, after=(done,), more=False)
+    (mine,) = add(mine, lax.ppermute(mine, LL, z_pairs()), more=False, dtype=F32)
     other = flip(mine, "lat", 1)
     first_half = lax.axis_index("lat") % 2 == 0
     whole = jnp.concatenate([jnp.where(first_half, mine, other), jnp.where(first_half, other, mine)])

time: 75.5 us -> 70.1 us (0.928)
  waiting for transfers between devices: 12.5 us -> 8.8 us
  starting transfers between devices: 45.3 us -> 41.9 us
  Pallas kernels: 15.3 us -> 16.2 us
    ppermute x11, waiting for transfers between devices: 11.2 us -> 5.09 us  [flip(): lax.ppermute(x, axis, [(i, i ^ bit) for i in range(lax.axis_size(axis))])]
    ppermute x1, starting transfers between devices: 7.26 us -> 3.37 us  [body(): mine, = add(mine, lax.ppermute(mine, LL, z_pairs()), more=False, dtype=F32)]
    ppermute x11, starting transfers between devices: 16.3 us -> 19 us  [flip(): lax.ppermute(x, axis, [(i, i ^ bit) for i in range(lax.axis_size(axis))])]
    ppermute x1, starting transfers between devices: 3.19 us -> 0.74 us  [body(): halo_a = lax.ppermute(lat_a, 'lat', pairs_of_lat(0))]
    ppermute x1, waiting for transfers between devices: 0.01 us -> 1.87 us  [body(): mine, = add(mine, lax.ppermute(mine, LL, z_pairs()), more=False, dtype=F32)]
    ppermute x1, waiting for transfers between devices: 0.01 us -> 1.82 us  [body(): halo_b = lax.ppermute(lat_b, 'lat', pairs_of_lat(1))]
    ppermute x5, waiting for transfers between devices: 1.32 us -> 0.01 us  [body(): lax.ppermute(messages[index], LL, pairs_of_lon(*targets[index]))]
    pallas_call x13 -> x14, Pallas kernels: 15.3 us -> 16.2 us  [call(): pl.pallas_call(kernel, out_shape=outs, in_specs=[SMEM] * len(scalars) + [...]
  transfers between devices with their start and end apart: 19 -> 19, of which waited for: 9 -> 9; matrix products, arithmetic and copies ran while one was open for 0% -> 0% of each run, Pallas kernels for 16% -> 18%
where the time goes in v4:
time: 70.1 us; the launch traced here: 69.8 us
  starting transfers between devices  41.9 us (60%)
  Pallas kernels  16.2 us (23%)
  waiting for transfers between devices  8.8 us (13%)
  local copies, waits for them, and re-layouts  1.36 us (2%)
  between operations  0.85 us (1%)
  other arithmetic  0.71 us (1%)
    ppermute x11, starting transfers between devices, flip(): lax.ppermute(x, axis, [(i, i ^ bit) for i in range(lax.axis_size(axis))])  19 us
    ppermute x5, starting transfers between devices, body(): lax.ppermute(messages[index], LL, pairs_of_lon(*targets[index]))  16.3 us
    pallas_call x14, Pallas kernels, call(): pl.pallas_call(kernel, out_shape=outs, in_specs=[SMEM] * len(scalars) + [...  16.2 us
    ppermute x11, waiting for transfers between devices, flip(): lax.ppermute(x, axis, [(i, i ^ bit) for i in range(lax.axis_size(axis))])  5.09 us
    ppermute x1, starting transfers between devices, body(): mine, = add(mine, lax.ppermute(mine, LL, z_pairs()), more=False, dtype=F32)  3.37 us
    ppermute x1, starting transfers between devices, body(): halo_b = lax.ppermute(lat_b, 'lat', pairs_of_lat(1))  2.46 us
    ppermute x1, waiting for transfers between devices, body(): mine, = add(mine, lax.ppermute(mine, LL, z_pairs()), more=False, dtype=F32)  1.87 us
    ppermute x1, waiting for transfers between devices, body(): halo_b = lax.ppermute(lat_b, 'lat', pairs_of_lat(1))  1.82 us
  transfers between devices with their start and end apart: 19, of which 9 were waited for; matrix products, arithmetic and copies ran while one was open for 0% of the time, Pallas kernels for 18%

profile of v4, /device:TPU:1, one launch (start us, length us, event | category | flops | bytes accessed | tf_op | source)
XLA Modules:
  0.0 69.8 jit_solution(15925249739729511604)
XLA Ops:
  0.6 1.1 %shard_map.78 = (bf16[2,10,16,128]{3,2,1,0:T(8,128)(2,1)S(1)}, bf16[2,18,16,128]{3,2,1,0:T(8,128)(2,1)S(1)}, bf16[2,65,16,128]{3,2,1,0:T(8,128)(2,1)S(1)}, bf16[...) custom-call(bf16[1,90,16,128]{3,2,1,0:T(8,128)(2,1)} %bitcast.13, bf16[1,90,16,128]{3,2,1,0:T(8,128)(2,1)} %bitcast.15), custom_call_target="tpu_custom_call" | custom-call | bytes 2105344 | tf_op jit(solution)/shard_map/pallas_call | solution.py:464
  1.8 0.7 collective-permute-start.2
  2.5 3.9 %collective-permute-start.4 = (bf16[2,65,16,128]{3,2,1,0:T(8,128)(2,1)S(1)}, bf16[2,65,16,128]{3,2,1,0:T(8,128)(2,1)S(1)}, u32[]{:S(2)}, u32[]{:S(2)}) collective-permute-start(bf16[2,65,16,128]{3,2,1,0:T(8,128)(2,1)S(1)} %get-tuple-element.45), channel_id=1, source_target_pairs={{0,4},{4,0},{8,12},{12,8},{16,20},{20,16},{24,28},{28,24},{32,36},... | collective-permute-start | bytes 1597448 | tf_op jit(solution)/shard_map/ppermute | solution.py:504
  6.4 10.4 %collective-permute-start.1 = (bf16[2,18,16,128]{3,2,1,0:T(8,128)(2,1)S(1)}, bf16[2,18,16,128]{3,2,1,0:T(8,128)(2,1)S(1)}, u32[]{:S(2)}, u32[]{:S(2)}) collective-permute-start(bf16[2,18,16,128]{3,2,1,0:T(8,128)(2,1)S(1)} %get-tuple-element.42), channel_id=1, source_target_pairs={{32,60},{36,40},{40,36},{44,48},{48,44},{52,56},{56,52},{60,32},{3... | collective-permute-start | bytes 442376 | tf_op jit(solution)/shard_map/ppermute | solution.py:504
  16.8 0.7 collective-permute-start
  17.5 0.7 collective-permute-start.3
  18.1 0.0 copy-start.3
  18.1 0.6 copy-done.3
  18.8 2.8 %shard_map.76 = (bf16[16,128,128]{2,1,0:T(8,128)(2,1)S(1)}, bf16[16,128,128]{2,1,0:T(8,128)(2,1)S(1)}, bf16[5760,256]{1,0:T(8,128)(2,1)S(1)}, bf16[5760,256]{1,0:T(8,128)(2,1)S(1)}, bf16[1440,256]{1,0:T(8,128)(2,1)S(1)}) custom-call(s32[128]{0:T(128)S(1)} %copy-done.3, bf16[1,90,16,128]{3,2,1,0:T(8,128)(2,1)} %bitcast.14, bf16[1,90,16,128]{3,2,1,0:T(8,128)(2,1)} %bitcast.16), custom_call_target="tpu_custom_call" | custom-call | flops 200000000 | bytes 8421376 | tf_op jit(solution)/shard_map/pallas_call | solution.py:464
  21.6 0.0 copy-start.1
  21.6 0.7 copy-done.1
  22.3 1.7 %shard_map.77.tie.center = f32[3456,128]{1,0:T(8,128)S(1)} custom-call(f32[5,3,128]{2,1,0:T(4,128)S(1)} %bitcast.8, bf16[16,128,128]{2,1,0:T(8,128)(2,1)S(1)} %get-tuple-element.38.own.old_f, bf16[5760,256]{1,0:T(8,128)(2,1)S(1)} %get-tuple-element.39.shape0), custom_call_target="tpu_custom_call" | custom-call | flops 100000000 | bytes 5242880 | tf_op jit(solution)/shard_map/pallas_call | solution.py:464
  24.0 0.0 copy-start.2
  24.0 0.0 collective-permute-done.3.near_b
  24.0 0.0 collective-permute-done.near_a
  24.0 0.0 collective-permute-done.1.second_a
  24.0 0.0 collective-permute-done.2.polar_a
  24.0 0.0 collective-permute-done.4.polar_b
  24.0 0.4 shard_map.79
  24.5 2.5 %collective-permute-start.6 = (bf16[2,2,176,128]{3,2,1,0:T(8,128)(2,1)S(1)}, bf16[2,2,176,128]{3,2,1,0:T(8,128)(2,1)S(1)}, u32[]{:S(2)}, u32[]{:S(2)}) collective-permute-start(bf16[2,2,176,128]{3,2,1,0:T(8,128)(2,1)S(1)} %get-tuple-element.54), channel_id=1, source_target_pairs={{32,64},{64,32},{96,128},{128,96},{160,192},{192,160},{33,65},{65,... | collective-permute-start | bytes 540680 | tf_op jit(solution)/shard_map/ppermute | solution.py:530
  26.9 0.7 %collective-permute-start.5 = (bf16[2,2,160,128]{3,2,1,0:T(8,128)(2,1)S(1)}, bf16[2,2,160,128]{3,2,1,0:T(8,128)(2,1)S(1)}, u32[]{:S(2)}, u32[]{:S(2)}) collective-permute-start(bf16[2,2,160,128]{3,2,1,0:T(8,128)(2,1)S(1)} %get-tuple-element.53), channel_id=1, source_target_pairs={{0,32},{32,0},{64,96},{96,64},{128,160},{160,128},{192,224},{224,1... | collective-permute-start | bytes 491528 | tf_op jit(solution)/shard_map/ppermute | solution.py:529
  27.7 0.0 copy-done.2
  27.7 1.8 %shard_map.80 = (bf16[1152,384]{1,0:T(8,128)(2,1)S(1)}, f32[128,384]{1,0:T(8,128)S(1)}) custom-call(f32[5,3,128]{2,1,0:T(4,128)S(1)} %bitcast.9, f32[3456,128]{1,0:T(8,128)S(1)} %shard_map.77.tie.center, bf16[16,128,128]{2,1,0:T(8,128)(2,1)S(1)} %get-tuple-element.46.own0, bf16[16,128,128]{2,1,0:T(8,128)(2,1)S(1)} %get-tuple-element.47.own1, ...), custom_call_target="tpu_custom_call" | custom-call | flops 566231040 | bytes 11100160 | tf_op jit(solution)/shard_map/pallas_call | solution.py:464
  29.5 0.0 collective-permute-done.5.halo_a
  29.5 1.8 %collective-permute-done.6.halo_b = bf16[2,2,176,128]{3,2,1,0:T(8,128)(2,1)S(1)} collective-permute-done((bf16[2,2,176,128]{3,2,1,0:T(8,128)(2,1)S(1)}, bf16[2,2,176,128]{3,2,1,0:T(8,128)(2,1)S(1)}, u32[]{:S(2)}, u32[]{:S(2)}) %collective-permute-start.6) | collective-permute-done | bytes 180256 | tf_op jit(solution)/shard_map/ppermute | solution.py:530
  31.3 0.0 copy-start
  31.3 1.7 %shard_map.81 = (bf16[384,384]{1,0:T(8,128)(2,1)S(1)}, f32[192,128]{1,0:T(8,128)S(1)}, f32[192,128]{1,0:T(8,128)S(1)}) custom-call(f32[5,3,128]{2,1,0:T(4,128)S(1)} %bitcast.10, bf16[16,128,128]{2,1,0:T(8,128)(2,1)S(1)} %get-tuple-element.46.own0, bf16[16,128,128]{2,1,0:T(8,128)(2,1)S(1)} %get-tuple-element.47.own1, ...), custom_call_target="tpu_custom_call" | custom-call | flops 188743680 | bytes 9281536 | tf_op jit(solution)/shard_map/pallas_call | solution.py:464
  33.0 0.1 collective-permute-start.7
  33.1 1.3 %collective-permute-done.7.refs_1_ = f32[192,128]{1,0:T(8,128)S(1)} collective-permute-done((f32[192,128]{1,0:T(8,128)S(1)}, f32[192,128]{1,0:T(8,128)S(1)}, u32[]{:S(2)}, u32[]{:S(2)}) %collective-permute-start.7) | collective-permute-done | bytes 98336 | tf_op jit(solution)/shard_map/ppermute | solution.py:455
  34.4 2.8 %collective-permute-start.10 = (bf16[192,128]{1,0:T(8,128)(2,1)S(1)}, bf16[192,128]{1,0:T(8,128)(2,1)S(1)}, u32[]{:S(2)}, u32[]{:S(2)}) collective-permute-start(bf16[192,128]{1,0:T(8,128)(2,1)S(1)} %get-tuple-element.63.refs_0_), channel_id=1, source_target_pairs={{0,3},{1,2},{2,1},{3,0},{4,7},{5,6},{6,5},{7,4},{8,11},{9,10},{10,... | collective-permute-start | bytes 147464 | tf_op jit(solution)/shard_map/ppermute | solution.py:455
  37.2 0.0 collective-permute-start.8
  37.2 1.3 %collective-permute-start.9 = (bf16[192,128]{1,0:T(8,128)(2,1)S(1)}, bf16[192,128]{1,0:T(8,128)(2,1)S(1)}, u32[]{:S(2)}, u32[]{:S(2)}) collective-permute-start(bf16[192,128]{1,0:T(8,128)(2,1)S(1)} %get-tuple-element.63.refs_0_), channel_id=1, source_target_pairs={{0,2},{1,3},{2,0},{3,1},{4,6},{5,7},{6,4},{7,5},{8,10},{9,11},{10,... | collective-permute-start | bytes 147464 | tf_op jit(solution)/shard_map/ppermute | solution.py:455
  38.5 0.0 copy-done
  38.5 1.3 %shard_map.83 = (bf16[1,90,16,128]{3,2,1,0:T(8,128)(2,1)}, f32[8,128]{1,0:T(8,128)S(1)}) custom-call(bf16[1152,384]{1,0:T(8,128)(2,1)S(1)} %get-tuple-element.52.inner, bf16[384,384]{1,0:T(8,128)(2,1)S(1)} %get-tuple-element.56.outer, bf16[384,128]{1,0:T(8,128)(2,1)S(1)} %bitcast.7, f32[8,128]{1,0:T(8,128)S(1)} %get-tuple-element.59.before), custom_call_target="tpu_custom_call" | custom-call | flops 150994944 | bytes 1654784 | tf_op jit(solution)/shard_map/pallas_call | solution.py:464
  39.8 0.0 collective-permute-done.10.refs_3_
  39.8 0.4 collective-permute-done.8.refs_1_
  40.1 1.5 %collective-permute-done.9.refs_2_ = bf16[192,128]{1,0:T(8,128)(2,1)S(1)} collective-permute-done((bf16[192,128]{1,0:T(8,128)(2,1)S(1)}, bf16[192,128]{1,0:T(8,128)(2,1)S(1)}, u32[]{:S(2)}, u32[]{:S(2)}) %collective-permute-start.9) | collective-permute-done | bytes 49184 | tf_op jit(solution)/shard_map/ppermute | solution.py:455
  41.7 1.6 %collective-permute-start.11 = (bf16[192,128]{1,0:T(8,128)(2,1)S(1)}, bf16[192,128]{1,0:T(8,128)(2,1)S(1)}, u32[]{:S(2)}, u32[]{:S(2)}) collective-permute-start(bf16[192,128]{1,0:T(8,128)(2,1)S(1)} %get-tuple-element.65.refs_0_), channel_id=1, source_target_pairs={{0,4},{4,0},{8,12},{12,8},{16,20},{20,16},{24,28},{28,24},{1,5},{5... | collective-permute-start | bytes 147464 | tf_op jit(solution)/shard_map/ppermute | solution.py:455
  43.3 0.7 %collective-permute-start.12 = (bf16[192,128]{1,0:T(8,128)(2,1)S(1)}, bf16[192,128]{1,0:T(8,128)(2,1)S(1)}, u32[]{:S(2)}, u32[]{:S(2)}) collective-permute-start(bf16[192,128]{1,0:T(8,128)(2,1)S(1)} %get-tuple-element.65.refs_0_), channel_id=1, source_target_pairs={{0,8},{4,12},{8,0},{12,4},{16,24},{20,28},{24,16},{28,20},{1,9},{5... | collective-permute-start | bytes 147464 | tf_op jit(solution)/shard_map/ppermute | solution.py:455
  44.0 1.8 %collective-permute-start.13 = (bf16[192,128]{1,0:T(8,128)(2,1)S(1)}, bf16[192,128]{1,0:T(8,128)(2,1)S(1)}, u32[]{:S(2)}, u32[]{:S(2)}) collective-permute-start(bf16[192,128]{1,0:T(8,128)(2,1)S(1)} %get-tuple-element.65.refs_0_), channel_id=1, source_target_pairs={{0,12},{4,8},{8,4},{12,0},{16,28},{20,24},{24,20},{28,16},{1,13},{... | collective-permute-start | bytes 147464 | tf_op jit(solution)/shard_map/ppermute | solution.py:455
  45.8 2.4 %shard_map.85 = (f32[1,90,16,128]{3,2,1,0:T(8,128)S(1)}, f32[8,128]{1,0:T(8,128)S(1)}) custom-call(f32[5,3,128]{2,1,0:T(4,128)S(1)} %bitcast.11, bf16[16,128,128]{2,1,0:T(8,128)(2,1)S(1)} %get-tuple-element.51.cot.own0, bf16[16,128,128]{2,1,0:T(8,128)(2,1)S(1)} %get-tuple-element.61.own1, bf16[5,32,128]{2,1,0:T(8,128)(2,1)S(1)} %get-tuple-element.62.own2, ...), custom_call_target="tpu_custom_call" | custom-call | flops 94371840 | bytes 8912896 | tf_op jit(solution)/shard_map/pallas_call | solution.py:464
  48.2 0.0 collective-permute-done.11.refs_1_
  48.2 0.1 collective-permute-done.12.refs_2_
  48.3 0.2 collective-permute-done.13.refs_3_
  48.5 2.0 %collective-permute-start.14 = (bf16[192,128]{1,0:T(8,128)(2,1)S(1)}, bf16[192,128]{1,0:T(8,128)(2,1)S(1)}, u32[]{:S(2)}, u32[]{:S(2)}) collective-permute-start(bf16[192,128]{1,0:T(8,128)(2,1)S(1)} %get-tuple-element.71.refs_0_), channel_id=1, source_target_pairs={{0,64},{32,96},{64,0},{96,32},{128,192},{160,224},{192,128},{224,1... | collective-permute-start | bytes 147464 | tf_op jit(solution)/shard_map/ppermute | solution.py:455
  50.5 1.6 %collective-permute-start.15 = (bf16[192,128]{1,0:T(8,128)(2,1)S(1)}, bf16[192,128]{1,0:T(8,128)(2,1)S(1)}, u32[]{:S(2)}, u32[]{:S(2)}) collective-permute-start(bf16[192,128]{1,0:T(8,128)(2,1)S(1)} %get-tuple-element.71.refs_0_), channel_id=1, source_target_pairs={{0,128},{32,160},{64,192},{96,224},{128,0},{160,32},{192,64},{224,... | collective-permute-start | bytes 147464 | tf_op jit(solution)/shard_map/ppermute | solution.py:455
  52.1 1.1 %collective-permute-start.16 = (bf16[192,128]{1,0:T(8,128)(2,1)S(1)}, bf16[192,128]{1,0:T(8,128)(2,1)S(1)}, u32[]{:S(2)}, u32[]{:S(2)}) collective-permute-start(bf16[192,128]{1,0:T(8,128)(2,1)S(1)} %get-tuple-element.71.refs_0_), channel_id=1, source_target_pairs={{0,192},{32,224},{64,128},{96,160},{128,64},{160,96},{192,0},{224,... | collective-permute-start | bytes 147464 | tf_op jit(solution)/shard_map/ppermute | solution.py:455
  53.2 2.9 %shard_map.87 = (f32[1,90,16,128]{3,2,1,0:T(8,128)}, f32[8,128]{1,0:T(8,128)S(1)}) custom-call(f32[5,3,128]{2,1,0:T(4,128)S(1)} %bitcast.12, bf16[16,128,128]{2,1,0:T(8,128)(2,1)S(1)} %get-tuple-element.51.cot.own0, bf16[16,128,128]{2,1,0:T(8,128)(2,1)S(1)} %get-tuple-element.61.own1, bf16[5,32,128]{2,1,0:T(8,128)(2,1)S(1)} %get-tuple-element.62.own2, ...), custom_call_target="tpu_custom_call" | custom-call | flops 94371840 | bytes 9650176 | tf_op jit(solution)/shard_map/pallas_call | solution.py:464
  56.1 0.0 collective-permute-done.14.refs_1_
  56.1 0.0 collective-permute-done.15.refs_2_
  56.1 0.7 %collective-permute-done.16.refs_3_ = bf16[192,128]{1,0:T(8,128)(2,1)S(1)} collective-permute-done((bf16[192,128]{1,0:T(8,128)(2,1)S(1)}, bf16[192,128]{1,0:T(8,128)(2,1)S(1)}, u32[]{:S(2)}, u32[]{:S(2)}) %collective-permute-start.16) | collective-permute-done | bytes 49184 | tf_op jit(solution)/shard_map/ppermute | solution.py:455
  56.9 3.4 %collective-permute-start.17 = (bf16[192,128]{1,0:T(8,128)(2,1)S(1)}, bf16[192,128]{1,0:T(8,128)(2,1)S(1)}, u32[]{:S(2)}, u32[]{:S(2)}) collective-permute-start(bf16[192,128]{1,0:T(8,128)(2,1)S(1)} %shard_map.88.refs_0_), channel_id=1, source_target_pairs={{0,144},{4,148},{8,152},{12,156},{16,128},{20,132},{24,136},{28,14... | collective-permute-start | bytes 147464 | tf_op jit(solution)/shard_map/ppermute | solution.py:577
  60.3 1.9 %collective-permute-done.17.refs_1_ = bf16[192,128]{1,0:T(8,128)(2,1)S(1)} collective-permute-done((bf16[192,128]{1,0:T(8,128)(2,1)S(1)}, bf16[192,128]{1,0:T(8,128)(2,1)S(1)}, u32[]{:S(2)}, u32[]{:S(2)}) %collective-permute-start.17) | collective-permute-done | bytes 49184 | tf_op jit(solution)/shard_map/ppermute | solution.py:577
  62.1 6.0 %collective-permute-start.18 = (f32[192,128]{1,0:T(8,128)S(1)}, f32[192,128]{1,0:T(8,128)S(1)}, u32[]{:S(2)}, u32[]{:S(2)}) collective-permute-start(f32[192,128]{1,0:T(8,128)S(1)} %shard_map.89), channel_id=1, source_target_pairs={{0,32},{32,0},{64,96},{96,64},{128,160},{160,128},{192,224},{224,1... | collective-permute-start | bytes 294920 | tf_op jit(solution)/shard_map/ppermute | solution.py:455
  68.1 0.9 %collective-permute-done.18 = f32[192,128]{1,0:T(8,128)S(1)} collective-permute-done((f32[192,128]{1,0:T(8,128)S(1)}, f32[192,128]{1,0:T(8,128)S(1)}, u32[]{:S(2)}, u32[]{:S(2)}) %collective-permute-start.18) | collective-permute-done | bytes 98336 | tf_op jit(solution)/shard_map/ppermute | solution.py:455
  69.1 0.7 maximum_multiply_fusion
  (6 shorter events, 0.1 us)
Async XLA Ops:
  1.8 22.2 %collective-permute-start.2 = (bf16[2,65,16,128]{3,2,1,0:T(8,128)(2,1)S(1)}, bf16[2,65,16,128]{3,2,1,0:T(8,128)(2,1)S(1)}, u32[]{:S(2)}, u32[]{:S(2)}) collective-permute-start(bf16[2,65,16,128]{3,2,1,0:T(8,128)(2,1)S(1)} %get-tuple-element.43), channel_id=1, source_target_pairs={{0,28},{4,8},{8,4},{12,16},{16,12},{20,24},{24,20},{28,0},{1,29},{... | collective-permute-start | bytes 1597448 | tf_op jit(solution)/shard_map/ppermute | solution.py:504
  2.5 21.5 %collective-permute-start.4 = (bf16[2,65,16,128]{3,2,1,0:T(8,128)(2,1)S(1)}, bf16[2,65,16,128]{3,2,1,0:T(8,128)(2,1)S(1)}, u32[]{:S(2)}, u32[]{:S(2)}) collective-permute-start(bf16[2,65,16,128]{3,2,1,0:T(8,128)(2,1)S(1)} %get-tuple-element.45), channel_id=1, source_target_pairs={{0,4},{4,0},{8,12},{12,8},{16,20},{20,16},{24,28},{28,24},{32,36},... | collective-permute-start | bytes 1597448 | tf_op jit(solution)/shard_map/ppermute | solution.py:504
  6.4 17.6 %collective-permute-start.1 = (bf16[2,18,16,128]{3,2,1,0:T(8,128)(2,1)S(1)}, bf16[2,18,16,128]{3,2,1,0:T(8,128)(2,1)S(1)}, u32[]{:S(2)}, u32[]{:S(2)}) collective-permute-start(bf16[2,18,16,128]{3,2,1,0:T(8,128)(2,1)S(1)} %get-tuple-element.42), channel_id=1, source_target_pairs={{32,60},{36,40},{40,36},{44,48},{48,44},{52,56},{56,52},{60,32},{3... | collective-permute-start | bytes 442376 | tf_op jit(solution)/shard_map/ppermute | solution.py:504
  16.8 7.2 %collective-permute-start = (bf16[2,10,16,128]{3,2,1,0:T(8,128)(2,1)S(1)}, bf16[2,10,16,128]{3,2,1,0:T(8,128)(2,1)S(1)}, u32[]{:S(2)}, u32[]{:S(2)}) collective-permute-start(bf16[2,10,16,128]{3,2,1,0:T(8,128)(2,1)S(1)} %get-tuple-element.41), channel_id=1, source_target_pairs={{64,92},{68,72},{72,68},{76,80},{80,76},{84,88},{88,84},{92,64},{9... | collective-permute-start | bytes 245768 | tf_op jit(solution)/shard_map/ppermute | solution.py:504
  17.5 6.5 %collective-permute-start.3 = (bf16[2,9,16,128]{3,2,1,0:T(8,128)(2,1)S(1)}, bf16[2,9,16,128]{3,2,1,0:T(8,128)(2,1)S(1)}, u32[]{:S(2)}, u32[]{:S(2)}) collective-permute-start(bf16[2,9,16,128]{3,2,1,0:T(8,128)(2,1)S(1)} %get-tuple-element.44), channel_id=1, source_target_pairs={{64,68},{68,64},{72,76},{76,72},{80,84},{84,80},{88,92},{92,88},{9... | collective-permute-start | bytes 221192 | tf_op jit(solution)/shard_map/ppermute | solution.py:504
  18.1 0.7 copy-start.3
  21.6 0.7 %copy-start.1 = (f32[3,128,5]{1,0,2:T(4,128)S(1)}, f32[3,128,5]{1,0,2:T(4,128)}, u32[]{:S(2)}) copy-start(f32[3,128,5]{1,0,2:T(4,128)} %param.8) | copy-start | bytes 23044
  24.0 3.7 %copy-start.2 = (f32[3,128,5]{1,0,2:T(4,128)S(1)}, f32[3,128,5]{1,0,2:T(4,128)}, u32[]{:S(2)}) copy-start(f32[3,128,5]{1,0,2:T(4,128)} %param.8) | copy-start | bytes 23044
  24.5 6.8 %collective-permute-start.6 = (bf16[2,2,176,128]{3,2,1,0:T(8,128)(2,1)S(1)}, bf16[2,2,176,128]{3,2,1,0:T(8,128)(2,1)S(1)}, u32[]{:S(2)}, u32[]{:S(2)}) collective-permute-start(bf16[2,2,176,128]{3,2,1,0:T(8,128)(2,1)S(1)} %get-tuple-element.54), channel_id=1, source_target_pairs={{32,64},{64,32},{96,128},{128,96},{160,192},{192,160},{33,65},{65,... | collective-permute-start | bytes 540680 | tf_op jit(solution)/shard_map/ppermute | solution.py:530
  26.9 2.5 %collective-permute-start.5 = (bf16[2,2,160,128]{3,2,1,0:T(8,128)(2,1)S(1)}, bf16[2,2,160,128]{3,2,1,0:T(8,128)(2,1)S(1)}, u32[]{:S(2)}, u32[]{:S(2)}) collective-permute-start(bf16[2,2,160,128]{3,2,1,0:T(8,128)(2,1)S(1)} %get-tuple-element.53), channel_id=1, source_target_pairs={{0,32},{32,0},{64,96},{96,64},{128,160},{160,128},{192,224},{224,1... | collective-permute-start | bytes 491528 | tf_op jit(solution)/shard_map/ppermute | solution.py:529
  31.3 7.2 %copy-start = (bf16[3,128,128]{2,1,0:T(8,128)(2,1)S(1)}, bf16[3,128,128]{2,1,0:T(8,128)(2,1)}, u32[]{:S(2)}) copy-start(bf16[3,128,128]{2,1,0:T(8,128)(2,1)} %weight.3) | copy-start | bytes 294916
  33.0 1.4 %collective-permute-start.7 = (f32[192,128]{1,0:T(8,128)S(1)}, f32[192,128]{1,0:T(8,128)S(1)}, u32[]{:S(2)}, u32[]{:S(2)}) collective-permute-start(f32[192,128]{1,0:T(8,128)S(1)} %get-tuple-element.58), channel_id=1, source_target_pairs={{0,32},{32,0},{64,96},{96,64},{128,160},{160,128},{192,224},{224,1... | collective-permute-start | bytes 294920 | tf_op jit(solution)/shard_map/ppermute | solution.py:455
  34.4 5.4 %collective-permute-start.10 = (bf16[192,128]{1,0:T(8,128)(2,1)S(1)}, bf16[192,128]{1,0:T(8,128)(2,1)S(1)}, u32[]{:S(2)}, u32[]{:S(2)}) collective-permute-start(bf16[192,128]{1,0:T(8,128)(2,1)S(1)} %get-tuple-element.63.refs_0_), channel_id=1, source_target_pairs={{0,3},{1,2},{2,1},{3,0},{4,7},{5,6},{6,5},{7,4},{8,11},{9,10},{10,... | collective-permute-start | bytes 147464 | tf_op jit(solution)/shard_map/ppermute | solution.py:455
  37.2 2.9 %collective-permute-start.8 = (bf16[192,128]{1,0:T(8,128)(2,1)S(1)}, bf16[192,128]{1,0:T(8,128)(2,1)S(1)}, u32[]{:S(2)}, u32[]{:S(2)}) collective-permute-start(bf16[192,128]{1,0:T(8,128)(2,1)S(1)} %get-tuple-element.63.refs_0_), channel_id=1, source_target_pairs={{0,1},{1,0},{2,3},{3,2},{4,5},{5,4},{6,7},{7,6},{8,9},{9,8},{10,11... | collective-permute-start | bytes 147464 | tf_op jit(solution)/shard_map/ppermute | solution.py:455
  37.2 4.4 %collective-permute-start.9 = (bf16[192,128]{1,0:T(8,128)(2,1)S(1)}, bf16[192,128]{1,0:T(8,128)(2,1)S(1)}, u32[]{:S(2)}, u32[]{:S(2)}) collective-permute-start(bf16[192,128]{1,0:T(8,128)(2,1)S(1)} %get-tuple-element.63.refs_0_), channel_id=1, source_target_pairs={{0,2},{1,3},{2,0},{3,1},{4,6},{5,7},{6,4},{7,5},{8,10},{9,11},{10,... | collective-permute-start | bytes 147464 | tf_op jit(solution)/shard_map/ppermute | solution.py:455
  41.7 6.5 %collective-permute-start.11 = (bf16[192,128]{1,0:T(8,128)(2,1)S(1)}, bf16[192,128]{1,0:T(8,128)(2,1)S(1)}, u32[]{:S(2)}, u32[]{:S(2)}) collective-permute-start(bf16[192,128]{1,0:T(8,128)(2,1)S(1)} %get-tuple-element.65.refs_0_), channel_id=1, source_target_pairs={{0,4},{4,0},{8,12},{12,8},{16,20},{20,16},{24,28},{28,24},{1,5},{5... | collective-permute-start | bytes 147464 | tf_op jit(solution)/shard_map/ppermute | solution.py:455
  43.3 5.0 %collective-permute-start.12 = (bf16[192,128]{1,0:T(8,128)(2,1)S(1)}, bf16[192,128]{1,0:T(8,128)(2,1)S(1)}, u32[]{:S(2)}, u32[]{:S(2)}) collective-permute-start(bf16[192,128]{1,0:T(8,128)(2,1)S(1)} %get-tuple-element.65.refs_0_), channel_id=1, source_target_pairs={{0,8},{4,12},{8,0},{12,4},{16,24},{20,28},{24,16},{28,20},{1,9},{5... | collective-permute-start | bytes 147464 | tf_op jit(solution)/shard_map/ppermute | solution.py:455
  44.0 4.5 %collective-permute-start.13 = (bf16[192,128]{1,0:T(8,128)(2,1)S(1)}, bf16[192,128]{1,0:T(8,128)(2,1)S(1)}, u32[]{:S(2)}, u32[]{:S(2)}) collective-permute-start(bf16[192,128]{1,0:T(8,128)(2,1)S(1)} %get-tuple-element.65.refs_0_), channel_id=1, source_target_pairs={{0,12},{4,8},{8,4},{12,0},{16,28},{20,24},{24,20},{28,16},{1,13},{... | collective-permute-start | bytes 147464 | tf_op jit(solution)/shard_map/ppermute | solution.py:455
  48.5 7.6 %collective-permute-start.14 = (bf16[192,128]{1,0:T(8,128)(2,1)S(1)}, bf16[192,128]{1,0:T(8,128)(2,1)S(1)}, u32[]{:S(2)}, u32[]{:S(2)}) collective-permute-start(bf16[192,128]{1,0:T(8,128)(2,1)S(1)} %get-tuple-element.71.refs_0_), channel_id=1, source_target_pairs={{0,64},{32,96},{64,0},{96,32},{128,192},{160,224},{192,128},{224,1... | collective-permute-start | bytes 147464 | tf_op jit(solution)/shard_map/ppermute | solution.py:455
  50.5 5.6 %collective-permute-start.15 = (bf16[192,128]{1,0:T(8,128)(2,1)S(1)}, bf16[192,128]{1,0:T(8,128)(2,1)S(1)}, u32[]{:S(2)}, u32[]{:S(2)}) collective-permute-start(bf16[192,128]{1,0:T(8,128)(2,1)S(1)} %get-tuple-element.71.refs_0_), channel_id=1, source_target_pairs={{0,128},{32,160},{64,192},{96,224},{128,0},{160,32},{192,64},{224,... | collective-permute-start | bytes 147464 | tf_op jit(solution)/shard_map/ppermute | solution.py:455
  52.1 4.7 %collective-permute-start.16 = (bf16[192,128]{1,0:T(8,128)(2,1)S(1)}, bf16[192,128]{1,0:T(8,128)(2,1)S(1)}, u32[]{:S(2)}, u32[]{:S(2)}) collective-permute-start(bf16[192,128]{1,0:T(8,128)(2,1)S(1)} %get-tuple-element.71.refs_0_), channel_id=1, source_target_pairs={{0,192},{32,224},{64,128},{96,160},{128,64},{160,96},{192,0},{224,... | collective-permute-start | bytes 147464 | tf_op jit(solution)/shard_map/ppermute | solution.py:455
  56.9 5.2 %collective-permute-start.17 = (bf16[192,128]{1,0:T(8,128)(2,1)S(1)}, bf16[192,128]{1,0:T(8,128)(2,1)S(1)}, u32[]{:S(2)}, u32[]{:S(2)}) collective-permute-start(bf16[192,128]{1,0:T(8,128)(2,1)S(1)} %shard_map.88.refs_0_), channel_id=1, source_target_pairs={{0,144},{4,148},{8,152},{12,156},{16,128},{20,132},{24,136},{28,14... | collective-permute-start | bytes 147464 | tf_op jit(solution)/shard_map/ppermute | solution.py:577
  62.1 6.9 %collective-permute-start.18 = (f32[192,128]{1,0:T(8,128)S(1)}, f32[192,128]{1,0:T(8,128)S(1)}, u32[]{:S(2)}, u32[]{:S(2)}) collective-permute-start(f32[192,128]{1,0:T(8,128)S(1)} %shard_map.89), channel_id=1, source_target_pairs={{0,32},{32,0},{64,96},{96,64},{128,160},{160,128},{192,224},{224,1... | collective-permute-start | bytes 294920 | tf_op jit(solution)/shard_map/ppermute | solution.py:455

commit v5 on v4

--- a/solution.py
+++ b/solution.py
@@ -97,7 +97,7 @@
             for copy in copies:
                 copy.wait()
 
-        pl.when(lat >= 2)(lambda: run(part(near_a, OTHERS + 1, is_odd, 0) + part(near_b, OTHERS, not is_odd, 2)))
+        pl.when(lat >= 2)(lambda: run(part(near_a, OTHERS, is_odd, 0) + part(near_b, OTHERS, not is_odd, 2)))
         pl.when(lat == 1)(lambda: run(part(second_a, SECOND, is_odd, 0) + part(polar_b, SECOND, not is_odd, 2)))
 
         @pl.when(lat == 0)
@@ -125,31 +125,42 @@
     pl.when(jnp.logical_not(odd))(lambda: edges(False))
 
 
-def pre_kernel(spans, field, cot, own_f, own_c, shape0, shape1, shape2, whole, sems):
+def prepare_kernel(field, cot, spans, amps, *refs):
+    own_f, own_c, shape0, shape1, shape2, center, amps_out, whole, spans_in, amps_in, sems = refs
     lat, first = position()
+    fetch = pltpu.make_async_copy(spans, spans_in, sems.at[6])
+    fetch_amps = pltpu.make_async_copy(amps, amps_in, sems.at[7])
+    hand_on = pltpu.make_async_copy(amps, amps_out, sems.at[8])
     loads = []
     for which, source in enumerate((field, cot)):
         for part in range(3):
             at = pl.ds(part * 30, 30)
             loads.append(pltpu.make_async_copy(source.at[0, at], whole.at[which, at], sems.at[which * 3 + part]))
-    for load in loads:
+    for load in (fetch, fetch_amps, hand_on, *loads):
         load.start()
-    fill_shapes(shape0, offsets_of(0), spans, first, 0, 20)
+    fetch.wait()
+    fill_shapes(shape0, offsets_of(0), spans_in, first, 0, 20)
 
     @pl.when(lat < 2)
     def _():
         low = jnp.where(lat == 0, 2, 0)
-        fill_shapes(shape1, offsets_of(1), spans, first, low, jnp.where(lat == 0, 18, 2))
+        fill_shapes(shape1, offsets_of(1), spans_in, first, low, jnp.where(lat == 0, 18, 2))
 
     @pl.when(lat == 0)
     def _():
-        fill_shapes(shape2, offsets_of(2), spans, first, 2, 5)
-
-    for load in loads:
+        fill_shapes(shape2, offsets_of(2), spans_in, first, 2, 5)
+
+    for load in (fetch_amps, hand_on, *loads):
         load.wait()
     for which, own in enumerate((own_f, own_c)):
         own[:, COLS:, :] = jnp.zeros((ROWS, 128 - COLS, CHAN), BF16)
         own[:, :COLS, :] = jnp.swapaxes(whole[which], 0, 1)
+    for row in range(ROWS):
+        rows = [own_f[row - 2 + tap, :PAD] if 0 <= row - 2 + tap < ROWS else None for tap in range(5)]
+        values = filtered(shape0, (row + 2) * 288, amps_in, first, row + 2, rows)
+        for k in range(3):
+            at = row * 288 + k * PAD
+            center[at : at + PAD, :] = values[k]
 
 
 def assemble_kernel(old_f, old_c, near_a, second_a, polar_a, near_b, polar_b, tie, *outs):
@@ -169,8 +180,8 @@
 
         @pl.when(lat >= 2)
         def _(which=which, own0=own0):
-            left = jnp.where(odd, near_b[which], near_a[which, 1:])
-            right = jnp.where(odd, near_a[which, :OTHERS], near_b[which])
+            left = jnp.where(odd, near_b[which], near_a[which])
+            right = jnp.where(odd, near_a[which], near_b[which])
             own0[:, 112 - OTHERS : 112, :] = jnp.swapaxes(left, 0, 1)
             own0[:, 112 : 112 + OTHERS, :] = jnp.swapaxes(right, 0, 1)
 
@@ -208,20 +219,25 @@
 
         even = lat % 2 == 0
         for row in range(2):
-            lat_a[which, row, :128, :] = jnp.where(even, own0[14 + row], own0[row])
-            lat_a[which, row, 128:, :] = jnp.where(even, own1[14 + row, 48:80, :], own1[row, 48:80, :])
+            lat_a[which, row] = jnp.where(even, own0[14 + row], own0[row])
             lat_b[which, row, :128, :] = jnp.where(even, own0[row], own0[14 + row])
 
+        @pl.when(lat < 2)
+        def _(which=which, own1=own1):
+            for row in range(2):
+                lat_a[which, row, COLS : COLS + 4, :] = jnp.where(even, own1[14 + row, 62:66, :], own1[row, 62:66, :])
+
 
 def tapped(amps, first, ext, rows):
-    factors = [[factor_of(amps, first, ext, k, tap) for tap in range(5)] for k in range(3)]
-    height = rows[0].shape[0]
+    taps = [tap for tap in range(5) if rows[tap] is not None]
+    factors = [{tap: factor_of(amps, first, ext, k, tap) for tap in taps} for k in range(3)]
+    height = rows[taps[0]].shape[0]
     parts = [[] for _ in range(3)]
     for at in range(0, height, 32):
-        wide = [row[at : at + 32].astype(F32) for row in rows]
+        wide = {tap: rows[tap][at : at + 32].astype(F32) for tap in taps}
         for k in range(3):
-            total = wide[0] * factors[k][0]
-            for tap in range(1, 5):
+            total = wide[taps[0]] * factors[k][taps[0]]
+            for tap in taps[1:]:
                 total += wide[tap] * factors[k][tap]
             parts[k].append(total.astype(BF16))
     return [jnp.concatenate(part, axis=0) if len(part) > 1 else part[0] for part in parts]
@@ -256,82 +272,68 @@
     return lax.dot_general(cot, basis, (((0,), (0,)), ((), ())), preferred_element_type=F32)
 
 
-def center_kernel(amps, own, shape0, center):
-    _, first = position()
-    for row in range(2, 14):
-        values = filtered(shape0, (row + 2) * 288, amps, first, row + 2, [own[row - 2 + tap, :PAD] for tap in range(5)])
-        for k in range(3):
-            at = (row - 2) * 288 + k * PAD
-            center[at : at + PAD, :] = values[k]
-
-
-def inner_kernel(amps, center, own0, own1, own2, shape0, shape1, shape2, cot, basis, part):
+def inner_kernel(amps, center, own0, own1, own2, shape0, shape1, shape2, cot, basis, part, ends):
     lat, first = position()
 
-    def one(row, wide, extra=None):
+    def one(row, wide):
+        def own(ref, low, high):
+            return [ref[row - 2 + tap, low:] if 0 <= row - 2 + tap < high else None for tap in range(5)]
+
         at = (row + 2) * 288
-        values = filtered(shape0, at, amps, first, row + 2, [own0[row - 2 + tap, PAD:] for tap in range(5)], PAD)
-        values = plus(values, [center[(row - 2) * 288 + k * PAD : (row - 2) * 288 + (k + 1) * PAD, :] for k in range(3)])
+        values = filtered(shape0, at, amps, first, row + 2, own(own0, PAD, ROWS), PAD)
+        values = plus(values, [center[row * 288 + k * PAD : row * 288 + (k + 1) * PAD, :] for k in range(3)])
         if wide:
-            values = plus(values, filtered(shape1, at, amps, first, row + 2, [own1[row - 2 + tap] for tap in range(5)]))
-        store_basis(basis, row - 2, values if extra is None else plus(values, extra))
-
-    def loop(start, wide):
-        for row in range(start, 14):
+            values = plus(values, filtered(shape1, at, amps, first, row + 2, own(own1, 0, ROWS)))
+        if wide and row < 3:
+            values = plus(values, filtered(shape2, at, amps, first, row + 2, own(own2, 0, 5)))
+        if 2 <= row < 14:
+            store_basis(basis, row - 2, values)
+        else:
+            place = row if row < 2 else row - 12
+            for k in range(3):
+                ends[place * 288 + k * PAD : place * 288 + (k + 1) * PAD, :] = values[k]
+
+    def run(wide):
+        for row in range(ROWS):
             one(row, wide)
 
-    @pl.when(lat != 0)
-    def _():
-        loop(2, False)
-
-    @pl.when(lat == 0)
-    def _():
-        far = filtered(shape2, 4 * 288, amps, first, 4, [own2[tap] for tap in range(5)])
-        one(2, True, far)
-        loop(3, True)
-
+    pl.when(lat != 0)(lambda: run(False))
+    pl.when(lat == 0)(lambda: run(True))
     part[...] = times_cotangent(cot[2:14, :PAD, :].reshape(12 * PAD, CHAN), basis[...])
 
 
 def halo_row(halo_a, halo_b, which, row, even, top):
-    a, b = halo_a[which, row, :128], halo_b[which, row, :128]
+    a, b = halo_a[which, row], halo_b[which, row, :128]
     return jnp.where(even, b, a) if top else jnp.where(even, a, b)
 
 
 def far_halo_row(halo_a, which, row):
-    zeros = jnp.zeros((48, CHAN), BF16)
-    return jnp.concatenate([zeros, halo_a[which, row, 128:], zeros], axis=0)
-
-
-def outer_kernel(amps, own0, own1, own2, shape0, shape1, shape2, cot, halo_a, halo_b, part, basis, mine, other, grad):
+    zeros = jnp.zeros((62, CHAN), BF16)
+    return jnp.concatenate([zeros, halo_a[which, row, COLS : COLS + 4], zeros], axis=0)
+
+
+def outer_kernel(amps, ends, shape0, shape1, cot, halo_a, halo_b, part, basis, mine, other, grad):
     lat, first = position()
     even = lat % 2 == 0
 
     def run(wide):
         for place, row in enumerate((0, 1, 14, 15)):
-            near, far, last = [], [], []
+            near, far = [], []
             for at in range(row - 2, row + 3):
-                inside = 0 <= at < ROWS
-                if inside:
-                    near.append(own0[at])
-                else:
-                    near.append(halo_row(halo_a, halo_b, 0, at + 2 if at < 0 else at - ROWS, even, at < 0))
-                if wide:
-                    zeros = jnp.zeros((128, CHAN), BF16)
-                    far.append(own1[at] if inside else zeros if at < 0 else far_halo_row(halo_a, 0, at - ROWS))
-                    last.append(own2[at] if 0 <= at < 5 else zeros[:32])
+                inside, index = 0 <= at < ROWS, at + 2 if at < 0 else at - ROWS
+                near.append(None if inside else halo_row(halo_a, halo_b, 0, index, even, at < 0))
+                far.append(None if inside or at < 0 else far_halo_row(halo_a, 0, index))
             at = (row + 2) * 288
             values = filtered(shape0, at, amps, first, row + 2, near)
-            if wide:
+            values = plus(values, [ends[place * 288 + k * PAD : place * 288 + (k + 1) * PAD, :] for k in range(3)])
+            if wide and row > 2:
                 values = plus(values, filtered(shape1, at, amps, first, row + 2, far))
-            if wide and row < 2:
-                values = plus(values, filtered(shape2, at, amps, first, row + 2, last))
             store_basis(basis, place, values)
 
     pl.when(lat != 0)(lambda: run(False))
     pl.when(lat == 0)(lambda: run(True))
-    ends = jnp.concatenate([cot[0:2, :PAD, :], cot[14:16, :PAD, :]], axis=0).reshape(4 * PAD, CHAN)
-    product = part[...] + times_cotangent(ends, basis[...])
+    cells = jnp.concatenate([cot[0:2, :PAD, :], cot[14:16, :PAD, :]], axis=0).reshape(4 * PAD, CHAN)
+    product = part[...] + times_cotangent(cells, basis[...])
     for k in range(3):
         grad[k * 128 : (k + 1) * 128, :] = product[:, k * 128 : (k + 1) * 128].T
     core = lat % 2
@@ -480,9 +482,9 @@
     amps = amplitude.transpose(2, 0, 1)
 
     field, cot = features.transpose(0, 2, 1, 3), cotangent.transpose(0, 2, 1, 3)
-    field, cot = (pltpu.with_memory_space_constraint(x, pltpu.HBM) for x in (field, cot))
+    field, cot, spans, amps = (pltpu.with_memory_space_constraint(x, pltpu.HBM) for x in (field, cot, row_spans, amps))
     token = shape((8, 128), F32)
-    near_a, near_b = shape((2, OTHERS + 1, ROWS, CHAN)), shape((2, OTHERS, ROWS, CHAN))
+    near_a, near_b = shape((2, OTHERS, ROWS, CHAN)), shape((2, OTHERS, ROWS, CHAN))
     second = shape((2, SECOND, ROWS, CHAN))
     polar = shape((2, 65, ROWS, CHAN))
     scratch = [
@@ -505,22 +507,20 @@
 
     gathered = shape((ROWS, 128, CHAN))
     tables = [shape((20 * 288, 256)), shape((20 * 288, 256)), shape((5 * 288, 256))]
-    own_f, own_c, *shapes = call(
-        pre_kernel,
-        [gathered, gathered, *tables],
-        [pltpu.VMEM((2, COLS, ROWS, CHAN), BF16), pltpu.SemaphoreType.DMA((6,))],
-        2 * 10**8,
-        (row_spans,),
-        (field, cot),
-        space=pltpu.HBM,
-    )
     row_flops = 2 * 288 * 640 * CHAN
+    scratch = [
+        pltpu.VMEM((2, COLS, ROWS, CHAN), BF16),
+        pltpu.SMEM((128,), jnp.int32),
+        pltpu.SMEM((5, 3, 128), F32),
+        pltpu.SemaphoreType.DMA((9,)),
+    ]
+    outs = [gathered, gathered, *tables, shape((ROWS * 288, CHAN), F32), shape((5, 3, 128), F32)]
+    own_f, own_c, *shapes, center, amps = call(prepare_kernel, outs, scratch, 2 * 10**8, (), (field, cot, spans, amps), space=pltpu.HBM)
     scalars = (amps,)
-    (center,) = call(center_kernel, [shape((12 * 288, CHAN), F32)], [], 10**8, scalars, (own_f, shapes[0]))
     own2 = shape((5, 32, CHAN))
     own0_f, own0_c, own1_f, own1_c, own2_f, own2_c, lat_a, lat_b = call(
         assemble_kernel,
-        [gathered] * 4 + [own2] * 2 + [shape((2, 2, 160, CHAN)), shape((2, 2, 176, CHAN))],
+        [gathered] * 4 + [own2] * 2 + [shape((2, 2, 128, CHAN)), shape((2, 2, 144, CHAN))],
         [],
         0,
         (),
@@ -529,17 +529,17 @@
     halo_a = lax.ppermute(lat_a, "lat", pairs_of_lat(0))
     halo_b = lax.ppermute(lat_b, "lat", pairs_of_lat(1))
 
-    filters = (own0_f, own1_f, own2_f, *shapes, own0_c)
-    outs = [shape((12 * PAD, 384)), shape((128, 384), F32)]
-    inner, part = call(inner_kernel, outs, [], 12 * row_flops, scalars, (center, *filters))
-    half = shape((192, CHAN), F32)
+    own = (own0_f, own1_f, own2_f, *shapes, own0_c)
+    half, ends = shape((192, CHAN), F32), shape((4 * 288, CHAN), F32)
+    outs = [shape((12 * PAD, 384)), shape((128, 384), F32), ends]
+    inner, part, ends = call(inner_kernel, outs, [], 12 * row_flops, scalars, (center, *own))
     outer, mine, other = call(
         outer_kernel,
         [shape((4 * PAD, 384)), half, half],
         [pltpu.VMEM((384, CHAN), F32)],
         4 * row_flops,
         scalars,
-        (*filters, halo_a, halo_b, part),
+        (ends, shapes[0], shapes[1], own0_c, halo_a, halo_b, part),
     )
 
     def add(*parts, after=(), more=True, dtype=BF16):
@@ -567,14 +567,15 @@
         (),
         (inner, outer, mix_weight.reshape(384, CHAN), before),
     )
-    mine, before = add(mine, *steps, after=(done,))
+    (mine,) = add(mine, *steps, after=(done,), more=False)
     steps = [flip(mine, "lon", bit) for bit in (1, 2, 3)]
+    mine, before = add(mine, *steps)
+    steps = [flip(mine, "lat", bit) for bit in (2, 4, 6)]
     grad, done = back(0, before)
     mine, before = add(mine, *steps, after=(done,))
-    steps = [flip(mine, "lat", bit) for bit in (2, 4, 6)]
+    step = lax.ppermute(mine, LL, z_pairs())
     grad, done = back(1, before, grad)
-    (mine,) = add(mine, *steps, after=(done,), more=False)
-    (mine,) = add(mine, lax.ppermute(mine, LL, z_pairs()), more=False, dtype=F32)
+    (mine,) = add(mine, step, after=(done,), more=False, dtype=F32)
     other = flip(mine, "lat", 1)
     first_half = lax.axis_index("lat") % 2 == 0
     whole = jnp.concatenate([jnp.where(first_half, mine, other), jnp.where(first_half, other, mine)])

time: 70.1 us -> 69.1 us (0.986)
  starting transfers between devices: 41.9 us -> 44.7 us
  waiting for transfers between devices: 8.8 us -> 6.66 us
  local copies, waits for them, and re-layouts: 1.36 us -> 0.01 us
    ppermute x11, starting transfers between devices: 19 us -> 21 us  [flip(): lax.ppermute(x, axis, [(i, i ^ bit) for i in range(lax.axis_size(axis))])]
    ppermute x1, waiting for transfers between devices: 1.87 us -> 0.01 us  [body(): step = lax.ppermute(mine, LL, z_pairs())]
    ppermute x1, waiting for transfers between devices: 1.82 us -> 0.01 us  [body(): halo_b = lax.ppermute(lat_b, 'lat', pairs_of_lat(1))]
    ppermute x11, waiting for transfers between devices: 5.09 us -> 6.64 us  [flip(): lax.ppermute(x, axis, [(i, i ^ bit) for i in range(lax.axis_size(axis))])]
    unnamed x8 -> x2, local copies, waits for them, and re-layouts: 1.36 us -> 0.01 us
    ppermute x1, starting transfers between devices: 0.74 us -> 2.02 us  [body(): halo_a = lax.ppermute(lat_a, 'lat', pairs_of_lat(0))]
    pallas_call x14 -> x13, Pallas kernels: 16.2 us -> 15.9 us  [call(): pl.pallas_call(kernel, out_shape=outs, in_specs=[SMEM] * len(scalars) + [...]
  transfers between devices with their start and end apart: 19 -> 19, of which waited for: 9 -> 7; matrix products, arithmetic and copies ran while one was open for 0% -> 0% of each run, Pallas kernels for 18% -> 19%
where the time goes in v5:
time: 69.1 us; the launch traced here: 68.9 us
  starting transfers between devices  44.7 us (65%)
  Pallas kernels  15.9 us (23%)
  waiting for transfers between devices  6.66 us (10%)
  between operations  0.83 us (1%)
  other arithmetic  0.71 us (1%)
    ppermute x11, starting transfers between devices, flip(): lax.ppermute(x, axis, [(i, i ^ bit) for i in range(lax.axis_size(axis))])  21 us
    ppermute x5, starting transfers between devices, body(): lax.ppermute(messages[index], LL, pairs_of_lon(*targets[index]))  16.3 us
    pallas_call x13, Pallas kernels, call(): pl.pallas_call(kernel, out_shape=outs, in_specs=[SMEM] * len(scalars) + [...  15.9 us
    ppermute x11, waiting for transfers between devices, flip(): lax.ppermute(x, axis, [(i, i ^ bit) for i in range(lax.axis_size(axis))])  6.64 us
    ppermute x1, starting transfers between devices, body(): step = lax.ppermute(mine, LL, z_pairs())  2.77 us
    ppermute x1, starting transfers between devices, body(): halo_b = lax.ppermute(lat_b, 'lat', pairs_of_lat(1))  2.63 us
    ppermute x1, starting transfers between devices, body(): halo_a = lax.ppermute(lat_a, 'lat', pairs_of_lat(0))  2.02 us
  transfers between devices with their start and end apart: 19, of which 7 were waited for; matrix products, arithmetic and copies ran while one was open for 0% of the time, Pallas kernels for 19%

profile of v5, /device:TPU:1, one launch (start us, length us, event | category | flops | bytes accessed | tf_op | source)
XLA Modules:
  0.0 68.9 jit_solution(2540264510236431105)
XLA Ops:
  0.6 1.1 %shard_map.77 = (bf16[2,9,16,128]{3,2,1,0:T(8,128)(2,1)S(1)}, bf16[2,18,16,128]{3,2,1,0:T(8,128)(2,1)S(1)}, bf16[2,65,16,128]{3,2,1,0:T(8,128)(2,1)S(1)}, bf16[2...) custom-call(bf16[1,90,16,128]{3,2,1,0:T(8,128)(2,1)} %bitcast.8, bf16[1,90,16,128]{3,2,1,0:T(8,128)(2,1)} %bitcast.10), custom_call_target="tpu_custom_call" | custom-call | bytes 2097152 | tf_op jit(solution)/shard_map/pallas_call | solution.py:466
  1.8 0.7 %collective-permute-start.2 = (bf16[2,65,16,128]{3,2,1,0:T(8,128)(2,1)S(1)}, bf16[2,65,16,128]{3,2,1,0:T(8,128)(2,1)S(1)}, u32[]{:S(2)}, u32[]{:S(2)}) collective-permute-start(bf16[2,65,16,128]{3,2,1,0:T(8,128)(2,1)S(1)} %get-tuple-element.47), channel_id=1, source_target_pairs={{0,28},{4,8},{8,4},{12,16},{16,12},{20,24},{24,20},{28,0},{1,29},{... | collective-permute-start | bytes 1597448 | tf_op jit(solution)/shard_map/ppermute | solution.py:506
  2.5 3.9 %collective-permute-start.4 = (bf16[2,65,16,128]{3,2,1,0:T(8,128)(2,1)S(1)}, bf16[2,65,16,128]{3,2,1,0:T(8,128)(2,1)S(1)}, u32[]{:S(2)}, u32[]{:S(2)}) collective-permute-start(bf16[2,65,16,128]{3,2,1,0:T(8,128)(2,1)S(1)} %get-tuple-element.49), channel_id=1, source_target_pairs={{0,4},{4,0},{8,12},{12,8},{16,20},{20,16},{24,28},{28,24},{32,36},... | collective-permute-start | bytes 1597448 | tf_op jit(solution)/shard_map/ppermute | solution.py:506
  6.4 10.4 %collective-permute-start.1 = (bf16[2,18,16,128]{3,2,1,0:T(8,128)(2,1)S(1)}, bf16[2,18,16,128]{3,2,1,0:T(8,128)(2,1)S(1)}, u32[]{:S(2)}, u32[]{:S(2)}) collective-permute-start(bf16[2,18,16,128]{3,2,1,0:T(8,128)(2,1)S(1)} %get-tuple-element.46), channel_id=1, source_target_pairs={{32,60},{36,40},{40,36},{44,48},{48,44},{52,56},{56,52},{60,32},{3... | collective-permute-start | bytes 442376 | tf_op jit(solution)/shard_map/ppermute | solution.py:506
  16.8 0.7 collective-permute-start
  17.5 0.7 collective-permute-start.3
  18.1 4.3 %shard_map.76 = (bf16[16,128,128]{2,1,0:T(8,128)(2,1)S(1)}, bf16[16,128,128]{2,1,0:T(8,128)(2,1)S(1)}, bf16[5760,256]{1,0:T(8,128)(2,1)S(1)}, bf16[5760,256]{1,0...) custom-call(bf16[1,90,16,128]{3,2,1,0:T(8,128)(2,1)} %bitcast.9, ...), custom_call_target="tpu_custom_call" | custom-call | flops 200000000 | bytes 10796544 | tf_op jit(solution)/shard_map/pallas_call | solution.py:466
  22.4 0.0 collective-permute-done.near_a
  22.4 0.0 collective-permute-done.3.near_b
  22.4 0.0 collective-permute-done.1.second_a
  22.4 0.0 collective-permute-done.2.polar_a
  22.5 0.0 collective-permute-done.4.polar_b
  22.5 0.4 shard_map.78
  22.9 2.6 %collective-permute-start.6 = (bf16[2,2,144,128]{3,2,1,0:T(8,128)(2,1)S(1)}, bf16[2,2,144,128]{3,2,1,0:T(8,128)(2,1)S(1)}, u32[]{:S(2)}, u32[]{:S(2)}) collective-permute-start(bf16[2,2,144,128]{3,2,1,0:T(8,128)(2,1)S(1)} %get-tuple-element.60), channel_id=1, source_target_pairs={{32,64},{64,32},{96,128},{128,96},{160,192},{192,160},{33,65},{65,... | collective-permute-start | bytes 442376 | tf_op jit(solution)/shard_map/ppermute | solution.py:530
  25.6 2.0 %collective-permute-start.5 = (bf16[2,2,128,128]{3,2,1,0:T(8,128)(2,1)S(1)}, bf16[2,2,128,128]{3,2,1,0:T(8,128)(2,1)S(1)}, u32[]{:S(2)}, u32[]{:S(2)}) collective-permute-start(bf16[2,2,128,128]{3,2,1,0:T(8,128)(2,1)S(1)} %get-tuple-element.59), channel_id=1, source_target_pairs={{0,32},{32,0},{64,96},{96,64},{128,160},{160,128},{192,224},{224,1... | collective-permute-start | bytes 393224 | tf_op jit(solution)/shard_map/ppermute | solution.py:529
  27.6 1.9 %shard_map.79 = (bf16[1152,384]{1,0:T(8,128)(2,1)S(1)}, f32[128,384]{1,0:T(8,128)S(1)}, f32[1152,128]{1,0:T(8,128)S(1)}) custom-call(f32[5,3,128]{2,1,0:T(4,128)S(1)} %get-tuple-element.41.amps, f32[4608,128]{1,0:T(8,128)S(1)} %get-tuple-element.42.tie.center, bf16[16,128,128]{2,1,0:T(8,128)(2,1)S(1)} %get-tuple-element.50.own0, ...), custom_call_target="tpu_custom_call" | custom-call | flops 566231040 | bytes 12279808 | tf_op jit(solution)/shard_map/pallas_call | solution.py:466
  29.5 0.0 collective-permute-done.5.halo_a
  29.5 0.0 collective-permute-done.6.halo_b
  29.5 0.0 copy-start
  29.5 1.5 %shard_map.80 = (bf16[384,384]{1,0:T(8,128)(2,1)S(1)}, f32[192,128]{1,0:T(8,128)S(1)}, f32[192,128]{1,0:T(8,128)S(1)}) custom-call(f32[5,3,128]{2,1,0:T(4,128)S(1)} %get-tuple-element.41.amps, f32[1152,128]{1,0:T(8,128)S(1)} %get-tuple-element.58.ends, bf16[5760,256]{1,0:T(8,128)(2,1)S(1)} %get-tuple-element.53.shape0, ...), custom_call_target="tpu_custom_call" | custom-call | flops 188743680 | bytes 7979008 | tf_op jit(solution)/shard_map/pallas_call | solution.py:466
  31.0 1.7 %collective-permute-start.7 = (f32[192,128]{1,0:T(8,128)S(1)}, f32[192,128]{1,0:T(8,128)S(1)}, u32[]{:S(2)}, u32[]{:S(2)}) collective-permute-start(f32[192,128]{1,0:T(8,128)S(1)} %get-tuple-element.64), channel_id=1, source_target_pairs={{0,32},{32,0},{64,96},{96,64},{128,160},{160,128},{192,224},{224,1... | collective-permute-start | bytes 294920 | tf_op jit(solution)/shard_map/ppermute | solution.py:457
  32.7 0.9 %collective-permute-done.7.refs_1_ = f32[192,128]{1,0:T(8,128)S(1)} collective-permute-done((f32[192,128]{1,0:T(8,128)S(1)}, f32[192,128]{1,0:T(8,128)S(1)}, u32[]{:S(2)}, u32[]{:S(2)}) %collective-permute-start.7) | collective-permute-done | bytes 98336 | tf_op jit(solution)/shard_map/ppermute | solution.py:457
  33.7 2.8 %collective-permute-start.10 = (bf16[192,128]{1,0:T(8,128)(2,1)S(1)}, bf16[192,128]{1,0:T(8,128)(2,1)S(1)}, u32[]{:S(2)}, u32[]{:S(2)}) collective-permute-start(bf16[192,128]{1,0:T(8,128)(2,1)S(1)} %get-tuple-element.69.refs_0_), channel_id=1, source_target_pairs={{0,3},{1,2},{2,1},{3,0},{4,7},{5,6},{6,5},{7,4},{8,11},{9,10},{10,... | collective-permute-start | bytes 147464 | tf_op jit(solution)/shard_map/ppermute | solution.py:457
  36.5 0.0 collective-permute-start.8
  36.5 1.3 %collective-permute-start.9 = (bf16[192,128]{1,0:T(8,128)(2,1)S(1)}, bf16[192,128]{1,0:T(8,128)(2,1)S(1)}, u32[]{:S(2)}, u32[]{:S(2)}) collective-permute-start(bf16[192,128]{1,0:T(8,128)(2,1)S(1)} %get-tuple-element.69.refs_0_), channel_id=1, source_target_pairs={{0,2},{1,3},{2,0},{3,1},{4,6},{5,7},{6,4},{7,5},{8,10},{9,11},{10,... | collective-permute-start | bytes 147464 | tf_op jit(solution)/shard_map/ppermute | solution.py:457
  37.8 0.0 copy-done
  37.8 1.3 %shard_map.82 = (bf16[1,90,16,128]{3,2,1,0:T(8,128)(2,1)}, f32[8,128]{1,0:T(8,128)S(1)}) custom-call(bf16[1152,384]{1,0:T(8,128)(2,1)S(1)} %get-tuple-element.57.inner, bf16[384,384]{1,0:T(8,128)(2,1)S(1)} %get-tuple-element.62.outer, bf16[384,128]{1,0:T(8,128)(2,1)S(1)} %bitcast.7, f32[8,128]{1,0:T(8,128)S(1)} %get-tuple-element.65.before), custom_call_target="tpu_custom_call" | custom-call | flops 150994944 | bytes 1654784 | tf_op jit(solution)/shard_map/pallas_call | solution.py:466
  39.1 0.0 collective-permute-done.10.refs_3_
  39.1 0.4 collective-permute-done.8.refs_1_
  39.5 1.5 %collective-permute-done.9.refs_2_ = bf16[192,128]{1,0:T(8,128)(2,1)S(1)} collective-permute-done((bf16[192,128]{1,0:T(8,128)(2,1)S(1)}, bf16[192,128]{1,0:T(8,128)(2,1)S(1)}, u32[]{:S(2)}, u32[]{:S(2)}) %collective-permute-start.9) | collective-permute-done | bytes 49184 | tf_op jit(solution)/shard_map/ppermute | solution.py:457
  41.0 0.4 collective-permute-start.11
  41.3 1.1 %collective-permute-start.12 = (bf16[192,128]{1,0:T(8,128)(2,1)S(1)}, bf16[192,128]{1,0:T(8,128)(2,1)S(1)}, u32[]{:S(2)}, u32[]{:S(2)}) collective-permute-start(bf16[192,128]{1,0:T(8,128)(2,1)S(1)} %shard_map.83.refs_0_), channel_id=1, source_target_pairs={{0,8},{4,12},{8,0},{12,4},{16,24},{20,28},{24,16},{28,20},{1,9},{5... | collective-permute-start | bytes 147464 | tf_op jit(solution)/shard_map/ppermute | solution.py:457
  42.5 2.5 %collective-permute-start.13 = (bf16[192,128]{1,0:T(8,128)(2,1)S(1)}, bf16[192,128]{1,0:T(8,128)(2,1)S(1)}, u32[]{:S(2)}, u32[]{:S(2)}) collective-permute-start(bf16[192,128]{1,0:T(8,128)(2,1)S(1)} %shard_map.83.refs_0_), channel_id=1, source_target_pairs={{0,12},{4,8},{8,4},{12,0},{16,28},{20,24},{24,20},{28,16},{1,13},{... | collective-permute-start | bytes 147464 | tf_op jit(solution)/shard_map/ppermute | solution.py:457
  44.9 0.0 collective-permute-done.11.refs_1_
  44.9 0.8 %collective-permute-done.12.refs_2_ = bf16[192,128]{1,0:T(8,128)(2,1)S(1)} collective-permute-done((bf16[192,128]{1,0:T(8,128)(2,1)S(1)}, bf16[192,128]{1,0:T(8,128)(2,1)S(1)}, u32[]{:S(2)}, u32[]{:S(2)}) %collective-permute-start.12) | collective-permute-done | bytes 49184 | tf_op jit(solution)/shard_map/ppermute | solution.py:457
  45.8 0.8 %collective-permute-done.13.refs_3_ = bf16[192,128]{1,0:T(8,128)(2,1)S(1)} collective-permute-done((bf16[192,128]{1,0:T(8,128)(2,1)S(1)}, bf16[192,128]{1,0:T(8,128)(2,1)S(1)}, u32[]{:S(2)}, u32[]{:S(2)}) %collective-permute-start.13) | collective-permute-done | bytes 49184 | tf_op jit(solution)/shard_map/ppermute | solution.py:457
  46.6 3.5 %collective-permute-start.14 = (bf16[192,128]{1,0:T(8,128)(2,1)S(1)}, bf16[192,128]{1,0:T(8,128)(2,1)S(1)}, u32[]{:S(2)}, u32[]{:S(2)}) collective-permute-start(bf16[192,128]{1,0:T(8,128)(2,1)S(1)} %get-tuple-element.71.refs_0_), channel_id=1, source_target_pairs={{0,64},{32,96},{64,0},{96,32},{128,192},{160,224},{192,128},{224,1... | collective-permute-start | bytes 147464 | tf_op jit(solution)/shard_map/ppermute | solution.py:457
  50.1 1.1 %collective-permute-start.15 = (bf16[192,128]{1,0:T(8,128)(2,1)S(1)}, bf16[192,128]{1,0:T(8,128)(2,1)S(1)}, u32[]{:S(2)}, u32[]{:S(2)}) collective-permute-start(bf16[192,128]{1,0:T(8,128)(2,1)S(1)} %get-tuple-element.71.refs_0_), channel_id=1, source_target_pairs={{0,128},{32,160},{64,192},{96,224},{128,0},{160,32},{192,64},{224,... | collective-permute-start | bytes 147464 | tf_op jit(solution)/shard_map/ppermute | solution.py:457
  51.2 1.1 %collective-permute-start.16 = (bf16[192,128]{1,0:T(8,128)(2,1)S(1)}, bf16[192,128]{1,0:T(8,128)(2,1)S(1)}, u32[]{:S(2)}, u32[]{:S(2)}) collective-permute-start(bf16[192,128]{1,0:T(8,128)(2,1)S(1)} %get-tuple-element.71.refs_0_), channel_id=1, source_target_pairs={{0,192},{32,224},{64,128},{96,160},{128,64},{160,96},{192,0},{224,... | collective-permute-start | bytes 147464 | tf_op jit(solution)/shard_map/ppermute | solution.py:457
  52.3 2.4 %shard_map.85 = (f32[1,90,16,128]{3,2,1,0:T(8,128)S(1)}, f32[8,128]{1,0:T(8,128)S(1)}) custom-call(f32[5,3,128]{2,1,0:T(4,128)S(1)} %get-tuple-element.41.amps, bf16[16,128,128]{2,1,0:T(8,128)(2,1)S(1)} %get-tuple-element.56.cot.own0, bf16[16,128,128]{2,1,0:T(8,128)(2,1)S(1)} %get-tuple-element.67.own1, bf16[5,32,128]{2,1,0:T(8,128)(2,1)S(1)} %get-tuple-element.68.own2, ...), custom_call_target="tpu_custom_call" | custom-call | flops 94371840 | bytes 8847360 | tf_op jit(solution)/shard_map/pallas_call | solution.py:466
  54.7 0.0 collective-permute-done.14.refs_1_
  54.7 0.0 collective-permute-done.15.refs_2_
  54.7 1.2 %collective-permute-done.16.refs_3_ = bf16[192,128]{1,0:T(8,128)(2,1)S(1)} collective-permute-done((bf16[192,128]{1,0:T(8,128)(2,1)S(1)}, bf16[192,128]{1,0:T(8,128)(2,1)S(1)}, u32[]{:S(2)}, u32[]{:S(2)}) %collective-permute-start.16) | collective-permute-done | bytes 49184 | tf_op jit(solution)/shard_map/ppermute | solution.py:457
  56.0 2.8 %collective-permute-start.17 = (bf16[192,128]{1,0:T(8,128)(2,1)S(1)}, bf16[192,128]{1,0:T(8,128)(2,1)S(1)}, u32[]{:S(2)}, u32[]{:S(2)}) collective-permute-start(bf16[192,128]{1,0:T(8,128)(2,1)S(1)} %get-tuple-element.77.refs_0_), channel_id=1, source_target_pairs={{0,144},{4,148},{8,152},{12,156},{16,128},{20,132},{24,136},{28,14... | collective-permute-start | bytes 147464 | tf_op jit(solution)/shard_map/ppermute | solution.py:576
  58.7 2.9 %shard_map.87 = (f32[1,90,16,128]{3,2,1,0:T(8,128)}, f32[8,128]{1,0:T(8,128)S(1)}) custom-call(f32[5,3,128]{2,1,0:T(4,128)S(1)} %get-tuple-element.41.amps, bf16[16,128,128]{2,1,0:T(8,128)(2,1)S(1)} %get-tuple-element.56.cot.own0, bf16[16,128,128]{2,1,0:T(8,128)(2,1)S(1)} %get-tuple-element.67.own1, bf16[5,32,128]{2,1,0:T(8,128)(2,1)S(1)} %get-tuple-element.68.own2, ...), custom_call_target="tpu_custom_call" | custom-call | flops 94371840 | bytes 9584640 | tf_op jit(solution)/shard_map/pallas_call | solution.py:466
  61.7 0.0 collective-permute-done.17.refs_1_
  61.7 5.5 %collective-permute-start.18 = (f32[192,128]{1,0:T(8,128)S(1)}, f32[192,128]{1,0:T(8,128)S(1)}, u32[]{:S(2)}, u32[]{:S(2)}) collective-permute-start(f32[192,128]{1,0:T(8,128)S(1)} %shard_map.88), channel_id=1, source_target_pairs={{0,32},{32,0},{64,96},{96,64},{128,160},{160,128},{192,224},{224,1... | collective-permute-start | bytes 294920 | tf_op jit(solution)/shard_map/ppermute | solution.py:457
  67.2 0.9 %collective-permute-done.18 = f32[192,128]{1,0:T(8,128)S(1)} collective-permute-done((f32[192,128]{1,0:T(8,128)S(1)}, f32[192,128]{1,0:T(8,128)S(1)}, u32[]{:S(2)}, u32[]{:S(2)}) %collective-permute-start.18) | collective-permute-done | bytes 98336 | tf_op jit(solution)/shard_map/ppermute | solution.py:457
  68.2 0.7 %maximum_multiply_fusion = f32[384,128]{1,0:T(8,128)} fusion(f32[192,128]{1,0:T(8,128)S(1)} %get-tuple-element.80, f32[192,128]{1,0:T(8,128)S(1)} %get-tuple-element.79), kind=kLoop, calls=%fused_computation | loop fusion | flops 98304 | bytes 393216 | tf_op jit(solution)/shard_map/mul | solution.py:582
  (6 shorter events, 0.1 us)
Async XLA Ops:
  1.8 20.7 %collective-permute-start.2 = (bf16[2,65,16,128]{3,2,1,0:T(8,128)(2,1)S(1)}, bf16[2,65,16,128]{3,2,1,0:T(8,128)(2,1)S(1)}, u32[]{:S(2)}, u32[]{:S(2)}) collective-permute-start(bf16[2,65,16,128]{3,2,1,0:T(8,128)(2,1)S(1)} %get-tuple-element.47), channel_id=1, source_target_pairs={{0,28},{4,8},{8,4},{12,16},{16,12},{20,24},{24,20},{28,0},{1,29},{... | collective-permute-start | bytes 1597448 | tf_op jit(solution)/shard_map/ppermute | solution.py:506
  2.5 20.0 %collective-permute-start.4 = (bf16[2,65,16,128]{3,2,1,0:T(8,128)(2,1)S(1)}, bf16[2,65,16,128]{3,2,1,0:T(8,128)(2,1)S(1)}, u32[]{:S(2)}, u32[]{:S(2)}) collective-permute-start(bf16[2,65,16,128]{3,2,1,0:T(8,128)(2,1)S(1)} %get-tuple-element.49), channel_id=1, source_target_pairs={{0,4},{4,0},{8,12},{12,8},{16,20},{20,16},{24,28},{28,24},{32,36},... | collective-permute-start | bytes 1597448 | tf_op jit(solution)/shard_map/ppermute | solution.py:506
  6.4 16.0 %collective-permute-start.1 = (bf16[2,18,16,128]{3,2,1,0:T(8,128)(2,1)S(1)}, bf16[2,18,16,128]{3,2,1,0:T(8,128)(2,1)S(1)}, u32[]{:S(2)}, u32[]{:S(2)}) collective-permute-start(bf16[2,18,16,128]{3,2,1,0:T(8,128)(2,1)S(1)} %get-tuple-element.46), channel_id=1, source_target_pairs={{32,60},{36,40},{40,36},{44,48},{48,44},{52,56},{56,52},{60,32},{3... | collective-permute-start | bytes 442376 | tf_op jit(solution)/shard_map/ppermute | solution.py:506
  16.8 5.6 %collective-permute-start = (bf16[2,9,16,128]{3,2,1,0:T(8,128)(2,1)S(1)}, bf16[2,9,16,128]{3,2,1,0:T(8,128)(2,1)S(1)}, u32[]{:S(2)}, u32[]{:S(2)}) collective-permute-start(bf16[2,9,16,128]{3,2,1,0:T(8,128)(2,1)S(1)} %get-tuple-element.45), channel_id=1, source_target_pairs={{64,92},{68,72},{72,68},{76,80},{80,76},{84,88},{88,84},{92,64},{9... | collective-permute-start | bytes 221192 | tf_op jit(solution)/shard_map/ppermute | solution.py:506
  17.5 5.0 %collective-permute-start.3 = (bf16[2,9,16,128]{3,2,1,0:T(8,128)(2,1)S(1)}, bf16[2,9,16,128]{3,2,1,0:T(8,128)(2,1)S(1)}, u32[]{:S(2)}, u32[]{:S(2)}) collective-permute-start(bf16[2,9,16,128]{3,2,1,0:T(8,128)(2,1)S(1)} %get-tuple-element.48), channel_id=1, source_target_pairs={{64,68},{68,64},{72,76},{76,72},{80,84},{84,80},{88,92},{92,88},{9... | collective-permute-start | bytes 221192 | tf_op jit(solution)/shard_map/ppermute | solution.py:506
  22.9 6.6 %collective-permute-start.6 = (bf16[2,2,144,128]{3,2,1,0:T(8,128)(2,1)S(1)}, bf16[2,2,144,128]{3,2,1,0:T(8,128)(2,1)S(1)}, u32[]{:S(2)}, u32[]{:S(2)}) collective-permute-start(bf16[2,2,144,128]{3,2,1,0:T(8,128)(2,1)S(1)} %get-tuple-element.60), channel_id=1, source_target_pairs={{32,64},{64,32},{96,128},{128,96},{160,192},{192,160},{33,65},{65,... | collective-permute-start | bytes 442376 | tf_op jit(solution)/shard_map/ppermute | solution.py:530
  25.6 4.0 %collective-permute-start.5 = (bf16[2,2,128,128]{3,2,1,0:T(8,128)(2,1)S(1)}, bf16[2,2,128,128]{3,2,1,0:T(8,128)(2,1)S(1)}, u32[]{:S(2)}, u32[]{:S(2)}) collective-permute-start(bf16[2,2,128,128]{3,2,1,0:T(8,128)(2,1)S(1)} %get-tuple-element.59), channel_id=1, source_target_pairs={{0,32},{32,0},{64,96},{96,64},{128,160},{160,128},{192,224},{224,1... | collective-permute-start | bytes 393224 | tf_op jit(solution)/shard_map/ppermute | solution.py:529
  29.5 8.3 %copy-start = (bf16[3,128,128]{2,1,0:T(8,128)(2,1)S(1)}, bf16[3,128,128]{2,1,0:T(8,128)(2,1)}, u32[]{:S(2)}) copy-start(bf16[3,128,128]{2,1,0:T(8,128)(2,1)} %weight.3) | copy-start | bytes 294916
  31.0 2.7 %collective-permute-start.7 = (f32[192,128]{1,0:T(8,128)S(1)}, f32[192,128]{1,0:T(8,128)S(1)}, u32[]{:S(2)}, u32[]{:S(2)}) collective-permute-start(f32[192,128]{1,0:T(8,128)S(1)} %get-tuple-element.64), channel_id=1, source_target_pairs={{0,32},{32,0},{64,96},{96,64},{128,160},{160,128},{192,224},{224,1... | collective-permute-start | bytes 294920 | tf_op jit(solution)/shard_map/ppermute | solution.py:457
  33.7 5.4 %collective-permute-start.10 = (bf16[192,128]{1,0:T(8,128)(2,1)S(1)}, bf16[192,128]{1,0:T(8,128)(2,1)S(1)}, u32[]{:S(2)}, u32[]{:S(2)}) collective-permute-start(bf16[192,128]{1,0:T(8,128)(2,1)S(1)} %get-tuple-element.69.refs_0_), channel_id=1, source_target_pairs={{0,3},{1,2},{2,1},{3,0},{4,7},{5,6},{6,5},{7,4},{8,11},{9,10},{10,... | collective-permute-start | bytes 147464 | tf_op jit(solution)/shard_map/ppermute | solution.py:457
  36.5 2.9 %collective-permute-start.8 = (bf16[192,128]{1,0:T(8,128)(2,1)S(1)}, bf16[192,128]{1,0:T(8,128)(2,1)S(1)}, u32[]{:S(2)}, u32[]{:S(2)}) collective-permute-start(bf16[192,128]{1,0:T(8,128)(2,1)S(1)} %get-tuple-element.69.refs_0_), channel_id=1, source_target_pairs={{0,1},{1,0},{2,3},{3,2},{4,5},{5,4},{6,7},{7,6},{8,9},{9,8},{10,11... | collective-permute-start | bytes 147464 | tf_op jit(solution)/shard_map/ppermute | solution.py:457
  36.5 4.4 %collective-permute-start.9 = (bf16[192,128]{1,0:T(8,128)(2,1)S(1)}, bf16[192,128]{1,0:T(8,128)(2,1)S(1)}, u32[]{:S(2)}, u32[]{:S(2)}) collective-permute-start(bf16[192,128]{1,0:T(8,128)(2,1)S(1)} %get-tuple-element.69.refs_0_), channel_id=1, source_target_pairs={{0,2},{1,3},{2,0},{3,1},{4,6},{5,7},{6,4},{7,5},{8,10},{9,11},{10,... | collective-permute-start | bytes 147464 | tf_op jit(solution)/shard_map/ppermute | solution.py:457
  41.0 3.9 %collective-permute-start.11 = (bf16[192,128]{1,0:T(8,128)(2,1)S(1)}, bf16[192,128]{1,0:T(8,128)(2,1)S(1)}, u32[]{:S(2)}, u32[]{:S(2)}) collective-permute-start(bf16[192,128]{1,0:T(8,128)(2,1)S(1)} %shard_map.83.refs_0_), channel_id=1, source_target_pairs={{0,4},{4,0},{8,12},{12,8},{16,20},{20,16},{24,28},{28,24},{1,5},{5... | collective-permute-start | bytes 147464 | tf_op jit(solution)/shard_map/ppermute | solution.py:457
  41.3 4.4 %collective-permute-start.12 = (bf16[192,128]{1,0:T(8,128)(2,1)S(1)}, bf16[192,128]{1,0:T(8,128)(2,1)S(1)}, u32[]{:S(2)}, u32[]{:S(2)}) collective-permute-start(bf16[192,128]{1,0:T(8,128)(2,1)S(1)} %shard_map.83.refs_0_), channel_id=1, source_target_pairs={{0,8},{4,12},{8,0},{12,4},{16,24},{20,28},{24,16},{28,20},{1,9},{5... | collective-permute-start | bytes 147464 | tf_op jit(solution)/shard_map/ppermute | solution.py:457
  42.5 4.2 %collective-permute-start.13 = (bf16[192,128]{1,0:T(8,128)(2,1)S(1)}, bf16[192,128]{1,0:T(8,128)(2,1)S(1)}, u32[]{:S(2)}, u32[]{:S(2)}) collective-permute-start(bf16[192,128]{1,0:T(8,128)(2,1)S(1)} %shard_map.83.refs_0_), channel_id=1, source_target_pairs={{0,12},{4,8},{8,4},{12,0},{16,28},{20,24},{24,20},{28,16},{1,13},{... | collective-permute-start | bytes 147464 | tf_op jit(solution)/shard_map/ppermute | solution.py:457
  46.6 8.1 %collective-permute-start.14 = (bf16[192,128]{1,0:T(8,128)(2,1)S(1)}, bf16[192,128]{1,0:T(8,128)(2,1)S(1)}, u32[]{:S(2)}, u32[]{:S(2)}) collective-permute-start(bf16[192,128]{1,0:T(8,128)(2,1)S(1)} %get-tuple-element.71.refs_0_), channel_id=1, source_target_pairs={{0,64},{32,96},{64,0},{96,32},{128,192},{160,224},{192,128},{224,1... | collective-permute-start | bytes 147464 | tf_op jit(solution)/shard_map/ppermute | solution.py:457
  50.1 4.6 %collective-permute-start.15 = (bf16[192,128]{1,0:T(8,128)(2,1)S(1)}, bf16[192,128]{1,0:T(8,128)(2,1)S(1)}, u32[]{:S(2)}, u32[]{:S(2)}) collective-permute-start(bf16[192,128]{1,0:T(8,128)(2,1)S(1)} %get-tuple-element.71.refs_0_), channel_id=1, source_target_pairs={{0,128},{32,160},{64,192},{96,224},{128,0},{160,32},{192,64},{224,... | collective-permute-start | bytes 147464 | tf_op jit(solution)/shard_map/ppermute | solution.py:457
  51.2 4.7 %collective-permute-start.16 = (bf16[192,128]{1,0:T(8,128)(2,1)S(1)}, bf16[192,128]{1,0:T(8,128)(2,1)S(1)}, u32[]{:S(2)}, u32[]{:S(2)}) collective-permute-start(bf16[192,128]{1,0:T(8,128)(2,1)S(1)} %get-tuple-element.71.refs_0_), channel_id=1, source_target_pairs={{0,192},{32,224},{64,128},{96,160},{128,64},{160,96},{192,0},{224,... | collective-permute-start | bytes 147464 | tf_op jit(solution)/shard_map/ppermute | solution.py:457
  56.0 5.7 %collective-permute-start.17 = (bf16[192,128]{1,0:T(8,128)(2,1)S(1)}, bf16[192,128]{1,0:T(8,128)(2,1)S(1)}, u32[]{:S(2)}, u32[]{:S(2)}) collective-permute-start(bf16[192,128]{1,0:T(8,128)(2,1)S(1)} %get-tuple-element.77.refs_0_), channel_id=1, source_target_pairs={{0,144},{4,148},{8,152},{12,156},{16,128},{20,132},{24,136},{28,14... | collective-permute-start | bytes 147464 | tf_op jit(solution)/shard_map/ppermute | solution.py:576
  61.7 6.5 %collective-permute-start.18 = (f32[192,128]{1,0:T(8,128)S(1)}, f32[192,128]{1,0:T(8,128)S(1)}, u32[]{:S(2)}, u32[]{:S(2)}) collective-permute-start(f32[192,128]{1,0:T(8,128)S(1)} %shard_map.88), channel_id=1, source_target_pairs={{0,32},{32,0},{64,96},{96,64},{128,160},{160,128},{192,224},{224,1... | collective-permute-start | bytes 294920 | tf_op jit(solution)/shard_map/ppermute | solution.py:457

commit v6 on v5

--- a/solution.py
+++ b/solution.py
@@ -17,7 +17,7 @@
 LL = ("lat", "lon")
 POLAR_FAR = 40
 SECOND = 18
-OTHERS = 9
+FEW = 5
 
 
 def offsets_of(group):
@@ -81,12 +81,12 @@
     return amps[tap, k, row_of(first, ext)]
 
 
-def pack_kernel(field, cot, near_a, second_a, polar_a, near_b, polar_b, whole, sems):
+def pack_kernel(field, cot, few_a, second_a, polar_a, few_b, polar_b, whole, sems):
     lat, odd = lax.axis_index("lat"), lax.axis_index("lon") % 2 == 1
 
     def edges(is_odd):
-        def part(out, width, right, sem):
-            source, target = pl.ds(COLS - width if right else 0, width), pl.ds(0, width)
+        def part(out, width, right, sem, skip=0):
+            source, target = pl.ds(COLS - width - skip if right else skip, width), pl.ds(0, width)
             return [
                 pltpu.make_async_copy(x.at[0, source], out.at[i, target], sems.at[sem + i]) for i, x in enumerate((field, cot))
             ]
@@ -97,8 +97,14 @@
             for copy in copies:
                 copy.wait()
 
-        pl.when(lat >= 2)(lambda: run(part(near_a, OTHERS, is_odd, 0) + part(near_b, OTHERS, not is_odd, 2)))
+        pl.when(lat >= 4)(lambda: run(part(few_a, FEW, is_odd, 0) + part(few_b, FEW, not is_odd, 2)))
         pl.when(lat == 1)(lambda: run(part(second_a, SECOND, is_odd, 0) + part(polar_b, SECOND, not is_odd, 2)))
+
+        @pl.when((lat == 2) | (lat == 3))
+        def _():
+            nearest = part(few_a, FEW, not is_odd, 2)
+            run(part(second_a, SECOND, is_odd, 0) + nearest + part(few_b, FEW, not is_odd, 4, skip=FEW))
+
 
         @pl.when(lat == 0)
         def _():
@@ -163,7 +169,7 @@
             center[at : at + PAD, :] = values[k]
 
 
-def assemble_kernel(old_f, old_c, near_a, second_a, polar_a, near_b, polar_b, tie, *outs):
+def assemble_kernel(old_f, old_c, few_a, second_a, polar_a, few_b, polar_b, tie, *outs):
     lat = lax.axis_index("lat")
     odd = lax.axis_index("lon") % 2 == 1
     groups = ((outs[0], outs[2], outs[4]), (outs[1], outs[3], outs[5]))
@@ -178,12 +184,22 @@
         own0, own1, own2 = groups[which]
         own0[...] = (old_f, old_c)[which][...]
 
-        @pl.when(lat >= 2)
-        def _(which=which, own0=own0):
-            left = jnp.where(odd, near_b[which], near_a[which])
-            right = jnp.where(odd, near_a[which], near_b[which])
-            own0[:, 112 - OTHERS : 112, :] = jnp.swapaxes(left, 0, 1)
-            own0[:, 112 : 112 + OTHERS, :] = jnp.swapaxes(right, 0, 1)
+        def put_near(left, right, own0=own0):
+            width = left.shape[0]
+            own0[:, 112 - width : 112, :] = jnp.swapaxes(left, 0, 1)
+            own0[:, 112 : 112 + width, :] = jnp.swapaxes(right, 0, 1)
+
+        @pl.when(lat >= 4)
+        def _(which=which, put_near=put_near):
+            a, b = few_a[which], few_b[which]
+            put_near(jnp.where(odd, b, a), jnp.where(odd, a, b))
+
+        @pl.when((lat == 2) | (lat == 3))
+        def _(which=which, put_near=put_near):
+            near, next_ones = few_a[which], few_b[which]
+            left = jnp.where(odd, jnp.concatenate([next_ones, near]), second_a[which, SECOND - 2 * FEW :])
+            right = jnp.where(odd, second_a[which, : 2 * FEW], jnp.concatenate([near, next_ones]))
+            put_near(left, right)
 
         @pl.when(lat == 1)
         def _(which=which, own0=own0, own1=own1):
@@ -484,7 +500,7 @@
     field, cot = features.transpose(0, 2, 1, 3), cotangent.transpose(0, 2, 1, 3)
     field, cot, spans, amps = (pltpu.with_memory_space_constraint(x, pltpu.HBM) for x in (field, cot, row_spans, amps))
     token = shape((8, 128), F32)
-    near_a, near_b = shape((2, OTHERS, ROWS, CHAN)), shape((2, OTHERS, ROWS, CHAN))
+    few = shape((2, FEW, ROWS, CHAN))
     second = shape((2, SECOND, ROWS, CHAN))
     polar = shape((2, 65, ROWS, CHAN))
     scratch = [
@@ -493,17 +509,24 @@
     ]
     messages = call(
         pack_kernel,
-        [near_a, second, polar, near_b, polar],
+        [few, second, polar, few, polar],
         scratch,
         0,
         (),
         (field, cot),
         space=pltpu.HBM,
     )
-    targets = ((1, range(2, 8)), (1, (1,)), (1, (0,)), (0, range(2, 8)), (0, (0, 1)))
+    a, b = 1, 0
+    targets = (
+        pairs_of_lon(a, range(4, 8)) + pairs_of_lon(b, (2, 3)),
+        pairs_of_lon(a, (1, 2, 3)),
+        pairs_of_lon(a, (0,)),
+        pairs_of_lon(b, range(2, 8)),
+        pairs_of_lon(b, (0, 1)),
+    )
     got = [None] * 5
     for index in (2, 1, 0, 4, 3):
-        got[index] = lax.ppermute(messages[index], LL, pairs_of_lon(*targets[index]))
+        got[index] = lax.ppermute(messages[index], LL, targets[index])
 
     gathered = shape((ROWS, 128, CHAN))
     tables = [shape((20 * 288, 256)), shape((20 * 288, 256)), shape((5 * 288, 256))]

time: 69.1 us -> 68.5 us (level)
  starting transfers between devices: 44.7 us -> 42.9 us
  waiting for transfers between devices: 6.66 us -> 7.84 us
    ppermute x1, starting transfers between devices: 2.63 us -> 5.8 us  [body(): halo_b = lax.ppermute(lat_b, 'lat', pairs_of_lat(1))]
    ppermute x11, starting transfers between devices: 21 us -> 18.6 us  [flip(): lax.ppermute(x, axis, [(i, i ^ bit) for i in range(lax.axis_size(axis))])]
    ppermute x1, starting transfers between devices: 2.02 us -> 0.09 us  [body(): halo_a = lax.ppermute(lat_a, 'lat', pairs_of_lat(0))]
    ppermute x1, waiting for transfers between devices: 0.01 us -> 0.77 us  [body(): halo_b = lax.ppermute(lat_b, 'lat', pairs_of_lat(1))]
  transfers between devices with their start and end apart: 19 -> 19, of which waited for: 7 -> 9; matrix products, arithmetic and copies ran while one was open for 0% -> 0% of each run, Pallas kernels for 19% -> 19%
where the time goes in v6:
time: 68.5 us; the launch traced here: 68.2 us
  starting transfers between devices  42.9 us (63%)
  Pallas kernels  15.9 us (23%)
  waiting for transfers between devices  7.84 us (11%)
  between operations  0.83 us (1%)
  other arithmetic  0.71 us (1%)
    ppermute x11, starting transfers between devices, flip(): lax.ppermute(x, axis, [(i, i ^ bit) for i in range(lax.axis_size(axis))])  18.6 us
    ppermute x5, starting transfers between devices, body(): got[index] = lax.ppermute(messages[index], LL, targets[index])  16.3 us
    pallas_call x13, Pallas kernels, call(): pl.pallas_call(kernel, out_shape=outs, in_specs=[SMEM] * len(scalars) + [...  15.9 us
    ppermute x11, waiting for transfers between devices, flip(): lax.ppermute(x, axis, [(i, i ^ bit) for i in range(lax.axis_size(axis))])  6.72 us
    ppermute x1, starting transfers between devices, body(): halo_b = lax.ppermute(lat_b, 'lat', pairs_of_lat(1))  5.8 us
    ppermute x1, starting transfers between devices, body(): step = lax.ppermute(mine, LL, z_pairs())  2.12 us
  transfers between devices with their start and end apart: 19, of which 9 were waited for; matrix products, arithmetic and copies ran while one was open for 0% of the time, Pallas kernels for 19%

profile of v6, /device:TPU:1, one launch (start us, length us, event | category | flops | bytes accessed | tf_op | source)
XLA Modules:
  0.0 68.2 jit_solution(3246306195581902810)
XLA Ops:
  0.6 1.1 %shard_map.77 = (bf16[2,5,16,128]{3,2,1,0:T(8,128)(2,1)S(1)}, bf16[2,18,16,128]{3,2,1,0:T(8,128)(2,1)S(1)}, bf16[2,65,16,128]{3,2,1,0:T(8,128)(2,1)S(1)}, bf16[2...) custom-call(bf16[1,90,16,128]{3,2,1,0:T(8,128)(2,1)} %bitcast.8, bf16[1,90,16,128]{3,2,1,0:T(8,128)(2,1)} %bitcast.10), custom_call_target="tpu_custom_call" | custom-call | bytes 2031616 | tf_op jit(solution)/shard_map/pallas_call | solution.py:482
  1.8 0.7 %collective-permute-start.2 = (bf16[2,65,16,128]{3,2,1,0:T(8,128)(2,1)S(1)}, bf16[2,65,16,128]{3,2,1,0:T(8,128)(2,1)S(1)}, u32[]{:S(2)}, u32[]{:S(2)}) collective-permute-start(bf16[2,65,16,128]{3,2,1,0:T(8,128)(2,1)S(1)} %get-tuple-element.47), channel_id=1, source_target_pairs={{0,28},{4,8},{8,4},{12,16},{16,12},{20,24},{24,20},{28,0},{1,29},{... | collective-permute-start | bytes 1597448 | tf_op jit(solution)/shard_map/ppermute | solution.py:529
  2.5 3.9 %collective-permute-start.4 = (bf16[2,65,16,128]{3,2,1,0:T(8,128)(2,1)S(1)}, bf16[2,65,16,128]{3,2,1,0:T(8,128)(2,1)S(1)}, u32[]{:S(2)}, u32[]{:S(2)}) collective-permute-start(bf16[2,65,16,128]{3,2,1,0:T(8,128)(2,1)S(1)} %get-tuple-element.49), channel_id=1, source_target_pairs={{0,4},{4,0},{8,12},{12,8},{16,20},{20,16},{24,28},{28,24},{32,36},... | collective-permute-start | bytes 1597448 | tf_op jit(solution)/shard_map/ppermute | solution.py:529
  6.4 10.4 %collective-permute-start.1 = (bf16[2,18,16,128]{3,2,1,0:T(8,128)(2,1)S(1)}, bf16[2,18,16,128]{3,2,1,0:T(8,128)(2,1)S(1)}, u32[]{:S(2)}, u32[]{:S(2)}) collective-permute-start(bf16[2,18,16,128]{3,2,1,0:T(8,128)(2,1)S(1)} %get-tuple-element.46), channel_id=1, source_target_pairs={{32,60},{36,40},{40,36},{44,48},{48,44},{52,56},{56,52},{60,32},{6... | collective-permute-start | bytes 442376 | tf_op jit(solution)/shard_map/ppermute | solution.py:529
  16.8 0.7 collective-permute-start
  17.5 0.7 collective-permute-start.3
  18.1 4.3 %shard_map.76 = (bf16[16,128,128]{2,1,0:T(8,128)(2,1)S(1)}, bf16[16,128,128]{2,1,0:T(8,128)(2,1)S(1)}, bf16[5760,256]{1,0:T(8,128)(2,1)S(1)}, bf16[5760,256]{1,0...) custom-call(bf16[1,90,16,128]{3,2,1,0:T(8,128)(2,1)} %bitcast.9, ...), custom_call_target="tpu_custom_call" | custom-call | flops 200000000 | bytes 10796544 | tf_op jit(solution)/shard_map/pallas_call | solution.py:482
  22.4 0.0 collective-permute-done.few_a
  22.4 0.0 collective-permute-done.3.few_b
  22.4 0.0 collective-permute-done.1.second_a
  22.4 0.0 collective-permute-done.2.polar_a
  22.5 0.0 collective-permute-done.4.polar_b
  22.5 0.4 shard_map.78
  22.9 5.8 %collective-permute-start.6 = (bf16[2,2,144,128]{3,2,1,0:T(8,128)(2,1)S(1)}, bf16[2,2,144,128]{3,2,1,0:T(8,128)(2,1)S(1)}, u32[]{:S(2)}, u32[]{:S(2)}) collective-permute-start(bf16[2,2,144,128]{3,2,1,0:T(8,128)(2,1)S(1)} %get-tuple-element.60), channel_id=1, source_target_pairs={{32,64},{64,32},{96,128},{128,96},{160,192},{192,160},{33,65},{65,... | collective-permute-start | bytes 442376 | tf_op jit(solution)/shard_map/ppermute | solution.py:553
  28.7 0.1 collective-permute-start.5
  28.8 1.9 %shard_map.79 = (bf16[1152,384]{1,0:T(8,128)(2,1)S(1)}, f32[128,384]{1,0:T(8,128)S(1)}, f32[1152,128]{1,0:T(8,128)S(1)}) custom-call(f32[5,3,128]{2,1,0:T(4,128)S(1)} %get-tuple-element.41.amps, f32[4608,128]{1,0:T(8,128)S(1)} %get-tuple-element.42.tie.center, bf16[16,128,128]{2,1,0:T(8,128)(2,1)S(1)} %get-tuple-element.50.own0, ...), custom_call_target="tpu_custom_call" | custom-call | flops 566231040 | bytes 12279808 | tf_op jit(solution)/shard_map/pallas_call | solution.py:482
  30.8 0.0 collective-permute-done.5.halo_a
  30.8 0.8 %collective-permute-done.6.halo_b = bf16[2,2,144,128]{3,2,1,0:T(8,128)(2,1)S(1)} collective-permute-done((bf16[2,2,144,128]{3,2,1,0:T(8,128)(2,1)S(1)}, bf16[2,2,144,128]{3,2,1,0:T(8,128)(2,1)S(1)}, u32[]{:S(2)}, u32[]{:S(2)}) %collective-permute-start.6) | collective-permute-done | bytes 147488 | tf_op jit(solution)/shard_map/ppermute | solution.py:553
  31.5 0.0 copy-start
  31.5 1.5 %shard_map.80 = (bf16[384,384]{1,0:T(8,128)(2,1)S(1)}, f32[192,128]{1,0:T(8,128)S(1)}, f32[192,128]{1,0:T(8,128)S(1)}) custom-call(f32[5,3,128]{2,1,0:T(4,128)S(1)} %get-tuple-element.41.amps, f32[1152,128]{1,0:T(8,128)S(1)} %get-tuple-element.58.ends, bf16[5760,256]{1,0:T(8,128)(2,1)S(1)} %get-tuple-element.53.shape0, ...), custom_call_target="tpu_custom_call" | custom-call | flops 188743680 | bytes 7979008 | tf_op jit(solution)/shard_map/pallas_call | solution.py:482
  33.0 1.5 %collective-permute-start.7 = (f32[192,128]{1,0:T(8,128)S(1)}, f32[192,128]{1,0:T(8,128)S(1)}, u32[]{:S(2)}, u32[]{:S(2)}) collective-permute-start(f32[192,128]{1,0:T(8,128)S(1)} %get-tuple-element.64), channel_id=1, source_target_pairs={{0,32},{32,0},{64,96},{96,64},{128,160},{160,128},{192,224},{224,1... | collective-permute-start | bytes 294920 | tf_op jit(solution)/shard_map/ppermute | solution.py:473
  34.5 0.9 %collective-permute-done.7.refs_1_ = f32[192,128]{1,0:T(8,128)S(1)} collective-permute-done((f32[192,128]{1,0:T(8,128)S(1)}, f32[192,128]{1,0:T(8,128)S(1)}, u32[]{:S(2)}, u32[]{:S(2)}) %collective-permute-start.7) | collective-permute-done | bytes 98336 | tf_op jit(solution)/shard_map/ppermute | solution.py:473
  35.4 2.8 %collective-permute-start.10 = (bf16[192,128]{1,0:T(8,128)(2,1)S(1)}, bf16[192,128]{1,0:T(8,128)(2,1)S(1)}, u32[]{:S(2)}, u32[]{:S(2)}) collective-permute-start(bf16[192,128]{1,0:T(8,128)(2,1)S(1)} %get-tuple-element.69.refs_0_), channel_id=1, source_target_pairs={{0,3},{1,2},{2,1},{3,0},{4,7},{5,6},{6,5},{7,4},{8,11},{9,10},{10,... | collective-permute-start | bytes 147464 | tf_op jit(solution)/shard_map/ppermute | solution.py:473
  38.2 0.0 collective-permute-start.8
  38.2 1.3 %collective-permute-start.9 = (bf16[192,128]{1,0:T(8,128)(2,1)S(1)}, bf16[192,128]{1,0:T(8,128)(2,1)S(1)}, u32[]{:S(2)}, u32[]{:S(2)}) collective-permute-start(bf16[192,128]{1,0:T(8,128)(2,1)S(1)} %get-tuple-element.69.refs_0_), channel_id=1, source_target_pairs={{0,2},{1,3},{2,0},{3,1},{4,6},{5,7},{6,4},{7,5},{8,10},{9,11},{10,... | collective-permute-start | bytes 147464 | tf_op jit(solution)/shard_map/ppermute | solution.py:473
  39.5 0.0 copy-done
  39.5 1.3 %shard_map.82 = (bf16[1,90,16,128]{3,2,1,0:T(8,128)(2,1)}, f32[8,128]{1,0:T(8,128)S(1)}) custom-call(bf16[1152,384]{1,0:T(8,128)(2,1)S(1)} %get-tuple-element.57.inner, bf16[384,384]{1,0:T(8,128)(2,1)S(1)} %get-tuple-element.62.outer, bf16[384,128]{1,0:T(8,128)(2,1)S(1)} %bitcast.7, f32[8,128]{1,0:T(8,128)S(1)} %get-tuple-element.65.before), custom_call_target="tpu_custom_call" | custom-call | flops 150994944 | bytes 1654784 | tf_op jit(solution)/shard_map/pallas_call | solution.py:482
  40.8 0.0 collective-permute-done.10.refs_3_
  40.8 0.4 collective-permute-done.8.refs_1_
  41.2 1.5 %collective-permute-done.9.refs_2_ = bf16[192,128]{1,0:T(8,128)(2,1)S(1)} collective-permute-done((bf16[192,128]{1,0:T(8,128)(2,1)S(1)}, bf16[192,128]{1,0:T(8,128)(2,1)S(1)}, u32[]{:S(2)}, u32[]{:S(2)}) %collective-permute-start.9) | collective-permute-done | bytes 49184 | tf_op jit(solution)/shard_map/ppermute | solution.py:473
  42.7 0.1 collective-permute-start.11
  42.8 1.4 %collective-permute-start.12 = (bf16[192,128]{1,0:T(8,128)(2,1)S(1)}, bf16[192,128]{1,0:T(8,128)(2,1)S(1)}, u32[]{:S(2)}, u32[]{:S(2)}) collective-permute-start(bf16[192,128]{1,0:T(8,128)(2,1)S(1)} %shard_map.83.refs_0_), channel_id=1, source_target_pairs={{0,8},{4,12},{8,0},{12,4},{16,24},{20,28},{24,16},{28,20},{1,9},{5... | collective-permute-start | bytes 147464 | tf_op jit(solution)/shard_map/ppermute | solution.py:473
  44.2 2.5 %collective-permute-start.13 = (bf16[192,128]{1,0:T(8,128)(2,1)S(1)}, bf16[192,128]{1,0:T(8,128)(2,1)S(1)}, u32[]{:S(2)}, u32[]{:S(2)}) collective-permute-start(bf16[192,128]{1,0:T(8,128)(2,1)S(1)} %shard_map.83.refs_0_), channel_id=1, source_target_pairs={{0,12},{4,8},{8,4},{12,0},{16,28},{20,24},{24,20},{28,16},{1,13},{... | collective-permute-start | bytes 147464 | tf_op jit(solution)/shard_map/ppermute | solution.py:473
  46.7 0.0 collective-permute-done.11.refs_1_
  46.7 0.7 collective-permute-done.12.refs_2_
  47.3 1.0 %collective-permute-done.13.refs_3_ = bf16[192,128]{1,0:T(8,128)(2,1)S(1)} collective-permute-done((bf16[192,128]{1,0:T(8,128)(2,1)S(1)}, bf16[192,128]{1,0:T(8,128)(2,1)S(1)}, u32[]{:S(2)}, u32[]{:S(2)}) %collective-permute-start.13) | collective-permute-done | bytes 49184 | tf_op jit(solution)/shard_map/ppermute | solution.py:473
  48.4 0.6 collective-permute-start.14
  48.9 1.9 %collective-permute-start.15 = (bf16[192,128]{1,0:T(8,128)(2,1)S(1)}, bf16[192,128]{1,0:T(8,128)(2,1)S(1)}, u32[]{:S(2)}, u32[]{:S(2)}) collective-permute-start(bf16[192,128]{1,0:T(8,128)(2,1)S(1)} %get-tuple-element.71.refs_0_), channel_id=1, source_target_pairs={{0,128},{32,160},{64,192},{96,224},{128,0},{160,32},{192,64},{224,... | collective-permute-start | bytes 147464 | tf_op jit(solution)/shard_map/ppermute | solution.py:473
  50.8 1.2 %collective-permute-start.16 = (bf16[192,128]{1,0:T(8,128)(2,1)S(1)}, bf16[192,128]{1,0:T(8,128)(2,1)S(1)}, u32[]{:S(2)}, u32[]{:S(2)}) collective-permute-start(bf16[192,128]{1,0:T(8,128)(2,1)S(1)} %get-tuple-element.71.refs_0_), channel_id=1, source_target_pairs={{0,192},{32,224},{64,128},{96,160},{128,64},{160,96},{192,0},{224,... | collective-permute-start | bytes 147464 | tf_op jit(solution)/shard_map/ppermute | solution.py:473
  52.0 2.4 %shard_map.85 = (f32[1,90,16,128]{3,2,1,0:T(8,128)S(1)}, f32[8,128]{1,0:T(8,128)S(1)}) custom-call(f32[5,3,128]{2,1,0:T(4,128)S(1)} %get-tuple-element.41.amps, bf16[16,128,128]{2,1,0:T(8,128)(2,1)S(1)} %get-tuple-element.56.cot.own0, bf16[16,128,128]{2,1,0:T(8,128)(2,1)S(1)} %get-tuple-element.67.own1, bf16[5,32,128]{2,1,0:T(8,128)(2,1)S(1)} %get-tuple-element.68.own2, ...), custom_call_target="tpu_custom_call" | custom-call | flops 94371840 | bytes 8847360 | tf_op jit(solution)/shard_map/pallas_call | solution.py:482
  54.4 0.0 collective-permute-done.14.refs_1_
  54.4 0.0 collective-permute-done.15.refs_2_
  54.4 1.3 %collective-permute-done.16.refs_3_ = bf16[192,128]{1,0:T(8,128)(2,1)S(1)} collective-permute-done((bf16[192,128]{1,0:T(8,128)(2,1)S(1)}, bf16[192,128]{1,0:T(8,128)(2,1)S(1)}, u32[]{:S(2)}, u32[]{:S(2)}) %collective-permute-start.16) | collective-permute-done | bytes 49184 | tf_op jit(solution)/shard_map/ppermute | solution.py:473
  55.7 2.1 %collective-permute-start.17 = (bf16[192,128]{1,0:T(8,128)(2,1)S(1)}, bf16[192,128]{1,0:T(8,128)(2,1)S(1)}, u32[]{:S(2)}, u32[]{:S(2)}) collective-permute-start(bf16[192,128]{1,0:T(8,128)(2,1)S(1)} %get-tuple-element.77.refs_0_), channel_id=1, source_target_pairs={{0,144},{4,148},{8,152},{12,156},{16,128},{20,132},{24,136},{28,14... | collective-permute-start | bytes 147464 | tf_op jit(solution)/shard_map/ppermute | solution.py:599
  57.8 2.9 %shard_map.87 = (f32[1,90,16,128]{3,2,1,0:T(8,128)}, f32[8,128]{1,0:T(8,128)S(1)}) custom-call(f32[5,3,128]{2,1,0:T(4,128)S(1)} %get-tuple-element.41.amps, bf16[16,128,128]{2,1,0:T(8,128)(2,1)S(1)} %get-tuple-element.56.cot.own0, bf16[16,128,128]{2,1,0:T(8,128)(2,1)S(1)} %get-tuple-element.67.own1, bf16[5,32,128]{2,1,0:T(8,128)(2,1)S(1)} %get-tuple-element.68.own2, ...), custom_call_target="tpu_custom_call" | custom-call | flops 94371840 | bytes 9584640 | tf_op jit(solution)/shard_map/pallas_call | solution.py:482
  60.8 0.3 collective-permute-done.17.refs_1_
  61.1 5.5 %collective-permute-start.18 = (f32[192,128]{1,0:T(8,128)S(1)}, f32[192,128]{1,0:T(8,128)S(1)}, u32[]{:S(2)}, u32[]{:S(2)}) collective-permute-start(f32[192,128]{1,0:T(8,128)S(1)} %shard_map.88), channel_id=1, source_target_pairs={{0,32},{32,0},{64,96},{96,64},{128,160},{160,128},{192,224},{224,1... | collective-permute-start | bytes 294920 | tf_op jit(solution)/shard_map/ppermute | solution.py:473
  66.6 0.9 %collective-permute-done.18 = f32[192,128]{1,0:T(8,128)S(1)} collective-permute-done((f32[192,128]{1,0:T(8,128)S(1)}, f32[192,128]{1,0:T(8,128)S(1)}, u32[]{:S(2)}, u32[]{:S(2)}) %collective-permute-start.18) | collective-permute-done | bytes 98336 | tf_op jit(solution)/shard_map/ppermute | solution.py:473
  67.5 0.7 %maximum_multiply_fusion = f32[384,128]{1,0:T(8,128)} fusion(f32[192,128]{1,0:T(8,128)S(1)} %get-tuple-element.80, f32[192,128]{1,0:T(8,128)S(1)} %get-tuple-element.79), kind=kLoop, calls=%fused_computation | loop fusion | flops 98304 | bytes 393216 | tf_op jit(solution)/shard_map/mul | solution.py:605
  (6 shorter events, 0.1 us)
Async XLA Ops:
  1.8 20.7 %collective-permute-start.2 = (bf16[2,65,16,128]{3,2,1,0:T(8,128)(2,1)S(1)}, bf16[2,65,16,128]{3,2,1,0:T(8,128)(2,1)S(1)}, u32[]{:S(2)}, u32[]{:S(2)}) collective-permute-start(bf16[2,65,16,128]{3,2,1,0:T(8,128)(2,1)S(1)} %get-tuple-element.47), channel_id=1, source_target_pairs={{0,28},{4,8},{8,4},{12,16},{16,12},{20,24},{24,20},{28,0},{1,29},{... | collective-permute-start | bytes 1597448 | tf_op jit(solution)/shard_map/ppermute | solution.py:529
  2.5 20.0 %collective-permute-start.4 = (bf16[2,65,16,128]{3,2,1,0:T(8,128)(2,1)S(1)}, bf16[2,65,16,128]{3,2,1,0:T(8,128)(2,1)S(1)}, u32[]{:S(2)}, u32[]{:S(2)}) collective-permute-start(bf16[2,65,16,128]{3,2,1,0:T(8,128)(2,1)S(1)} %get-tuple-element.49), channel_id=1, source_target_pairs={{0,4},{4,0},{8,12},{12,8},{16,20},{20,16},{24,28},{28,24},{32,36},... | collective-permute-start | bytes 1597448 | tf_op jit(solution)/shard_map/ppermute | solution.py:529
  6.4 16.0 %collective-permute-start.1 = (bf16[2,18,16,128]{3,2,1,0:T(8,128)(2,1)S(1)}, bf16[2,18,16,128]{3,2,1,0:T(8,128)(2,1)S(1)}, u32[]{:S(2)}, u32[]{:S(2)}) collective-permute-start(bf16[2,18,16,128]{3,2,1,0:T(8,128)(2,1)S(1)} %get-tuple-element.46), channel_id=1, source_target_pairs={{32,60},{36,40},{40,36},{44,48},{48,44},{52,56},{56,52},{60,32},{6... | collective-permute-start | bytes 442376 | tf_op jit(solution)/shard_map/ppermute | solution.py:529
  16.8 5.6 %collective-permute-start = (bf16[2,5,16,128]{3,2,1,0:T(8,128)(2,1)S(1)}, bf16[2,5,16,128]{3,2,1,0:T(8,128)(2,1)S(1)}, u32[]{:S(2)}, u32[]{:S(2)}) collective-permute-start(bf16[2,5,16,128]{3,2,1,0:T(8,128)(2,1)S(1)} %get-tuple-element.45), channel_id=1, source_target_pairs={{128,156},{132,136},{136,132},{140,144},{144,140},{148,152},{152,1... | collective-permute-start | bytes 122888 | tf_op jit(solution)/shard_map/ppermute | solution.py:529
  17.5 5.0 %collective-permute-start.3 = (bf16[2,5,16,128]{3,2,1,0:T(8,128)(2,1)S(1)}, bf16[2,5,16,128]{3,2,1,0:T(8,128)(2,1)S(1)}, u32[]{:S(2)}, u32[]{:S(2)}) collective-permute-start(bf16[2,5,16,128]{3,2,1,0:T(8,128)(2,1)S(1)} %get-tuple-element.48), channel_id=1, source_target_pairs={{64,68},{68,64},{72,76},{76,72},{80,84},{84,80},{88,92},{92,88},{9... | collective-permute-start | bytes 122888 | tf_op jit(solution)/shard_map/ppermute | solution.py:529
  22.9 8.6 %collective-permute-start.6 = (bf16[2,2,144,128]{3,2,1,0:T(8,128)(2,1)S(1)}, bf16[2,2,144,128]{3,2,1,0:T(8,128)(2,1)S(1)}, u32[]{:S(2)}, u32[]{:S(2)}) collective-permute-start(bf16[2,2,144,128]{3,2,1,0:T(8,128)(2,1)S(1)} %get-tuple-element.60), channel_id=1, source_target_pairs={{32,64},{64,32},{96,128},{128,96},{160,192},{192,160},{33,65},{65,... | collective-permute-start | bytes 442376 | tf_op jit(solution)/shard_map/ppermute | solution.py:553
  28.7 2.0 %collective-permute-start.5 = (bf16[2,2,128,128]{3,2,1,0:T(8,128)(2,1)S(1)}, bf16[2,2,128,128]{3,2,1,0:T(8,128)(2,1)S(1)}, u32[]{:S(2)}, u32[]{:S(2)}) collective-permute-start(bf16[2,2,128,128]{3,2,1,0:T(8,128)(2,1)S(1)} %get-tuple-element.59), channel_id=1, source_target_pairs={{0,32},{32,0},{64,96},{96,64},{128,160},{160,128},{192,224},{224,1... | collective-permute-start | bytes 393224 | tf_op jit(solution)/shard_map/ppermute | solution.py:552
  31.5 8.0 %copy-start = (bf16[3,128,128]{2,1,0:T(8,128)(2,1)S(1)}, bf16[3,128,128]{2,1,0:T(8,128)(2,1)}, u32[]{:S(2)}) copy-start(bf16[3,128,128]{2,1,0:T(8,128)(2,1)} %weight.3) | copy-start | bytes 294916
  33.0 2.4 %collective-permute-start.7 = (f32[192,128]{1,0:T(8,128)S(1)}, f32[192,128]{1,0:T(8,128)S(1)}, u32[]{:S(2)}, u32[]{:S(2)}) collective-permute-start(f32[192,128]{1,0:T(8,128)S(1)} %get-tuple-element.64), channel_id=1, source_target_pairs={{0,32},{32,0},{64,96},{96,64},{128,160},{160,128},{192,224},{224,1... | collective-permute-start | bytes 294920 | tf_op jit(solution)/shard_map/ppermute | solution.py:473
  35.4 5.4 %collective-permute-start.10 = (bf16[192,128]{1,0:T(8,128)(2,1)S(1)}, bf16[192,128]{1,0:T(8,128)(2,1)S(1)}, u32[]{:S(2)}, u32[]{:S(2)}) collective-permute-start(bf16[192,128]{1,0:T(8,128)(2,1)S(1)} %get-tuple-element.69.refs_0_), channel_id=1, source_target_pairs={{0,3},{1,2},{2,1},{3,0},{4,7},{5,6},{6,5},{7,4},{8,11},{9,10},{10,... | collective-permute-start | bytes 147464 | tf_op jit(solution)/shard_map/ppermute | solution.py:473
  38.2 2.9 %collective-permute-start.8 = (bf16[192,128]{1,0:T(8,128)(2,1)S(1)}, bf16[192,128]{1,0:T(8,128)(2,1)S(1)}, u32[]{:S(2)}, u32[]{:S(2)}) collective-permute-start(bf16[192,128]{1,0:T(8,128)(2,1)S(1)} %get-tuple-element.69.refs_0_), channel_id=1, source_target_pairs={{0,1},{1,0},{2,3},{3,2},{4,5},{5,4},{6,7},{7,6},{8,9},{9,8},{10,11... | collective-permute-start | bytes 147464 | tf_op jit(solution)/shard_map/ppermute | solution.py:473
  38.2 4.4 %collective-permute-start.9 = (bf16[192,128]{1,0:T(8,128)(2,1)S(1)}, bf16[192,128]{1,0:T(8,128)(2,1)S(1)}, u32[]{:S(2)}, u32[]{:S(2)}) collective-permute-start(bf16[192,128]{1,0:T(8,128)(2,1)S(1)} %get-tuple-element.69.refs_0_), channel_id=1, source_target_pairs={{0,2},{1,3},{2,0},{3,1},{4,6},{5,7},{6,4},{7,5},{8,10},{9,11},{10,... | collective-permute-start | bytes 147464 | tf_op jit(solution)/shard_map/ppermute | solution.py:473
  42.7 3.9 %collective-permute-start.11 = (bf16[192,128]{1,0:T(8,128)(2,1)S(1)}, bf16[192,128]{1,0:T(8,128)(2,1)S(1)}, u32[]{:S(2)}, u32[]{:S(2)}) collective-permute-start(bf16[192,128]{1,0:T(8,128)(2,1)S(1)} %shard_map.83.refs_0_), channel_id=1, source_target_pairs={{0,4},{4,0},{8,12},{12,8},{16,20},{20,16},{24,28},{28,24},{1,5},{5... | collective-permute-start | bytes 147464 | tf_op jit(solution)/shard_map/ppermute | solution.py:473
  42.8 4.5 %collective-permute-start.12 = (bf16[192,128]{1,0:T(8,128)(2,1)S(1)}, bf16[192,128]{1,0:T(8,128)(2,1)S(1)}, u32[]{:S(2)}, u32[]{:S(2)}) collective-permute-start(bf16[192,128]{1,0:T(8,128)(2,1)S(1)} %shard_map.83.refs_0_), channel_id=1, source_target_pairs={{0,8},{4,12},{8,0},{12,4},{16,24},{20,28},{24,16},{28,20},{1,9},{5... | collective-permute-start | bytes 147464 | tf_op jit(solution)/shard_map/ppermute | solution.py:473
  44.2 4.2 %collective-permute-start.13 = (bf16[192,128]{1,0:T(8,128)(2,1)S(1)}, bf16[192,128]{1,0:T(8,128)(2,1)S(1)}, u32[]{:S(2)}, u32[]{:S(2)}) collective-permute-start(bf16[192,128]{1,0:T(8,128)(2,1)S(1)} %shard_map.83.refs_0_), channel_id=1, source_target_pairs={{0,12},{4,8},{8,4},{12,0},{16,28},{20,24},{24,20},{28,16},{1,13},{... | collective-permute-start | bytes 147464 | tf_op jit(solution)/shard_map/ppermute | solution.py:473
  48.4 6.0 %collective-permute-start.14 = (bf16[192,128]{1,0:T(8,128)(2,1)S(1)}, bf16[192,128]{1,0:T(8,128)(2,1)S(1)}, u32[]{:S(2)}, u32[]{:S(2)}) collective-permute-start(bf16[192,128]{1,0:T(8,128)(2,1)S(1)} %get-tuple-element.71.refs_0_), channel_id=1, source_target_pairs={{0,64},{32,96},{64,0},{96,32},{128,192},{160,224},{192,128},{224,1... | collective-permute-start | bytes 147464 | tf_op jit(solution)/shard_map/ppermute | solution.py:473
  48.9 5.5 %collective-permute-start.15 = (bf16[192,128]{1,0:T(8,128)(2,1)S(1)}, bf16[192,128]{1,0:T(8,128)(2,1)S(1)}, u32[]{:S(2)}, u32[]{:S(2)}) collective-permute-start(bf16[192,128]{1,0:T(8,128)(2,1)S(1)} %get-tuple-element.71.refs_0_), channel_id=1, source_target_pairs={{0,128},{32,160},{64,192},{96,224},{128,0},{160,32},{192,64},{224,... | collective-permute-start | bytes 147464 | tf_op jit(solution)/shard_map/ppermute | solution.py:473
  50.8 4.8 %collective-permute-start.16 = (bf16[192,128]{1,0:T(8,128)(2,1)S(1)}, bf16[192,128]{1,0:T(8,128)(2,1)S(1)}, u32[]{:S(2)}, u32[]{:S(2)}) collective-permute-start(bf16[192,128]{1,0:T(8,128)(2,1)S(1)} %get-tuple-element.71.refs_0_), channel_id=1, source_target_pairs={{0,192},{32,224},{64,128},{96,160},{128,64},{160,96},{192,0},{224,... | collective-permute-start | bytes 147464 | tf_op jit(solution)/shard_map/ppermute | solution.py:473
  55.7 5.4 %collective-permute-start.17 = (bf16[192,128]{1,0:T(8,128)(2,1)S(1)}, bf16[192,128]{1,0:T(8,128)(2,1)S(1)}, u32[]{:S(2)}, u32[]{:S(2)}) collective-permute-start(bf16[192,128]{1,0:T(8,128)(2,1)S(1)} %get-tuple-element.77.refs_0_), channel_id=1, source_target_pairs={{0,144},{4,148},{8,152},{12,156},{16,128},{20,132},{24,136},{28,14... | collective-permute-start | bytes 147464 | tf_op jit(solution)/shard_map/ppermute | solution.py:599
  61.1 6.4 %collective-permute-start.18 = (f32[192,128]{1,0:T(8,128)S(1)}, f32[192,128]{1,0:T(8,128)S(1)}, u32[]{:S(2)}, u32[]{:S(2)}) collective-permute-start(f32[192,128]{1,0:T(8,128)S(1)} %shard_map.88), channel_id=1, source_target_pairs={{0,32},{32,0},{64,96},{96,64},{128,160},{160,128},{192,224},{224,1... | collective-permute-start | bytes 294920 | tf_op jit(solution)/shard_map/ppermute | solution.py:473

commit v7 on v6

--- a/solution.py
+++ b/solution.py
@@ -81,15 +81,47 @@
     return amps[tap, k, row_of(first, ext)]
 
 
+def pack_polar(whole, out, right):
+    def begin(width):
+        return COLS - width if right else 0
+
+    def two(which, at, width, rows):
+        middle = at + width // 2
+        return jnp.concatenate([whole[which, at:middle, rows], whole[which, middle : at + width, rows]], axis=1)
+
+    low, high = slice(0, 8), slice(8, 16)
+    out[0:45] = two(0, 0, COLS, low)
+    out[45:65] = two(0, begin(40), 40, high)
+    out[65:95] = two(1, begin(60), 60, low)
+    far = 0 if right else COLS - 32
+    out[95:103] = jnp.concatenate([whole[1, far + 8 * i : far + 8 * i + 8, 0:4] for i in range(4)], axis=1)
+    out[103:119] = two(1, begin(32), 32, high)
+
+
+def open_polar(message, which, is_left):
+    def two(low, high):
+        return jnp.concatenate([message[low:high, :8], message[low:high, 8:]], axis=0)
+
+    if which == 0:
+        low, high = two(0, 45), two(45, 65)
+    else:
+        far = jnp.concatenate([message[95:103, 4 * i : 4 * i + 4] for i in range(4)], axis=0)
+        far = jnp.concatenate([far, jnp.zeros((32, 4, CHAN), BF16)], axis=1)
+        near, nothing = two(65, 95), jnp.zeros((8, 8, CHAN), BF16)
+        low = jnp.concatenate([far[:30], near] if is_left else [near, far[2:]], axis=0)
+        high = jnp.concatenate([nothing, two(103, 119)] if is_left else [two(103, 119), nothing], axis=0)
+    return jnp.swapaxes(low, 0, 1), jnp.swapaxes(high, 0, 1)
+
+
 def pack_kernel(field, cot, few_a, second_a, polar_a, few_b, polar_b, whole, sems):
     lat, odd = lax.axis_index("lat"), lax.axis_index("lon") % 2 == 1
 
     def edges(is_odd):
         def part(out, width, right, sem, skip=0):
-            source, target = pl.ds(COLS - width - skip if right else skip, width), pl.ds(0, width)
-            return [
-                pltpu.make_async_copy(x.at[0, source], out.at[i, target], sems.at[sem + i]) for i, x in enumerate((field, cot))
-            ]
+            source = pl.ds(COLS - width - skip if right else skip, width)
+            targets = [out.at[pl.ds(i * width, width)] if out is polar_b else out.at[i] for i in range(2)]
+            pairs = enumerate(zip((field, cot), targets))
+            return [pltpu.make_async_copy(x.at[0, source], target, sems.at[sem + i]) for i, (x, target) in pairs]
 
         def run(copies):
             for copy in copies:
@@ -104,7 +136,6 @@
         def _():
             nearest = part(few_a, FEW, not is_odd, 2)
             run(part(second_a, SECOND, is_odd, 0) + nearest + part(few_b, FEW, not is_odd, 4, skip=FEW))
-
 
         @pl.when(lat == 0)
         def _():
@@ -118,14 +149,8 @@
                 load.start()
             for load in loads:
                 load.wait()
-            for which in range(2):
-                low = jnp.concatenate([whole[which, :45, :8], whole[which, 45:, :8]], axis=1)
-                left = jnp.concatenate([whole[which, :20, 8:], whole[which, 20:40, 8:]], axis=1)
-                right = jnp.concatenate([whole[which, 50:70, 8:], whole[which, 70:, 8:]], axis=1)
-                polar_a[which, :45] = low
-                polar_b[which, :45] = low
-                polar_a[which, 45:] = right if is_odd else left
-                polar_b[which, 45:] = left if is_odd else right
+            pack_polar(whole, polar_a, is_odd)
+            pack_polar(whole, polar_b, not is_odd)
 
     pl.when(odd)(lambda: edges(True))
     pl.when(jnp.logical_not(odd))(lambda: edges(False))
@@ -175,10 +200,8 @@
     groups = ((outs[0], outs[2], outs[4]), (outs[1], outs[3], outs[5]))
     lat_a, lat_b = outs[6], outs[7]
 
-    def left_right(a_ref, b_ref, which, lo, hi):
-        left = jnp.where(odd, b_ref[which, lo:hi], a_ref[which, lo:hi])
-        right = jnp.where(odd, a_ref[which, lo:hi], b_ref[which, lo:hi])
-        return jnp.swapaxes(left, 0, 1), jnp.swapaxes(right, 0, 1)
+    def left_right(a, b):
+        return jnp.swapaxes(jnp.where(odd, b, a), 0, 1), jnp.swapaxes(jnp.where(odd, a, b), 0, 1)
 
     for which in range(2):
         own0, own1, own2 = groups[which]
@@ -203,7 +226,7 @@
 
         @pl.when(lat == 1)
         def _(which=which, own0=own0, own1=own1):
-            left, right = left_right(second_a, polar_b, which, 0, SECOND)
+            left, right = left_right(second_a[which], polar_b[which * SECOND : (which + 1) * SECOND])
             own0[:, 96:112, :] = left[:, 2:]
             own0[:, 112:128, :] = right[:, :16]
             own1[...] = jnp.zeros(own1.shape, BF16)
@@ -212,14 +235,9 @@
 
         @pl.when(lat == 0)
         def _(which=which, own0=own0, own1=own1, own2=own2):
-            a, b = polar_a[which], polar_b[which]
-            left, right = jnp.where(odd, b, a), jnp.where(odd, a, b)
-
-            def opened(lo, hi):
-                return [jnp.swapaxes(jnp.concatenate([x[lo:hi, :8], x[lo:hi, 8:]], axis=0), 0, 1) for x in (left, right)]
-
-            high_left, high_right = opened(45, 65)
-            left, right = opened(0, 45)
+            a, b = polar_a[...], polar_b[...]
+            left, high_left = open_polar(jnp.where(odd, b, a), which, True)
+            right, high_right = open_polar(jnp.where(odd, a, b), which, False)
             own0[:8, 96:112, :] = left[:, 74:90]
             own0[:8, 112:128, :] = right[:, 0:16]
             own1[:8, :64, :] = left[:, 10:74]
@@ -233,15 +251,19 @@
             own1[8:, 40:64, :] = left[:, 0:24]
             own1[8:, 64:88, :] = right[:, 16:40]
 
-        even = lat % 2 == 0
+    lat_messages(lat, outs[0], outs[2], lat_a, lat_b)
+
+
+def lat_messages(lat, own0, own1, lat_a, lat_b):
+    even = lat % 2 == 0
+    for row in range(2):
+        lat_a[row] = jnp.where(even, own0[14 + row], own0[row])
+        lat_b[row, :128, :] = jnp.where(even, own0[row], own0[14 + row])
+
+    @pl.when(lat < 2)
+    def _():
         for row in range(2):
-            lat_a[which, row] = jnp.where(even, own0[14 + row], own0[row])
-            lat_b[which, row, :128, :] = jnp.where(even, own0[row], own0[14 + row])
-
-        @pl.when(lat < 2)
-        def _(which=which, own1=own1):
-            for row in range(2):
-                lat_a[which, row, COLS : COLS + 4, :] = jnp.where(even, own1[14 + row, 62:66, :], own1[row, 62:66, :])
+            lat_a[row, COLS : COLS + 4, :] = jnp.where(even, own1[14 + row, 62:66, :], own1[row, 62:66, :])
 
 
 def tapped(amps, first, ext, rows):
@@ -288,20 +310,21 @@
     return lax.dot_general(cot, basis, (((0,), (0,)), ((), ())), preferred_element_type=F32)
 
 
-def inner_kernel(amps, center, own0, own1, own2, shape0, shape1, shape2, cot, basis, part, ends):
+def inner_kernel(amps, center, own0, own1, own2, shape0, shape1, shape2, cot, cot1, basis, part, ends, lat_a, lat_b):
     lat, first = position()
 
     def one(row, wide):
-        def own(ref, low, high):
-            return [ref[row - 2 + tap, low:] if 0 <= row - 2 + tap < high else None for tap in range(5)]
+        def own(ref, low, high, end=128):
+            return [ref[row - 2 + tap, low:end] if 0 <= row - 2 + tap < high else None for tap in range(5)]
 
         at = (row + 2) * 288
         values = filtered(shape0, at, amps, first, row + 2, own(own0, PAD, ROWS), PAD)
         values = plus(values, [center[row * 288 + k * PAD : row * 288 + (k + 1) * PAD, :] for k in range(3)])
         if wide:
-            values = plus(values, filtered(shape1, at, amps, first, row + 2, own(own1, 0, ROWS)))
+            low = 0 if row < 5 else 32 if row < 8 else 48
+            values = plus(values, filtered(shape1, at, amps, first, row + 2, own(own1, low, ROWS, 128 - low), low))
         if wide and row < 3:
-            values = plus(values, filtered(shape2, at, amps, first, row + 2, own(own2, 0, 5)))
+            values = plus(values, filtered(shape2, at, amps, first, row + 2, own(own2, 0, 5, 32)))
         if 2 <= row < 14:
             store_basis(basis, row - 2, values)
         else:
@@ -316,16 +339,17 @@
     pl.when(lat != 0)(lambda: run(False))
     pl.when(lat == 0)(lambda: run(True))
     part[...] = times_cotangent(cot[2:14, :PAD, :].reshape(12 * PAD, CHAN), basis[...])
-
-
-def halo_row(halo_a, halo_b, which, row, even, top):
-    a, b = halo_a[which, row], halo_b[which, row, :128]
+    lat_messages(lat, cot, cot1, lat_a, lat_b)
+
+
+def halo_row(halo_a, halo_b, row, even, top):
+    a, b = halo_a[row], halo_b[row, :128]
     return jnp.where(even, b, a) if top else jnp.where(even, a, b)
 
 
-def far_halo_row(halo_a, which, row):
+def far_halo_row(halo_a, row):
     zeros = jnp.zeros((62, CHAN), BF16)
-    return jnp.concatenate([zeros, halo_a[which, row, COLS : COLS + 4], zeros], axis=0)
+    return jnp.concatenate([zeros, halo_a[row, COLS : COLS + 4], zeros], axis=0)
 
 
 def outer_kernel(amps, ends, shape0, shape1, cot, halo_a, halo_b, part, basis, mine, other, grad):
@@ -337,8 +361,8 @@
             near, far = [], []
             for at in range(row - 2, row + 3):
                 inside, index = 0 <= at < ROWS, at + 2 if at < 0 else at - ROWS
-                near.append(None if inside else halo_row(halo_a, halo_b, 0, index, even, at < 0))
-                far.append(None if inside or at < 0 else far_halo_row(halo_a, 0, index))
+                near.append(None if inside else halo_row(halo_a, halo_b, index, even, at < 0))
+                far.append(None if inside or at < 0 else far_halo_row(halo_a, index))
             at = (row + 2) * 288
             values = filtered(shape0, at, amps, first, row + 2, near)
             values = plus(values, [ends[place * 288 + k * PAD : place * 288 + (k + 1) * PAD, :] for k in range(3)])
@@ -397,14 +421,14 @@
     pl.when(lat == 0)(lambda: own_rows(low, high, True))
     for row in range(2):
         ext = row if piece == 0 else 18 + row
-        gathered = halo_row(halo_a, halo_b, 1, row, even, piece == 0)
+        gathered = halo_row(halo_a, halo_b, row, even, piece == 0)
         put(ext - begin, twice(shape0[ext * 288 : (ext + 1) * 288, :], gathered), True)
     if piece == 0:
 
         @pl.when(lat == 1)
         def _():
             for row in range(2):
-                far = far_halo_row(halo_a, 1, row)
+                far = far_halo_row(halo_a, row)
                 put(row, twice(shape1[row * 288 : (row + 1) * 288, :], far), False)
 
         @pl.when(lat == 0)
@@ -502,7 +526,7 @@
     token = shape((8, 128), F32)
     few = shape((2, FEW, ROWS, CHAN))
     second = shape((2, SECOND, ROWS, CHAN))
-    polar = shape((2, 65, ROWS, CHAN))
+    polar = shape((119, ROWS, CHAN))
     scratch = [
         pltpu.VMEM((2, COLS, ROWS, CHAN), BF16),
         pltpu.SemaphoreType.DMA((12,)),
@@ -541,9 +565,10 @@
     own_f, own_c, *shapes, center, amps = call(prepare_kernel, outs, scratch, 2 * 10**8, (), (field, cot, spans, amps), space=pltpu.HBM)
     scalars = (amps,)
     own2 = shape((5, 32, CHAN))
+    lat_shapes = [shape((2, 128, CHAN)), shape((2, 144, CHAN))]
     own0_f, own0_c, own1_f, own1_c, own2_f, own2_c, lat_a, lat_b = call(
         assemble_kernel,
-        [gathered] * 4 + [own2] * 2 + [shape((2, 2, 128, CHAN)), shape((2, 2, 144, CHAN))],
+        [gathered] * 4 + [own2] * 2 + [*lat_shapes],
         [],
         0,
         (),
@@ -554,8 +579,10 @@
 
     own = (own0_f, own1_f, own2_f, *shapes, own0_c)
     half, ends = shape((192, CHAN), F32), shape((4 * 288, CHAN), F32)
-    outs = [shape((12 * PAD, 384)), shape((128, 384), F32), ends]
-    inner, part, ends = call(inner_kernel, outs, [], 12 * row_flops, scalars, (center, *own))
+    outs = [shape((12 * PAD, 384)), shape((128, 384), F32), ends, *lat_shapes]
+    inner, part, ends, lat_a, lat_b = call(inner_kernel, outs, [], 12 * row_flops, scalars, (center, *own, own1_c))
+    cot_halo_a = lax.ppermute(lat_a, "lat", pairs_of_lat(0))
+    cot_halo_b = lax.ppermute(lat_b, "lat", pairs_of_lat(1))
     outer, mine, other = call(
         outer_kernel,
         [shape((4 * PAD, 384)), half, half],
@@ -577,7 +604,7 @@
             [pltpu.VMEM((12 * 288, CHAN), F32), pltpu.VMEM((8 * PAD, 384), BF16)],
             2 * row_flops,
             scalars,
-            (own0_c, own1_c, own2_c, *shapes, halo_a, halo_b, mix_weight, before, *done),
+            (own0_c, own1_c, own2_c, *shapes, cot_halo_a, cot_halo_b, mix_weight, before, *done),
         )
 
     mine, before = add(mine, flip(other, "lat", 1))

time: 68.5 us -> 68.6 us (level)
  starting transfers between devices: 42.9 us -> 44.5 us
  waiting for transfers between devices: 7.84 us -> 6.31 us
    ppermute x0 -> x2, starting transfers between devices: none -> 5.05 us  [the longest x1 4.96 us: body(): cot_halo_b = lax.ppermute(lat_b, 'lat', pairs_of_lat(1))]
    ppermute x11, starting transfers between devices: 18.6 us -> 16.5 us  [flip(): lax.ppermute(x, axis, [(i, i ^ bit) for i in range(lax.axis_size(axis))])]
    ppermute x11, waiting for transfers between devices: 6.72 us -> 4.77 us  [flip(): lax.ppermute(x, axis, [(i, i ^ bit) for i in range(lax.axis_size(axis))])]
    ppermute x1, starting transfers between devices: 2.12 us -> 0.69 us  [body(): step = lax.ppermute(mine, LL, z_pairs())]
    ppermute x1, waiting for transfers between devices: 0.34 us -> 1.52 us  [body(): step = lax.ppermute(mine, LL, z_pairs())]
    ppermute x1, waiting for transfers between devices: 0.77 us -> 0.01 us  [body(): halo_b = lax.ppermute(lat_b, 'lat', pairs_of_lat(1))]
  transfers between devices with their start and end apart: 19 -> 21, of which waited for: 9 -> 5; matrix products, arithmetic and copies ran while one was open for 0% -> 0% of each run, Pallas kernels for 19% -> 19%
where the time goes in v7:
time: 68.6 us; the launch traced here: 68.3 us
  starting transfers between devices  44.5 us (65%)
  Pallas kernels  15.9 us (23%)
  waiting for transfers between devices  6.31 us (9%)
  between operations  0.9 us (1%)
  other arithmetic  0.71 us (1%)
    ppermute x11, starting transfers between devices, flip(): lax.ppermute(x, axis, [(i, i ^ bit) for i in range(lax.axis_size(axis))])  16.5 us
    ppermute x5, starting transfers between devices, body(): got[index] = lax.ppermute(messages[index], LL, targets[index])  16.3 us
    pallas_call x13, Pallas kernels, call(): pl.pallas_call(kernel, out_shape=outs, in_specs=[SMEM] * len(scalars) + [...  15.9 us
    ppermute x1, starting transfers between devices, body(): halo_b = lax.ppermute(lat_b, 'lat', pairs_of_lat(1))  5.8 us
    ppermute x1, starting transfers between devices, body(): cot_halo_b = lax.ppermute(lat_b, 'lat', pairs_of_lat(1))  4.96 us
    ppermute x11, waiting for transfers between devices, flip(): lax.ppermute(x, axis, [(i, i ^ bit) for i in range(lax.axis_size(axis))])  4.77 us
    ppermute x1, waiting for transfers between devices, body(): step = lax.ppermute(mine, LL, z_pairs())  1.52 us
  transfers between devices with their start and end apart: 21, of which 5 were waited for; matrix products, arithmetic and copies ran while one was open for 0% of the time, Pallas kernels for 19%

profile of v7, /device:TPU:1, one launch (start us, length us, event | category | flops | bytes accessed | tf_op | source)
XLA Modules:
  0.0 68.3 jit_solution(6152695165726296376)
XLA Ops:
  0.6 1.1 %shard_map.77 = (bf16[2,5,16,128]{3,2,1,0:T(8,128)(2,1)S(1)}, bf16[2,18,16,128]{3,2,1,0:T(8,128)(2,1)S(1)}, bf16[119,16,128]{2,1,0:T(8,128)(2,1)S(1)}, bf16[2,5,...) custom-call(bf16[1,90,16,128]{3,2,1,0:T(8,128)(2,1)} %bitcast.8, bf16[1,90,16,128]{3,2,1,0:T(8,128)(2,1)} %bitcast.10), custom_call_target="tpu_custom_call" | custom-call | bytes 1941504 | tf_op jit(solution)/shard_map/pallas_call | solution.py:506
  1.8 0.7 %collective-permute-start.2 = (bf16[119,16,128]{2,1,0:T(8,128)(2,1)S(1)}, bf16[119,16,128]{2,1,0:T(8,128)(2,1)S(1)}, u32[]{:S(2)}, u32[]{:S(2)}) collective-permute-start(bf16[119,16,128]{2,1,0:T(8,128)(2,1)S(1)} %get-tuple-element.49), channel_id=1, source_target_pairs={{0,28},{4,8},{8,4},{12,16},{16,12},{20,24},{24,20},{28,0},{1,29},{... | collective-permute-start | bytes 1462280 | tf_op jit(solution)/shard_map/ppermute | solution.py:553
  2.5 3.9 %collective-permute-start.4 = (bf16[119,16,128]{2,1,0:T(8,128)(2,1)S(1)}, bf16[119,16,128]{2,1,0:T(8,128)(2,1)S(1)}, u32[]{:S(2)}, u32[]{:S(2)}) collective-permute-start(bf16[119,16,128]{2,1,0:T(8,128)(2,1)S(1)} %get-tuple-element.51), channel_id=1, source_target_pairs={{0,4},{4,0},{8,12},{12,8},{16,20},{20,16},{24,28},{28,24},{32,36},... | collective-permute-start | bytes 1462280 | tf_op jit(solution)/shard_map/ppermute | solution.py:553
  6.4 10.4 %collective-permute-start.1 = (bf16[2,18,16,128]{3,2,1,0:T(8,128)(2,1)S(1)}, bf16[2,18,16,128]{3,2,1,0:T(8,128)(2,1)S(1)}, u32[]{:S(2)}, u32[]{:S(2)}) collective-permute-start(bf16[2,18,16,128]{3,2,1,0:T(8,128)(2,1)S(1)} %get-tuple-element.48), channel_id=1, source_target_pairs={{32,60},{36,40},{40,36},{44,48},{48,44},{52,56},{56,52},{60,32},{6... | collective-permute-start | bytes 442376 | tf_op jit(solution)/shard_map/ppermute | solution.py:553
  16.8 0.7 collective-permute-start
  17.5 0.7 collective-permute-start.3
  18.1 4.3 %shard_map.76 = (bf16[16,128,128]{2,1,0:T(8,128)(2,1)S(1)}, bf16[16,128,128]{2,1,0:T(8,128)(2,1)S(1)}, bf16[5760,256]{1,0:T(8,128)(2,1)S(1)}, bf16[5760,256]{1,0...) custom-call(bf16[1,90,16,128]{3,2,1,0:T(8,128)(2,1)} %bitcast.9, ...), custom_call_target="tpu_custom_call" | custom-call | flops 200000000 | bytes 10796544 | tf_op jit(solution)/shard_map/pallas_call | solution.py:506
  22.4 0.0 collective-permute-done.few_a
  22.4 0.0 collective-permute-done.3.few_b
  22.4 0.0 collective-permute-done.1.second_a
  22.4 0.0 collective-permute-done.2.polar_a
  22.4 0.0 collective-permute-done.4.polar_b
  22.4 0.4 shard_map.78
  22.9 5.8 %collective-permute-start.6 = (bf16[2,144,128]{2,1,0:T(8,128)(2,1)S(1)}, bf16[2,144,128]{2,1,0:T(8,128)(2,1)S(1)}, u32[]{:S(2)}, u32[]{:S(2)}) collective-permute-start(bf16[2,144,128]{2,1,0:T(8,128)(2,1)S(1)} %get-tuple-element.63), channel_id=1, source_target_pairs={{32,64},{64,32},{96,128},{128,96},{160,192},{192,160},{33,65},{65,... | collective-permute-start | bytes 221192 | tf_op jit(solution)/shard_map/ppermute | solution.py:578
  28.7 0.1 collective-permute-start.5
  28.8 1.9 %shard_map.79 = (bf16[1152,384]{1,0:T(8,128)(2,1)S(1)}, f32[128,384]{1,0:T(8,128)S(1)}, f32[1152,128]{1,0:T(8,128)S(1)}, bf16[2,128,128]{2,1,0:T(8,128)(2,1)S(1)}, bf16[2,144,128]{2,1,0:T(8,128)(2,1)S(1)}) custom-call(f32[5,3,128]{2,1,0:T(4,128)S(1)} %get-tuple-element.43.amps, f32[4608,128]{1,0:T(8,128)S(1)} %get-tuple-element.44.tie.center, ...), custom_call_target="tpu_custom_call" | custom-call | flops 566231040 | bytes 12943360 | tf_op jit(solution)/shard_map/pallas_call | solution.py:506
  30.7 0.0 collective-permute-done.5.halo_a
  30.7 0.0 collective-permute-done.6.halo_b
  30.8 0.0 copy-start
  30.8 1.5 %shard_map.80 = (bf16[384,384]{1,0:T(8,128)(2,1)S(1)}, f32[192,128]{1,0:T(8,128)S(1)}, f32[192,128]{1,0:T(8,128)S(1)}) custom-call(f32[5,3,128]{2,1,0:T(4,128)S(1)} %get-tuple-element.43.amps, f32[1152,128]{1,0:T(8,128)S(1)} %get-tuple-element.61.ends, bf16[5760,256]{1,0:T(8,128)(2,1)S(1)} %get-tuple-element.55.shape0, ...), custom_call_target="tpu_custom_call" | custom-call | flops 188743680 | bytes 7839744 | tf_op jit(solution)/shard_map/pallas_call | solution.py:506
  32.2 1.6 %collective-permute-start.7 = (f32[192,128]{1,0:T(8,128)S(1)}, f32[192,128]{1,0:T(8,128)S(1)}, u32[]{:S(2)}, u32[]{:S(2)}) collective-permute-start(f32[192,128]{1,0:T(8,128)S(1)} %get-tuple-element.67), channel_id=1, source_target_pairs={{0,32},{32,0},{64,96},{96,64},{128,160},{160,128},{192,224},{224,1... | collective-permute-start | bytes 294920 | tf_op jit(solution)/shard_map/ppermute | solution.py:497
  33.8 0.9 %collective-permute-done.7.refs_1_ = f32[192,128]{1,0:T(8,128)S(1)} collective-permute-done((f32[192,128]{1,0:T(8,128)S(1)}, f32[192,128]{1,0:T(8,128)S(1)}, u32[]{:S(2)}, u32[]{:S(2)}) %collective-permute-start.7) | collective-permute-done | bytes 98336 | tf_op jit(solution)/shard_map/ppermute | solution.py:497
  34.8 1.4 %collective-permute-start.10 = (bf16[192,128]{1,0:T(8,128)(2,1)S(1)}, bf16[192,128]{1,0:T(8,128)(2,1)S(1)}, u32[]{:S(2)}, u32[]{:S(2)}) collective-permute-start(bf16[192,128]{1,0:T(8,128)(2,1)S(1)} %get-tuple-element.73.refs_0_), channel_id=1, source_target_pairs={{0,1},{1,0},{2,3},{3,2},{4,5},{5,4},{6,7},{7,6},{8,9},{9,8},{10,11... | collective-permute-start | bytes 147464 | tf_op jit(solution)/shard_map/ppermute | solution.py:497
  36.2 2.6 %collective-permute-start.11 = (bf16[192,128]{1,0:T(8,128)(2,1)S(1)}, bf16[192,128]{1,0:T(8,128)(2,1)S(1)}, u32[]{:S(2)}, u32[]{:S(2)}) collective-permute-start(bf16[192,128]{1,0:T(8,128)(2,1)S(1)} %get-tuple-element.73.refs_0_), channel_id=1, source_target_pairs={{0,2},{1,3},{2,0},{3,1},{4,6},{5,7},{6,4},{7,5},{8,10},{9,11},{10,... | collective-permute-start | bytes 147464 | tf_op jit(solution)/shard_map/ppermute | solution.py:497
  38.8 0.0 collective-permute-start.12
  38.8 0.0 copy-done
  38.8 1.3 %shard_map.82 = (bf16[1,90,16,128]{3,2,1,0:T(8,128)(2,1)}, f32[8,128]{1,0:T(8,128)S(1)}) custom-call(bf16[1152,384]{1,0:T(8,128)(2,1)S(1)} %get-tuple-element.60.inner, bf16[384,384]{1,0:T(8,128)(2,1)S(1)} %get-tuple-element.65.outer, bf16[384,128]{1,0:T(8,128)(2,1)S(1)} %bitcast.7, f32[8,128]{1,0:T(8,128)S(1)} %get-tuple-element.68.before), custom_call_target="tpu_custom_call" | custom-call | flops 150994944 | bytes 1654784 | tf_op jit(solution)/shard_map/pallas_call | solution.py:506
  40.1 0.0 collective-permute-done.10.refs_1_
  40.1 1.0 %collective-permute-done.11.refs_2_ = bf16[192,128]{1,0:T(8,128)(2,1)S(1)} collective-permute-done((bf16[192,128]{1,0:T(8,128)(2,1)S(1)}, bf16[192,128]{1,0:T(8,128)(2,1)S(1)}, u32[]{:S(2)}, u32[]{:S(2)}) %collective-permute-start.11) | collective-permute-done | bytes 49184 | tf_op jit(solution)/shard_map/ppermute | solution.py:497
  41.1 1.9 %collective-permute-done.12.refs_3_ = bf16[192,128]{1,0:T(8,128)(2,1)S(1)} collective-permute-done((bf16[192,128]{1,0:T(8,128)(2,1)S(1)}, bf16[192,128]{1,0:T(8,128)(2,1)S(1)}, u32[]{:S(2)}, u32[]{:S(2)}) %collective-permute-start.12) | collective-permute-done | bytes 49184 | tf_op jit(solution)/shard_map/ppermute | solution.py:497
  43.0 0.3 collective-permute-start.13
  43.3 1.4 %collective-permute-start.14 = (bf16[192,128]{1,0:T(8,128)(2,1)S(1)}, bf16[192,128]{1,0:T(8,128)(2,1)S(1)}, u32[]{:S(2)}, u32[]{:S(2)}) collective-permute-start(bf16[192,128]{1,0:T(8,128)(2,1)S(1)} %shard_map.83.refs_0_), channel_id=1, source_target_pairs={{0,8},{4,12},{8,0},{12,4},{16,24},{20,28},{24,16},{28,20},{1,9},{5... | collective-permute-start | bytes 147464 | tf_op jit(solution)/shard_map/ppermute | solution.py:497
  44.6 2.5 %collective-permute-start.15 = (bf16[192,128]{1,0:T(8,128)(2,1)S(1)}, bf16[192,128]{1,0:T(8,128)(2,1)S(1)}, u32[]{:S(2)}, u32[]{:S(2)}) collective-permute-start(bf16[192,128]{1,0:T(8,128)(2,1)S(1)} %shard_map.83.refs_0_), channel_id=1, source_target_pairs={{0,12},{4,8},{8,4},{12,0},{16,28},{20,24},{24,20},{28,16},{1,13},{... | collective-permute-start | bytes 147464 | tf_op jit(solution)/shard_map/ppermute | solution.py:497
  47.1 5.0 %collective-permute-start.9 = (bf16[2,144,128]{2,1,0:T(8,128)(2,1)S(1)}, bf16[2,144,128]{2,1,0:T(8,128)(2,1)S(1)}, u32[]{:S(2)}, u32[]{:S(2)}) collective-permute-start(bf16[2,144,128]{2,1,0:T(8,128)(2,1)S(1)} %get-tuple-element.72), channel_id=1, source_target_pairs={{32,64},{64,32},{96,128},{128,96},{160,192},{192,160},{33,65},{65,... | collective-permute-start | bytes 221192 | tf_op jit(solution)/shard_map/ppermute | solution.py:585
  52.1 0.1 collective-permute-start.8
  52.2 0.0 collective-permute-done.13.refs_1_
  52.2 0.0 collective-permute-done.14.refs_2_
  52.2 0.0 collective-permute-done.15.refs_3_
  52.2 0.2 collective-permute-start.16
  52.4 0.0 collective-permute-start.17
  52.4 3.4 %collective-permute-start.18 = (bf16[192,128]{1,0:T(8,128)(2,1)S(1)}, bf16[192,128]{1,0:T(8,128)(2,1)S(1)}, u32[]{:S(2)}, u32[]{:S(2)}) collective-permute-start(bf16[192,128]{1,0:T(8,128)(2,1)S(1)} %get-tuple-element.75.refs_0_), channel_id=1, source_target_pairs={{0,192},{32,224},{64,128},{96,160},{128,64},{160,96},{192,0},{224,... | collective-permute-start | bytes 147464 | tf_op jit(solution)/shard_map/ppermute | solution.py:497
  55.9 0.0 collective-permute-done.8.halo_a
  55.9 0.0 collective-permute-done.9.halo_b
  55.9 2.4 %shard_map.85 = (f32[1,90,16,128]{3,2,1,0:T(8,128)S(1)}, f32[8,128]{1,0:T(8,128)S(1)}) custom-call(f32[5,3,128]{2,1,0:T(4,128)S(1)} %get-tuple-element.43.amps, bf16[16,128,128]{2,1,0:T(8,128)(2,1)S(1)} %get-tuple-element.58.cot.own0, bf16[16,128,128]{2,1,0:T(8,128)(2,1)S(1)} %get-tuple-element.59.cot1.own1, bf16[5,32,128]{2,1,0:T(8,128)(2,1)S(1)} %get-tuple-element.70.own2, ...), custom_call_target="tpu_custom_call" | custom-call | flops 94371840 | bytes 8708096 | tf_op jit(solution)/shard_map/pallas_call | solution.py:506
  58.3 0.0 collective-permute-done.16.refs_1_
  58.3 0.0 collective-permute-done.17.refs_2_
  58.3 0.0 collective-permute-done.18.refs_3_
  58.3 0.7 %collective-permute-start.19 = (bf16[192,128]{1,0:T(8,128)(2,1)S(1)}, bf16[192,128]{1,0:T(8,128)(2,1)S(1)}, u32[]{:S(2)}, u32[]{:S(2)}) collective-permute-start(bf16[192,128]{1,0:T(8,128)(2,1)S(1)} %get-tuple-element.81.refs_0_), channel_id=1, source_target_pairs={{0,144},{4,148},{8,152},{12,156},{16,128},{20,132},{24,136},{28,14... | collective-permute-start | bytes 147464 | tf_op jit(solution)/shard_map/ppermute | solution.py:626
  59.0 2.9 %shard_map.87 = (f32[1,90,16,128]{3,2,1,0:T(8,128)}, f32[8,128]{1,0:T(8,128)S(1)}) custom-call(f32[5,3,128]{2,1,0:T(4,128)S(1)} %get-tuple-element.43.amps, bf16[16,128,128]{2,1,0:T(8,128)(2,1)S(1)} %get-tuple-element.58.cot.own0, bf16[16,128,128]{2,1,0:T(8,128)(2,1)S(1)} %get-tuple-element.59.cot1.own1, bf16[5,32,128]{2,1,0:T(8,128)(2,1)S(1)} %get-tuple-element.70.own2, ...), custom_call_target="tpu_custom_call" | custom-call | flops 94371840 | bytes 9445376 | tf_op jit(solution)/shard_map/pallas_call | solution.py:506
  62.0 1.5 %collective-permute-done.19.refs_1_ = bf16[192,128]{1,0:T(8,128)(2,1)S(1)} collective-permute-done((bf16[192,128]{1,0:T(8,128)(2,1)S(1)}, bf16[192,128]{1,0:T(8,128)(2,1)S(1)}, u32[]{:S(2)}, u32[]{:S(2)}) %collective-permute-start.19) | collective-permute-done | bytes 49184 | tf_op jit(solution)/shard_map/ppermute | solution.py:626
  63.5 3.2 %collective-permute-start.20 = (f32[192,128]{1,0:T(8,128)S(1)}, f32[192,128]{1,0:T(8,128)S(1)}, u32[]{:S(2)}, u32[]{:S(2)}) collective-permute-start(f32[192,128]{1,0:T(8,128)S(1)} %shard_map.88), channel_id=1, source_target_pairs={{0,32},{32,0},{64,96},{96,64},{128,160},{160,128},{192,224},{224,1... | collective-permute-start | bytes 294920 | tf_op jit(solution)/shard_map/ppermute | solution.py:497
  66.7 0.9 %collective-permute-done.20 = f32[192,128]{1,0:T(8,128)S(1)} collective-permute-done((f32[192,128]{1,0:T(8,128)S(1)}, f32[192,128]{1,0:T(8,128)S(1)}, u32[]{:S(2)}, u32[]{:S(2)}) %collective-permute-start.20) | collective-permute-done | bytes 98336 | tf_op jit(solution)/shard_map/ppermute | solution.py:497
  67.6 0.7 %maximum_multiply_fusion = f32[384,128]{1,0:T(8,128)} fusion(f32[192,128]{1,0:T(8,128)S(1)} %get-tuple-element.84, f32[192,128]{1,0:T(8,128)S(1)} %get-tuple-element.83), kind=kLoop, calls=%fused_computation | loop fusion | flops 98304 | bytes 393216 | tf_op jit(solution)/shard_map/mul | solution.py:632
  (6 shorter events, 0.1 us)
Async XLA Ops:
  1.8 20.7 %collective-permute-start.2 = (bf16[119,16,128]{2,1,0:T(8,128)(2,1)S(1)}, bf16[119,16,128]{2,1,0:T(8,128)(2,1)S(1)}, u32[]{:S(2)}, u32[]{:S(2)}) collective-permute-start(bf16[119,16,128]{2,1,0:T(8,128)(2,1)S(1)} %get-tuple-element.49), channel_id=1, source_target_pairs={{0,28},{4,8},{8,4},{12,16},{16,12},{20,24},{24,20},{28,0},{1,29},{... | collective-permute-start | bytes 1462280 | tf_op jit(solution)/shard_map/ppermute | solution.py:553
  2.5 20.0 %collective-permute-start.4 = (bf16[119,16,128]{2,1,0:T(8,128)(2,1)S(1)}, bf16[119,16,128]{2,1,0:T(8,128)(2,1)S(1)}, u32[]{:S(2)}, u32[]{:S(2)}) collective-permute-start(bf16[119,16,128]{2,1,0:T(8,128)(2,1)S(1)} %get-tuple-element.51), channel_id=1, source_target_pairs={{0,4},{4,0},{8,12},{12,8},{16,20},{20,16},{24,28},{28,24},{32,36},... | collective-permute-start | bytes 1462280 | tf_op jit(solution)/shard_map/ppermute | solution.py:553
  6.4 16.0 %collective-permute-start.1 = (bf16[2,18,16,128]{3,2,1,0:T(8,128)(2,1)S(1)}, bf16[2,18,16,128]{3,2,1,0:T(8,128)(2,1)S(1)}, u32[]{:S(2)}, u32[]{:S(2)}) collective-permute-start(bf16[2,18,16,128]{3,2,1,0:T(8,128)(2,1)S(1)} %get-tuple-element.48), channel_id=1, source_target_pairs={{32,60},{36,40},{40,36},{44,48},{48,44},{52,56},{56,52},{60,32},{6... | collective-permute-start | bytes 442376 | tf_op jit(solution)/shard_map/ppermute | solution.py:553
  16.8 5.6 %collective-permute-start = (bf16[2,5,16,128]{3,2,1,0:T(8,128)(2,1)S(1)}, bf16[2,5,16,128]{3,2,1,0:T(8,128)(2,1)S(1)}, u32[]{:S(2)}, u32[]{:S(2)}) collective-permute-start(bf16[2,5,16,128]{3,2,1,0:T(8,128)(2,1)S(1)} %get-tuple-element.47), channel_id=1, source_target_pairs={{128,156},{132,136},{136,132},{140,144},{144,140},{148,152},{152,1... | collective-permute-start | bytes 122888 | tf_op jit(solution)/shard_map/ppermute | solution.py:553
  17.5 5.0 %collective-permute-start.3 = (bf16[2,5,16,128]{3,2,1,0:T(8,128)(2,1)S(1)}, bf16[2,5,16,128]{3,2,1,0:T(8,128)(2,1)S(1)}, u32[]{:S(2)}, u32[]{:S(2)}) collective-permute-start(bf16[2,5,16,128]{3,2,1,0:T(8,128)(2,1)S(1)} %get-tuple-element.50), channel_id=1, source_target_pairs={{64,68},{68,64},{72,76},{76,72},{80,84},{84,80},{88,92},{92,88},{9... | collective-permute-start | bytes 122888 | tf_op jit(solution)/shard_map/ppermute | solution.py:553
  22.9 7.9 %collective-permute-start.6 = (bf16[2,144,128]{2,1,0:T(8,128)(2,1)S(1)}, bf16[2,144,128]{2,1,0:T(8,128)(2,1)S(1)}, u32[]{:S(2)}, u32[]{:S(2)}) collective-permute-start(bf16[2,144,128]{2,1,0:T(8,128)(2,1)S(1)} %get-tuple-element.63), channel_id=1, source_target_pairs={{32,64},{64,32},{96,128},{128,96},{160,192},{192,160},{33,65},{65,... | collective-permute-start | bytes 221192 | tf_op jit(solution)/shard_map/ppermute | solution.py:578
  28.7 2.0 %collective-permute-start.5 = (bf16[2,128,128]{2,1,0:T(8,128)(2,1)S(1)}, bf16[2,128,128]{2,1,0:T(8,128)(2,1)S(1)}, u32[]{:S(2)}, u32[]{:S(2)}) collective-permute-start(bf16[2,128,128]{2,1,0:T(8,128)(2,1)S(1)} %get-tuple-element.62), channel_id=1, source_target_pairs={{0,32},{32,0},{64,96},{96,64},{128,160},{160,128},{192,224},{224,1... | collective-permute-start | bytes 196616 | tf_op jit(solution)/shard_map/ppermute | solution.py:577
  30.8 8.1 %copy-start = (bf16[3,128,128]{2,1,0:T(8,128)(2,1)S(1)}, bf16[3,128,128]{2,1,0:T(8,128)(2,1)}, u32[]{:S(2)}) copy-start(bf16[3,128,128]{2,1,0:T(8,128)(2,1)} %weight.3) | copy-start | bytes 294916
  32.2 2.5 %collective-permute-start.7 = (f32[192,128]{1,0:T(8,128)S(1)}, f32[192,128]{1,0:T(8,128)S(1)}, u32[]{:S(2)}, u32[]{:S(2)}) collective-permute-start(f32[192,128]{1,0:T(8,128)S(1)} %get-tuple-element.67), channel_id=1, source_target_pairs={{0,32},{32,0},{64,96},{96,64},{128,160},{160,128},{192,224},{224,1... | collective-permute-start | bytes 294920 | tf_op jit(solution)/shard_map/ppermute | solution.py:497
  34.8 5.3 %collective-permute-start.10 = (bf16[192,128]{1,0:T(8,128)(2,1)S(1)}, bf16[192,128]{1,0:T(8,128)(2,1)S(1)}, u32[]{:S(2)}, u32[]{:S(2)}) collective-permute-start(bf16[192,128]{1,0:T(8,128)(2,1)S(1)} %get-tuple-element.73.refs_0_), channel_id=1, source_target_pairs={{0,1},{1,0},{2,3},{3,2},{4,5},{5,4},{6,7},{7,6},{8,9},{9,8},{10,11... | collective-permute-start | bytes 147464 | tf_op jit(solution)/shard_map/ppermute | solution.py:497
  36.2 4.9 %collective-permute-start.11 = (bf16[192,128]{1,0:T(8,128)(2,1)S(1)}, bf16[192,128]{1,0:T(8,128)(2,1)S(1)}, u32[]{:S(2)}, u32[]{:S(2)}) collective-permute-start(bf16[192,128]{1,0:T(8,128)(2,1)S(1)} %get-tuple-element.73.refs_0_), channel_id=1, source_target_pairs={{0,2},{1,3},{2,0},{3,1},{4,6},{5,7},{6,4},{7,5},{8,10},{9,11},{10,... | collective-permute-start | bytes 147464 | tf_op jit(solution)/shard_map/ppermute | solution.py:497
  38.8 4.2 %collective-permute-start.12 = (bf16[192,128]{1,0:T(8,128)(2,1)S(1)}, bf16[192,128]{1,0:T(8,128)(2,1)S(1)}, u32[]{:S(2)}, u32[]{:S(2)}) collective-permute-start(bf16[192,128]{1,0:T(8,128)(2,1)S(1)} %get-tuple-element.73.refs_0_), channel_id=1, source_target_pairs={{0,3},{1,2},{2,1},{3,0},{4,7},{5,6},{6,5},{7,4},{8,11},{9,10},{10,... | collective-permute-start | bytes 147464 | tf_op jit(solution)/shard_map/ppermute | solution.py:497
  43.0 9.2 %collective-permute-start.13 = (bf16[192,128]{1,0:T(8,128)(2,1)S(1)}, bf16[192,128]{1,0:T(8,128)(2,1)S(1)}, u32[]{:S(2)}, u32[]{:S(2)}) collective-permute-start(bf16[192,128]{1,0:T(8,128)(2,1)S(1)} %shard_map.83.refs_0_), channel_id=1, source_target_pairs={{0,4},{4,0},{8,12},{12,8},{16,20},{20,16},{24,28},{28,24},{1,5},{5... | collective-permute-start | bytes 147464 | tf_op jit(solution)/shard_map/ppermute | solution.py:497
  43.3 8.9 %collective-permute-start.14 = (bf16[192,128]{1,0:T(8,128)(2,1)S(1)}, bf16[192,128]{1,0:T(8,128)(2,1)S(1)}, u32[]{:S(2)}, u32[]{:S(2)}) collective-permute-start(bf16[192,128]{1,0:T(8,128)(2,1)S(1)} %shard_map.83.refs_0_), channel_id=1, source_target_pairs={{0,8},{4,12},{8,0},{12,4},{16,24},{20,28},{24,16},{28,20},{1,9},{5... | collective-permute-start | bytes 147464 | tf_op jit(solution)/shard_map/ppermute | solution.py:497
  44.6 7.6 %collective-permute-start.15 = (bf16[192,128]{1,0:T(8,128)(2,1)S(1)}, bf16[192,128]{1,0:T(8,128)(2,1)S(1)}, u32[]{:S(2)}, u32[]{:S(2)}) collective-permute-start(bf16[192,128]{1,0:T(8,128)(2,1)S(1)} %shard_map.83.refs_0_), channel_id=1, source_target_pairs={{0,12},{4,8},{8,4},{12,0},{16,28},{20,24},{24,20},{28,16},{1,13},{... | collective-permute-start | bytes 147464 | tf_op jit(solution)/shard_map/ppermute | solution.py:497
  47.1 8.8 %collective-permute-start.9 = (bf16[2,144,128]{2,1,0:T(8,128)(2,1)S(1)}, bf16[2,144,128]{2,1,0:T(8,128)(2,1)S(1)}, u32[]{:S(2)}, u32[]{:S(2)}) collective-permute-start(bf16[2,144,128]{2,1,0:T(8,128)(2,1)S(1)} %get-tuple-element.72), channel_id=1, source_target_pairs={{32,64},{64,32},{96,128},{128,96},{160,192},{192,160},{33,65},{65,... | collective-permute-start | bytes 221192 | tf_op jit(solution)/shard_map/ppermute | solution.py:585
  52.1 3.8 %collective-permute-start.8 = (bf16[2,128,128]{2,1,0:T(8,128)(2,1)S(1)}, bf16[2,128,128]{2,1,0:T(8,128)(2,1)S(1)}, u32[]{:S(2)}, u32[]{:S(2)}) collective-permute-start(bf16[2,128,128]{2,1,0:T(8,128)(2,1)S(1)} %get-tuple-element.71), channel_id=1, source_target_pairs={{0,32},{32,0},{64,96},{96,64},{128,160},{160,128},{192,224},{224,1... | collective-permute-start | bytes 196616 | tf_op jit(solution)/shard_map/ppermute | solution.py:584
  52.2 6.0 %collective-permute-start.16 = (bf16[192,128]{1,0:T(8,128)(2,1)S(1)}, bf16[192,128]{1,0:T(8,128)(2,1)S(1)}, u32[]{:S(2)}, u32[]{:S(2)}) collective-permute-start(bf16[192,128]{1,0:T(8,128)(2,1)S(1)} %get-tuple-element.75.refs_0_), channel_id=1, source_target_pairs={{0,64},{32,96},{64,0},{96,32},{128,192},{160,224},{192,128},{224,1... | collective-permute-start | bytes 147464 | tf_op jit(solution)/shard_map/ppermute | solution.py:497
  52.4 5.9 %collective-permute-start.17 = (bf16[192,128]{1,0:T(8,128)(2,1)S(1)}, bf16[192,128]{1,0:T(8,128)(2,1)S(1)}, u32[]{:S(2)}, u32[]{:S(2)}) collective-permute-start(bf16[192,128]{1,0:T(8,128)(2,1)S(1)} %get-tuple-element.75.refs_0_), channel_id=1, source_target_pairs={{0,128},{32,160},{64,192},{96,224},{128,0},{160,32},{192,64},{224,... | collective-permute-start | bytes 147464 | tf_op jit(solution)/shard_map/ppermute | solution.py:497
  52.4 5.8 %collective-permute-start.18 = (bf16[192,128]{1,0:T(8,128)(2,1)S(1)}, bf16[192,128]{1,0:T(8,128)(2,1)S(1)}, u32[]{:S(2)}, u32[]{:S(2)}) collective-permute-start(bf16[192,128]{1,0:T(8,128)(2,1)S(1)} %get-tuple-element.75.refs_0_), channel_id=1, source_target_pairs={{0,192},{32,224},{64,128},{96,160},{128,64},{160,96},{192,0},{224,... | collective-permute-start | bytes 147464 | tf_op jit(solution)/shard_map/ppermute | solution.py:497
  58.3 5.1 %collective-permute-start.19 = (bf16[192,128]{1,0:T(8,128)(2,1)S(1)}, bf16[192,128]{1,0:T(8,128)(2,1)S(1)}, u32[]{:S(2)}, u32[]{:S(2)}) collective-permute-start(bf16[192,128]{1,0:T(8,128)(2,1)S(1)} %get-tuple-element.81.refs_0_), channel_id=1, source_target_pairs={{0,144},{4,148},{8,152},{12,156},{16,128},{20,132},{24,136},{28,14... | collective-permute-start | bytes 147464 | tf_op jit(solution)/shard_map/ppermute | solution.py:626
  63.5 4.1 %collective-permute-start.20 = (f32[192,128]{1,0:T(8,128)S(1)}, f32[192,128]{1,0:T(8,128)S(1)}, u32[]{:S(2)}, u32[]{:S(2)}) collective-permute-start(f32[192,128]{1,0:T(8,128)S(1)} %shard_map.88), channel_id=1, source_target_pairs={{0,32},{32,0},{64,96},{96,64},{128,160},{160,128},{192,224},{224,1... | collective-permute-start | bytes 294920 | tf_op jit(solution)/shard_map/ppermute | solution.py:497

commit v8 on v7

--- a/solution.py
+++ b/solution.py
@@ -306,8 +306,8 @@
         basis[pl.ds(at, PAD), k * 128 : (k + 1) * 128] = values[k].astype(BF16)
 
 
-def times_cotangent(cot, basis):
-    return lax.dot_general(cot, basis, (((0,), (0,)), ((), ())), preferred_element_type=F32)
+def times_cotangent(left, right):
+    return lax.dot_general(left, right, (((0,), (0,)), ((), ())), preferred_element_type=F32)
 
 
 def inner_kernel(amps, center, own0, own1, own2, shape0, shape1, shape2, cot, cot1, basis, part, ends, lat_a, lat_b):
@@ -338,7 +338,9 @@
 
     pl.when(lat != 0)(lambda: run(False))
     pl.when(lat == 0)(lambda: run(True))
-    part[...] = times_cotangent(cot[2:14, :PAD, :].reshape(12 * PAD, CHAN), basis[...])
+    product = times_cotangent(cot[2:14, :PAD, :].reshape(12 * PAD, CHAN), basis[...])
+    for k in range(3):
+        part[k * 128 : (k + 1) * 128, :] = product[:, k * 128 : (k + 1) * 128].T
     lat_messages(lat, cot, cot1, lat_a, lat_b)
 
 
@@ -352,7 +354,7 @@
     return jnp.concatenate([zeros, halo_a[row, COLS : COLS + 4], zeros], axis=0)
 
 
-def outer_kernel(amps, ends, shape0, shape1, cot, halo_a, halo_b, part, basis, mine, other, grad):
+def outer_kernel(amps, ends, shape0, shape1, cot, halo_a, halo_b, part, basis, mine, other):
     lat, first = position()
     even = lat % 2 == 0
 
@@ -373,12 +375,16 @@
     pl.when(lat != 0)(lambda: run(False))
     pl.when(lat == 0)(lambda: run(True))
     cells = jnp.concatenate([cot[0:2, :PAD, :], cot[14:16, :PAD, :]], axis=0).reshape(4 * PAD, CHAN)
-    product = part[...] + times_cotangent(cells, basis[...])
-    for k in range(3):
-        grad[k * 128 : (k + 1) * 128, :] = product[:, k * 128 : (k + 1) * 128].T
-    core = lat % 2
-    mine[...] = grad[pl.ds(pl.multiple_of(core * 192, 192), 192), :]
-    other[...] = grad[pl.ds(pl.multiple_of((1 - core) * 192, 192), 192), :]
+    sums = [part[k * 128 : (k + 1) * 128, :] + times_cotangent(basis[:, k * 128 : (k + 1) * 128], cells) for k in range(3)]
+
+    def halves(low, high):
+        low[:128, :] = sums[0]
+        low[128:, :] = sums[1][:64]
+        high[:64, :] = sums[1][64:]
+        high[64:, :] = sums[2]
+
+    pl.when(even)(lambda: halves(mine, other))
+    pl.when(jnp.logical_not(even))(lambda: halves(other, mine))
 
 
 def mix_kernel(inner, outer, weight, before, out, token):
@@ -579,14 +585,14 @@
 
     own = (own0_f, own1_f, own2_f, *shapes, own0_c)
     half, ends = shape((192, CHAN), F32), shape((4 * 288, CHAN), F32)
-    outs = [shape((12 * PAD, 384)), shape((128, 384), F32), ends, *lat_shapes]
+    outs = [shape((12 * PAD, 384)), shape((384, CHAN), F32), ends, *lat_shapes]
     inner, part, ends, lat_a, lat_b = call(inner_kernel, outs, [], 12 * row_flops, scalars, (center, *own, own1_c))
     cot_halo_a = lax.ppermute(lat_a, "lat", pairs_of_lat(0))
     cot_halo_b = lax.ppermute(lat_b, "lat", pairs_of_lat(1))
     outer, mine, other = call(
         outer_kernel,
         [shape((4 * PAD, 384)), half, half],
-        [pltpu.VMEM((384, CHAN), F32)],
+        [],
         4 * row_flops,
         scalars,
         (ends, shapes[0], shapes[1], own0_c, halo_a, halo_b, part),

time: 68.6 us -> 68.5 us (level)
  no operation moved by 1% of the time
where the time goes in v8:
time: 68.5 us; the launch traced here: 68.2 us
  starting transfers between devices  44.3 us (65%)
  Pallas kernels  15.9 us (23%)
  waiting for transfers between devices  6.38 us (9%)
  between operations  0.9 us (1%)
  other arithmetic  0.71 us (1%)
    ppermute x11, starting transfers between devices, flip(): lax.ppermute(x, axis, [(i, i ^ bit) for i in range(lax.axis_size(axis))])  16.5 us
    ppermute x5, starting transfers between devices, body(): got[index] = lax.ppermute(messages[index], LL, targets[index])  16.3 us
    pallas_call x13, Pallas kernels, call(): pl.pallas_call(kernel, out_shape=outs, in_specs=[SMEM] * len(scalars) + [...  15.9 us
    ppermute x1, starting transfers between devices, body(): halo_b = lax.ppermute(lat_b, 'lat', pairs_of_lat(1))  5.8 us
    ppermute x1, starting transfers between devices, body(): cot_halo_b = lax.ppermute(lat_b, 'lat', pairs_of_lat(1))  4.87 us
    ppermute x11, waiting for transfers between devices, flip(): lax.ppermute(x, axis, [(i, i ^ bit) for i in range(lax.axis_size(axis))])  4.77 us
    ppermute x1, waiting for transfers between devices, body(): step = lax.ppermute(mine, LL, z_pairs())  1.59 us
  transfers between devices with their start and end apart: 21, of which 5 were waited for; matrix products, arithmetic and copies ran while one was open for 0% of the time, Pallas kernels for 19%

profile of v8, /device:TPU:1, one launch (start us, length us, event | category | flops | bytes accessed | tf_op | source)
XLA Modules:
  0.0 68.2 jit_solution(8264054289258329676)
XLA Ops:
  0.6 1.1 %shard_map.77 = (bf16[2,5,16,128]{3,2,1,0:T(8,128)(2,1)S(1)}, bf16[2,18,16,128]{3,2,1,0:T(8,128)(2,1)S(1)}, bf16[119,16,128]{2,1,0:T(8,128)(2,1)S(1)}, bf16[2,5,...) custom-call(bf16[1,90,16,128]{3,2,1,0:T(8,128)(2,1)} %bitcast.8, bf16[1,90,16,128]{3,2,1,0:T(8,128)(2,1)} %bitcast.10), custom_call_target="tpu_custom_call" | custom-call | bytes 1941504 | tf_op jit(solution)/shard_map/pallas_call | solution.py:512
  1.8 0.7 %collective-permute-start.2 = (bf16[119,16,128]{2,1,0:T(8,128)(2,1)S(1)}, bf16[119,16,128]{2,1,0:T(8,128)(2,1)S(1)}, u32[]{:S(2)}, u32[]{:S(2)}) collective-permute-start(bf16[119,16,128]{2,1,0:T(8,128)(2,1)S(1)} %get-tuple-element.49), channel_id=1, source_target_pairs={{0,28},{4,8},{8,4},{12,16},{16,12},{20,24},{24,20},{28,0},{1,29},{... | collective-permute-start | bytes 1462280 | tf_op jit(solution)/shard_map/ppermute | solution.py:559
  2.5 3.9 %collective-permute-start.4 = (bf16[119,16,128]{2,1,0:T(8,128)(2,1)S(1)}, bf16[119,16,128]{2,1,0:T(8,128)(2,1)S(1)}, u32[]{:S(2)}, u32[]{:S(2)}) collective-permute-start(bf16[119,16,128]{2,1,0:T(8,128)(2,1)S(1)} %get-tuple-element.51), channel_id=1, source_target_pairs={{0,4},{4,0},{8,12},{12,8},{16,20},{20,16},{24,28},{28,24},{32,36},... | collective-permute-start | bytes 1462280 | tf_op jit(solution)/shard_map/ppermute | solution.py:559
  6.4 10.4 %collective-permute-start.1 = (bf16[2,18,16,128]{3,2,1,0:T(8,128)(2,1)S(1)}, bf16[2,18,16,128]{3,2,1,0:T(8,128)(2,1)S(1)}, u32[]{:S(2)}, u32[]{:S(2)}) collective-permute-start(bf16[2,18,16,128]{3,2,1,0:T(8,128)(2,1)S(1)} %get-tuple-element.48), channel_id=1, source_target_pairs={{32,60},{36,40},{40,36},{44,48},{48,44},{52,56},{56,52},{60,32},{6... | collective-permute-start | bytes 442376 | tf_op jit(solution)/shard_map/ppermute | solution.py:559
  16.8 0.7 collective-permute-start
  17.5 0.7 collective-permute-start.3
  18.1 4.3 %shard_map.76 = (bf16[16,128,128]{2,1,0:T(8,128)(2,1)S(1)}, bf16[16,128,128]{2,1,0:T(8,128)(2,1)S(1)}, bf16[5760,256]{1,0:T(8,128)(2,1)S(1)}, bf16[5760,256]{1,0...) custom-call(bf16[1,90,16,128]{3,2,1,0:T(8,128)(2,1)} %bitcast.9, ...), custom_call_target="tpu_custom_call" | custom-call | flops 200000000 | bytes 10796544 | tf_op jit(solution)/shard_map/pallas_call | solution.py:512
  22.4 0.0 collective-permute-done.few_a
  22.4 0.0 collective-permute-done.3.few_b
  22.4 0.0 collective-permute-done.1.second_a
  22.4 0.0 collective-permute-done.2.polar_a
  22.4 0.0 collective-permute-done.4.polar_b
  22.4 0.4 shard_map.78
  22.9 5.8 %collective-permute-start.6 = (bf16[2,144,128]{2,1,0:T(8,128)(2,1)S(1)}, bf16[2,144,128]{2,1,0:T(8,128)(2,1)S(1)}, u32[]{:S(2)}, u32[]{:S(2)}) collective-permute-start(bf16[2,144,128]{2,1,0:T(8,128)(2,1)S(1)} %get-tuple-element.63), channel_id=1, source_target_pairs={{32,64},{64,32},{96,128},{128,96},{160,192},{192,160},{33,65},{65,... | collective-permute-start | bytes 221192 | tf_op jit(solution)/shard_map/ppermute | solution.py:584
  28.7 0.1 collective-permute-start.5
  28.8 2.0 %shard_map.79 = (bf16[1152,384]{1,0:T(8,128)(2,1)S(1)}, f32[384,128]{1,0:T(8,128)S(1)}, f32[1152,128]{1,0:T(8,128)S(1)}, bf16[2,128,128]{2,1,0:T(8,128)(2,1)S(1)}, bf16[2,144,128]{2,1,0:T(8,128)(2,1)S(1)}) custom-call(f32[5,3,128]{2,1,0:T(4,128)S(1)} %get-tuple-element.43.amps, f32[4608,128]{1,0:T(8,128)S(1)} %get-tuple-element.44.tie.center, ...), custom_call_target="tpu_custom_call" | custom-call | flops 566231040 | bytes 12943360 | tf_op jit(solution)/shard_map/pallas_call | solution.py:512
  30.8 0.0 collective-permute-done.5.halo_a
  30.8 0.0 collective-permute-done.6.halo_b
  30.9 0.0 copy-start
  30.9 1.3 %shard_map.80 = (bf16[384,384]{1,0:T(8,128)(2,1)S(1)}, f32[192,128]{1,0:T(8,128)S(1)}, f32[192,128]{1,0:T(8,128)S(1)}) custom-call(f32[5,3,128]{2,1,0:T(4,128)S(1)} %get-tuple-element.43.amps, f32[1152,128]{1,0:T(8,128)S(1)} %get-tuple-element.61.ends, bf16[5760,256]{1,0:T(8,128)(2,1)S(1)} %get-tuple-element.55.shape0, ...), custom_call_target="tpu_custom_call" | custom-call | flops 188743680 | bytes 7839744 | tf_op jit(solution)/shard_map/pallas_call | solution.py:512
  32.2 1.6 %collective-permute-start.7 = (f32[192,128]{1,0:T(8,128)S(1)}, f32[192,128]{1,0:T(8,128)S(1)}, u32[]{:S(2)}, u32[]{:S(2)}) collective-permute-start(f32[192,128]{1,0:T(8,128)S(1)} %get-tuple-element.67), channel_id=1, source_target_pairs={{0,32},{32,0},{64,96},{96,64},{128,160},{160,128},{192,224},{224,1... | collective-permute-start | bytes 294920 | tf_op jit(solution)/shard_map/ppermute | solution.py:503
  33.8 0.9 %collective-permute-done.7.refs_1_ = f32[192,128]{1,0:T(8,128)S(1)} collective-permute-done((f32[192,128]{1,0:T(8,128)S(1)}, f32[192,128]{1,0:T(8,128)S(1)}, u32[]{:S(2)}, u32[]{:S(2)}) %collective-permute-start.7) | collective-permute-done | bytes 98336 | tf_op jit(solution)/shard_map/ppermute | solution.py:503
  34.8 1.4 %collective-permute-start.10 = (bf16[192,128]{1,0:T(8,128)(2,1)S(1)}, bf16[192,128]{1,0:T(8,128)(2,1)S(1)}, u32[]{:S(2)}, u32[]{:S(2)}) collective-permute-start(bf16[192,128]{1,0:T(8,128)(2,1)S(1)} %get-tuple-element.73.refs_0_), channel_id=1, source_target_pairs={{0,1},{1,0},{2,3},{3,2},{4,5},{5,4},{6,7},{7,6},{8,9},{9,8},{10,11... | collective-permute-start | bytes 147464 | tf_op jit(solution)/shard_map/ppermute | solution.py:503
  36.1 2.6 %collective-permute-start.11 = (bf16[192,128]{1,0:T(8,128)(2,1)S(1)}, bf16[192,128]{1,0:T(8,128)(2,1)S(1)}, u32[]{:S(2)}, u32[]{:S(2)}) collective-permute-start(bf16[192,128]{1,0:T(8,128)(2,1)S(1)} %get-tuple-element.73.refs_0_), channel_id=1, source_target_pairs={{0,2},{1,3},{2,0},{3,1},{4,6},{5,7},{6,4},{7,5},{8,10},{9,11},{10,... | collective-permute-start | bytes 147464 | tf_op jit(solution)/shard_map/ppermute | solution.py:503
  38.8 0.0 collective-permute-start.12
  38.8 0.0 copy-done
  38.8 1.3 %shard_map.82 = (bf16[1,90,16,128]{3,2,1,0:T(8,128)(2,1)}, f32[8,128]{1,0:T(8,128)S(1)}) custom-call(bf16[1152,384]{1,0:T(8,128)(2,1)S(1)} %get-tuple-element.60.inner, bf16[384,384]{1,0:T(8,128)(2,1)S(1)} %get-tuple-element.65.outer, bf16[384,128]{1,0:T(8,128)(2,1)S(1)} %bitcast.7, f32[8,128]{1,0:T(8,128)S(1)} %get-tuple-element.68.before), custom_call_target="tpu_custom_call" | custom-call | flops 150994944 | bytes 1654784 | tf_op jit(solution)/shard_map/pallas_call | solution.py:512
  40.1 0.0 collective-permute-done.10.refs_1_
  40.1 1.0 %collective-permute-done.11.refs_2_ = bf16[192,128]{1,0:T(8,128)(2,1)S(1)} collective-permute-done((bf16[192,128]{1,0:T(8,128)(2,1)S(1)}, bf16[192,128]{1,0:T(8,128)(2,1)S(1)}, u32[]{:S(2)}, u32[]{:S(2)}) %collective-permute-start.11) | collective-permute-done | bytes 49184 | tf_op jit(solution)/shard_map/ppermute | solution.py:503
  41.0 1.9 %collective-permute-done.12.refs_3_ = bf16[192,128]{1,0:T(8,128)(2,1)S(1)} collective-permute-done((bf16[192,128]{1,0:T(8,128)(2,1)S(1)}, bf16[192,128]{1,0:T(8,128)(2,1)S(1)}, u32[]{:S(2)}, u32[]{:S(2)}) %collective-permute-start.12) | collective-permute-done | bytes 49184 | tf_op jit(solution)/shard_map/ppermute | solution.py:503
  43.0 0.3 collective-permute-start.13
  43.2 1.4 %collective-permute-start.14 = (bf16[192,128]{1,0:T(8,128)(2,1)S(1)}, bf16[192,128]{1,0:T(8,128)(2,1)S(1)}, u32[]{:S(2)}, u32[]{:S(2)}) collective-permute-start(bf16[192,128]{1,0:T(8,128)(2,1)S(1)} %shard_map.83.refs_0_), channel_id=1, source_target_pairs={{0,8},{4,12},{8,0},{12,4},{16,24},{20,28},{24,16},{28,20},{1,9},{5... | collective-permute-start | bytes 147464 | tf_op jit(solution)/shard_map/ppermute | solution.py:503
  44.6 2.5 %collective-permute-start.15 = (bf16[192,128]{1,0:T(8,128)(2,1)S(1)}, bf16[192,128]{1,0:T(8,128)(2,1)S(1)}, u32[]{:S(2)}, u32[]{:S(2)}) collective-permute-start(bf16[192,128]{1,0:T(8,128)(2,1)S(1)} %shard_map.83.refs_0_), channel_id=1, source_target_pairs={{0,12},{4,8},{8,4},{12,0},{16,28},{20,24},{24,20},{28,16},{1,13},{... | collective-permute-start | bytes 147464 | tf_op jit(solution)/shard_map/ppermute | solution.py:503
  47.1 4.9 %collective-permute-start.9 = (bf16[2,144,128]{2,1,0:T(8,128)(2,1)S(1)}, bf16[2,144,128]{2,1,0:T(8,128)(2,1)S(1)}, u32[]{:S(2)}, u32[]{:S(2)}) collective-permute-start(bf16[2,144,128]{2,1,0:T(8,128)(2,1)S(1)} %get-tuple-element.72), channel_id=1, source_target_pairs={{32,64},{64,32},{96,128},{128,96},{160,192},{192,160},{33,65},{65,... | collective-permute-start | bytes 221192 | tf_op jit(solution)/shard_map/ppermute | solution.py:591
  52.0 0.1 collective-permute-start.8
  52.1 0.0 collective-permute-done.13.refs_1_
  52.1 0.0 collective-permute-done.14.refs_2_
  52.1 0.0 collective-permute-done.15.refs_3_
  52.1 0.2 collective-permute-start.16
  52.3 0.0 collective-permute-start.17
  52.3 3.4 %collective-permute-start.18 = (bf16[192,128]{1,0:T(8,128)(2,1)S(1)}, bf16[192,128]{1,0:T(8,128)(2,1)S(1)}, u32[]{:S(2)}, u32[]{:S(2)}) collective-permute-start(bf16[192,128]{1,0:T(8,128)(2,1)S(1)} %get-tuple-element.75.refs_0_), channel_id=1, source_target_pairs={{0,192},{32,224},{64,128},{96,160},{128,64},{160,96},{192,0},{224,... | collective-permute-start | bytes 147464 | tf_op jit(solution)/shard_map/ppermute | solution.py:503
  55.8 0.0 collective-permute-done.8.halo_a
  55.8 0.0 collective-permute-done.9.halo_b
  55.8 2.4 %shard_map.85 = (f32[1,90,16,128]{3,2,1,0:T(8,128)S(1)}, f32[8,128]{1,0:T(8,128)S(1)}) custom-call(f32[5,3,128]{2,1,0:T(4,128)S(1)} %get-tuple-element.43.amps, bf16[16,128,128]{2,1,0:T(8,128)(2,1)S(1)} %get-tuple-element.58.cot.own0, bf16[16,128,128]{2,1,0:T(8,128)(2,1)S(1)} %get-tuple-element.59.cot1.own1, bf16[5,32,128]{2,1,0:T(8,128)(2,1)S(1)} %get-tuple-element.70.own2, ...), custom_call_target="tpu_custom_call" | custom-call | flops 94371840 | bytes 8708096 | tf_op jit(solution)/shard_map/pallas_call | solution.py:512
  58.1 0.0 collective-permute-done.16.refs_1_
  58.2 0.0 collective-permute-done.17.refs_2_
  58.2 0.0 collective-permute-done.18.refs_3_
  58.2 0.7 %collective-permute-start.19 = (bf16[192,128]{1,0:T(8,128)(2,1)S(1)}, bf16[192,128]{1,0:T(8,128)(2,1)S(1)}, u32[]{:S(2)}, u32[]{:S(2)}) collective-permute-start(bf16[192,128]{1,0:T(8,128)(2,1)S(1)} %get-tuple-element.81.refs_0_), channel_id=1, source_target_pairs={{0,144},{4,148},{8,152},{12,156},{16,128},{20,132},{24,136},{28,14... | collective-permute-start | bytes 147464 | tf_op jit(solution)/shard_map/ppermute | solution.py:632
  58.9 2.9 %shard_map.87 = (f32[1,90,16,128]{3,2,1,0:T(8,128)}, f32[8,128]{1,0:T(8,128)S(1)}) custom-call(f32[5,3,128]{2,1,0:T(4,128)S(1)} %get-tuple-element.43.amps, bf16[16,128,128]{2,1,0:T(8,128)(2,1)S(1)} %get-tuple-element.58.cot.own0, bf16[16,128,128]{2,1,0:T(8,128)(2,1)S(1)} %get-tuple-element.59.cot1.own1, bf16[5,32,128]{2,1,0:T(8,128)(2,1)S(1)} %get-tuple-element.70.own2, ...), custom_call_target="tpu_custom_call" | custom-call | flops 94371840 | bytes 9445376 | tf_op jit(solution)/shard_map/pallas_call | solution.py:512
  61.8 1.6 %collective-permute-done.19.refs_1_ = bf16[192,128]{1,0:T(8,128)(2,1)S(1)} collective-permute-done((bf16[192,128]{1,0:T(8,128)(2,1)S(1)}, bf16[192,128]{1,0:T(8,128)(2,1)S(1)}, u32[]{:S(2)}, u32[]{:S(2)}) %collective-permute-start.19) | collective-permute-done | bytes 49184 | tf_op jit(solution)/shard_map/ppermute | solution.py:632
  63.4 3.1 %collective-permute-start.20 = (f32[192,128]{1,0:T(8,128)S(1)}, f32[192,128]{1,0:T(8,128)S(1)}, u32[]{:S(2)}, u32[]{:S(2)}) collective-permute-start(f32[192,128]{1,0:T(8,128)S(1)} %shard_map.88), channel_id=1, source_target_pairs={{0,32},{32,0},{64,96},{96,64},{128,160},{160,128},{192,224},{224,1... | collective-permute-start | bytes 294920 | tf_op jit(solution)/shard_map/ppermute | solution.py:503
  66.6 0.9 %collective-permute-done.20 = f32[192,128]{1,0:T(8,128)S(1)} collective-permute-done((f32[192,128]{1,0:T(8,128)S(1)}, f32[192,128]{1,0:T(8,128)S(1)}, u32[]{:S(2)}, u32[]{:S(2)}) %collective-permute-start.20) | collective-permute-done | bytes 98336 | tf_op jit(solution)/shard_map/ppermute | solution.py:503
  67.5 0.7 %maximum_multiply_fusion = f32[384,128]{1,0:T(8,128)} fusion(f32[192,128]{1,0:T(8,128)S(1)} %get-tuple-element.84, f32[192,128]{1,0:T(8,128)S(1)} %get-tuple-element.83), kind=kLoop, calls=%fused_computation | loop fusion | flops 98304 | bytes 393216 | tf_op jit(solution)/shard_map/mul | solution.py:638
  (6 shorter events, 0.1 us)
Async XLA Ops:
  1.8 20.7 %collective-permute-start.2 = (bf16[119,16,128]{2,1,0:T(8,128)(2,1)S(1)}, bf16[119,16,128]{2,1,0:T(8,128)(2,1)S(1)}, u32[]{:S(2)}, u32[]{:S(2)}) collective-permute-start(bf16[119,16,128]{2,1,0:T(8,128)(2,1)S(1)} %get-tuple-element.49), channel_id=1, source_target_pairs={{0,28},{4,8},{8,4},{12,16},{16,12},{20,24},{24,20},{28,0},{1,29},{... | collective-permute-start | bytes 1462280 | tf_op jit(solution)/shard_map/ppermute | solution.py:559
  2.5 20.0 %collective-permute-start.4 = (bf16[119,16,128]{2,1,0:T(8,128)(2,1)S(1)}, bf16[119,16,128]{2,1,0:T(8,128)(2,1)S(1)}, u32[]{:S(2)}, u32[]{:S(2)}) collective-permute-start(bf16[119,16,128]{2,1,0:T(8,128)(2,1)S(1)} %get-tuple-element.51), channel_id=1, source_target_pairs={{0,4},{4,0},{8,12},{12,8},{16,20},{20,16},{24,28},{28,24},{32,36},... | collective-permute-start | bytes 1462280 | tf_op jit(solution)/shard_map/ppermute | solution.py:559
  6.4 16.0 %collective-permute-start.1 = (bf16[2,18,16,128]{3,2,1,0:T(8,128)(2,1)S(1)}, bf16[2,18,16,128]{3,2,1,0:T(8,128)(2,1)S(1)}, u32[]{:S(2)}, u32[]{:S(2)}) collective-permute-start(bf16[2,18,16,128]{3,2,1,0:T(8,128)(2,1)S(1)} %get-tuple-element.48), channel_id=1, source_target_pairs={{32,60},{36,40},{40,36},{44,48},{48,44},{52,56},{56,52},{60,32},{6... | collective-permute-start | bytes 442376 | tf_op jit(solution)/shard_map/ppermute | solution.py:559
  16.8 5.6 %collective-permute-start = (bf16[2,5,16,128]{3,2,1,0:T(8,128)(2,1)S(1)}, bf16[2,5,16,128]{3,2,1,0:T(8,128)(2,1)S(1)}, u32[]{:S(2)}, u32[]{:S(2)}) collective-permute-start(bf16[2,5,16,128]{3,2,1,0:T(8,128)(2,1)S(1)} %get-tuple-element.47), channel_id=1, source_target_pairs={{128,156},{132,136},{136,132},{140,144},{144,140},{148,152},{152,1... | collective-permute-start | bytes 122888 | tf_op jit(solution)/shard_map/ppermute | solution.py:559
  17.5 5.0 %collective-permute-start.3 = (bf16[2,5,16,128]{3,2,1,0:T(8,128)(2,1)S(1)}, bf16[2,5,16,128]{3,2,1,0:T(8,128)(2,1)S(1)}, u32[]{:S(2)}, u32[]{:S(2)}) collective-permute-start(bf16[2,5,16,128]{3,2,1,0:T(8,128)(2,1)S(1)} %get-tuple-element.50), channel_id=1, source_target_pairs={{64,68},{68,64},{72,76},{76,72},{80,84},{84,80},{88,92},{92,88},{9... | collective-permute-start | bytes 122888 | tf_op jit(solution)/shard_map/ppermute | solution.py:559
  22.9 8.0 %collective-permute-start.6 = (bf16[2,144,128]{2,1,0:T(8,128)(2,1)S(1)}, bf16[2,144,128]{2,1,0:T(8,128)(2,1)S(1)}, u32[]{:S(2)}, u32[]{:S(2)}) collective-permute-start(bf16[2,144,128]{2,1,0:T(8,128)(2,1)S(1)} %get-tuple-element.63), channel_id=1, source_target_pairs={{32,64},{64,32},{96,128},{128,96},{160,192},{192,160},{33,65},{65,... | collective-permute-start | bytes 221192 | tf_op jit(solution)/shard_map/ppermute | solution.py:584
  28.7 2.1 %collective-permute-start.5 = (bf16[2,128,128]{2,1,0:T(8,128)(2,1)S(1)}, bf16[2,128,128]{2,1,0:T(8,128)(2,1)S(1)}, u32[]{:S(2)}, u32[]{:S(2)}) collective-permute-start(bf16[2,128,128]{2,1,0:T(8,128)(2,1)S(1)} %get-tuple-element.62), channel_id=1, source_target_pairs={{0,32},{32,0},{64,96},{96,64},{128,160},{160,128},{192,224},{224,1... | collective-permute-start | bytes 196616 | tf_op jit(solution)/shard_map/ppermute | solution.py:583
  30.9 7.9 %copy-start = (bf16[3,128,128]{2,1,0:T(8,128)(2,1)S(1)}, bf16[3,128,128]{2,1,0:T(8,128)(2,1)}, u32[]{:S(2)}) copy-start(bf16[3,128,128]{2,1,0:T(8,128)(2,1)} %weight.3) | copy-start | bytes 294916
  32.2 2.5 %collective-permute-start.7 = (f32[192,128]{1,0:T(8,128)S(1)}, f32[192,128]{1,0:T(8,128)S(1)}, u32[]{:S(2)}, u32[]{:S(2)}) collective-permute-start(f32[192,128]{1,0:T(8,128)S(1)} %get-tuple-element.67), channel_id=1, source_target_pairs={{0,32},{32,0},{64,96},{96,64},{128,160},{160,128},{192,224},{224,1... | collective-permute-start | bytes 294920 | tf_op jit(solution)/shard_map/ppermute | solution.py:503
  34.8 5.3 %collective-permute-start.10 = (bf16[192,128]{1,0:T(8,128)(2,1)S(1)}, bf16[192,128]{1,0:T(8,128)(2,1)S(1)}, u32[]{:S(2)}, u32[]{:S(2)}) collective-permute-start(bf16[192,128]{1,0:T(8,128)(2,1)S(1)} %get-tuple-element.73.refs_0_), channel_id=1, source_target_pairs={{0,1},{1,0},{2,3},{3,2},{4,5},{5,4},{6,7},{7,6},{8,9},{9,8},{10,11... | collective-permute-start | bytes 147464 | tf_op jit(solution)/shard_map/ppermute | solution.py:503
  36.1 4.9 %collective-permute-start.11 = (bf16[192,128]{1,0:T(8,128)(2,1)S(1)}, bf16[192,128]{1,0:T(8,128)(2,1)S(1)}, u32[]{:S(2)}, u32[]{:S(2)}) collective-permute-start(bf16[192,128]{1,0:T(8,128)(2,1)S(1)} %get-tuple-element.73.refs_0_), channel_id=1, source_target_pairs={{0,2},{1,3},{2,0},{3,1},{4,6},{5,7},{6,4},{7,5},{8,10},{9,11},{10,... | collective-permute-start | bytes 147464 | tf_op jit(solution)/shard_map/ppermute | solution.py:503
  38.8 4.2 %collective-permute-start.12 = (bf16[192,128]{1,0:T(8,128)(2,1)S(1)}, bf16[192,128]{1,0:T(8,128)(2,1)S(1)}, u32[]{:S(2)}, u32[]{:S(2)}) collective-permute-start(bf16[192,128]{1,0:T(8,128)(2,1)S(1)} %get-tuple-element.73.refs_0_), channel_id=1, source_target_pairs={{0,3},{1,2},{2,1},{3,0},{4,7},{5,6},{6,5},{7,4},{8,11},{9,10},{10,... | collective-permute-start | bytes 147464 | tf_op jit(solution)/shard_map/ppermute | solution.py:503
  43.0 9.1 %collective-permute-start.13 = (bf16[192,128]{1,0:T(8,128)(2,1)S(1)}, bf16[192,128]{1,0:T(8,128)(2,1)S(1)}, u32[]{:S(2)}, u32[]{:S(2)}) collective-permute-start(bf16[192,128]{1,0:T(8,128)(2,1)S(1)} %shard_map.83.refs_0_), channel_id=1, source_target_pairs={{0,4},{4,0},{8,12},{12,8},{16,20},{20,16},{24,28},{28,24},{1,5},{5... | collective-permute-start | bytes 147464 | tf_op jit(solution)/shard_map/ppermute | solution.py:503
  43.2 8.8 %collective-permute-start.14 = (bf16[192,128]{1,0:T(8,128)(2,1)S(1)}, bf16[192,128]{1,0:T(8,128)(2,1)S(1)}, u32[]{:S(2)}, u32[]{:S(2)}) collective-permute-start(bf16[192,128]{1,0:T(8,128)(2,1)S(1)} %shard_map.83.refs_0_), channel_id=1, source_target_pairs={{0,8},{4,12},{8,0},{12,4},{16,24},{20,28},{24,16},{28,20},{1,9},{5... | collective-permute-start | bytes 147464 | tf_op jit(solution)/shard_map/ppermute | solution.py:503
  44.6 7.5 %collective-permute-start.15 = (bf16[192,128]{1,0:T(8,128)(2,1)S(1)}, bf16[192,128]{1,0:T(8,128)(2,1)S(1)}, u32[]{:S(2)}, u32[]{:S(2)}) collective-permute-start(bf16[192,128]{1,0:T(8,128)(2,1)S(1)} %shard_map.83.refs_0_), channel_id=1, source_target_pairs={{0,12},{4,8},{8,4},{12,0},{16,28},{20,24},{24,20},{28,16},{1,13},{... | collective-permute-start | bytes 147464 | tf_op jit(solution)/shard_map/ppermute | solution.py:503
  47.1 8.7 %collective-permute-start.9 = (bf16[2,144,128]{2,1,0:T(8,128)(2,1)S(1)}, bf16[2,144,128]{2,1,0:T(8,128)(2,1)S(1)}, u32[]{:S(2)}, u32[]{:S(2)}) collective-permute-start(bf16[2,144,128]{2,1,0:T(8,128)(2,1)S(1)} %get-tuple-element.72), channel_id=1, source_target_pairs={{32,64},{64,32},{96,128},{128,96},{160,192},{192,160},{33,65},{65,... | collective-permute-start | bytes 221192 | tf_op jit(solution)/shard_map/ppermute | solution.py:591
  52.0 3.8 %collective-permute-start.8 = (bf16[2,128,128]{2,1,0:T(8,128)(2,1)S(1)}, bf16[2,128,128]{2,1,0:T(8,128)(2,1)S(1)}, u32[]{:S(2)}, u32[]{:S(2)}) collective-permute-start(bf16[2,128,128]{2,1,0:T(8,128)(2,1)S(1)} %get-tuple-element.71), channel_id=1, source_target_pairs={{0,32},{32,0},{64,96},{96,64},{128,160},{160,128},{192,224},{224,1... | collective-permute-start | bytes 196616 | tf_op jit(solution)/shard_map/ppermute | solution.py:590
  52.1 6.0 %collective-permute-start.16 = (bf16[192,128]{1,0:T(8,128)(2,1)S(1)}, bf16[192,128]{1,0:T(8,128)(2,1)S(1)}, u32[]{:S(2)}, u32[]{:S(2)}) collective-permute-start(bf16[192,128]{1,0:T(8,128)(2,1)S(1)} %get-tuple-element.75.refs_0_), channel_id=1, source_target_pairs={{0,64},{32,96},{64,0},{96,32},{128,192},{160,224},{192,128},{224,1... | collective-permute-start | bytes 147464 | tf_op jit(solution)/shard_map/ppermute | solution.py:503
  52.3 5.9 %collective-permute-start.17 = (bf16[192,128]{1,0:T(8,128)(2,1)S(1)}, bf16[192,128]{1,0:T(8,128)(2,1)S(1)}, u32[]{:S(2)}, u32[]{:S(2)}) collective-permute-start(bf16[192,128]{1,0:T(8,128)(2,1)S(1)} %get-tuple-element.75.refs_0_), channel_id=1, source_target_pairs={{0,128},{32,160},{64,192},{96,224},{128,0},{160,32},{192,64},{224,... | collective-permute-start | bytes 147464 | tf_op jit(solution)/shard_map/ppermute | solution.py:503
  52.3 5.8 %collective-permute-start.18 = (bf16[192,128]{1,0:T(8,128)(2,1)S(1)}, bf16[192,128]{1,0:T(8,128)(2,1)S(1)}, u32[]{:S(2)}, u32[]{:S(2)}) collective-permute-start(bf16[192,128]{1,0:T(8,128)(2,1)S(1)} %get-tuple-element.75.refs_0_), channel_id=1, source_target_pairs={{0,192},{32,224},{64,128},{96,160},{128,64},{160,96},{192,0},{224,... | collective-permute-start | bytes 147464 | tf_op jit(solution)/shard_map/ppermute | solution.py:503
  58.2 5.2 %collective-permute-start.19 = (bf16[192,128]{1,0:T(8,128)(2,1)S(1)}, bf16[192,128]{1,0:T(8,128)(2,1)S(1)}, u32[]{:S(2)}, u32[]{:S(2)}) collective-permute-start(bf16[192,128]{1,0:T(8,128)(2,1)S(1)} %get-tuple-element.81.refs_0_), channel_id=1, source_target_pairs={{0,144},{4,148},{8,152},{12,156},{16,128},{20,132},{24,136},{28,14... | collective-permute-start | bytes 147464 | tf_op jit(solution)/shard_map/ppermute | solution.py:632
  63.4 4.1 %collective-permute-start.20 = (f32[192,128]{1,0:T(8,128)S(1)}, f32[192,128]{1,0:T(8,128)S(1)}, u32[]{:S(2)}, u32[]{:S(2)}) collective-permute-start(f32[192,128]{1,0:T(8,128)S(1)} %shard_map.88), channel_id=1, source_target_pairs={{0,32},{32,0},{64,96},{96,64},{128,160},{160,128},{192,224},{224,1... | collective-permute-start | bytes 294920 | tf_op jit(solution)/shard_map/ppermute | solution.py:503

commit v9 on v8

--- a/solution.py
+++ b/solution.py
@@ -141,9 +141,9 @@
         def _():
             loads = []
             for which, source in enumerate((field, cot)):
-                for part in range(3):
-                    at = pl.ds(part * 30, 30)
-                    sem = sems.at[6 + which * 3 + part]
+                for part in range(5):
+                    at = pl.ds(part * 18, 18)
+                    sem = sems.at[6 + which * 5 + part]
                     loads.append(pltpu.make_async_copy(source.at[0, at], whole.at[which, at], sem))
             for load in loads:
                 load.start()
@@ -535,7 +535,7 @@
     polar = shape((119, ROWS, CHAN))
     scratch = [
         pltpu.VMEM((2, COLS, ROWS, CHAN), BF16),
-        pltpu.SemaphoreType.DMA((12,)),
+        pltpu.SemaphoreType.DMA((16,)),
     ]
     messages = call(
         pack_kernel,

time: 68.5 us -> 68.5 us (level)
  no operation moved by 1% of the time
where the time goes in v9:
time: 68.5 us; the launch traced here: 68.2 us
  starting transfers between devices  44.3 us (65%)
  Pallas kernels  15.9 us (23%)
  waiting for transfers between devices  6.38 us (9%)
  between operations  0.9 us (1%)
  other arithmetic  0.71 us (1%)
    ppermute x11, starting transfers between devices, flip(): lax.ppermute(x, axis, [(i, i ^ bit) for i in range(lax.axis_size(axis))])  16.5 us
    ppermute x5, starting transfers between devices, body(): got[index] = lax.ppermute(messages[index], LL, targets[index])  16.3 us
    pallas_call x13, Pallas kernels, call(): pl.pallas_call(kernel, out_shape=outs, in_specs=[SMEM] * len(scalars) + [...  15.9 us
    ppermute x1, starting transfers between devices, body(): halo_b = lax.ppermute(lat_b, 'lat', pairs_of_lat(1))  5.8 us
    ppermute x1, starting transfers between devices, body(): cot_halo_b = lax.ppermute(lat_b, 'lat', pairs_of_lat(1))  4.86 us
    ppermute x11, waiting for transfers between devices, flip(): lax.ppermute(x, axis, [(i, i ^ bit) for i in range(lax.axis_size(axis))])  4.77 us
    ppermute x1, waiting for transfers between devices, body(): step = lax.ppermute(mine, LL, z_pairs())  1.59 us
  transfers between devices with their start and end apart: 21, of which 5 were waited for; matrix products, arithmetic and copies ran while one was open for 0% of the time, Pallas kernels for 19%

profile of v9, /device:TPU:1, one launch (start us, length us, event | category | flops | bytes accessed | tf_op | source)
XLA Modules:
  0.0 68.2 jit_solution(4340747882925893151)
XLA Ops:
  0.6 1.2 %shard_map.77 = (bf16[2,5,16,128]{3,2,1,0:T(8,128)(2,1)S(1)}, bf16[2,18,16,128]{3,2,1,0:T(8,128)(2,1)S(1)}, bf16[119,16,128]{2,1,0:T(8,128)(2,1)S(1)}, bf16[2,5,...) custom-call(bf16[1,90,16,128]{3,2,1,0:T(8,128)(2,1)} %bitcast.8, bf16[1,90,16,128]{3,2,1,0:T(8,128)(2,1)} %bitcast.10), custom_call_target="tpu_custom_call" | custom-call | bytes 1941504 | tf_op jit(solution)/shard_map/pallas_call | solution.py:512
  1.8 0.7 %collective-permute-start.2 = (bf16[119,16,128]{2,1,0:T(8,128)(2,1)S(1)}, bf16[119,16,128]{2,1,0:T(8,128)(2,1)S(1)}, u32[]{:S(2)}, u32[]{:S(2)}) collective-permute-start(bf16[119,16,128]{2,1,0:T(8,128)(2,1)S(1)} %get-tuple-element.49), channel_id=1, source_target_pairs={{0,28},{4,8},{8,4},{12,16},{16,12},{20,24},{24,20},{28,0},{1,29},{... | collective-permute-start | bytes 1462280 | tf_op jit(solution)/shard_map/ppermute | solution.py:559
  2.5 3.9 %collective-permute-start.4 = (bf16[119,16,128]{2,1,0:T(8,128)(2,1)S(1)}, bf16[119,16,128]{2,1,0:T(8,128)(2,1)S(1)}, u32[]{:S(2)}, u32[]{:S(2)}) collective-permute-start(bf16[119,16,128]{2,1,0:T(8,128)(2,1)S(1)} %get-tuple-element.51), channel_id=1, source_target_pairs={{0,4},{4,0},{8,12},{12,8},{16,20},{20,16},{24,28},{28,24},{32,36},... | collective-permute-start | bytes 1462280 | tf_op jit(solution)/shard_map/ppermute | solution.py:559
  6.5 10.4 %collective-permute-start.1 = (bf16[2,18,16,128]{3,2,1,0:T(8,128)(2,1)S(1)}, bf16[2,18,16,128]{3,2,1,0:T(8,128)(2,1)S(1)}, u32[]{:S(2)}, u32[]{:S(2)}) collective-permute-start(bf16[2,18,16,128]{3,2,1,0:T(8,128)(2,1)S(1)} %get-tuple-element.48), channel_id=1, source_target_pairs={{32,60},{36,40},{40,36},{44,48},{48,44},{52,56},{56,52},{60,32},{6... | collective-permute-start | bytes 442376 | tf_op jit(solution)/shard_map/ppermute | solution.py:559
  16.8 0.7 collective-permute-start
  17.5 0.7 collective-permute-start.3
  18.2 4.3 %shard_map.76 = (bf16[16,128,128]{2,1,0:T(8,128)(2,1)S(1)}, bf16[16,128,128]{2,1,0:T(8,128)(2,1)S(1)}, bf16[5760,256]{1,0:T(8,128)(2,1)S(1)}, bf16[5760,256]{1,0...) custom-call(bf16[1,90,16,128]{3,2,1,0:T(8,128)(2,1)} %bitcast.9, ...), custom_call_target="tpu_custom_call" | custom-call | flops 200000000 | bytes 10796544 | tf_op jit(solution)/shard_map/pallas_call | solution.py:512
  22.4 0.0 collective-permute-done.few_a
  22.4 0.0 collective-permute-done.3.few_b
  22.5 0.0 collective-permute-done.1.second_a
  22.5 0.0 collective-permute-done.2.polar_a
  22.5 0.0 collective-permute-done.4.polar_b
  22.5 0.4 shard_map.78
  22.9 5.8 %collective-permute-start.6 = (bf16[2,144,128]{2,1,0:T(8,128)(2,1)S(1)}, bf16[2,144,128]{2,1,0:T(8,128)(2,1)S(1)}, u32[]{:S(2)}, u32[]{:S(2)}) collective-permute-start(bf16[2,144,128]{2,1,0:T(8,128)(2,1)S(1)} %get-tuple-element.63), channel_id=1, source_target_pairs={{32,64},{64,32},{96,128},{128,96},{160,192},{192,160},{33,65},{65,... | collective-permute-start | bytes 221192 | tf_op jit(solution)/shard_map/ppermute | solution.py:584
  28.7 0.1 collective-permute-start.5
  28.8 2.0 %shard_map.79 = (bf16[1152,384]{1,0:T(8,128)(2,1)S(1)}, f32[384,128]{1,0:T(8,128)S(1)}, f32[1152,128]{1,0:T(8,128)S(1)}, bf16[2,128,128]{2,1,0:T(8,128)(2,1)S(1)}, bf16[2,144,128]{2,1,0:T(8,128)(2,1)S(1)}) custom-call(f32[5,3,128]{2,1,0:T(4,128)S(1)} %get-tuple-element.43.amps, f32[4608,128]{1,0:T(8,128)S(1)} %get-tuple-element.44.tie.center, ...), custom_call_target="tpu_custom_call" | custom-call | flops 566231040 | bytes 12943360 | tf_op jit(solution)/shard_map/pallas_call | solution.py:512
  30.9 0.0 collective-permute-done.5.halo_a
  30.9 0.0 collective-permute-done.6.halo_b
  30.9 0.0 copy-start
  30.9 1.3 %shard_map.80 = (bf16[384,384]{1,0:T(8,128)(2,1)S(1)}, f32[192,128]{1,0:T(8,128)S(1)}, f32[192,128]{1,0:T(8,128)S(1)}) custom-call(f32[5,3,128]{2,1,0:T(4,128)S(1)} %get-tuple-element.43.amps, f32[1152,128]{1,0:T(8,128)S(1)} %get-tuple-element.61.ends, bf16[5760,256]{1,0:T(8,128)(2,1)S(1)} %get-tuple-element.55.shape0, ...), custom_call_target="tpu_custom_call" | custom-call | flops 188743680 | bytes 7839744 | tf_op jit(solution)/shard_map/pallas_call | solution.py:512
  32.2 1.6 %collective-permute-start.7 = (f32[192,128]{1,0:T(8,128)S(1)}, f32[192,128]{1,0:T(8,128)S(1)}, u32[]{:S(2)}, u32[]{:S(2)}) collective-permute-start(f32[192,128]{1,0:T(8,128)S(1)} %get-tuple-element.67), channel_id=1, source_target_pairs={{0,32},{32,0},{64,96},{96,64},{128,160},{160,128},{192,224},{224,1... | collective-permute-start | bytes 294920 | tf_op jit(solution)/shard_map/ppermute | solution.py:503
  33.8 0.9 %collective-permute-done.7.refs_1_ = f32[192,128]{1,0:T(8,128)S(1)} collective-permute-done((f32[192,128]{1,0:T(8,128)S(1)}, f32[192,128]{1,0:T(8,128)S(1)}, u32[]{:S(2)}, u32[]{:S(2)}) %collective-permute-start.7) | collective-permute-done | bytes 98336 | tf_op jit(solution)/shard_map/ppermute | solution.py:503
  34.8 1.4 %collective-permute-start.10 = (bf16[192,128]{1,0:T(8,128)(2,1)S(1)}, bf16[192,128]{1,0:T(8,128)(2,1)S(1)}, u32[]{:S(2)}, u32[]{:S(2)}) collective-permute-start(bf16[192,128]{1,0:T(8,128)(2,1)S(1)} %get-tuple-element.73.refs_0_), channel_id=1, source_target_pairs={{0,1},{1,0},{2,3},{3,2},{4,5},{5,4},{6,7},{7,6},{8,9},{9,8},{10,11... | collective-permute-start | bytes 147464 | tf_op jit(solution)/shard_map/ppermute | solution.py:503
  36.2 2.6 %collective-permute-start.11 = (bf16[192,128]{1,0:T(8,128)(2,1)S(1)}, bf16[192,128]{1,0:T(8,128)(2,1)S(1)}, u32[]{:S(2)}, u32[]{:S(2)}) collective-permute-start(bf16[192,128]{1,0:T(8,128)(2,1)S(1)} %get-tuple-element.73.refs_0_), channel_id=1, source_target_pairs={{0,2},{1,3},{2,0},{3,1},{4,6},{5,7},{6,4},{7,5},{8,10},{9,11},{10,... | collective-permute-start | bytes 147464 | tf_op jit(solution)/shard_map/ppermute | solution.py:503
  38.8 0.0 collective-permute-start.12
  38.8 0.0 copy-done
  38.8 1.3 %shard_map.82 = (bf16[1,90,16,128]{3,2,1,0:T(8,128)(2,1)}, f32[8,128]{1,0:T(8,128)S(1)}) custom-call(bf16[1152,384]{1,0:T(8,128)(2,1)S(1)} %get-tuple-element.60.inner, bf16[384,384]{1,0:T(8,128)(2,1)S(1)} %get-tuple-element.65.outer, bf16[384,128]{1,0:T(8,128)(2,1)S(1)} %bitcast.7, f32[8,128]{1,0:T(8,128)S(1)} %get-tuple-element.68.before), custom_call_target="tpu_custom_call" | custom-call | flops 150994944 | bytes 1654784 | tf_op jit(solution)/shard_map/pallas_call | solution.py:512
  40.1 0.0 collective-permute-done.10.refs_1_
  40.1 1.0 %collective-permute-done.11.refs_2_ = bf16[192,128]{1,0:T(8,128)(2,1)S(1)} collective-permute-done((bf16[192,128]{1,0:T(8,128)(2,1)S(1)}, bf16[192,128]{1,0:T(8,128)(2,1)S(1)}, u32[]{:S(2)}, u32[]{:S(2)}) %collective-permute-start.11) | collective-permute-done | bytes 49184 | tf_op jit(solution)/shard_map/ppermute | solution.py:503
  41.1 1.9 %collective-permute-done.12.refs_3_ = bf16[192,128]{1,0:T(8,128)(2,1)S(1)} collective-permute-done((bf16[192,128]{1,0:T(8,128)(2,1)S(1)}, bf16[192,128]{1,0:T(8,128)(2,1)S(1)}, u32[]{:S(2)}, u32[]{:S(2)}) %collective-permute-start.12) | collective-permute-done | bytes 49184 | tf_op jit(solution)/shard_map/ppermute | solution.py:503
  43.0 0.3 collective-permute-start.13
  43.3 1.4 %collective-permute-start.14 = (bf16[192,128]{1,0:T(8,128)(2,1)S(1)}, bf16[192,128]{1,0:T(8,128)(2,1)S(1)}, u32[]{:S(2)}, u32[]{:S(2)}) collective-permute-start(bf16[192,128]{1,0:T(8,128)(2,1)S(1)} %shard_map.83.refs_0_), channel_id=1, source_target_pairs={{0,8},{4,12},{8,0},{12,4},{16,24},{20,28},{24,16},{28,20},{1,9},{5... | collective-permute-start | bytes 147464 | tf_op jit(solution)/shard_map/ppermute | solution.py:503
  44.6 2.5 %collective-permute-start.15 = (bf16[192,128]{1,0:T(8,128)(2,1)S(1)}, bf16[192,128]{1,0:T(8,128)(2,1)S(1)}, u32[]{:S(2)}, u32[]{:S(2)}) collective-permute-start(bf16[192,128]{1,0:T(8,128)(2,1)S(1)} %shard_map.83.refs_0_), channel_id=1, source_target_pairs={{0,12},{4,8},{8,4},{12,0},{16,28},{20,24},{24,20},{28,16},{1,13},{... | collective-permute-start | bytes 147464 | tf_op jit(solution)/shard_map/ppermute | solution.py:503
  47.1 4.9 %collective-permute-start.9 = (bf16[2,144,128]{2,1,0:T(8,128)(2,1)S(1)}, bf16[2,144,128]{2,1,0:T(8,128)(2,1)S(1)}, u32[]{:S(2)}, u32[]{:S(2)}) collective-permute-start(bf16[2,144,128]{2,1,0:T(8,128)(2,1)S(1)} %get-tuple-element.72), channel_id=1, source_target_pairs={{32,64},{64,32},{96,128},{128,96},{160,192},{192,160},{33,65},{65,... | collective-permute-start | bytes 221192 | tf_op jit(solution)/shard_map/ppermute | solution.py:591
  52.0 0.1 collective-permute-start.8
  52.1 0.0 collective-permute-done.13.refs_1_
  52.1 0.0 collective-permute-done.14.refs_2_
  52.1 0.0 collective-permute-done.15.refs_3_
  52.1 0.2 collective-permute-start.16
  52.3 0.0 collective-permute-start.17
  52.3 3.4 %collective-permute-start.18 = (bf16[192,128]{1,0:T(8,128)(2,1)S(1)}, bf16[192,128]{1,0:T(8,128)(2,1)S(1)}, u32[]{:S(2)}, u32[]{:S(2)}) collective-permute-start(bf16[192,128]{1,0:T(8,128)(2,1)S(1)} %get-tuple-element.75.refs_0_), channel_id=1, source_target_pairs={{0,192},{32,224},{64,128},{96,160},{128,64},{160,96},{192,0},{224,... | collective-permute-start | bytes 147464 | tf_op jit(solution)/shard_map/ppermute | solution.py:503
  55.8 0.0 collective-permute-done.8.halo_a
  55.8 0.0 collective-permute-done.9.halo_b
  55.8 2.4 %shard_map.85 = (f32[1,90,16,128]{3,2,1,0:T(8,128)S(1)}, f32[8,128]{1,0:T(8,128)S(1)}) custom-call(f32[5,3,128]{2,1,0:T(4,128)S(1)} %get-tuple-element.43.amps, bf16[16,128,128]{2,1,0:T(8,128)(2,1)S(1)} %get-tuple-element.58.cot.own0, bf16[16,128,128]{2,1,0:T(8,128)(2,1)S(1)} %get-tuple-element.59.cot1.own1, bf16[5,32,128]{2,1,0:T(8,128)(2,1)S(1)} %get-tuple-element.70.own2, ...), custom_call_target="tpu_custom_call" | custom-call | flops 94371840 | bytes 8708096 | tf_op jit(solution)/shard_map/pallas_call | solution.py:512
  58.2 0.0 collective-permute-done.16.refs_1_
  58.2 0.0 collective-permute-done.17.refs_2_
  58.2 0.0 collective-permute-done.18.refs_3_
  58.2 0.7 %collective-permute-start.19 = (bf16[192,128]{1,0:T(8,128)(2,1)S(1)}, bf16[192,128]{1,0:T(8,128)(2,1)S(1)}, u32[]{:S(2)}, u32[]{:S(2)}) collective-permute-start(bf16[192,128]{1,0:T(8,128)(2,1)S(1)} %get-tuple-element.81.refs_0_), channel_id=1, source_target_pairs={{0,144},{4,148},{8,152},{12,156},{16,128},{20,132},{24,136},{28,14... | collective-permute-start | bytes 147464 | tf_op jit(solution)/shard_map/ppermute | solution.py:632
  58.9 2.9 %shard_map.87 = (f32[1,90,16,128]{3,2,1,0:T(8,128)}, f32[8,128]{1,0:T(8,128)S(1)}) custom-call(f32[5,3,128]{2,1,0:T(4,128)S(1)} %get-tuple-element.43.amps, bf16[16,128,128]{2,1,0:T(8,128)(2,1)S(1)} %get-tuple-element.58.cot.own0, bf16[16,128,128]{2,1,0:T(8,128)(2,1)S(1)} %get-tuple-element.59.cot1.own1, bf16[5,32,128]{2,1,0:T(8,128)(2,1)S(1)} %get-tuple-element.70.own2, ...), custom_call_target="tpu_custom_call" | custom-call | flops 94371840 | bytes 9445376 | tf_op jit(solution)/shard_map/pallas_call | solution.py:512
  61.9 1.6 %collective-permute-done.19.refs_1_ = bf16[192,128]{1,0:T(8,128)(2,1)S(1)} collective-permute-done((bf16[192,128]{1,0:T(8,128)(2,1)S(1)}, bf16[192,128]{1,0:T(8,128)(2,1)S(1)}, u32[]{:S(2)}, u32[]{:S(2)}) %collective-permute-start.19) | collective-permute-done | bytes 49184 | tf_op jit(solution)/shard_map/ppermute | solution.py:632
  63.5 3.1 %collective-permute-start.20 = (f32[192,128]{1,0:T(8,128)S(1)}, f32[192,128]{1,0:T(8,128)S(1)}, u32[]{:S(2)}, u32[]{:S(2)}) collective-permute-start(f32[192,128]{1,0:T(8,128)S(1)} %shard_map.88), channel_id=1, source_target_pairs={{0,32},{32,0},{64,96},{96,64},{128,160},{160,128},{192,224},{224,1... | collective-permute-start | bytes 294920 | tf_op jit(solution)/shard_map/ppermute | solution.py:503
  66.6 0.9 %collective-permute-done.20 = f32[192,128]{1,0:T(8,128)S(1)} collective-permute-done((f32[192,128]{1,0:T(8,128)S(1)}, f32[192,128]{1,0:T(8,128)S(1)}, u32[]{:S(2)}, u32[]{:S(2)}) %collective-permute-start.20) | collective-permute-done | bytes 98336 | tf_op jit(solution)/shard_map/ppermute | solution.py:503
  67.5 0.7 %maximum_multiply_fusion = f32[384,128]{1,0:T(8,128)} fusion(f32[192,128]{1,0:T(8,128)S(1)} %get-tuple-element.84, f32[192,128]{1,0:T(8,128)S(1)} %get-tuple-element.83), kind=kLoop, calls=%fused_computation | loop fusion | flops 98304 | bytes 393216 | tf_op jit(solution)/shard_map/mul | solution.py:638
  (6 shorter events, 0.1 us)
Async XLA Ops:
  1.8 20.7 %collective-permute-start.2 = (bf16[119,16,128]{2,1,0:T(8,128)(2,1)S(1)}, bf16[119,16,128]{2,1,0:T(8,128)(2,1)S(1)}, u32[]{:S(2)}, u32[]{:S(2)}) collective-permute-start(bf16[119,16,128]{2,1,0:T(8,128)(2,1)S(1)} %get-tuple-element.49), channel_id=1, source_target_pairs={{0,28},{4,8},{8,4},{12,16},{16,12},{20,24},{24,20},{28,0},{1,29},{... | collective-permute-start | bytes 1462280 | tf_op jit(solution)/shard_map/ppermute | solution.py:559
  2.5 20.0 %collective-permute-start.4 = (bf16[119,16,128]{2,1,0:T(8,128)(2,1)S(1)}, bf16[119,16,128]{2,1,0:T(8,128)(2,1)S(1)}, u32[]{:S(2)}, u32[]{:S(2)}) collective-permute-start(bf16[119,16,128]{2,1,0:T(8,128)(2,1)S(1)} %get-tuple-element.51), channel_id=1, source_target_pairs={{0,4},{4,0},{8,12},{12,8},{16,20},{20,16},{24,28},{28,24},{32,36},... | collective-permute-start | bytes 1462280 | tf_op jit(solution)/shard_map/ppermute | solution.py:559
  6.5 16.0 %collective-permute-start.1 = (bf16[2,18,16,128]{3,2,1,0:T(8,128)(2,1)S(1)}, bf16[2,18,16,128]{3,2,1,0:T(8,128)(2,1)S(1)}, u32[]{:S(2)}, u32[]{:S(2)}) collective-permute-start(bf16[2,18,16,128]{3,2,1,0:T(8,128)(2,1)S(1)} %get-tuple-element.48), channel_id=1, source_target_pairs={{32,60},{36,40},{40,36},{44,48},{48,44},{52,56},{56,52},{60,32},{6... | collective-permute-start | bytes 442376 | tf_op jit(solution)/shard_map/ppermute | solution.py:559
  16.8 5.6 %collective-permute-start = (bf16[2,5,16,128]{3,2,1,0:T(8,128)(2,1)S(1)}, bf16[2,5,16,128]{3,2,1,0:T(8,128)(2,1)S(1)}, u32[]{:S(2)}, u32[]{:S(2)}) collective-permute-start(bf16[2,5,16,128]{3,2,1,0:T(8,128)(2,1)S(1)} %get-tuple-element.47), channel_id=1, source_target_pairs={{128,156},{132,136},{136,132},{140,144},{144,140},{148,152},{152,1... | collective-permute-start | bytes 122888 | tf_op jit(solution)/shard_map/ppermute | solution.py:559
  17.5 5.0 %collective-permute-start.3 = (bf16[2,5,16,128]{3,2,1,0:T(8,128)(2,1)S(1)}, bf16[2,5,16,128]{3,2,1,0:T(8,128)(2,1)S(1)}, u32[]{:S(2)}, u32[]{:S(2)}) collective-permute-start(bf16[2,5,16,128]{3,2,1,0:T(8,128)(2,1)S(1)} %get-tuple-element.50), channel_id=1, source_target_pairs={{64,68},{68,64},{72,76},{76,72},{80,84},{84,80},{88,92},{92,88},{9... | collective-permute-start | bytes 122888 | tf_op jit(solution)/shard_map/ppermute | solution.py:559
  22.9 8.0 %collective-permute-start.6 = (bf16[2,144,128]{2,1,0:T(8,128)(2,1)S(1)}, bf16[2,144,128]{2,1,0:T(8,128)(2,1)S(1)}, u32[]{:S(2)}, u32[]{:S(2)}) collective-permute-start(bf16[2,144,128]{2,1,0:T(8,128)(2,1)S(1)} %get-tuple-element.63), channel_id=1, source_target_pairs={{32,64},{64,32},{96,128},{128,96},{160,192},{192,160},{33,65},{65,... | collective-permute-start | bytes 221192 | tf_op jit(solution)/shard_map/ppermute | solution.py:584
  28.7 2.2 %collective-permute-start.5 = (bf16[2,128,128]{2,1,0:T(8,128)(2,1)S(1)}, bf16[2,128,128]{2,1,0:T(8,128)(2,1)S(1)}, u32[]{:S(2)}, u32[]{:S(2)}) collective-permute-start(bf16[2,128,128]{2,1,0:T(8,128)(2,1)S(1)} %get-tuple-element.62), channel_id=1, source_target_pairs={{0,32},{32,0},{64,96},{96,64},{128,160},{160,128},{192,224},{224,1... | collective-permute-start | bytes 196616 | tf_op jit(solution)/shard_map/ppermute | solution.py:583
  30.9 7.9 %copy-start = (bf16[3,128,128]{2,1,0:T(8,128)(2,1)S(1)}, bf16[3,128,128]{2,1,0:T(8,128)(2,1)}, u32[]{:S(2)}) copy-start(bf16[3,128,128]{2,1,0:T(8,128)(2,1)} %weight.3) | copy-start | bytes 294916
  32.2 2.5 %collective-permute-start.7 = (f32[192,128]{1,0:T(8,128)S(1)}, f32[192,128]{1,0:T(8,128)S(1)}, u32[]{:S(2)}, u32[]{:S(2)}) collective-permute-start(f32[192,128]{1,0:T(8,128)S(1)} %get-tuple-element.67), channel_id=1, source_target_pairs={{0,32},{32,0},{64,96},{96,64},{128,160},{160,128},{192,224},{224,1... | collective-permute-start | bytes 294920 | tf_op jit(solution)/shard_map/ppermute | solution.py:503
  34.8 5.3 %collective-permute-start.10 = (bf16[192,128]{1,0:T(8,128)(2,1)S(1)}, bf16[192,128]{1,0:T(8,128)(2,1)S(1)}, u32[]{:S(2)}, u32[]{:S(2)}) collective-permute-start(bf16[192,128]{1,0:T(8,128)(2,1)S(1)} %get-tuple-element.73.refs_0_), channel_id=1, source_target_pairs={{0,1},{1,0},{2,3},{3,2},{4,5},{5,4},{6,7},{7,6},{8,9},{9,8},{10,11... | collective-permute-start | bytes 147464 | tf_op jit(solution)/shard_map/ppermute | solution.py:503
  36.2 4.9 %collective-permute-start.11 = (bf16[192,128]{1,0:T(8,128)(2,1)S(1)}, bf16[192,128]{1,0:T(8,128)(2,1)S(1)}, u32[]{:S(2)}, u32[]{:S(2)}) collective-permute-start(bf16[192,128]{1,0:T(8,128)(2,1)S(1)} %get-tuple-element.73.refs_0_), channel_id=1, source_target_pairs={{0,2},{1,3},{2,0},{3,1},{4,6},{5,7},{6,4},{7,5},{8,10},{9,11},{10,... | collective-permute-start | bytes 147464 | tf_op jit(solution)/shard_map/ppermute | solution.py:503
  38.8 4.2 %collective-permute-start.12 = (bf16[192,128]{1,0:T(8,128)(2,1)S(1)}, bf16[192,128]{1,0:T(8,128)(2,1)S(1)}, u32[]{:S(2)}, u32[]{:S(2)}) collective-permute-start(bf16[192,128]{1,0:T(8,128)(2,1)S(1)} %get-tuple-element.73.refs_0_), channel_id=1, source_target_pairs={{0,3},{1,2},{2,1},{3,0},{4,7},{5,6},{6,5},{7,4},{8,11},{9,10},{10,... | collective-permute-start | bytes 147464 | tf_op jit(solution)/shard_map/ppermute | solution.py:503
  43.0 9.1 %collective-permute-start.13 = (bf16[192,128]{1,0:T(8,128)(2,1)S(1)}, bf16[192,128]{1,0:T(8,128)(2,1)S(1)}, u32[]{:S(2)}, u32[]{:S(2)}) collective-permute-start(bf16[192,128]{1,0:T(8,128)(2,1)S(1)} %shard_map.83.refs_0_), channel_id=1, source_target_pairs={{0,4},{4,0},{8,12},{12,8},{16,20},{20,16},{24,28},{28,24},{1,5},{5... | collective-permute-start | bytes 147464 | tf_op jit(solution)/shard_map/ppermute | solution.py:503
  43.3 8.8 %collective-permute-start.14 = (bf16[192,128]{1,0:T(8,128)(2,1)S(1)}, bf16[192,128]{1,0:T(8,128)(2,1)S(1)}, u32[]{:S(2)}, u32[]{:S(2)}) collective-permute-start(bf16[192,128]{1,0:T(8,128)(2,1)S(1)} %shard_map.83.refs_0_), channel_id=1, source_target_pairs={{0,8},{4,12},{8,0},{12,4},{16,24},{20,28},{24,16},{28,20},{1,9},{5... | collective-permute-start | bytes 147464 | tf_op jit(solution)/shard_map/ppermute | solution.py:503
  44.6 7.5 %collective-permute-start.15 = (bf16[192,128]{1,0:T(8,128)(2,1)S(1)}, bf16[192,128]{1,0:T(8,128)(2,1)S(1)}, u32[]{:S(2)}, u32[]{:S(2)}) collective-permute-start(bf16[192,128]{1,0:T(8,128)(2,1)S(1)} %shard_map.83.refs_0_), channel_id=1, source_target_pairs={{0,12},{4,8},{8,4},{12,0},{16,28},{20,24},{24,20},{28,16},{1,13},{... | collective-permute-start | bytes 147464 | tf_op jit(solution)/shard_map/ppermute | solution.py:503
  47.1 8.7 %collective-permute-start.9 = (bf16[2,144,128]{2,1,0:T(8,128)(2,1)S(1)}, bf16[2,144,128]{2,1,0:T(8,128)(2,1)S(1)}, u32[]{:S(2)}, u32[]{:S(2)}) collective-permute-start(bf16[2,144,128]{2,1,0:T(8,128)(2,1)S(1)} %get-tuple-element.72), channel_id=1, source_target_pairs={{32,64},{64,32},{96,128},{128,96},{160,192},{192,160},{33,65},{65,... | collective-permute-start | bytes 221192 | tf_op jit(solution)/shard_map/ppermute | solution.py:591
  52.0 3.8 %collective-permute-start.8 = (bf16[2,128,128]{2,1,0:T(8,128)(2,1)S(1)}, bf16[2,128,128]{2,1,0:T(8,128)(2,1)S(1)}, u32[]{:S(2)}, u32[]{:S(2)}) collective-permute-start(bf16[2,128,128]{2,1,0:T(8,128)(2,1)S(1)} %get-tuple-element.71), channel_id=1, source_target_pairs={{0,32},{32,0},{64,96},{96,64},{128,160},{160,128},{192,224},{224,1... | collective-permute-start | bytes 196616 | tf_op jit(solution)/shard_map/ppermute | solution.py:590
  52.1 6.0 %collective-permute-start.16 = (bf16[192,128]{1,0:T(8,128)(2,1)S(1)}, bf16[192,128]{1,0:T(8,128)(2,1)S(1)}, u32[]{:S(2)}, u32[]{:S(2)}) collective-permute-start(bf16[192,128]{1,0:T(8,128)(2,1)S(1)} %get-tuple-element.75.refs_0_), channel_id=1, source_target_pairs={{0,64},{32,96},{64,0},{96,32},{128,192},{160,224},{192,128},{224,1... | collective-permute-start | bytes 147464 | tf_op jit(solution)/shard_map/ppermute | solution.py:503
  52.3 5.9 %collective-permute-start.17 = (bf16[192,128]{1,0:T(8,128)(2,1)S(1)}, bf16[192,128]{1,0:T(8,128)(2,1)S(1)}, u32[]{:S(2)}, u32[]{:S(2)}) collective-permute-start(bf16[192,128]{1,0:T(8,128)(2,1)S(1)} %get-tuple-element.75.refs_0_), channel_id=1, source_target_pairs={{0,128},{32,160},{64,192},{96,224},{128,0},{160,32},{192,64},{224,... | collective-permute-start | bytes 147464 | tf_op jit(solution)/shard_map/ppermute | solution.py:503
  52.3 5.8 %collective-permute-start.18 = (bf16[192,128]{1,0:T(8,128)(2,1)S(1)}, bf16[192,128]{1,0:T(8,128)(2,1)S(1)}, u32[]{:S(2)}, u32[]{:S(2)}) collective-permute-start(bf16[192,128]{1,0:T(8,128)(2,1)S(1)} %get-tuple-element.75.refs_0_), channel_id=1, source_target_pairs={{0,192},{32,224},{64,128},{96,160},{128,64},{160,96},{192,0},{224,... | collective-permute-start | bytes 147464 | tf_op jit(solution)/shard_map/ppermute | solution.py:503
  58.2 5.2 %collective-permute-start.19 = (bf16[192,128]{1,0:T(8,128)(2,1)S(1)}, bf16[192,128]{1,0:T(8,128)(2,1)S(1)}, u32[]{:S(2)}, u32[]{:S(2)}) collective-permute-start(bf16[192,128]{1,0:T(8,128)(2,1)S(1)} %get-tuple-element.81.refs_0_), channel_id=1, source_target_pairs={{0,144},{4,148},{8,152},{12,156},{16,128},{20,132},{24,136},{28,14... | collective-permute-start | bytes 147464 | tf_op jit(solution)/shard_map/ppermute | solution.py:632
  63.5 4.1 %collective-permute-start.20 = (f32[192,128]{1,0:T(8,128)S(1)}, f32[192,128]{1,0:T(8,128)S(1)}, u32[]{:S(2)}, u32[]{:S(2)}) collective-permute-start(f32[192,128]{1,0:T(8,128)S(1)} %shard_map.88), channel_id=1, source_target_pairs={{0,32},{32,0},{64,96},{96,64},{128,160},{160,128},{192,224},{224,1... | collective-permute-start | bytes 294920 | tf_op jit(solution)/shard_map/ppermute | solution.py:503
